TPU v7x, 32 devices: a whole 2x2x4 slice. The times are simulated.
32 devices in a mesh: dp: 8 (over z, y), sp: 4 (over x, core).
Axes of the slice: x: 2, y: 2, z: 4, core: 2. Of those that a mesh axis runs over, the one named last changes fastest.
Arguments:
- inputs: bfloat16 [8, 512, 1024], P('dp', 'sp'), may hold values from -6 to 6
- qkv_weight: bfloat16 [1024, 3072], P('dp'), may hold values from -0.1875 to 0.1875
- out_weight: bfloat16 [1024, 1024], P('dp'), may hold values from -1 to 1
- in_weight: bfloat16 [1024, 4096], P('dp'), may hold values from -0.1875 to 0.1875
- down_weight: bfloat16 [4096, 1024], P('dp'), may hold values from -0.09375 to 0.09375
- norm_gain: float32 [2, 1024], replicated, may hold values from 0.5 to 1.5
- norm_shift: float32 [2, 1024], replicated, may hold values from -1.8 to 1.8
- bias_table: float32 [16, 32], replicated, may hold values from -4 to 4
- segment_ids: int32 [8, 512], P('dp'), may hold values from 0 to 2, as said below
- bucket_index: int32 [512], replicated, may hold values from 0 to 31, as said below
- cotangent: bfloat16 [8, 512, 1024], P('dp', 'sp'), may hold values from -6 to 6
Outputs:
- output: bfloat16 [8, 512, 1024], P('dp', 'sp')
- input_grad: float32 [8, 512, 1024], P('dp', 'sp')
- query_key_value_gradient: float32 [1024, 3072], P('dp')
- out_grad: float32 [1024, 1024], P('dp')
- in_grad: float32 [1024, 4096], P('dp')
- down_grad: float32 [4096, 1024], P('dp')
- gain_grad: float32 [2, 1024], P(None, 'dp')
- shift_grad: float32 [2, 1024], P(None, 'dp')
- table_grad: float32 [512], P('dp')
Inputs may be any that keep to these rules, and one draw needn't show every extreme that they name: `segment_ids`: in each group the item ids never fall along the sequence, and item 1 begins before position 128 and ends at or after position 384. `bucket_index`: never falls as the distance grows; equals the distance below 16.
All inputs are finite; a program needn't handle non-finite values.
Results may differ from a plain program's by a relative error of at most 0.014.
Values may be sent and summed in bfloat16 or wider, within the bound.
No kernel may reach another device: no remote copies, remote signals or barrier semaphores. Data moves between devices by JAX's collectives and lax.ppermute only.
A program may use at most 384 MiB of HBM per device.

v0:
```python
import math

import jax
import jax.numpy as jnp
from jax import lax
from jax.sharding import PartitionSpec as P

QBLOCK = 512


largest_score = lax.Precision.HIGHEST


def layer_norm(values, gain, shift):
    average = jnp.mean(values, axis=-1, keepdims=True)
    centred = values - average
    inverse = lax.rsqrt(jnp.mean(centred * centred, axis=-1, keepdims=True) + 1e-05)
    normed = centred * inverse
    return (normed * gain + shift, normed, inverse)


def norm_back(upstream, normed, inverse, gain):
    scaled = upstream * gain
    centre_term = jnp.mean(scaled, axis=-1, keepdims=True)
    slope_term = jnp.mean(scaled * normed, axis=-1, keepdims=True)
    return inverse * (scaled - centre_term - normed * slope_term)


def matmul_plain(left, right):
    return jnp.dot(left, right, preferred_element_type=jnp.float32)


def matmul_inner(left, right):
    return lax.dot_general(
        left, right, (((0,), (0,)), ((), ())), preferred_element_type=jnp.float32
    )


def matmul_outer(left, right):
    return lax.dot_general(
        left, right, (((1,), (1,)), ((), ())), preferred_element_type=jnp.float32
    )


def block_scores(query_block, key_heads, block_start, bias_rows, seg_all, scale):
    seq_len = key_heads.shape[0]
    row_index = block_start + lax.broadcasted_iota(jnp.int32, (QBLOCK, seq_len), 0)
    col_index = lax.broadcasted_iota(jnp.int32, (QBLOCK, seq_len), 1)
    distance = row_index - col_index
    allowed = (distance >= 0) & (seg_all[:, None] == seg_all[None, :])
    distance = jnp.maximum(distance, 0)
    bias_block = jnp.take(bias_rows, distance, axis=1)
    raw_scores = jnp.einsum(
        "qhd,khd->hqk", query_block, key_heads, preferred_element_type=jnp.float32
    )
    scores = jnp.where(allowed[None], raw_scores * scale + bias_block, -1e30)
    return (scores, distance)


def bucket_sums(grad_scores, distance, bucket_index, bucket_count):
    heads_here = grad_scores.shape[0]
    seq_len = grad_scores.shape[2]
    piece_width = math.gcd(seq_len, 128)
    piece_count = seq_len // piece_width
    bucket_block = jnp.take(bucket_index, distance, axis=0)
    score_pieces = jnp.moveaxis(
        grad_scores.reshape(heads_here, QBLOCK, piece_count, piece_width), 2, 0
    )
    bucket_pieces = jnp.moveaxis(bucket_block.reshape(QBLOCK, piece_count, piece_width), 1, 0)
    bucket_iota = lax.broadcasted_iota(jnp.int32, (bucket_count, QBLOCK, piece_width), 0)

    def add_piece(running_total, piece_pair):
        score_portion, bucket_portion = piece_pair
        indicator_matrix = (bucket_portion[None, :, :] == bucket_iota).astype(jnp.float32)
        return (
            running_total
            + jnp.einsum("tyv,lyv->tl", score_portion, indicator_matrix, precision=largest_score),
            None,
        )

    running_total, unused = lax.scan(
        add_piece, jnp.zeros((heads_here, bucket_count), jnp.float32), (score_pieces, bucket_pieces)
    )
    return running_total


def on_device(
    inputs,
    qkv_weight,
    out_weight,
    in_weight,
    down_weight,
    norm_gain,
    norm_shift,
    bias_table,
    segment_ids,
    bucket_index,
    cotangent,
):
    tokens = inputs[0].astype(jnp.float32)
    tok_count = tokens.shape[0]
    width = tokens.shape[1]
    sp_count = lax.axis_size("sp")
    head_total = bias_table.shape[0]
    bucket_count = bias_table.shape[1]
    heads_here = head_total // sp_count
    head_dim = width // head_total
    scale = head_dim ** (-0.5)
    seg_all = segment_ids[0]
    seq_len = seg_all.shape[0]
    block_starts = jnp.arange(seq_len // QBLOCK, dtype=jnp.int32) * QBLOCK
    full_qkv, full_out, full_in, full_down = (
        lax.all_gather(qkv_weight, "dp", axis=0, tiled=True),
        lax.all_gather(out_weight, "dp", axis=0, tiled=True),
        lax.all_gather(in_weight, "dp", axis=0, tiled=True),
        lax.all_gather(down_weight, "dp", axis=0, tiled=True),
    )
    normed_out_one, first_normalized, inverse_one = layer_norm(tokens, norm_gain[0], norm_shift[0])
    first_activation = normed_out_one.astype(jnp.bfloat16)
    qkv_rows = (
        matmul_plain(first_activation, full_qkv).astype(jnp.bfloat16).reshape(tok_count, 3, width)
    )
    qkv_heads = lax.all_to_all(qkv_rows, "sp", split_axis=2, concat_axis=0, tiled=True)
    query_heads = qkv_heads[:, 0].reshape(seq_len, heads_here, head_dim)
    key_heads = qkv_heads[:, 1].reshape(seq_len, heads_here, head_dim)
    value_heads = qkv_heads[:, 2].reshape(seq_len, heads_here, head_dim)
    head_offset = lax.axis_index("sp") * heads_here
    table_here = lax.dynamic_slice_in_dim(bias_table, head_offset, heads_here, 0)
    bucket_onehot = (
        bucket_index[:, None] == lax.broadcasted_iota(jnp.int32, (seq_len, bucket_count), 1)
    ).astype(jnp.float32)
    bias_rows = lax.dot_general(
        table_here, bucket_onehot, (((1,), (1,)), ((), ())), precision=largest_score
    )

    def forward_block(block_start):
        scores, distance = block_scores(
            query_heads, key_heads, block_start, bias_rows, seg_all, scale
        )
        largest = jnp.max(scores, axis=-1, keepdims=True)
        row_total = jnp.sum(jnp.exp(scores - largest), axis=-1, keepdims=True)
        log_total = largest + jnp.log(row_total)
        weights_block = jnp.exp(scores - log_total).astype(jnp.bfloat16)
        mixed_block = jnp.einsum(
            "hqk,khd->qhd", weights_block, value_heads, preferred_element_type=jnp.float32
        )
        return (mixed_block.astype(jnp.bfloat16), log_total[..., 0])

    mixed_blocks, log_totals = lax.map(forward_block, block_starts)
    attn_heads = mixed_blocks.reshape(seq_len, heads_here * head_dim)
    attn_rows = lax.all_to_all(attn_heads, "sp", split_axis=0, concat_axis=1, tiled=True)
    residual = tokens + matmul_plain(attn_rows, full_out)
    normed_out_two, normed_two, inverse_two = layer_norm(residual, norm_gain[1], norm_shift[1])
    act_two = normed_out_two.astype(jnp.bfloat16)
    hidden = matmul_plain(act_two, full_in)
    activated, gelu_back = jax.vjp(jax.nn.gelu, hidden)
    fed_rows = activated.astype(jnp.bfloat16)
    output = (residual + matmul_plain(fed_rows, full_down)).astype(jnp.bfloat16)
    upstream = cotangent[0].astype(jnp.float32)
    grad_branch = upstream.astype(jnp.bfloat16)
    grad_down = matmul_inner(fed_rows, grad_branch)
    grad_fed = matmul_outer(grad_branch, full_down)
    grad_hidden = gelu_back(grad_fed)[0].astype(jnp.bfloat16)
    grad_in = matmul_inner(act_two, grad_hidden)
    grad_act_two = matmul_outer(grad_hidden, full_in)
    gain_two = jnp.sum(grad_act_two * normed_two, axis=0)
    shift_two = jnp.sum(grad_act_two, axis=0)
    grad_resid = upstream + norm_back(grad_act_two, normed_two, inverse_two, norm_gain[1])
    grad_attn_out = grad_resid.astype(jnp.bfloat16)
    grad_out_weight = matmul_inner(attn_rows, grad_attn_out)
    grad_attn_rows = matmul_outer(grad_attn_out, full_out).astype(jnp.bfloat16)
    grad_heads = lax.all_to_all(
        grad_attn_rows, "sp", split_axis=1, concat_axis=0, tiled=True
    ).reshape(seq_len, heads_here, head_dim)

    def backward_block(carry, block_input):
        grad_keys, grad_values, table_carry = carry
        block_start, log_total = block_input
        scores, distance = block_scores(
            query_heads, key_heads, block_start, bias_rows, seg_all, scale
        )
        probs = jnp.exp(scores - log_total[:, :, None])
        grad_values = grad_values + jnp.einsum(
            "hqk,qhd->khd",
            probs.astype(jnp.bfloat16),
            grad_heads,
            preferred_element_type=jnp.float32,
        )
        grad_probs = jnp.einsum(
            "qhd,khd->hqk", grad_heads, value_heads, preferred_element_type=jnp.float32
        )
        row_term = jnp.sum(probs * grad_probs, axis=-1, keepdims=True)
        grad_scores = probs * (grad_probs - row_term)
        table_carry = table_carry + bucket_sums(grad_scores, distance, bucket_index, bucket_count)
        grad_raw = (grad_scores * scale).astype(jnp.bfloat16)
        grad_query = jnp.einsum(
            "hqk,khd->qhd", grad_raw, key_heads, preferred_element_type=jnp.float32
        )
        grad_keys = grad_keys + jnp.einsum(
            "hqk,qhd->khd", grad_raw, query_heads, preferred_element_type=jnp.float32
        )
        return ((grad_keys, grad_values, table_carry), grad_query)

    zero_heads = jnp.zeros((seq_len, heads_here, head_dim), jnp.float32)
    zero_table = jnp.zeros((heads_here, bucket_count), jnp.float32)
    final_carry, grad_queries = lax.scan(
        backward_block, (zero_heads, zero_heads, zero_table), (block_starts, log_totals)
    )
    grad_keys, grad_values, table_here_grad = final_carry
    grad_queries = grad_queries.reshape(seq_len, heads_here, head_dim)
    grad_qkv_heads = (
        jnp.stack([grad_queries, grad_keys, grad_values], axis=1)
        .reshape(seq_len, 3, heads_here * head_dim)
        .astype(jnp.bfloat16)
    )
    grad_qkv_rows = lax.all_to_all(
        grad_qkv_heads, "sp", split_axis=0, concat_axis=2, tiled=True
    ).reshape(tok_count, 3 * width)
    grad_qkv = matmul_inner(first_activation, grad_qkv_rows)
    grad_act_one = matmul_outer(grad_qkv_rows, full_qkv)
    gain_one = jnp.sum(grad_act_one * first_normalized, axis=0)
    shift_one = jnp.sum(grad_act_one, axis=0)
    grad_input = grad_resid + norm_back(grad_act_one, first_normalized, inverse_one, norm_gain[0])
    table_whole = lax.dynamic_update_slice_in_dim(
        jnp.zeros((head_total, bucket_count), jnp.float32), table_here_grad, head_offset, 0
    ).reshape(-1)
    gain_both = jnp.stack([gain_one, gain_two])
    shift_both = jnp.stack([shift_one, shift_two])
    part_qkv, part_out, part_in, part_down, part_gain, part_shift, part_table = (
        lax.psum_scatter(grad_qkv, "dp", scatter_dimension=0, tiled=True),
        lax.psum_scatter(grad_out_weight, "dp", scatter_dimension=0, tiled=True),
        lax.psum_scatter(grad_in, "dp", scatter_dimension=0, tiled=True),
        lax.psum_scatter(grad_down, "dp", scatter_dimension=0, tiled=True),
        lax.psum_scatter(gain_both, "dp", scatter_dimension=1, tiled=True),
        lax.psum_scatter(shift_both, "dp", scatter_dimension=1, tiled=True),
        lax.psum_scatter(table_whole, "dp", scatter_dimension=0, tiled=True),
    )
    sum_qkv, sum_out, sum_in, sum_down, sum_gain, sum_shift, sum_table = (
        lax.psum(part_qkv.astype(jnp.bfloat16), "sp").astype(jnp.float32),
        lax.psum(part_out.astype(jnp.bfloat16), "sp").astype(jnp.float32),
        lax.psum(part_in.astype(jnp.bfloat16), "sp").astype(jnp.float32),
        lax.psum(part_down.astype(jnp.bfloat16), "sp").astype(jnp.float32),
        lax.psum(part_gain.astype(jnp.bfloat16), "sp").astype(jnp.float32),
        lax.psum(part_shift.astype(jnp.bfloat16), "sp").astype(jnp.float32),
        lax.psum(part_table.astype(jnp.bfloat16), "sp").astype(jnp.float32),
    )
    return (
        output[None],
        grad_input[None],
        sum_qkv,
        sum_out,
        sum_in,
        sum_down,
        sum_gain,
        sum_shift,
        sum_table,
    )


def solution(mesh):
    in_specs = (
        P("dp", "sp", None),
        P("dp", None),
        P("dp", None),
        P("dp", None),
        P("dp", None),
        P(),
        P(),
        P(),
        P("dp", None),
        P(),
        P("dp", "sp", None),
    )
    out_specs = (
        P("dp", "sp", None),
        P("dp", "sp", None),
        P("dp", None),
        P("dp", None),
        P("dp", None),
        P("dp", None),
        P(None, "dp"),
        P(None, "dp"),
        P("dp"),
    )
    return jax.shard_map(
        on_device, mesh=mesh, in_specs=in_specs, out_specs=out_specs, check_vma=False
    )
```

profile of v0, /device:TPU:0, one launch (start us, length us, event | category | flops | bytes accessed | tf_op | source)
XLA Modules:
  0.0 4167.0 jit_solution(99987588731631294)
XLA Ops:
  10.1 1.2 copy.103
  11.8 100.2 %all-gather.5.cloned.1.call-done = bf16[1024,3072]{1,0:T(8,128)(2,1)} async-done(((bf16[128,3072]{1,0:T(8,128)(2,1)}), bf16[1024,3072]{1,0:T(8,128)(2,1)}) %all-gather.5.cloned.1.call-update) | async-done | bytes 6291472 | tf_op jit(solution)/shard_map/all_gather | solution.py:113
  112.0 3.9 convolution_convert_fusion
  116.3 1.7 copy.65
  118.0 3.5 all-to-all-start
  121.5 1.4 broadcast_clamp_fusion.1
  123.2 860.0 %gather_fusion.1 = f32[262144,4]{1,0:T(8,128)} fusion(f32[4,512]{0,1:T(8,128)S(1)} %fusion.81, s32[262144]{0:T(1024)S(1)} %broadcast_clamp_fusion.1), kind=kCustom, calls=%fused_computation.clone | custom fusion | bytes 9437184 | tf_op jit(solution)/shard_map/while/body/eval_jaxpr/jit(_take)/gather | solution.py:52
  983.2 71.7 %copy.75 = f32[512,512,4]{0,1,2:T(8,128)} copy(f32[512,512,4]{2,1,0:T(8,128)} %bitcast.11) | data formatting | bytes 8388608 | tf_op jit(solution)/shard_map/while/body/eval_jaxpr/jit(_take)/gather | solution.py:52
  1057.0 3.8 fusion.97
  1061.4 1.3 copy-done.3
  1064.3 3.4 all-to-all-start.1
  1068.2 5.5 all-to-all-done.1
  1073.7 2.2 fusion.98
  1076.2 4.8 fusion.93
  1081.0 7.8 fusion.21
  1088.9 3.5 multiply_reduce_fusion.1
  1092.8 2.7 fusion.82
  1095.5 2.4 convolution_convert_fusion.4
  1098.0 8.6 all_to_all.68
  1106.9 3.7 fusion.99
  1110.6 8.9 convolution_convert_fusion.3
  1119.5 1.9 copy.83
  1121.4 8.7 convolution_convert_fusion.2
  1130.2 2.0 copy.84
  1132.1 3.7 convolution_convert_fusion.1
  1135.8 1.3 copy.85
  1137.1 3.0 pad_maximum_fusion
  1140.2 16.9 all_to_all.69
  1157.0 1.0 copy.86
  1158.0 2.3 copy.87
  1160.3 7.6 fusion.64
  1168.2 9.4 fusion.92
  1178.6 8.1 fusion.67
  1187.2 1.1 broadcast_clamp_fusion
  1188.4 2754.8 %gather_fusion = s32[262144]{0:T(1024)} fusion(s32[512]{0:T(512)S(1)} %copy-done.2, s32[262144]{0:T(1024)} %broadcast_clamp_fusion), kind=kCustom, calls=%fused_computation.1 | custom fusion | bytes 3145728 | tf_op jit(solution)/shard_map/while/body/eval_jaxpr/jit(_take)/gather | solution.py:65
  3944.4 2.8 select_bitcast_fusion
  3947.2 5.8 fusion.25
  3953.2 2.4 fusion.47
  3955.6 1.0 copy.99
  3956.7 1.0 copy.97
  3958.1 7.3 subtract_multiply_fusion
  3965.4 6.9 copy.107
  3972.3 1.8 convert_element_type.121
  3974.1 2.4 convert_element_type.119
  3976.5 2.7 convert_element_type.123
  3979.2 2.7 convert_element_type.125
  3982.0 28.9 while.14
  3982.0 1.5 constant_dynamic-slice_fusion.2
  3983.6 5.6 fusion.129
  3989.2 1.5 constant_dynamic-slice_fusion.2
  3990.8 5.6 fusion.129
  3996.4 1.5 constant_dynamic-slice_fusion.2
  3998.0 5.6 fusion.129
  4003.6 1.5 constant_dynamic-slice_fusion.2
  4005.2 5.6 fusion.129
  4010.9 18.6 all-reduce
  4029.7 1.1 fusion.46
  4030.7 0.9 copy.100
  4031.6 49.2 %reduce-scatter.19.cloned.1.call-done = f32[128,2]{1,0:T(8,128)} async-done(((f32[1024,2]{1,0:T(8,128)}), f32[128,2]{1,0:T(8,128)}) %reduce-scatter.19.cloned.1.call-update) | async-done | bytes 1040
  4081.8 5.7 all-reduce.1
  4089.1 63.1 %all-reduce.5.cloned.1.call-done = (bf16[128,3072]{1,0:T(8,128)(2,1)}, bf16[128,1024]{1,0:T(8,128)(2,1)}, bf16[128,4096]{1,0:T(8,128)(2,1)}, bf16[512,1024]{1,0:T(8,128)(2,1)}) async-done(((bf16[128,3072]{1,0:T(8,128)(2,1)}, bf16[128,1024]{1,0:T(8,128)(2,1)}, bf16[128,4096]{1,0:T(8,128)(2,1)}, bf16[512,1024]{1,0:T(8,128)(2,1)}), (bf16[128,3072]{1,0:T(8,128)(2,1)}, bf16[128,1024]{1,0:T(8,128)(2,1)}, ...) | async-done | bytes 3145744 | tf_op jit(solution)/shard_map/psum | solution.py:239
  4152.2 2.8 convert_element_type.124
  4155.1 2.8 convert_element_type.126
  4157.9 1.3 convert_element_type.120
  (177 shorter events, 16.5 us)
Async XLA Ops:
  7.2 115.7 %copy-start = (f32[16,32]{1,0:T(8,128)S(1)}, f32[16,32]{1,0:T(8,128)}, u32[]{:S(2)}) copy-start(f32[16,32]{1,0:T(8,128)} %param.22) | copy-start | bytes 6148
  7.2 4.2 copy-start.7
  7.2 4.5 copy-start.40
  7.2 4.6 copy-start.41
  7.2 104.8 %all-gather.5.cloned.1.call-start = ((), (), s32[]{:S(2)}) async-start(), calls=%async_computation.10 | async-start | bytes 7077888 | tf_op jit(solution)/shard_map/all_gather | solution.py:113
  8.0 1060.3 %all-gather.7.cloned.1.call-start = ((), (), s32[]{:S(2)}) async-start(), calls=%async_computation.11 | async-start | bytes 2359296 | tf_op jit(solution)/shard_map/all_gather | solution.py:114
  8.7 1067.5 %all-gather.9.cloned.1.call-start = ((), (), s32[]{:S(2)}) async-start(), calls=%async_computation.12 | async-start | bytes 9437184 | tf_op jit(solution)/shard_map/all_gather | solution.py:115
  9.4 1071.6 %all-gather.11.cloned.1.call-start = ((), (), s32[]{:S(2)}) async-start(), calls=%async_computation.13 | async-start | bytes 9437184 | tf_op jit(solution)/shard_map/all_gather | solution.py:116
  11.5 1148.8 %copy-start.33 = (f32[128]{0:T(128)}, f32[128]{0:T(128)S(1)}, u32[]{:S(2)}) copy-start(f32[128]{0:T(128)S(1)} %broadcast_multiply_fusion.5) | copy-start | bytes 1540
  11.8 1148.6 %copy-start.35 = (f32[128]{0:T(128)}, f32[128]{0:T(128)S(1)}, u32[]{:S(2)}) copy-start(f32[128]{0:T(128)S(1)} %add_rsqrt_fusion.1) | copy-start | bytes 1540
  11.8 1148.5 %copy-start.28 = (f32[1,1024]{1,0:T(1,128)}, f32[1,1024]{1,0:T(1,128)S(1)}, u32[]{:S(2)}) copy-start(f32[1,1024]{1,0:T(1,128)S(1)} %get-tuple-element.157) | copy-start | bytes 12292
  115.9 7.0 copy-start.2
  118.0 938.0 %all-to-all-start = ((bf16[128,3,1024]{0,1,2:T(4,128)(2,1)}), bf16[128,3,1024]{0,1,2:T(4,128)(2,1)S(1)}, u32[]{:S(2)}, u32[]{:S(2)}) async-start(bf16[128,3,1024]{0,1,2:T(4,128)(2,1)} %copy.65), calls=%async_computation | async-start | bytes 2097152 | tf_op jit(solution)/shard_map/all_to_all | solution.py:123
  983.2 71.7 %copy-start.39 = (s32[1,512]{1,0:T(1,128)S(1)}, s32[1,512]{1,0:T(1,128)}, u32[]{:S(2)}) copy-start(s32[1,512]{1,0:T(1,128)} %param.23) | copy-start | bytes 6148
  1056.6 4.1 copy-start.26
  1056.8 3.9 copy-start.24
  1057.0 4.4 copy-start.14
  1060.7 1.9 copy-start.3
  1061.4 70.7 %copy-start.31 = (f32[4,512]{1,0:T(4,128)}, f32[4,512]{1,0:T(4,128)S(1)}, u32[]{:S(2)}) copy-start(f32[4,512]{1,0:T(4,128)S(1)} %log_add_fusion) | copy-start | bytes 24580
  1064.3 9.4 all-to-all-start.1
  1067.7 2904.6 %reduce-scatter.13.cloned.1.call-start = ((), (), s32[]{:S(2)}) async-start(), calls=%async_computation.15 | async-start | bytes 4718592 | tf_op jit(solution)/shard_map/reduce_scatter | solution.py:231
  1073.7 2.5 copy-start.19
  1075.9 92.3 %copy-start.5 = (f32[128,1024]{1,0:T(8,128)}, f32[128,1024]{1,0:T(8,128)S(1)}, u32[]{:S(2)}) copy-start(f32[128,1024]{1,0:T(8,128)S(1)} %get-tuple-element.163) | copy-start | bytes 1572868
  1076.2 4.8 copy-start.21
  1081.0 96.8 %copy-start.9 = (f32[128,4096]{1,0:T(8,128)}, f32[128,4096]{1,0:T(8,128)S(1)}, u32[]{:S(2)}) copy-start(f32[128,4096]{1,0:T(8,128)S(1)} %fusion.93) | copy-start | bytes 6291460
  1081.0 7.9 copy-start.4
  1088.9 3.6 copy-start.18
  1088.9 3.6 copy-start.22
  1088.9 3.8 copy-start.20
  1092.8 2.8 copy-start.11
  1095.5 2878.6 %reduce-scatter.11.cloned.1.call-start = ((), (), s32[]{:S(2)}) async-start(), calls=%async_computation.14 | async-start | bytes 14155776 | tf_op jit(solution)/shard_map/reduce_scatter | solution.py:230
  1106.9 25.2 copy-start.16
  1110.6 10.8 copy-start.25
  1167.9 2808.5 %reduce-scatter.15.cloned.1.call-start = ((), (), s32[]{:S(2)}) async-start(), calls=%async_computation.16 | async-start | bytes 18874368 | tf_op jit(solution)/shard_map/reduce_scatter | solution.py:232
  1177.7 0.9 copy-start.23
  1177.7 2801.5 %reduce-scatter.17.cloned.1.call-start = ((), (), s32[]{:S(2)}) async-start(), calls=%async_computation.17 | async-start | bytes 18874368 | tf_op jit(solution)/shard_map/reduce_scatter | solution.py:233
  1186.8 2843.9 %reduce-scatter.21.cloned.1.call-start = ((), (), s32[]{:S(2)}) async-start(), calls=%async_computation.19 | async-start | bytes 589824
  1188.4 2754.8 %copy-start.43 = (u32[32]{0:T(128)S(1)}, u32[32]{0:T(128)}, u32[]{:S(2)}) copy-start(u32[32]{0:T(128)} %constant.132) | copy-start | bytes 388
  1188.4 2758.8 %copy-start.6 = (f32[128,1024]{1,0:T(8,128)S(1)}, f32[128,1024]{1,0:T(8,128)}, u32[]{:S(2)}) copy-start(f32[128,1024]{1,0:T(8,128)} %copy-done.5) | copy-start | bytes 1572868
  1188.4 2758.8 %copy-start.10 = (f32[128,4096]{1,0:T(8,128)S(1)}, f32[128,4096]{1,0:T(8,128)}, u32[]{:S(2)}) copy-start(f32[128,4096]{1,0:T(8,128)} %copy-done.9) | copy-start | bytes 6291460
  3944.4 8.7 slice-start
  3947.2 5.9 slice-start.1
  3947.2 5.9 copy-start.8
  3947.2 5.9 copy-start.13
  3947.2 5.9 copy-start.29
  3947.2 5.9 copy-start.34
  3947.2 5.9 copy-start.36
  3953.1 2.4 copy-start.38
  3953.2 3.6 copy-start.37
  3953.2 4.9 copy-start.15
  3953.2 4.9 copy-start.17
  3953.2 4.9 copy-start.32
  3956.7 124.2 %reduce-scatter.19.cloned.1.call-start = ((), (), s32[]{:S(2)}) async-start(), calls=%async_computation.18 | async-start | bytes 589824
  3957.8 194.4 %all-reduce.5.cloned.1.call-start = ((), (), s32[]{:S(2)}) async-start(), calls=%async_computation.20 | async-start | bytes 6291456 | tf_op jit(solution)/shard_map/psum | solution.py:239
  3976.5 5.5 copy-start.42
  3981.9 47.7 %copy-start.12 = (f32[128,1024]{1,0:T(8,128)S(1)}, f32[128,1024]{1,0:T(8,128)}, u32[]{:S(2)}) copy-start(f32[128,1024]{1,0:T(8,128)} %copy-done.11) | copy-start | bytes 1572868
  4152.2 5.6 copy-start.27
  4152.2 7.8 copy-start.1
  4152.2 6.9 copy-start.30
Sparse Core Ops, SparseCore 0:
  10.2 101.7 all-gather.4
  114.1 47.4 all-gather.6
  163.8 123.4 all-gather.8
  289.2 123.0 all-gather.10
  1095.6 85.2 reduce-scatter.12
  1184.7 207.0 reduce-scatter.10
  1396.1 281.8 reduce-scatter.14
  1681.8 281.6 reduce-scatter.16
  3956.8 59.3 reduce-scatter.20
  4020.0 60.8 reduce-scatter.18
  4084.2 67.9 all-reduce.4
where the time goes:
time: 4180 us; the launch traced here: 4170 us
  local copies, waits for them, and re-layouts  3720 us (89%)
  waiting for transfers between devices  221 us (5%)
  matrix products  120 us (3%)
  blocking collectives  49.8 us (1%)
    gather x1, local copies, waits for them, and re-layouts, bucket_sums(): bucket_block = jnp.take(bucket_index, distance, axis=0)  2750 us
    gather x2, local copies, waits for them, and re-layouts, block_scores(): bias_block = jnp.take(bias_rows, distance, axis=1)  932 us
    all_gather x1, waiting for transfers between devices, on_device(): lax.all_gather(qkv_weight, 'dp', axis=0, tiled=True)  100 us
  transfers between devices with their start and end apart: 13, of which 4 were waited for; matrix products, arithmetic and copies ran while one was open for 92% of the time, Pallas kernels for 0%

commit v1 on v0

v1 whole, which is shorter than its diff:
```python
import functools

import jax
import jax.numpy as jnp
import numpy as np
from jax import lax
from jax.experimental import pallas as pl
from jax.experimental.pallas import tpu as pltpu
from jax.sharding import PartitionSpec as P

BLOCK = 128
NEG = -1e30
BF16 = jnp.bfloat16
F32 = jnp.float32


def dot(left, right, left_dim=1, right_dim=0):
    return lax.dot_general(
        left, right, (((left_dim,), (right_dim,)), ((), ())), preferred_element_type=F32
    )


def layer_norm(values, gain, shift):
    average = jnp.mean(values, axis=-1, keepdims=True)
    centred = values - average
    inverse = lax.rsqrt(jnp.mean(centred * centred, axis=-1, keepdims=True) + 1e-05)
    normed = centred * inverse
    return (normed * gain + shift, normed, inverse)


def norm_back(upstream, normed, inverse, gain):
    scaled = upstream * gain
    centre_term = jnp.mean(scaled, axis=-1, keepdims=True)
    slope_term = jnp.mean(scaled * normed, axis=-1, keepdims=True)
    return inverse * (scaled - centre_term - normed * slope_term)


def rank_at(position, count):
    position = lax.rem(position + 2 * count, count)
    return jnp.where(position < count // 2, 2 * position, 2 * (count - 1 - position) + 1)


def position_of(rank, count):
    return jnp.where(rank % 2 == 0, rank // 2, count - 1 - rank // 2)


def ring_pairs(count):
    order = list(range(0, count, 2)) + list(range(count - 1, 0, -2))
    forward = [(order[i], order[(i + 1) % count]) for i in range(count)]
    return forward, [(b, a) for a, b in forward]


def gather_dp(shard, count):
    if count != 8:
        return lax.all_gather(shard, "dp", axis=0)
    forward, backward = ring_pairs(count)
    me = lax.axis_index("dp")
    at = position_of(me, count)
    half = shard.shape[0] // 2
    whole = jnp.zeros((count,) + shard.shape, shard.dtype)
    whole = lax.dynamic_update_index_in_dim(whole, shard, me, 0)
    up = down = shard
    for step in range(1, count // 2):
        up = lax.ppermute(up, "dp", forward)
        down = lax.ppermute(down, "dp", backward)
        whole = lax.dynamic_update_index_in_dim(whole, up, rank_at(at - step, count), 0)
        whole = lax.dynamic_update_index_in_dim(whole, down, rank_at(at + step, count), 0)
    up = lax.ppermute(up[:half], "dp", forward)
    down = lax.ppermute(down[half:], "dp", backward)
    last = rank_at(at + count // 2, count)
    whole = lax.dynamic_update_slice(whole, up[None], (last, 0, 0))
    return lax.dynamic_update_slice(whole, down[None], (last, half, 0))


def scatter_dp(parts, count):
    if count != 8:
        return lax.psum_scatter(parts.astype(BF16), "dp", scatter_dimension=0).astype(F32)
    forward, backward = ring_pairs(count)
    me = lax.axis_index("dp")
    at = position_of(me, count)
    half = parts.shape[1] // 2

    def own(position):
        return lax.dynamic_index_in_dim(parts, rank_at(position, count), 0, keepdims=False).astype(F32)

    far = own(at + count // 2)
    up = lax.ppermute(far[:half].astype(BF16), "dp", forward)
    down = lax.ppermute(far[half:].astype(BF16), "dp", backward)
    for step in range(count // 2 - 1, 0, -1):
        for_up, for_down = own(at + step), own(at - step)
        if step == count // 2 - 1:
            for_up = for_up.at[:half].add(up.astype(F32))
            for_down = for_down.at[half:].add(down.astype(F32))
        else:
            for_up = for_up + up.astype(F32)
            for_down = for_down + down.astype(F32)
        up = lax.ppermute(for_up.astype(BF16), "dp", forward)
        down = lax.ppermute(for_down.astype(BF16), "dp", backward)
    return own(at) + up.astype(F32) + down.astype(F32)


def swap(values, bit):
    count = lax.axis_size("sp")
    return lax.ppermute(values, "sp", [(i, i ^ bit) for i in range(count)])


def gather_sp(piece):
    near = swap(piece, 1)
    far = swap(piece, 2)
    return [piece, near, far, swap(far, 1)]


def ordered(pieces):
    me = lax.axis_index("sp")
    whole = jnp.zeros((len(pieces),) + pieces[0].shape, pieces[0].dtype)
    for step, piece in enumerate(pieces):
        whole = lax.dynamic_update_index_in_dim(whole, piece, me ^ step, 0)
    return whole


def pick(stacked, step):
    return lax.dynamic_index_in_dim(stacked, lax.axis_index("sp") ^ step, 0, keepdims=False)


def exchange_sp(stacked):
    return ordered([pick(stacked, 0)] + [swap(pick(stacked, step), step) for step in (1, 2, 3)])


def reduce_sp(pieces):
    near = [swap(pieces[1].astype(BF16), 1), swap(pieces[3].astype(BF16), 1)]
    own = pieces[0] + near[0].astype(F32)
    far = pieces[2] + near[1].astype(F32)
    return own + swap(far.astype(BF16), 2).astype(F32)


def bias_kernel(reversed_ref, bias_ref):
    heads, diagonals, width = reversed_ref.shape
    for head in range(heads):
        for diagonal in range(diagonals):
            row = reversed_ref[head, diagonal : diagonal + 1, :]
            spread = jnp.broadcast_to(row, (BLOCK, width))
            rolled = pltpu.roll(spread, 0, 1, stride=1, stride_axis=0)
            bias_ref[head, diagonal] = rolled[:, :BLOCK]


def bias_blocks(reversed_rows):
    heads, diagonals, _ = reversed_rows.shape
    return pl.pallas_call(
        bias_kernel, out_shape=jax.ShapeDtypeStruct((heads, diagonals, BLOCK, BLOCK), F32)
    )(reversed_rows)


def mask_rows(index, seg_col_ref, seg_row_ref):
    width = (index + 1) * BLOCK
    same = seg_col_ref[index * BLOCK : width, :] == seg_row_ref[:, :width]
    row = index * BLOCK + lax.broadcasted_iota(jnp.int32, (BLOCK, width), 0)
    column = lax.broadcasted_iota(jnp.int32, (BLOCK, width), 1)
    return jnp.where(same & (row >= column), 0.0, NEG).astype(F32)


def half_mask(side):
    lane = lax.broadcasted_iota(jnp.int32, (1, BLOCK), 1)
    return (lane // (BLOCK // 2) == side).astype(F32).astype(BF16)


def score_rows(query, keys, bias_ref, head, index, mask):
    raw = dot(query, keys, 1, 1)
    bias = jnp.concatenate([bias_ref[head, index - block] for block in range(index + 1)], axis=1)
    return raw + bias + mask


def attend_kernel(scale, qkv_ref, bias_ref, seg_col_ref, seg_row_ref, attn_ref, log_ref):
    seq_len = qkv_ref.shape[0]
    columns = qkv_ref.shape[1] // 3
    lane = lax.broadcasted_iota(jnp.int32, (1, BLOCK), 1)
    for index in range(seq_len // BLOCK):
        rows = slice(index * BLOCK, (index + 1) * BLOCK)
        width = (index + 1) * BLOCK
        mask = mask_rows(index, seg_col_ref, seg_row_ref)
        logs = jnp.zeros((BLOCK, BLOCK), F32)
        for pair in range(columns // BLOCK):
            lanes = slice(pair * BLOCK, (pair + 1) * BLOCK)
            query = qkv_ref[rows, lanes] * scale
            keys = qkv_ref[:width, columns + pair * BLOCK : columns + (pair + 1) * BLOCK]
            values = qkv_ref[:width, 2 * columns + pair * BLOCK : 2 * columns + (pair + 1) * BLOCK]
            mixed = []
            for side in range(2):
                head = 2 * pair + side
                scores = score_rows(query * half_mask(side), keys, bias_ref, head, index, mask)
                largest = jnp.max(scores, axis=1, keepdims=True)
                weights = jnp.exp(scores - largest)
                total = jnp.sum(weights, axis=1, keepdims=True)
                mixed.append(dot(weights.astype(BF16), values) / total)
                logs = jnp.where(lane == head, largest + jnp.log(total), logs)
            attn_ref[rows, lanes] = jnp.where(lane < BLOCK // 2, mixed[0], mixed[1]).astype(BF16)
        log_ref[rows, :] = logs


def attend(qkv, bias, seg_col, seg_row, scale):
    seq_len = qkv.shape[0]
    return pl.pallas_call(
        functools.partial(attend_kernel, scale),
        out_shape=(
            jax.ShapeDtypeStruct((seq_len, qkv.shape[1] // 3), BF16),
            jax.ShapeDtypeStruct((seq_len, BLOCK), F32),
        ),
        compiler_params=pltpu.CompilerParams(vmem_limit_bytes=48 * 1024 * 1024),
    )(qkv, bias, seg_col, seg_row)


def attend_back_kernel(
    scale,
    qkv_ref,
    grad_ref,
    log_ref,
    bias_ref,
    seg_col_ref,
    seg_row_ref,
    grad_qkv_ref,
    sums_ref,
    key_acc,
    value_acc,
    diagonal_acc,
):
    seq_len = qkv_ref.shape[0]
    columns = qkv_ref.shape[1] // 3
    heads, diagonals = diagonal_acc.shape[:2]
    key_acc[...] = jnp.zeros_like(key_acc)
    value_acc[...] = jnp.zeros_like(value_acc)
    diagonal_acc[...] = jnp.zeros_like(diagonal_acc)
    for index in range(seq_len // BLOCK):
        rows = slice(index * BLOCK, (index + 1) * BLOCK)
        width = (index + 1) * BLOCK
        mask = mask_rows(index, seg_col_ref, seg_row_ref)
        for pair in range(columns // BLOCK):
            lanes = slice(pair * BLOCK, (pair + 1) * BLOCK)
            query = qkv_ref[rows, lanes] * scale
            keys = qkv_ref[:width, columns + pair * BLOCK : columns + (pair + 1) * BLOCK]
            values = qkv_ref[:width, 2 * columns + pair * BLOCK : 2 * columns + (pair + 1) * BLOCK]
            grad_rows = grad_ref[rows, lanes]
            grad_query = jnp.zeros((BLOCK, BLOCK), F32)
            for side in range(2):
                head = 2 * pair + side
                query_one = query * half_mask(side)
                grad_one = grad_rows * half_mask(side)
                scores = score_rows(query_one, keys, bias_ref, head, index, mask)
                probs = jnp.exp(scores - log_ref[rows, head : head + 1])
                grad_probs = dot(grad_one, values, 1, 1)
                row_term = jnp.sum(probs * grad_probs, axis=1, keepdims=True)
                grad_scores = probs * (grad_probs - row_term)
                for block in range(index + 1):
                    diagonal_acc[head, index - block] += grad_scores[
                        :, block * BLOCK : (block + 1) * BLOCK
                    ]
                grad_raw = grad_scores.astype(BF16)
                grad_query += dot(grad_raw, keys * half_mask(side))
                key_acc[:width, lanes] += dot(grad_raw, query_one, 0, 0)
                value_acc[:width, lanes] += dot(probs.astype(BF16), grad_one, 0, 0)
            grad_qkv_ref[rows, lanes] = (grad_query * scale).astype(BF16)
    grad_qkv_ref[:, columns : 2 * columns] = key_acc[...].astype(BF16)
    grad_qkv_ref[:, 2 * columns :] = value_acc[...].astype(BF16)
    row = lax.broadcasted_iota(jnp.int32, (BLOCK, BLOCK), 0)
    column = lax.broadcasted_iota(jnp.int32, (BLOCK, BLOCK), 1)
    flip = (row + column == BLOCK - 1).astype(F32)
    for head in range(heads):
        for diagonal in range(diagonals):
            block = lax.dot_general(
                diagonal_acc[head, diagonal],
                flip,
                (((1,), (0,)), ((), ())),
                precision=lax.Precision.HIGHEST,
                preferred_element_type=F32,
            )
            wide = jnp.concatenate([block, jnp.zeros_like(block)], axis=1)
            rolled = pltpu.roll(wide, 0, 1, stride=1, stride_axis=0)
            sums_ref[head, diagonal : diagonal + 1, :] = jnp.sum(rolled, axis=0, keepdims=True)


def attend_back(qkv, grad_heads, logs, bias, seg_col, seg_row, scale):
    seq_len = qkv.shape[0]
    columns = qkv.shape[1] // 3
    heads, diagonals = bias.shape[:2]
    return pl.pallas_call(
        functools.partial(attend_back_kernel, scale),
        out_shape=(
            jax.ShapeDtypeStruct(qkv.shape, BF16),
            jax.ShapeDtypeStruct((heads, diagonals, 2 * BLOCK), F32),
        ),
        scratch_shapes=[
            pltpu.VMEM((seq_len, columns), F32),
            pltpu.VMEM((seq_len, columns), F32),
            pltpu.VMEM((heads, diagonals, BLOCK, BLOCK), F32),
        ],
        compiler_params=pltpu.CompilerParams(vmem_limit_bytes=48 * 1024 * 1024),
    )(qkv, grad_heads, logs, bias, seg_col, seg_row)


def on_device(
    inputs,
    qkv_weight,
    out_weight,
    in_weight,
    down_weight,
    norm_gain,
    norm_shift,
    bias_table,
    segment_ids,
    bucket_index,
    cotangent,
):
    dp_count, sp_count = lax.axis_size("dp"), lax.axis_size("sp")
    me_sp = lax.axis_index("sp")
    tok_count, width = inputs.shape[1:]
    head_total, bucket_count = bias_table.shape
    heads_here = head_total // sp_count
    head_dim = width // head_total
    scale = head_dim ** (-0.5)
    seq_len = segment_ids.shape[1]
    rows_here = qkv_weight.shape[0]
    ff = in_weight.shape[1]
    ff_rows = ff // dp_count // sp_count
    part = width // sp_count

    def own_sp(stacked, axis):
        return lax.dynamic_index_in_dim(stacked, me_sp, axis, keepdims=False)

    qkv_part = own_sp(qkv_weight.reshape(rows_here, 3, sp_count, part), 2).reshape(rows_here, 3 * part)
    out_part = own_sp(out_weight.reshape(rows_here, sp_count, part), 1)
    in_part = own_sp(in_weight.reshape(rows_here, dp_count, sp_count, ff_rows), 2).reshape(
        rows_here, ff // sp_count
    )
    down_part = own_sp(down_weight.reshape(sp_count, ff_rows, width), 0)
    full_qkv = gather_dp(qkv_part, dp_count).reshape(width, 3 * part)
    in_out = gather_dp(jnp.concatenate([out_part, in_part], axis=1), dp_count).reshape(width, -1)
    out_columns, full_in = in_out[:, :part], in_out[:, part:]
    full_down = gather_dp(down_part, dp_count).reshape(ff // sp_count, width)
    full_out = jnp.moveaxis(ordered(gather_sp(out_columns)), 0, 1).reshape(width, width)

    diagonals = seq_len // BLOCK
    place = np.arange(2 * BLOCK)
    distance = BLOCK * np.arange(diagonals)[:, None] + np.where(place <= BLOCK, -place, 2 * BLOCK - place)
    bucket_rows = bucket_index[np.clip(distance, 0, seq_len - 1)]
    summed = BLOCK * np.arange(diagonals)[:, None] + place - (BLOCK - 1)
    sum_buckets = bucket_index[np.clip(summed, 0, seq_len - 1)]
    sum_onehot = (sum_buckets[..., None] == jnp.arange(bucket_count)).astype(F32)
    table_here = lax.dynamic_slice_in_dim(bias_table, me_sp * heads_here, heads_here, 0)
    onehot = (bucket_rows[..., None] == jnp.arange(bucket_count)).astype(F32)
    reversed_rows = jnp.sum(table_here[:, None, None, :] * onehot[None], axis=-1)
    bias = bias_blocks(reversed_rows)
    seg_row = segment_ids
    seg_col = segment_ids.reshape(seq_len, 1)

    tokens_all = ordered(gather_sp(inputs[0])).reshape(seq_len, width).astype(F32)
    normed_out_one, normed_one, inverse_one = layer_norm(tokens_all, norm_gain[0], norm_shift[0])
    act_one = normed_out_one.astype(BF16)
    tokens = inputs[0].astype(F32)
    upstream = cotangent[0].astype(F32)
    upstream_all = jnp.concatenate(gather_sp(cotangent[0]), axis=0)
    qkv = dot(act_one, full_qkv).astype(BF16)
    attn, logs = attend(qkv, bias, seg_col, seg_row, scale)
    attn_all = ordered(gather_sp(attn))
    attn_rows = lax.dynamic_slice_in_dim(attn_all, me_sp * tok_count, tok_count, 1)
    attn_rows = jnp.moveaxis(attn_rows, 0, 1).reshape(tok_count, width)
    residual = tokens + dot(attn_rows, full_out)
    normed_out_two, normed_two, inverse_two = layer_norm(residual, norm_gain[1], norm_shift[1])
    act_two = jnp.concatenate(gather_sp(normed_out_two.astype(BF16)), axis=0)
    hidden = dot(act_two, full_in)
    activated, gelu_back = jax.vjp(jax.nn.gelu, hidden)
    fed = activated.astype(BF16)

    grad_fed = dot(upstream_all, full_down, 1, 1)
    grad_hidden = gelu_back(grad_fed)[0].astype(BF16)
    grad_act_two = reduce_sp(list(dot(grad_hidden, full_in, 1, 1).reshape(sp_count, tok_count, width)))
    grad_down = dot(fed, upstream_all, 0, 0)
    grad_in = dot(act_two, grad_hidden, 0, 0)
    output = residual + reduce_sp(list(dot(fed, full_down).reshape(sp_count, tok_count, width)))

    gain_two = jnp.sum(grad_act_two * normed_two, axis=0)
    shift_two = jnp.sum(grad_act_two, axis=0)
    grad_resid = upstream + norm_back(grad_act_two, normed_two, inverse_two, norm_gain[1])
    grad_branch = grad_resid.astype(BF16)
    grad_attn_rows = dot(grad_branch, full_out, 1, 1).astype(BF16)
    grad_heads = exchange_sp(
        jnp.moveaxis(grad_attn_rows.reshape(tok_count, sp_count, part), 1, 0)
    ).reshape(seq_len, part)
    grad_branch_columns = exchange_sp(
        jnp.moveaxis(grad_branch.reshape(tok_count, sp_count, part), 1, 0)
    ).reshape(seq_len, part)
    grad_out = jnp.concatenate(
        [dot(attn_all[step], grad_branch_columns, 0, 0) for step in range(sp_count)], axis=0
    )
    grad_qkv_here, diagonal_sums = attend_back(qkv, grad_heads, logs, bias, seg_col, seg_row, scale)
    table_here_grad = lax.dot_general(
        diagonal_sums, sum_onehot, (((1, 2), (0, 1)), ((), ())), precision=lax.Precision.HIGHEST
    )
    grad_qkv = dot(act_one, grad_qkv_here, 0, 0)
    partial_one = dot(grad_qkv_here, full_qkv, 1, 1)
    gain_one = jnp.sum(partial_one * normed_one, axis=0)
    shift_one = jnp.sum(partial_one, axis=0)
    stacked_one = partial_one.reshape(sp_count, tok_count, width)
    grad_act_one = reduce_sp([pick(stacked_one, step) for step in range(sp_count)])

    def mine(values):
        return lax.dynamic_slice_in_dim(values, me_sp * tok_count, tok_count, 0)

    grad_input = grad_resid + norm_back(
        grad_act_one, mine(normed_one), mine(inverse_one), norm_gain[0]
    )

    table_whole = lax.dynamic_update_slice_in_dim(
        jnp.zeros((head_total, bucket_count), F32), table_here_grad, me_sp * heads_here, 0
    )
    small = jnp.concatenate(
        [
            value.reshape(dp_count, -1)
            for value in (gain_one, gain_two, shift_one, shift_two, table_whole)
        ],
        axis=1,
    )
    small_count = small.shape[1]
    small = jnp.pad(small, ((0, 0), (0, 16 * 4 * part - small_count))).reshape(dp_count, 16, 4 * part)
    sum_down = scatter_dp(grad_down.reshape(dp_count, ff_rows, width), dp_count)
    sum_in = scatter_dp(grad_in.reshape(dp_count, rows_here, ff // sp_count), dp_count)
    last = jnp.concatenate(
        [
            jnp.concatenate([grad_qkv, grad_out], axis=1).reshape(dp_count, rows_here, 4 * part),
            small,
        ],
        axis=1,
    )
    sum_last = scatter_dp(last, dp_count)

    all_down = ordered(gather_sp(sum_down.astype(BF16))).astype(F32)
    all_in = ordered(gather_sp(sum_in.astype(BF16))).astype(F32)
    all_last = ordered(gather_sp(sum_last.astype(BF16))).astype(F32)
    out_down = all_down.reshape(sp_count * ff_rows, width)
    out_in = jnp.moveaxis(all_in.reshape(sp_count, rows_here, dp_count, ff_rows), 0, 2).reshape(
        rows_here, ff
    )
    out_qkv = jnp.moveaxis(
        all_last[:, :rows_here, : 3 * part].reshape(sp_count, rows_here, 3, part), 0, 2
    ).reshape(rows_here, 3 * width)
    out_out = jnp.moveaxis(all_last[:, :rows_here, 3 * part :], 0, 1).reshape(rows_here, width)
    small_sum = jnp.sum(all_last[:, rows_here:], axis=0).reshape(-1)
    piece = width // dp_count
    gains = small_sum[: 2 * piece].reshape(2, piece)
    shifts = small_sum[2 * piece : 4 * piece].reshape(2, piece)
    tables = small_sum[4 * piece : small_count]
    return (
        output.astype(BF16)[None],
        grad_input[None],
        out_qkv,
        out_out,
        out_in,
        out_down,
        gains,
        shifts,
        tables,
    )


def solution(mesh):
    in_specs = (
        P("dp", "sp", None),
        P("dp", None),
        P("dp", None),
        P("dp", None),
        P("dp", None),
        P(),
        P(),
        P(),
        P("dp", None),
        P(),
        P("dp", "sp", None),
    )
    out_specs = (
        P("dp", "sp", None),
        P("dp", "sp", None),
        P("dp", None),
        P("dp", None),
        P("dp", None),
        P("dp", None),
        P(None, "dp"),
        P(None, "dp"),
        P("dp"),
    )
    return jax.shard_map(
        on_device, mesh=mesh, in_specs=in_specs, out_specs=out_specs, check_vma=False
    )
```

time: 4180 us -> 580 us (0.14)
  local copies, waits for them, and re-layouts: 3720 us -> 346 us
  waiting for transfers between devices: 221 us -> 84.1 us
  matrix products: 120 us -> 25.2 us
  starting transfers between devices: 8.31 us -> 72.9 us
  blocking collectives: 49.8 us -> 0 us
    gather x3 -> x4, local copies, waits for them, and re-layouts: 3690 us -> 14.3 us  [the longest x2 7.46 us: on_device(): sum_buckets = bucket_index[np.clip(summed, 0, seq_len - 1)]]
    dynamic_update_slice x1 -> x56, local copies, waits for them, and re-layouts: 0.01 us -> 265 us  [the longest x3 219 us: gather_dp(): return lax.dynamic_update_slice(whole, down[None], (last, half, 0))]
    all_gather x4 -> x0, waiting for transfers between devices: 100 us -> none  [the longest x1 100 us: on_device(): lax.all_gather(qkv_weight, 'dp', axis=0, tiled=True)]
    dot_general x23 -> x16, matrix products: 113 us -> 25.2 us  [the longest x15 25 us: dot(): lax.dot_general(left, right, (((left_dim,), (right_dim,)), ((), ())), pre...]
    ppermute x0 -> x87, waiting for transfers between devices: none -> 84.1 us  [the longest x39 32.6 us: swap(): return lax.ppermute(values, 'sp', [(i, i ^ bit) for i in range(count)])]
    ppermute x0 -> x87, starting transfers between devices: none -> 72.9 us  [the longest x39 17.1 us: swap(): return lax.ppermute(values, 'sp', [(i, i ^ bit) for i in range(count)])]
    psum x1 -> x0, waiting for transfers between devices: 63.1 us -> none  [on_device(): lax.psum(part_qkv.astype(jnp.bfloat16), 'sp').astype(jnp.float32)]
    unnamed x13 -> x0, waiting for transfers between devices: 51.9 us -> none
  transfers between devices with their start and end apart: 13 -> 87, of which waited for: 4 -> 29; matrix products, arithmetic and copies ran while one was open for 92% -> 66% of each run, Pallas kernels for 0% -> 2%
where the time goes in v1:
time: 580 us; the launch traced here: 572 us
  local copies, waits for them, and re-layouts  346 us (60%)
  waiting for transfers between devices  84.1 us (14%)
  starting transfers between devices  72.9 us (13%)
  other arithmetic  28.7 us (5%)
  matrix products  25.2 us (4%)
  Pallas kernels  12.6 us (2%)
    dynamic_update_slice x3, local copies, waits for them, and re-layouts, gather_dp(): return lax.dynamic_update_slice(whole, down[None], (last, half, 0))  219 us
    ppermute x39, waiting for transfers between devices, swap(): return lax.ppermute(values, 'sp', [(i, i ^ bit) for i in range(count)])  32.6 us
    dot_general x15, matrix products, dot(): lax.dot_general(left, right, (((left_dim,), (right_dim,)), ((), ())), pre...  25 us
    ppermute x39, starting transfers between devices, swap(): return lax.ppermute(values, 'sp', [(i, i ^ bit) for i in range(count)])  17.1 us
    ppermute x9, waiting for transfers between devices, scatter_dp(): down = lax.ppermute(for_down.astype(BF16), 'dp', backward)  16.4 us
    dynamic_update_slice x30, local copies, waits for them, and re-layouts, ordered(): whole = lax.dynamic_update_index_in_dim(whole, piece, me ^ step, 0)  16 us
    dynamic_update_slice x4, local copies, waits for them, and re-layouts, gather_dp(): whole = lax.dynamic_update_slice(whole, up[None], (last, 0, 0))  14.7 us
    ppermute x9, starting transfers between devices, gather_dp(): up = lax.ppermute(up, 'dp', forward)  14.6 us
  transfers between devices with their start and end apart: 87, of which 29 were waited for; matrix products, arithmetic and copies ran while one was open for 66% of the time, Pallas kernels for 2%

profile of v1, /device:TPU:0, one launch (start us, length us, event | category | flops | bytes accessed | tf_op | source)
XLA Modules:
  0.0 572.4 jit_solution(5884080356104590759)
XLA Ops:
  1.2 2.6 collective-permute-start.1
  9.0 1.8 dynamic-slice_bitcast_fusion.4
  13.8 6.9 %gather_fusion = s32[1024]{0:T(1024)S(1)} fusion(s32[512]{0:T(512)S(1)} %copy-done.4, s32[1024]{0:T(1024)S(1)} %broadcast_clamp_fusion.1), kind=kCustom, calls=%fused_computation | custom fusion | bytes 12288 | tf_op jit(solution)/shard_map/gather | solution.py:342
  22.6 1.9 broadcast_in_dim.244
  27.1 2.3 shard_map.214.bias_ref
  29.6 6.9 %gather_fusion.1 = s32[1024]{0:T(1024)S(1)} fusion(s32[512]{0:T(512)S(1)} %copy-done.4, s32[1024]{0:T(1024)S(1)} %copy-done.45), kind=kCustom, calls=%fused_computation.1 | custom fusion | bytes 12288 | tf_op jit(solution)/shard_map/gather | solution.py:344
  43.5 3.1 collective-permute-done.29
  52.9 1.7 bitcast_dynamic-update-slice_fusion.9
  70.3 4.5 collective-permute-done.7
  81.7 5.5 collective-permute-done.9
  92.5 2.8 convolution_convert_fusion.qkv_ref
  95.3 3.8 shard_map.215
  111.1 4.7 collective-permute-done.20
  115.8 3.9 dynamic_update_slice.212
  119.8 9.2 %copy.218 = bf16[8,128,1280]{1,0,2:T(8,128)(2,1)} copy(bf16[8,128,1280]{1,2,0:T(8,128)(2,1)} %dynamic_update_slice.212) | data formatting | bytes 5242880 | tf_op jit(solution)/shard_map/dynamic_update_slice | solution.py:71
  128.9 3.6 copy.219
  132.6 218.3 %dynamic_update_slice.213 = bf16[8,128,1280]{1,0,2:T(8,128)(2,1)} dynamic-update-slice(bf16[8,128,1280]{1,0,2:T(8,128)(2,1)} %copy.218, bf16[1,64,1280]{1,0,2:T(2,128)(2,1)S(1)} %copy.219, s32[]{:T(128)S(6)} %select_n.282, s32[]{:T(128)} %constant.622.clone.1, s32[]{:T(128)} %constant.602.clone.1) | dynamic-update-slice | bytes 327684 | tf_op jit(solution)/shard_map/dynamic_update_slice | solution.py:72
  350.9 2.4 copy.280
  359.4 1.9 bitcast_dynamic-update-slice_fusion.3
  362.9 1.8 copy.213
  365.7 1.9 collective-permute-done.23
  367.7 2.0 collective-permute-start.35
  369.7 1.9 bitcast_dynamic-update-slice_fusion.2
  371.6 1.9 bitcast_dynamic-update-slice_fusion.1
  374.3 2.6 fusion.107
  380.3 5.5 collective-permute-done.26
  389.3 3.1 fusion.109
  392.4 4.2 fusion.6
  399.2 2.6 fusion.79
  406.5 3.4 collective-permute-done.65
  412.7 2.2 collective-permute-done.76
  420.0 4.6 collective-permute-done.66
  425.9 3.4 collective-permute-done.77
  433.5 3.0 collective-permute-start.78
  436.6 2.2 collective-permute-done.38
  440.6 2.8 convolution_convert_fusion.1
  443.3 1.9 reshape.459
  445.2 1.8 reshape.456
  447.0 1.9 constant_dynamic-slice_fusion.4
  449.0 1.9 constant_dynamic-slice_fusion
  452.7 3.7 collective-permute-done.52
  456.5 3.7 collective-permute-done.53
  462.7 3.2 collective-permute-done.46
  466.2 4.0 collective-permute-done.47
  470.2 6.4 %shard_map.216 = (bf16[512,768]{1,0:T(8,128)(2,1)S(1)}, f32[4,4,256]{2,1,0:T(4,128)S(1)}) custom-call(bf16[512,768]{1,0:T(8,128)(2,1)S(1)} %convolution_convert_fusion.qkv_ref, bf16[512,256]{1,0:T(8,128)(2,1)S(1)} %bitcast.383, f32[512,128]{1,0:T(8,128)S(1)} %get-tuple-element.86.log_ref, f32[4,4,128,128]{3,2,1,0:T(8,128)S(1)} %copy-done.2, ...), custom_call_target="tpu_custom_call" | custom-call | tf_op jit(solution)/shard_map/pallas_call | solution.py:283
  479.1 2.4 maximum_maximum_fusion
  481.5 5.4 copy.250
  490.3 1.7 fusion.58
  492.1 1.7 collective-permute-start.58
  497.1 1.8 collective-permute-done.58
  502.2 2.3 collective-permute-done.71
  507.3 2.8 collective-permute-done.82
  512.0 3.1 collective-permute-done.59
  517.0 1.7 collective-permute-start.83
  519.3 1.7 collective-permute-start.60
  521.1 3.3 collective-permute-done.72
  526.9 3.1 collective-permute-done.83
  532.4 1.8 collective-permute-done.60
  536.4 3.9 collective-permute-done.85
  549.8 3.3 collective-permute-done.63
  554.4 2.7 copy.281
  557.1 3.1 reshape.487
  564.0 2.4 convert_element_type.321
  569.1 1.8 slice_reduce_fusion
  (429 shorter events, 154.6 us)
Async XLA Ops:
  0.7 48.1 %collective-permute-start = (bf16[128,1024]{1,0:T(8,128)(2,1)}, bf16[128,1024]{1,0:T(8,128)(2,1)}, u32[]{:S(2)}, u32[]{:S(2)}) collective-permute-start(bf16[128,1024]{1,0:T(8,128)(2,1)} %bitcast.435), channel_id=1, source_target_pairs={{0,1},{1,0},{2,3},{3,2},{4,5},{5,4},{6,7},{7,6},{8,9},{9,8},{10,11... | collective-permute-start | bytes 786440 | tf_op jit(solution)/shard_map/ppermute | solution.py:104
  1.2 50.2 %collective-permute-start.1 = (bf16[128,1024]{1,0:T(8,128)(2,1)}, bf16[128,1024]{1,0:T(8,128)(2,1)}, u32[]{:S(2)}, u32[]{:S(2)}) collective-permute-start(bf16[128,1024]{1,0:T(8,128)(2,1)} %bitcast.436), channel_id=1, source_target_pairs={{0,2},{1,3},{2,0},{3,1},{4,6},{5,7},{6,4},{7,5},{8,10},{9,11},{10,... | collective-permute-start | bytes 786440 | tf_op jit(solution)/shard_map/ppermute | solution.py:104
  5.3 31.7 %collective-permute-start.3 = (bf16[128,768]{0,1:T(8,128)(2,1)S(1)}, bf16[128,768]{0,1:T(8,128)(2,1)}, u32[]{:S(2)}, u32[]{:S(2)}) collective-permute-start(bf16[128,768]{0,1:T(8,128)(2,1)S(1)} %bitcast.438), channel_id=1, source_target_pairs={{0,8},{8,16},{16,24},{24,28},{28,20},{20,12},{12,4},{4,0},{1,9},{9... | collective-permute-start | bytes 589832 | tf_op jit(solution)/shard_map/ppermute | solution.py:64
  7.0 31.6 %collective-permute-start.4 = (bf16[128,768]{0,1:T(8,128)(2,1)S(1)}, bf16[128,768]{0,1:T(8,128)(2,1)}, u32[]{:S(2)}, u32[]{:S(2)}) collective-permute-start(bf16[128,768]{0,1:T(8,128)(2,1)S(1)} %bitcast.439), channel_id=1, source_target_pairs={{8,0},{16,8},{24,16},{28,24},{20,28},{12,20},{4,12},{0,4},{9,1},{1... | collective-permute-start | bytes 589832 | tf_op jit(solution)/shard_map/ppermute | solution.py:65
  10.8 30.5 %collective-permute-start.28 = (bf16[128,1024]{1,0:T(8,128)(2,1)}, bf16[128,1024]{1,0:T(8,128)(2,1)}, u32[]{:S(2)}, u32[]{:S(2)}) collective-permute-start(bf16[128,1024]{1,0:T(8,128)(2,1)} %get-tuple-element.180), channel_id=1, source_target_pairs={{0,8},{8,16},{16,24},{24,28},{28,20},{20,12},{12,4},{4,0},{1,9},{9... | collective-permute-start | bytes 786440 | tf_op jit(solution)/shard_map/ppermute | solution.py:64
  37.0 9.6 %collective-permute-start.29 = (bf16[128,1024]{1,0:T(8,128)(2,1)}, bf16[128,1024]{1,0:T(8,128)(2,1)}, u32[]{:S(2)}, u32[]{:S(2)}) collective-permute-start(bf16[128,1024]{1,0:T(8,128)(2,1)} %get-tuple-element.180), channel_id=1, source_target_pairs={{8,0},{16,8},{24,16},{28,24},{20,28},{12,20},{4,12},{0,4},{9,1},{1... | collective-permute-start | bytes 786440 | tf_op jit(solution)/shard_map/ppermute | solution.py:65
  38.5 14.3 %collective-permute-start.14 = (bf16[128,1280]{0,1:T(8,128)(2,1)}, bf16[128,1280]{0,1:T(8,128)(2,1)}, u32[]{:S(2)}, u32[]{:S(2)}) collective-permute-start(bf16[128,1280]{0,1:T(8,128)(2,1)} %pad_maximum_fusion.2), channel_id=1, source_target_pairs={{0,8},{8,16},{16,24},{24,28},{28,20},{20,12},{12,4},{4,0},{1,9},{9... | collective-permute-start | bytes 983048 | tf_op jit(solution)/shard_map/ppermute | solution.py:64
  41.3 13.3 %collective-permute-start.15 = (bf16[128,1280]{0,1:T(8,128)(2,1)}, bf16[128,1280]{0,1:T(8,128)(2,1)S(1)}, u32[]{:S(2)}, u32[]{:S(2)}) collective-permute-start(bf16[128,1280]{0,1:T(8,128)(2,1)} %pad_maximum_fusion.2), channel_id=1, source_target_pairs={{8,0},{16,8},{24,16},{28,24},{20,28},{12,20},{4,12},{0,4},{9,1},{1... | collective-permute-start | bytes 983048 | tf_op jit(solution)/shard_map/ppermute | solution.py:65
  46.6 54.4 %collective-permute-start.40 = (bf16[128,1024]{1,0:T(8,128)(2,1)}, bf16[128,1024]{1,0:T(8,128)(2,1)}, u32[]{:S(2)}, u32[]{:S(2)}) collective-permute-start(bf16[128,1024]{1,0:T(8,128)(2,1)} %bitcast.444), channel_id=1, source_target_pairs={{0,2},{1,3},{2,0},{3,1},{4,6},{5,7},{6,4},{7,5},{8,10},{9,11},{10,... | collective-permute-start | bytes 786440 | tf_op jit(solution)/shard_map/ppermute | solution.py:104
  48.8 8.2 %collective-permute-start.5 = (bf16[128,768]{0,1:T(8,128)(2,1)}, bf16[128,768]{0,1:T(8,128)(2,1)S(1)}, u32[]{:S(2)}, u32[]{:S(2)}) collective-permute-start(bf16[128,768]{0,1:T(8,128)(2,1)} %collective-permute-done.3), channel_id=1, source_target_pairs={{0,8},{8,16},{16,24},{24,28},{28,20},{20,12},{12,4},{4,0},{1,9},{9... | collective-permute-start | bytes 589832 | tf_op jit(solution)/shard_map/ppermute | solution.py:64
  54.7 9.3 %collective-permute-start.30 = (bf16[128,1024]{1,0:T(8,128)(2,1)}, bf16[128,1024]{1,0:T(8,128)(2,1)S(1)}, u32[]{:S(2)}, u32[]{:S(2)}) collective-permute-start(bf16[128,1024]{1,0:T(8,128)(2,1)} %collective-permute-done.28), channel_id=1, source_target_pairs={{0,8},{8,16},{16,24},{24,28},{28,20},{20,12},{12,4},{4,0},{1,9},{9... | collective-permute-start | bytes 786440 | tf_op jit(solution)/shard_map/ppermute | solution.py:64
  57.0 10.7 %collective-permute-start.31 = (bf16[128,1024]{1,0:T(8,128)(2,1)}, bf16[128,1024]{1,0:T(8,128)(2,1)}, u32[]{:S(2)}, u32[]{:S(2)}) collective-permute-start(bf16[128,1024]{1,0:T(8,128)(2,1)} %collective-permute-done.29), channel_id=1, source_target_pairs={{8,0},{16,8},{24,16},{28,24},{20,28},{12,20},{4,12},{0,4},{9,1},{1... | collective-permute-start | bytes 786440 | tf_op jit(solution)/shard_map/ppermute | solution.py:65
  57.6 21.8 %collective-permute-start.16 = (bf16[128,1280]{0,1:T(8,128)(2,1)}, bf16[128,1280]{0,1:T(8,128)(2,1)}, u32[]{:S(2)}, u32[]{:S(2)}) collective-permute-start(bf16[128,1280]{0,1:T(8,128)(2,1)} %collective-permute-done.14), channel_id=1, source_target_pairs={{0,8},{8,16},{16,24},{24,28},{28,20},{20,12},{12,4},{4,0},{1,9},{9... | collective-permute-start | bytes 983048 | tf_op jit(solution)/shard_map/ppermute | solution.py:64
  60.5 28.4 %collective-permute-start.17 = (bf16[128,1280]{0,1:T(8,128)(2,1)}, bf16[128,1280]{0,1:T(8,128)(2,1)S(1)}, u32[]{:S(2)}, u32[]{:S(2)}) collective-permute-start(bf16[128,1280]{0,1:T(8,128)(2,1)} %copy-done.29), channel_id=1, source_target_pairs={{8,0},{16,8},{24,16},{28,24},{20,28},{12,20},{4,12},{0,4},{9,1},{1... | collective-permute-start | bytes 983048 | tf_op jit(solution)/shard_map/ppermute | solution.py:65
  64.0 10.8 %collective-permute-start.7 = (bf16[128,768]{0,1:T(8,128)(2,1)S(1)}, bf16[128,768]{0,1:T(8,128)(2,1)S(1)}, u32[]{:S(2)}, u32[]{:S(2)}) collective-permute-start(bf16[128,768]{0,1:T(8,128)(2,1)S(1)} %copy-done.36), channel_id=1, source_target_pairs={{0,8},{8,16},{16,24},{24,28},{28,20},{20,12},{12,4},{4,0},{1,9},{9... | collective-permute-start | bytes 589832 | tf_op jit(solution)/shard_map/ppermute | solution.py:64
  67.7 9.8 %collective-permute-start.8 = (bf16[128,768]{0,1:T(8,128)(2,1)}, bf16[128,768]{0,1:T(8,128)(2,1)S(1)}, u32[]{:S(2)}, u32[]{:S(2)}) collective-permute-start(bf16[128,768]{0,1:T(8,128)(2,1)} %collective-permute-done.6), channel_id=1, source_target_pairs={{8,0},{16,8},{24,16},{28,24},{20,28},{12,20},{4,12},{0,4},{9,1},{1... | collective-permute-start | bytes 589832 | tf_op jit(solution)/shard_map/ppermute | solution.py:65
  74.8 24.3 %collective-permute-start.32 = (bf16[128,1024]{1,0:T(8,128)(2,1)}, bf16[128,1024]{1,0:T(8,128)(2,1)S(1)}, u32[]{:S(2)}, u32[]{:S(2)}) collective-permute-start(bf16[128,1024]{1,0:T(8,128)(2,1)} %copy-done.33), channel_id=1, source_target_pairs={{0,8},{8,16},{16,24},{24,28},{28,20},{20,12},{12,4},{4,0},{1,9},{9... | collective-permute-start | bytes 786440 | tf_op jit(solution)/shard_map/ppermute | solution.py:64
  77.6 9.5 %collective-permute-start.9 = (bf16[64,768]{0,1:T(8,128)(2,1)}, bf16[64,768]{0,1:T(8,128)(2,1)S(1)}, u32[]{:S(2)}, u32[]{:S(2)}) collective-permute-start(bf16[64,768]{0,1:T(8,128)(2,1)} %bitcast.453), channel_id=1, source_target_pairs={{0,8},{8,16},{16,24},{24,28},{28,20},{20,12},{12,4},{4,0},{1,9},{9... | collective-permute-start | bytes 294920 | tf_op jit(solution)/shard_map/ppermute | solution.py:68
  79.4 11.1 %collective-permute-start.10 = (bf16[64,768]{0,1:T(8,128)(2,1)S(1)}, bf16[64,768]{0,1:T(8,128)(2,1)S(1)}, u32[]{:S(2)}, u32[]{:S(2)}) collective-permute-start(bf16[64,768]{0,1:T(8,128)(2,1)S(1)} %slice.244), channel_id=1, source_target_pairs={{8,0},{16,8},{24,16},{28,24},{20,28},{12,20},{4,12},{0,4},{9,1},{1... | collective-permute-start | bytes 294920 | tf_op jit(solution)/shard_map/ppermute | solution.py:69
  87.2 14.3 %collective-permute-start.33 = (bf16[128,1024]{1,0:T(8,128)(2,1)}, bf16[128,1024]{1,0:T(8,128)(2,1)}, u32[]{:S(2)}, u32[]{:S(2)}) collective-permute-start(bf16[128,1024]{1,0:T(8,128)(2,1)} %collective-permute-done.31), channel_id=1, source_target_pairs={{8,0},{16,8},{24,16},{28,24},{20,28},{12,20},{4,12},{0,4},{9,1},{1... | collective-permute-start | bytes 786440 | tf_op jit(solution)/shard_map/ppermute | solution.py:65
  88.9 16.8 %collective-permute-start.18 = (bf16[128,1280]{0,1:T(8,128)(2,1)}, bf16[128,1280]{0,1:T(8,128)(2,1)}, u32[]{:S(2)}, u32[]{:S(2)}) collective-permute-start(bf16[128,1280]{0,1:T(8,128)(2,1)} %collective-permute-done.16), channel_id=1, source_target_pairs={{0,8},{8,16},{16,24},{24,28},{28,20},{20,12},{12,4},{4,0},{1,9},{9... | collective-permute-start | bytes 983048 | tf_op jit(solution)/shard_map/ppermute | solution.py:64
  90.6 16.8 %collective-permute-start.19 = (bf16[128,1280]{0,1:T(8,128)(2,1)}, bf16[128,1280]{0,1:T(8,128)(2,1)S(1)}, u32[]{:S(2)}, u32[]{:S(2)}) collective-permute-start(bf16[128,1280]{0,1:T(8,128)(2,1)} %copy-done.30), channel_id=1, source_target_pairs={{8,0},{16,8},{24,16},{28,24},{20,28},{12,20},{4,12},{0,4},{9,1},{1... | collective-permute-start | bytes 983048 | tf_op jit(solution)/shard_map/ppermute | solution.py:65
  101.0 291.4 %collective-permute-start.39 = (bf16[128,1024]{1,0:T(8,128)(2,1)}, bf16[128,1024]{1,0:T(8,128)(2,1)}, u32[]{:S(2)}, u32[]{:S(2)}) collective-permute-start(bf16[128,1024]{1,0:T(8,128)(2,1)} %bitcast.445), channel_id=1, source_target_pairs={{0,1},{1,0},{2,3},{3,2},{4,5},{5,4},{6,7},{7,6},{8,9},{9,8},{10,11... | collective-permute-start | bytes 786440 | tf_op jit(solution)/shard_map/ppermute | solution.py:104
  101.4 291.0 %collective-permute-start.41 = (bf16[128,1024]{1,0:T(8,128)(2,1)}, bf16[128,1024]{1,0:T(8,128)(2,1)}, u32[]{:S(2)}, u32[]{:S(2)}) collective-permute-start(bf16[128,1024]{1,0:T(8,128)(2,1)} %collective-permute-done.40), channel_id=1, source_target_pairs={{0,1},{1,0},{2,3},{3,2},{4,5},{5,4},{6,7},{7,6},{8,9},{9,8},{10,11... | collective-permute-start | bytes 786440 | tf_op jit(solution)/shard_map/ppermute | solution.py:104
  103.1 252.3 %collective-permute-start.12 = (bf16[512,256]{1,0:T(8,128)(2,1)S(1)}, bf16[512,256]{1,0:T(8,128)(2,1)}, u32[]{:S(2)}, u32[]{:S(2)}) collective-permute-start(bf16[512,256]{1,0:T(8,128)(2,1)S(1)} %get-tuple-element.85), channel_id=1, source_target_pairs={{0,2},{1,3},{2,0},{3,1},{4,6},{5,7},{6,4},{7,5},{8,10},{9,11},{10,... | collective-permute-start | bytes 786440 | tf_op jit(solution)/shard_map/ppermute | solution.py:104
  105.7 10.1 %collective-permute-start.20 = (bf16[64,1280]{0,1:T(8,128)(2,1)}, bf16[64,1280]{0,1:T(8,128)(2,1)}, u32[]{:S(2)}, u32[]{:S(2)}) collective-permute-start(bf16[64,1280]{0,1:T(8,128)(2,1)} %bitcast.382), channel_id=1, source_target_pairs={{0,8},{8,16},{16,24},{24,28},{28,20},{20,12},{12,4},{4,0},{1,9},{9... | collective-permute-start | bytes 491528 | tf_op jit(solution)/shard_map/ppermute | solution.py:68
  108.2 20.7 %collective-permute-start.21 = (bf16[64,1280]{0,1:T(8,128)(2,1)}, bf16[64,1280]{0,1:T(8,128)(2,1)}, u32[]{:S(2)}, u32[]{:S(2)}) collective-permute-start(bf16[64,1280]{0,1:T(8,128)(2,1)} %slice.246), channel_id=1, source_target_pairs={{8,0},{16,8},{24,16},{28,24},{20,28},{12,20},{4,12},{0,4},{9,1},{1... | collective-permute-start | bytes 491528 | tf_op jit(solution)/shard_map/ppermute | solution.py:69
  354.2 13.5 %collective-permute-start.23 = (bf16[1024,256]{0,1:T(8,128)(2,1)}, bf16[1024,256]{0,1:T(8,128)(2,1)}, u32[]{:S(2)}, u32[]{:S(2)}) collective-permute-start(bf16[1024,256]{0,1:T(8,128)(2,1)} %slice.247), channel_id=1, source_target_pairs={{0,2},{1,3},{2,0},{3,1},{4,6},{5,7},{6,4},{7,5},{8,10},{9,11},{10,... | collective-permute-start | bytes 1572872 | tf_op jit(solution)/shard_map/ppermute | solution.py:104
  356.6 11.1 %collective-permute-start.22 = (bf16[1024,256]{0,1:T(8,128)(2,1)}, bf16[1024,256]{0,1:T(8,128)(2,1)}, u32[]{:S(2)}, u32[]{:S(2)}) collective-permute-start(bf16[1024,256]{0,1:T(8,128)(2,1)} %slice.247), channel_id=1, source_target_pairs={{0,1},{1,0},{2,3},{3,2},{4,5},{5,4},{6,7},{7,6},{8,9},{9,8},{10,11... | collective-permute-start | bytes 1572872 | tf_op jit(solution)/shard_map/ppermute | solution.py:104
  361.3 19.0 %collective-permute-start.34 = (bf16[64,1024]{1,0:T(8,128)(2,1)}, bf16[64,1024]{1,0:T(8,128)(2,1)}, u32[]{:S(2)}, u32[]{:S(2)}) collective-permute-start(bf16[64,1024]{1,0:T(8,128)(2,1)} %slice.249), channel_id=1, source_target_pairs={{0,8},{8,16},{16,24},{24,28},{28,20},{20,12},{12,4},{4,0},{1,9},{9... | collective-permute-start | bytes 393224 | tf_op jit(solution)/shard_map/ppermute | solution.py:68
  367.7 19.6 %collective-permute-start.35 = (bf16[64,1024]{1,0:T(8,128)(2,1)S(1)}, bf16[64,1024]{1,0:T(8,128)(2,1)S(1)}, u32[]{:S(2)}, u32[]{:S(2)}) collective-permute-start(bf16[64,1024]{1,0:T(8,128)(2,1)S(1)} %copy-done.40), channel_id=1, source_target_pairs={{8,0},{16,8},{24,16},{28,24},{20,28},{12,20},{4,12},{0,4},{9,1},{1... | collective-permute-start | bytes 393224 | tf_op jit(solution)/shard_map/ppermute | solution.py:69
  377.3 8.5 %collective-permute-start.26 = (bf16[128,1024]{1,0:T(8,128)(2,1)S(1)}, bf16[128,1024]{1,0:T(8,128)(2,1)S(1)}, u32[]{:S(2)}, u32[]{:S(2)}) collective-permute-start(bf16[128,1024]{1,0:T(8,128)(2,1)S(1)} %add_convert_fusion.3), channel_id=1, source_target_pairs={{0,2},{1,3},{2,0},{3,1},{4,6},{5,7},{6,4},{7,5},{8,10},{9,11},{10,... | collective-permute-start | bytes 786440 | tf_op jit(solution)/shard_map/ppermute | solution.py:104
  398.0 19.8 %collective-permute-start.43 = (bf16[128,1024]{1,0:T(8,128)(2,1)S(1)}, bf16[128,1024]{1,0:T(8,128)(2,1)S(1)}, u32[]{:S(2)}, u32[]{:S(2)}) collective-permute-start(bf16[128,1024]{1,0:T(8,128)(2,1)S(1)} %get-tuple-element.177), channel_id=1, source_target_pairs={{0,1},{1,0},{2,3},{3,2},{4,5},{5,4},{6,7},{7,6},{8,9},{9,8},{10,11... | collective-permute-start | bytes 786440 | tf_op jit(solution)/shard_map/ppermute | solution.py:104
  398.6 33.0 %collective-permute-start.42 = (bf16[128,1024]{1,0:T(8,128)(2,1)S(1)}, bf16[128,1024]{1,0:T(8,128)(2,1)S(1)}, u32[]{:S(2)}, u32[]{:S(2)}) collective-permute-start(bf16[128,1024]{1,0:T(8,128)(2,1)S(1)} %get-tuple-element.176), channel_id=1, source_target_pairs={{0,1},{1,0},{2,3},{3,2},{4,5},{5,4},{6,7},{7,6},{8,9},{9,8},{10,11... | collective-permute-start | bytes 786440 | tf_op jit(solution)/shard_map/ppermute | solution.py:104
  398.7 19.5 %collective-permute-start.37 = (bf16[128,1024]{1,0:T(8,128)(2,1)S(1)}, bf16[128,1024]{1,0:T(8,128)(2,1)S(1)}, u32[]{:S(2)}, u32[]{:S(2)}) collective-permute-start(bf16[128,1024]{1,0:T(8,128)(2,1)S(1)} %get-tuple-element.179), channel_id=1, source_target_pairs={{0,1},{1,0},{2,3},{3,2},{4,5},{5,4},{6,7},{7,6},{8,9},{9,8},{10,11... | collective-permute-start | bytes 786440 | tf_op jit(solution)/shard_map/ppermute | solution.py:104
  414.9 18.6 %collective-permute-start.36 = (bf16[128,1024]{1,0:T(8,128)(2,1)S(1)}, bf16[128,1024]{1,0:T(8,128)(2,1)S(1)}, u32[]{:S(2)}, u32[]{:S(2)}) collective-permute-start(bf16[128,1024]{1,0:T(8,128)(2,1)S(1)} %get-tuple-element.178), channel_id=1, source_target_pairs={{0,1},{1,0},{2,3},{3,2},{4,5},{5,4},{6,7},{7,6},{8,9},{9,8},{10,11... | collective-permute-start | bytes 786440 | tf_op jit(solution)/shard_map/ppermute | solution.py:104
  415.4 9.2 %collective-permute-start.66 = (bf16[128,1024]{1,0:T(8,128)(2,1)S(1)}, bf16[128,1024]{1,0:T(8,128)(2,1)S(1)}, u32[]{:S(2)}, u32[]{:S(2)}) collective-permute-start(bf16[128,1024]{1,0:T(8,128)(2,1)S(1)} %get-tuple-element.168), channel_id=1, source_target_pairs={{0,8},{8,16},{16,24},{24,28},{28,20},{20,12},{12,4},{4,0},{1,9},{9... | collective-permute-start | bytes 786440 | tf_op jit(solution)/shard_map/ppermute | solution.py:97
  417.7 71.5 %collective-permute-start.70 = (bf16[128,1024]{1,0:T(8,128)(2,1)}, bf16[128,1024]{1,0:T(8,128)(2,1)}, u32[]{:S(2)}, u32[]{:S(2)}) collective-permute-start(bf16[128,1024]{1,0:T(8,128)(2,1)} %get-tuple-element.169), channel_id=1, source_target_pairs={{8,0},{16,8},{24,16},{28,24},{20,28},{12,20},{4,12},{0,4},{9,1},{1... | collective-permute-start | bytes 786440 | tf_op jit(solution)/shard_map/ppermute | solution.py:98
  418.2 11.0 %collective-permute-start.77 = (bf16[128,1024]{1,0:T(8,128)(2,1)S(1)}, bf16[128,1024]{1,0:T(8,128)(2,1)S(1)}, u32[]{:S(2)}, u32[]{:S(2)}) collective-permute-start(bf16[128,1024]{1,0:T(8,128)(2,1)S(1)} %get-tuple-element.161), channel_id=1, source_target_pairs={{0,8},{8,16},{16,24},{24,28},{28,20},{20,12},{12,4},{4,0},{1,9},{9... | collective-permute-start | bytes 786440 | tf_op jit(solution)/shard_map/ppermute | solution.py:97
  429.2 62.8 %collective-permute-start.81 = (bf16[128,1024]{1,0:T(8,128)(2,1)}, bf16[128,1024]{1,0:T(8,128)(2,1)}, u32[]{:S(2)}, u32[]{:S(2)}) collective-permute-start(bf16[128,1024]{1,0:T(8,128)(2,1)} %get-tuple-element.162), channel_id=1, source_target_pairs={{8,0},{16,8},{24,16},{28,24},{20,28},{12,20},{4,12},{0,4},{9,1},{1... | collective-permute-start | bytes 786440 | tf_op jit(solution)/shard_map/ppermute | solution.py:98
  432.1 57.6 %collective-permute-start.67 = (bf16[128,1024]{1,0:T(8,128)(2,1)}, bf16[128,1024]{1,0:T(8,128)(2,1)}, u32[]{:S(2)}, u32[]{:S(2)}) collective-permute-start(bf16[128,1024]{1,0:T(8,128)(2,1)} %fusion.57), channel_id=1, source_target_pairs={{0,8},{8,16},{16,24},{24,28},{28,20},{20,12},{12,4},{4,0},{1,9},{9... | collective-permute-start | bytes 786440 | tf_op jit(solution)/shard_map/ppermute | solution.py:97
  433.5 60.2 %collective-permute-start.78 = (bf16[128,1024]{1,0:T(8,128)(2,1)}, bf16[128,1024]{1,0:T(8,128)(2,1)}, u32[]{:S(2)}, u32[]{:S(2)}) collective-permute-start(bf16[128,1024]{1,0:T(8,128)(2,1)} %fusion.51), channel_id=1, source_target_pairs={{0,8},{8,16},{16,24},{24,28},{28,20},{20,12},{12,4},{4,0},{1,9},{9... | collective-permute-start | bytes 786440 | tf_op jit(solution)/shard_map/ppermute | solution.py:97
  477.9 22.7 %collective-permute-start.49 = (bf16[128,1024]{1,0:T(8,128)(2,1)S(1)}, bf16[128,1024]{1,0:T(8,128)(2,1)S(1)}, u32[]{:S(2)}, u32[]{:S(2)}) collective-permute-start(bf16[128,1024]{1,0:T(8,128)(2,1)S(1)} %get-tuple-element.174), channel_id=1, source_target_pairs={{0,1},{1,0},{2,3},{3,2},{4,5},{5,4},{6,7},{7,6},{8,9},{9,8},{10,11... | collective-permute-start | bytes 786440 | tf_op jit(solution)/shard_map/ppermute | solution.py:104
  489.2 27.8 %collective-permute-start.48 = (bf16[128,1024]{1,0:T(8,128)(2,1)S(1)}, bf16[128,1024]{1,0:T(8,128)(2,1)S(1)}, u32[]{:S(2)}, u32[]{:S(2)}) collective-permute-start(bf16[128,1024]{1,0:T(8,128)(2,1)S(1)} %get-tuple-element.173), channel_id=1, source_target_pairs={{0,1},{1,0},{2,3},{3,2},{4,5},{5,4},{6,7},{7,6},{8,9},{9,8},{10,11... | collective-permute-start | bytes 786440 | tf_op jit(solution)/shard_map/ppermute | solution.py:104
  493.8 10.7 %collective-permute-start.71 = (bf16[128,1024]{1,0:T(8,128)(2,1)S(1)}, bf16[128,1024]{1,0:T(8,128)(2,1)S(1)}, u32[]{:S(2)}, u32[]{:S(2)}) collective-permute-start(bf16[128,1024]{1,0:T(8,128)(2,1)S(1)} %get-tuple-element.167), channel_id=1, source_target_pairs={{8,0},{16,8},{24,16},{28,24},{20,28},{12,20},{4,12},{0,4},{9,1},{1... | collective-permute-start | bytes 786440 | tf_op jit(solution)/shard_map/ppermute | solution.py:98
  496.3 23.0 %collective-permute-start.68 = (bf16[128,1024]{1,0:T(8,128)(2,1)S(1)}, bf16[128,1024]{1,0:T(8,128)(2,1)S(1)}, u32[]{:S(2)}, u32[]{:S(2)}) collective-permute-start(bf16[128,1024]{1,0:T(8,128)(2,1)S(1)} %get-tuple-element.166), channel_id=1, source_target_pairs={{0,8},{8,16},{16,24},{24,28},{28,20},{20,12},{12,4},{4,0},{1,9},{9... | collective-permute-start | bytes 786440 | tf_op jit(solution)/shard_map/ppermute | solution.py:97
  498.9 11.2 %collective-permute-start.82 = (bf16[128,1024]{1,0:T(8,128)(2,1)S(1)}, bf16[128,1024]{1,0:T(8,128)(2,1)S(1)}, u32[]{:S(2)}, u32[]{:S(2)}) collective-permute-start(bf16[128,1024]{1,0:T(8,128)(2,1)S(1)} %get-tuple-element.160), channel_id=1, source_target_pairs={{8,0},{16,8},{24,16},{28,24},{20,28},{12,20},{4,12},{0,4},{9,1},{1... | collective-permute-start | bytes 786440 | tf_op jit(solution)/shard_map/ppermute | solution.py:98
  500.6 10.6 %collective-permute-start.55 = (bf16[144,1024]{1,0:T(8,128)(2,1)S(1)}, bf16[144,1024]{1,0:T(8,128)(2,1)S(1)}, u32[]{:S(2)}, u32[]{:S(2)}) collective-permute-start(bf16[144,1024]{1,0:T(8,128)(2,1)S(1)} %get-tuple-element.154), channel_id=1, source_target_pairs={{0,8},{8,16},{16,24},{24,28},{28,20},{20,12},{12,4},{4,0},{1,9},{9... | collective-permute-start | bytes 884744 | tf_op jit(solution)/shard_map/ppermute | solution.py:97
  504.5 10.7 %collective-permute-start.59 = (bf16[144,1024]{1,0:T(8,128)(2,1)S(1)}, bf16[144,1024]{1,0:T(8,128)(2,1)S(1)}, u32[]{:S(2)}, u32[]{:S(2)}) collective-permute-start(bf16[144,1024]{1,0:T(8,128)(2,1)S(1)} %get-tuple-element.155), channel_id=1, source_target_pairs={{8,0},{16,8},{24,16},{28,24},{20,28},{12,20},{4,12},{0,4},{9,1},{1... | collective-permute-start | bytes 884744 | tf_op jit(solution)/shard_map/ppermute | solution.py:98
  510.1 8.6 %collective-permute-start.50 = (bf16[128,1024]{1,0:T(8,128)(2,1)S(1)}, bf16[128,1024]{1,0:T(8,128)(2,1)S(1)}, u32[]{:S(2)}, u32[]{:S(2)}) collective-permute-start(bf16[128,1024]{1,0:T(8,128)(2,1)S(1)} %fusion.61), channel_id=1, source_target_pairs={{0,2},{1,3},{2,0},{3,1},{4,6},{5,7},{6,4},{7,5},{8,10},{9,11},{10,... | collective-permute-start | bytes 786440 | tf_op jit(solution)/shard_map/ppermute | solution.py:104
  511.2 14.6 %collective-permute-start.79 = (bf16[128,1024]{1,0:T(8,128)(2,1)S(1)}, bf16[128,1024]{1,0:T(8,128)(2,1)S(1)}, u32[]{:S(2)}, u32[]{:S(2)}) collective-permute-start(bf16[128,1024]{1,0:T(8,128)(2,1)S(1)} %get-tuple-element.159), channel_id=1, source_target_pairs={{0,8},{8,16},{16,24},{24,28},{28,20},{20,12},{12,4},{4,0},{1,9},{9... | collective-permute-start | bytes 786440 | tf_op jit(solution)/shard_map/ppermute | solution.py:97
  515.1 9.2 %collective-permute-start.72 = (bf16[128,1024]{1,0:T(8,128)(2,1)S(1)}, bf16[128,1024]{1,0:T(8,128)(2,1)S(1)}, u32[]{:S(2)}, u32[]{:S(2)}) collective-permute-start(bf16[128,1024]{1,0:T(8,128)(2,1)S(1)} %fusion.56), channel_id=1, source_target_pairs={{8,0},{16,8},{24,16},{28,24},{20,28},{12,20},{4,12},{0,4},{9,1},{1... | collective-permute-start | bytes 786440 | tf_op jit(solution)/shard_map/ppermute | solution.py:98
  517.0 13.0 %collective-permute-start.83 = (bf16[128,1024]{1,0:T(8,128)(2,1)S(1)}, bf16[128,1024]{1,0:T(8,128)(2,1)S(1)}, u32[]{:S(2)}, u32[]{:S(2)}) collective-permute-start(bf16[128,1024]{1,0:T(8,128)(2,1)S(1)} %fusion.50), channel_id=1, source_target_pairs={{8,0},{16,8},{24,16},{28,24},{20,28},{12,20},{4,12},{0,4},{9,1},{1... | collective-permute-start | bytes 786440 | tf_op jit(solution)/shard_map/ppermute | solution.py:98
  518.7 13.6 %collective-permute-start.56 = (bf16[144,1024]{1,0:T(8,128)(2,1)S(1)}, bf16[144,1024]{1,0:T(8,128)(2,1)S(1)}, u32[]{:S(2)}, u32[]{:S(2)}) collective-permute-start(bf16[144,1024]{1,0:T(8,128)(2,1)S(1)} %get-tuple-element.152), channel_id=1, source_target_pairs={{0,8},{8,16},{16,24},{24,28},{28,20},{20,12},{12,4},{4,0},{1,9},{9... | collective-permute-start | bytes 884744 | tf_op jit(solution)/shard_map/ppermute | solution.py:97
  519.3 14.8 %collective-permute-start.60 = (bf16[144,1024]{1,0:T(8,128)(2,1)S(1)}, bf16[144,1024]{1,0:T(8,128)(2,1)S(1)}, u32[]{:S(2)}, u32[]{:S(2)}) collective-permute-start(bf16[144,1024]{1,0:T(8,128)(2,1)S(1)} %get-tuple-element.153), channel_id=1, source_target_pairs={{8,0},{16,8},{24,16},{28,24},{20,28},{12,20},{4,12},{0,4},{9,1},{1... | collective-permute-start | bytes 884744 | tf_op jit(solution)/shard_map/ppermute | solution.py:98
  525.7 10.3 %collective-permute-start.73 = (bf16[128,1024]{1,0:T(8,128)(2,1)S(1)}, bf16[128,1024]{1,0:T(8,128)(2,1)S(1)}, u32[]{:S(2)}, u32[]{:S(2)}) collective-permute-start(bf16[128,1024]{1,0:T(8,128)(2,1)S(1)} %get-tuple-element.145), channel_id=1, source_target_pairs={{0,1},{1,0},{2,3},{3,2},{4,5},{5,4},{6,7},{7,6},{8,9},{9,8},{10,11... | collective-permute-start | bytes 786440 | tf_op jit(solution)/shard_map/ppermute | solution.py:104
  525.8 10.6 %collective-permute-start.74 = (bf16[128,1024]{1,0:T(8,128)(2,1)S(1)}, bf16[128,1024]{1,0:T(8,128)(2,1)}, u32[]{:S(2)}, u32[]{:S(2)}) collective-permute-start(bf16[128,1024]{1,0:T(8,128)(2,1)S(1)} %get-tuple-element.145), channel_id=1, source_target_pairs={{0,2},{1,3},{2,0},{3,1},{4,6},{5,7},{6,4},{7,5},{8,10},{9,11},{10,... | collective-permute-start | bytes 786440 | tf_op jit(solution)/shard_map/ppermute | solution.py:104
  530.3 10.0 %collective-permute-start.85 = (bf16[128,1024]{1,0:T(8,128)(2,1)S(1)}, bf16[128,1024]{1,0:T(8,128)(2,1)}, u32[]{:S(2)}, u32[]{:S(2)}) collective-permute-start(bf16[128,1024]{1,0:T(8,128)(2,1)S(1)} %get-tuple-element.143), channel_id=1, source_target_pairs={{0,2},{1,3},{2,0},{3,1},{4,6},{5,7},{6,4},{7,5},{8,10},{9,11},{10,... | collective-permute-start | bytes 786440 | tf_op jit(solution)/shard_map/ppermute | solution.py:104
  532.4 8.9 %collective-permute-start.84 = (bf16[128,1024]{1,0:T(8,128)(2,1)S(1)}, bf16[128,1024]{1,0:T(8,128)(2,1)S(1)}, u32[]{:S(2)}, u32[]{:S(2)}) collective-permute-start(bf16[128,1024]{1,0:T(8,128)(2,1)S(1)} %get-tuple-element.143), channel_id=1, source_target_pairs={{0,1},{1,0},{2,3},{3,2},{4,5},{5,4},{6,7},{7,6},{8,9},{9,8},{10,11... | collective-permute-start | bytes 786440 | tf_op jit(solution)/shard_map/ppermute | solution.py:104
  534.3 8.0 %collective-permute-start.61 = (bf16[144,1024]{1,0:T(8,128)(2,1)S(1)}, bf16[144,1024]{1,0:T(8,128)(2,1)S(1)}, u32[]{:S(2)}, u32[]{:S(2)}) collective-permute-start(bf16[144,1024]{1,0:T(8,128)(2,1)S(1)} %get-tuple-element.151), channel_id=1, source_target_pairs={{8,0},{16,8},{24,16},{28,24},{20,28},{12,20},{4,12},{0,4},{9,1},{1... | collective-permute-start | bytes 884744 | tf_op jit(solution)/shard_map/ppermute | solution.py:98
  536.4 16.8 %collective-permute-start.75 = (bf16[128,1024]{1,0:T(8,128)(2,1)}, bf16[128,1024]{1,0:T(8,128)(2,1)}, u32[]{:S(2)}, u32[]{:S(2)}) collective-permute-start(bf16[128,1024]{1,0:T(8,128)(2,1)} %collective-permute-done.74), channel_id=1, source_target_pairs={{0,1},{1,0},{2,3},{3,2},{4,5},{5,4},{6,7},{7,6},{8,9},{9,8},{10,11... | collective-permute-start | bytes 786440 | tf_op jit(solution)/shard_map/ppermute | solution.py:104
  543.6 16.6 %collective-permute-start.62 = (bf16[144,1024]{1,0:T(8,128)(2,1)S(1)}, bf16[144,1024]{1,0:T(8,128)(2,1)}, u32[]{:S(2)}, u32[]{:S(2)}) collective-permute-start(bf16[144,1024]{1,0:T(8,128)(2,1)S(1)} %fusion.20), channel_id=1, source_target_pairs={{0,1},{1,0},{2,3},{3,2},{4,5},{5,4},{6,7},{7,6},{8,9},{9,8},{10,11... | collective-permute-start | bytes 884744 | tf_op jit(solution)/shard_map/ppermute | solution.py:104
  543.8 9.4 %collective-permute-start.63 = (bf16[144,1024]{1,0:T(8,128)(2,1)S(1)}, bf16[144,1024]{1,0:T(8,128)(2,1)}, u32[]{:S(2)}, u32[]{:S(2)}) collective-permute-start(bf16[144,1024]{1,0:T(8,128)(2,1)S(1)} %fusion.20), channel_id=1, source_target_pairs={{0,2},{1,3},{2,0},{3,1},{4,6},{5,7},{6,4},{7,5},{8,10},{9,11},{10,... | collective-permute-start | bytes 884744 | tf_op jit(solution)/shard_map/ppermute | solution.py:104
  553.2 9.4 %collective-permute-start.64 = (bf16[144,1024]{1,0:T(8,128)(2,1)}, bf16[144,1024]{1,0:T(8,128)(2,1)}, u32[]{:S(2)}, u32[]{:S(2)}) collective-permute-start(bf16[144,1024]{1,0:T(8,128)(2,1)} %collective-permute-done.63), channel_id=1, source_target_pairs={{0,1},{1,0},{2,3},{3,2},{4,5},{5,4},{6,7},{7,6},{8,9},{9,8},{10,11... | collective-permute-start | bytes 884744 | tf_op jit(solution)/shard_map/ppermute | solution.py:104
  (77 other events, 477.0 us)

commit v2 on v1

v2 whole, which is shorter than its diff:
```python
import functools

import jax
import jax.numpy as jnp
from jax import lax
from jax.experimental import pallas as pl
from jax.experimental.pallas import tpu as pltpu
from jax.sharding import PartitionSpec as P

BLOCK = 128
SMALL_ROWS = 16
NEG = -1e30
BF16 = jnp.bfloat16
F32 = jnp.float32
VMEM_LIMIT = 56 * 1024 * 1024
ROOT = 0.7978845608028654
CUBE = 0.044715


def dot(left, right, left_dim=1, right_dim=0):
    return lax.dot_general(
        left, right, (((left_dim,), (right_dim,)), ((), ())), preferred_element_type=F32
    )


def layer_norm(values):
    average = jnp.mean(values, axis=-1, keepdims=True)
    centred = values - average
    inverse = lax.rsqrt(jnp.mean(centred * centred, axis=-1, keepdims=True) + 1e-05)
    return centred * inverse, inverse


def norm_back(upstream, normed, inverse, gain):
    scaled = upstream * gain
    centre_term = jnp.mean(scaled, axis=-1, keepdims=True)
    slope_term = jnp.mean(scaled * normed, axis=-1, keepdims=True)
    return inverse * (scaled - centre_term - normed * slope_term)


def shaped(shape, dtype):
    return jax.ShapeDtypeStruct(tuple(shape), dtype)


def call(kernel, outs, args, any_args=(), smem_args=(), scratch=(), cost=(0, 0)):
    specs = [pl.BlockSpec(memory_space=pltpu.VMEM)] * len(args)
    specs += [pl.BlockSpec(memory_space=pl.ANY)] * len(any_args)
    specs += [pl.BlockSpec(memory_space=pltpu.SMEM)] * len(smem_args)
    return pl.pallas_call(
        kernel,
        out_shape=tuple(outs),
        in_specs=specs,
        out_specs=tuple(pl.BlockSpec(memory_space=pltpu.VMEM) for _ in outs),
        scratch_shapes=list(scratch),
        compiler_params=pltpu.CompilerParams(vmem_limit_bytes=VMEM_LIMIT),
        cost_estimate=pl.CostEstimate(flops=cost[0], bytes_accessed=cost[1], transcendentals=0),
    )(*args, *any_args, *smem_args)


def rank_at(position, count):
    position = lax.rem(position + 2 * count, count)
    return jnp.where(position < count // 2, 2 * position, 2 * (count - 1 - position) + 1)


def position_of(rank, count):
    return jnp.where(rank % 2 == 0, rank // 2, count - 1 - rank // 2)


def ring_pairs(count):
    order = list(range(0, count, 2)) + list(range(count - 1, 0, -2))
    forward = [(order[i], order[(i + 1) % count]) for i in range(count)]
    return forward, [(b, a) for a, b in forward]


def half_rows(rows):
    return rows // 2 // 16 * 16


def gather_offsets(rows, count):
    if count != 8:
        return jnp.zeros((1,), jnp.int32)
    at = position_of(lax.axis_index("dp"), count)
    steps = [0, -1, 1, -2, 2, -3, 3, 4]
    places = [rank_at(at + step, count) * rows for step in steps]
    return jnp.stack(places + [places[-1] + half_rows(rows)]).astype(jnp.int32)


def gather_dp(shard, count):
    if count != 8:
        return [lax.all_gather(shard, "dp", axis=0, tiled=True)]
    forward, backward = ring_pairs(count)
    half = half_rows(shard.shape[0])
    pieces = [shard]
    up = down = shard
    for step in range(1, count // 2):
        up = lax.ppermute(up, "dp", forward)
        down = lax.ppermute(down, "dp", backward)
        pieces += [up, down]
    up = lax.ppermute(up[:half], "dp", forward)
    down = lax.ppermute(down[half:], "dp", backward)
    return pieces + [up, down]


def scatter_dp(parts, count):
    if count != 8:
        return lax.psum_scatter(parts, "dp", scatter_dimension=0)
    forward, backward = ring_pairs(count)
    at = position_of(lax.axis_index("dp"), count)
    half = half_rows(parts.shape[1])

    def own(position):
        return lax.dynamic_index_in_dim(parts, rank_at(position, count), 0, keepdims=False)

    far = own(at + count // 2)
    up = lax.ppermute(far[:half], "dp", forward)
    down = lax.ppermute(far[half:], "dp", backward)
    for step in range(count // 2 - 1, 0, -1):
        for_up, for_down = own(at + step).astype(F32), own(at - step).astype(F32)
        if step == count // 2 - 1:
            up = jnp.pad(up, ((0, parts.shape[1] - half), (0, 0)))
            down = jnp.pad(down, ((half, 0), (0, 0)))
        up = lax.ppermute((for_up + up.astype(F32)).astype(BF16), "dp", forward)
        down = lax.ppermute((for_down + down.astype(F32)).astype(BF16), "dp", backward)
    return (own(at).astype(F32) + up.astype(F32) + down.astype(F32)).astype(BF16)


def swap(values, bit):
    count = lax.axis_size("sp")
    return lax.ppermute(values, "sp", [(i, i ^ bit) for i in range(count)])


def gather_sp(piece):
    far = swap(piece, 2)
    near = swap(piece, 1)
    return [piece, near, far, swap(far, 1)]


def reduce_sp(far, send):
    near = swap(send, 1)
    tok = far.shape[0]
    return near, swap((far + near[tok:].astype(F32)).astype(BF16), 2)


def place(step, size, me_ref):
    return pl.multiple_of((me_ref[0] ^ step) * size, size)


def load(pieces, offsets_ref, target, sems, lanes=slice(None)):
    copies = []
    for at, piece in enumerate(pieces):
        rows = pl.ds(pl.multiple_of(offsets_ref[at], 16), piece.shape[0])
        copies.append(pltpu.make_async_copy(piece.at[:, lanes], target.at[rows, :], sems.at[at]))
    for copy in copies:
        copy.start()
    return copies


def finish(copies):
    for copy in copies:
        copy.wait()


def share_kernel(plan, refs):
    *sources, me_ref, target, sems = refs
    copies = []
    for at, (source, axis, start, step, size, to) in enumerate(plan):
        start = pl.multiple_of(start + step * me_ref[0], step)
        block = sources[source]
        if axis == 1:
            block = block.at[:, pl.ds(start, size)]
        else:
            block = block.at[pl.ds(start, size), :]
        copies.append(pltpu.make_async_copy(block, target.at[:, to : to + size if axis else None], sems.at[at]))
    for copy in copies:
        copy.start()
    finish(copies)


def share(sources, me, plan, rows):
    columns = sum(size if axis else sources[source].shape[1] for source, axis, _, _, size, _ in plan)

    def kernel(*refs):
        share_kernel(plan, refs)

    return call(
        kernel,
        [shaped((rows, columns), BF16)],
        [],
        sources,
        [me],
        [pltpu.SemaphoreType.DMA((len(plan),))],
        (0, 4 * rows * columns),
    )[0]


def bias_kernel(table_ref, bucket_ref, bias_ref):
    heads, diagonals = bias_ref.shape[:2]
    wide = bucket_ref.shape[1]
    bucket = lax.broadcasted_iota(jnp.int32, (table_ref.shape[1], wide), 0)
    chosen = (bucket == bucket_ref[...]).astype(F32)
    rows = lax.dot_general(
        table_ref[...],
        chosen,
        (((1,), (0,)), ((), ())),
        precision=lax.Precision.HIGHEST,
        preferred_element_type=F32,
    )
    for head in range(heads):
        for diagonal in range(diagonals):
            start = wide - (diagonal + 2) * BLOCK
            row = rows[head : head + 1, start : start + 2 * BLOCK]
            spread = jnp.broadcast_to(row, (BLOCK, 2 * BLOCK))
            rolled = pltpu.roll(spread, BLOCK, 1, stride=1, stride_axis=0)
            bias_ref[head, diagonal] = rolled[:, :BLOCK]


def norm_kernel(*refs):
    *pieces, gain_ref, shift_ref, me_ref, act_ref, normed_ref = refs
    for step, piece in enumerate(pieces):
        rows = pl.ds(place(step, piece.shape[0], me_ref), piece.shape[0])
        normed, _ = layer_norm(piece[...].astype(F32))
        act_ref[rows, :] = (normed * gain_ref[0:1, :] + shift_ref[0:1, :]).astype(BF16)
        normed_ref[rows, :] = normed.astype(BF16)


def mask_rows(index, seg_col_ref, seg_row_ref):
    width = (index + 1) * BLOCK
    same = seg_col_ref[index * BLOCK : width, :] == seg_row_ref[:, :width]
    row = index * BLOCK + lax.broadcasted_iota(jnp.int32, (BLOCK, width), 0)
    column = lax.broadcasted_iota(jnp.int32, (BLOCK, width), 1)
    return jnp.where(same & (row >= column), 0.0, NEG).astype(F32)


def half_mask(side):
    lane = lax.broadcasted_iota(jnp.int32, (1, BLOCK), 1)
    return (lane // (BLOCK // 2) == side).astype(F32).astype(BF16)


def score_rows(query, keys, bias_ref, head, index, mask):
    raw = dot(query, keys, 1, 1)
    bias = jnp.concatenate([bias_ref[head, index - block] for block in range(index + 1)], axis=1)
    return raw + bias + mask


def attend_kernel(scale, count, *refs):
    act_ref, bias_ref, seg_col_ref, seg_row_ref = refs[:4]
    pieces, offsets_ref = refs[4 : 4 + count], refs[4 + count]
    qkv_ref, attn_ref, log_ref, weight, sems = refs[5 + count :]
    copies = load(pieces, offsets_ref, weight, sems)
    seq_len = qkv_ref.shape[0]
    columns = qkv_ref.shape[1] // 3
    lane = lax.broadcasted_iota(jnp.int32, (1, BLOCK), 1)
    finish(copies)
    for index in range(seq_len // BLOCK):
        rows = slice(index * BLOCK, (index + 1) * BLOCK)
        qkv_ref[rows, :] = dot(act_ref[rows, :], weight[...]).astype(BF16)
    for index in range(seq_len // BLOCK):
        rows = slice(index * BLOCK, (index + 1) * BLOCK)
        width = (index + 1) * BLOCK
        mask = mask_rows(index, seg_col_ref, seg_row_ref)
        logs = jnp.zeros((BLOCK, BLOCK), F32)
        for pair in range(columns // BLOCK):
            lanes = slice(pair * BLOCK, (pair + 1) * BLOCK)
            query = qkv_ref[rows, lanes] * scale
            keys = qkv_ref[:width, columns + pair * BLOCK : columns + (pair + 1) * BLOCK]
            values = qkv_ref[:width, 2 * columns + pair * BLOCK : 2 * columns + (pair + 1) * BLOCK]
            mixed = []
            for side in range(2):
                head = 2 * pair + side
                scores = score_rows(query * half_mask(side), keys, bias_ref, head, index, mask)
                largest = jnp.max(scores, axis=1, keepdims=True)
                weights = jnp.exp(scores - largest)
                total = jnp.sum(weights, axis=1, keepdims=True)
                mixed.append(dot(weights.astype(BF16), values) / total)
                logs = jnp.where(lane == head, largest + jnp.log(total), logs)
            attn_ref[rows, lanes] = jnp.where(lane < BLOCK // 2, mixed[0], mixed[1]).astype(BF16)
        log_ref[rows, :] = logs


def branch_kernel(*refs):
    attn_refs, weight_refs = refs[:4], refs[4:8]
    tokens_ref, gain_ref, shift_ref, me_ref, resid_ref, act_ref, own = refs[8:]
    tok = tokens_ref.shape[0]
    part = weight_refs[0].shape[1]
    for step, attn in enumerate(attn_refs):
        own[:, pl.ds(place(step, part, me_ref), part)] = attn[pl.ds(place(0, tok, me_ref), tok), :]
    for step, weight in enumerate(weight_refs):
        columns = pl.ds(place(step, part, me_ref), part)
        resid_ref[:, columns] = tokens_ref[:, columns].astype(F32) + dot(own[...], weight[...])
    normed, _ = layer_norm(resid_ref[...])
    act_ref[...] = (normed * gain_ref[1:2, :] + shift_ref[1:2, :]).astype(BF16)


def feed_kernel(count, part, *refs):
    act_refs, up_refs, pieces = refs[:4], refs[4:8], refs[8 : 8 + count]
    offsets_ref, fed_ref, slope_ref, grad_ref, weight, upstream, sems = refs[8 + count :]
    copies = load(pieces, offsets_ref, weight, sems, slice(part, None))
    tok = act_refs[0].shape[0]
    for step, up in enumerate(up_refs):
        upstream[step * tok : (step + 1) * tok, :] = up[...]
    finish(copies)
    for step, act in enumerate(act_refs):
        rows = slice(step * tok, (step + 1) * tok)
        hidden = dot(act[...], weight[...])
        square = hidden * hidden
        bend = jnp.tanh(ROOT * hidden * (1.0 + CUBE * square))
        fed_ref[rows, :] = (0.5 * hidden * (1.0 + bend)).astype(BF16)
        slope_ref[rows, :] = 0.5 * (1.0 + bend) + 0.5 * hidden * (1.0 - bend * bend) * ROOT * (
            1.0 + 3.0 * CUBE * square
        )
    width = grad_ref.shape[0]
    for start in range(0, width, 2 * BLOCK):
        rows = slice(start, start + 2 * BLOCK)
        grad_ref[rows, :] = dot(fed_ref[:, rows], upstream[...], 0, 0).astype(BF16)


def feed_back_kernel(count, part, *refs):
    slope_ref, up_refs = refs[0], refs[1:5]
    down_refs, in_refs = refs[5 : 5 + count], refs[5 + count : 5 + 2 * count]
    down_at, in_at = refs[5 + 2 * count : 7 + 2 * count]
    hidden_ref, own_ref, far_ref, send_ref, down, weight, down_sems, in_sems = refs[7 + 2 * count :]
    down_copies = load(down_refs, down_at, down, down_sems)
    in_copies = load(in_refs, in_at, weight, in_sems, slice(part, None))
    tok = up_refs[0].shape[0]
    finish(down_copies)
    finish(in_copies)
    for step, up in enumerate(up_refs):
        rows = slice(step * tok, (step + 1) * tok)
        grad = (dot(up[...], down[...], 1, 1) * slope_ref[rows, :]).astype(BF16)
        hidden_ref[rows, :] = grad
        share_of = dot(grad, weight[...], 1, 1)
        if step == 0:
            own_ref[...] = share_of
        elif step == 2:
            far_ref[...] = share_of
        else:
            send_ref[(step // 2) * tok : (step // 2 + 1) * tok, :] = share_of.astype(BF16)


def feed_rest_kernel(count, *refs):
    fed_ref, hidden_ref, act_refs, down_refs = refs[0], refs[1], refs[2:6], refs[6 : 6 + count]
    down_at, grad_ref, own_ref, far_ref, send_ref, act_all, down, sems = refs[6 + count :]
    copies = load(down_refs, down_at, down, sems)
    tok = act_refs[0].shape[0]
    for step, act in enumerate(act_refs):
        act_all[step * tok : (step + 1) * tok, :] = act[...]
    for start in range(0, grad_ref.shape[0], 2 * BLOCK):
        rows = slice(start, start + 2 * BLOCK)
        grad_ref[rows, :] = dot(act_all[:, rows], hidden_ref[...], 0, 0).astype(BF16)
    finish(copies)
    for step in range(4):
        share_of = dot(fed_ref[step * tok : (step + 1) * tok, :], down[...])
        if step == 0:
            own_ref[...] = share_of
        elif step == 2:
            far_ref[...] = share_of
        else:
            send_ref[(step // 2) * tok : (step // 2 + 1) * tok, :] = share_of.astype(BF16)


def branch_back_kernel(*refs):
    own_ref, near_ref, far_ref, resid_ref, up_ref, gain_ref = refs[:6]
    weight_refs, me_ref, grad_ref, sums_ref = refs[6:10], refs[10], refs[11], refs[12]
    send_refs, branch, grad_attn = refs[13:17], refs[17], refs[18]
    tok = up_ref.shape[0]
    part = weight_refs[0].shape[1]
    upstream = own_ref[...] + near_ref[:tok, :].astype(F32) + far_ref[...].astype(F32)
    normed, inverse = layer_norm(resid_ref[...])
    sums_ref[0:1, :] = jnp.sum(upstream * normed, axis=0, keepdims=True)
    sums_ref[1:2, :] = jnp.sum(upstream, axis=0, keepdims=True)
    sums_ref[2:, :] = jnp.zeros_like(sums_ref[2:, :])
    grad = up_ref[...].astype(F32) + norm_back(upstream, normed, inverse, gain_ref[1:2, :])
    grad_ref[...] = grad
    branch[...] = grad.astype(BF16)
    total = jnp.zeros(grad.shape, F32)
    for step, weight in enumerate(weight_refs):
        total += dot(branch[:, pl.ds(place(step, part, me_ref), part)], weight[...], 1, 1)
    grad_attn[...] = total.astype(BF16)
    for step, send in enumerate(send_refs):
        columns = pl.ds(place(step, part, me_ref), part)
        send[:, :part] = grad_attn[:, columns]
        send[:, part:] = branch[:, columns]


def attend_back_kernel(scale, count, *refs):
    qkv_ref, log_ref, bias_ref, seg_col_ref, seg_row_ref, act_ref, normed_ref, sums_ref, bucket_ref = refs[:9]
    attn_refs, grad_refs = refs[9:13], refs[13:17]
    pieces, offsets_ref, me_ref = refs[17 : 17 + count], refs[17 + count], refs[18 + count]
    last_ref, small_ref, own_ref, far_ref, send_ref = refs[19 + count : 24 + count]
    weight, grads, branch, grad_qkv, key_acc, value_acc, diagonal_acc, stacked, sems = refs[24 + count :]
    copies = load(pieces, offsets_ref, weight, sems)
    seq_len = qkv_ref.shape[0]
    columns = qkv_ref.shape[1] // 3
    heads, diagonals = diagonal_acc.shape[:2]
    tok = grad_refs[0].shape[0]
    for step, grad in enumerate(grad_refs):
        rows = pl.ds(place(step, tok, me_ref), tok)
        grads[rows, :] = grad[:, :columns]
        branch[rows, :] = grad[:, columns:]
    key_acc[...] = jnp.zeros_like(key_acc)
    value_acc[...] = jnp.zeros_like(value_acc)
    diagonal_acc[...] = jnp.zeros_like(diagonal_acc)
    for index in range(seq_len // BLOCK):
        rows = slice(index * BLOCK, (index + 1) * BLOCK)
        width = (index + 1) * BLOCK
        mask = mask_rows(index, seg_col_ref, seg_row_ref)
        for pair in range(columns // BLOCK):
            lanes = slice(pair * BLOCK, (pair + 1) * BLOCK)
            query = qkv_ref[rows, lanes] * scale
            keys = qkv_ref[:width, columns + pair * BLOCK : columns + (pair + 1) * BLOCK]
            values = qkv_ref[:width, 2 * columns + pair * BLOCK : 2 * columns + (pair + 1) * BLOCK]
            grad_rows = grads[rows, lanes]
            grad_query = jnp.zeros((BLOCK, BLOCK), F32)
            for side in range(2):
                head = 2 * pair + side
                query_one = query * half_mask(side)
                grad_one = grad_rows * half_mask(side)
                scores = score_rows(query_one, keys, bias_ref, head, index, mask)
                probs = jnp.exp(scores - log_ref[rows, head : head + 1])
                grad_probs = dot(grad_one, values, 1, 1)
                row_term = jnp.sum(probs * grad_probs, axis=1, keepdims=True)
                grad_scores = probs * (grad_probs - row_term)
                for block in range(index + 1):
                    diagonal_acc[head, index - block] += grad_scores[
                        :, block * BLOCK : (block + 1) * BLOCK
                    ]
                grad_raw = grad_scores.astype(BF16)
                grad_query += dot(grad_raw, keys * half_mask(side))
                key_acc[:width, lanes] += dot(grad_raw, query_one, 0, 0)
                value_acc[:width, lanes] += dot(probs.astype(BF16), grad_one, 0, 0)
            grad_qkv[rows, lanes] = (grad_query * scale).astype(BF16)
    grad_qkv[:, columns : 2 * columns] = key_acc[...].astype(BF16)
    grad_qkv[:, 2 * columns :] = value_acc[...].astype(BF16)

    finish(copies)
    gain_sum = jnp.zeros((1, act_ref.shape[1]), F32)
    shift_sum = jnp.zeros((1, act_ref.shape[1]), F32)
    for step in range(4):
        rows = pl.ds(place(step, tok, me_ref), tok)
        share_of = dot(grad_qkv[rows, :], weight[...], 1, 1)
        gain_sum += jnp.sum(share_of * normed_ref[rows, :].astype(F32), axis=0, keepdims=True)
        shift_sum += jnp.sum(share_of, axis=0, keepdims=True)
        if step == 0:
            own_ref[...] = share_of
        elif step == 2:
            far_ref[...] = share_of
        else:
            send_ref[(step // 2) * tok : (step // 2 + 1) * tok, :] = share_of.astype(BF16)

    parts, last_rows = last_ref.shape[:2]
    rows_here = act_ref.shape[1] // parts
    for start in range(0, act_ref.shape[1], 2 * BLOCK):
        block = dot(act_ref[:, start : start + 2 * BLOCK], grad_qkv[...], 0, 0).astype(BF16)
        for sub in range(2 * BLOCK // rows_here):
            part = start // rows_here + sub
            last_ref[part, :rows_here, : 3 * columns] = block[sub * rows_here : (sub + 1) * rows_here, :]
    for step, attn in enumerate(attn_refs):
        block = dot(attn[...], branch[...], 0, 0).astype(BF16)
        for sub in range(columns // rows_here):
            part = (me_ref[0] ^ step) * (columns // rows_here) + sub
            last_ref[part, :rows_here, 3 * columns :] = block[sub * rows_here : (sub + 1) * rows_here, :]

    row = lax.broadcasted_iota(jnp.int32, (BLOCK, BLOCK), 0)
    column = lax.broadcasted_iota(jnp.int32, (BLOCK, BLOCK), 1)
    flip = (row + column == BLOCK - 1).astype(F32)
    stacked[...] = jnp.zeros_like(stacked)
    for head in range(heads):
        for diagonal in range(diagonals):
            block = lax.dot_general(
                diagonal_acc[head, diagonal],
                flip,
                (((1,), (0,)), ((), ())),
                precision=lax.Precision.HIGHEST,
                preferred_element_type=F32,
            )
            wide = jnp.concatenate([block, jnp.zeros_like(block)], axis=1)
            rolled = pltpu.roll(wide, 0, 1, stride=1, stride_axis=0)
            at = slice(diagonal * BLOCK, (diagonal + 2) * BLOCK)
            stacked[head : head + 1, at] += jnp.sum(rolled, axis=0, keepdims=True)
    buckets = BLOCK // heads
    bucket = lax.broadcasted_iota(jnp.int32, (BLOCK, bucket_ref.shape[1]), 0) % buckets
    chosen = (bucket == bucket_ref[...]).astype(F32)
    by_head = lax.dot_general(
        stacked[...],
        chosen,
        (((1,), (1,)), ((), ())),
        precision=lax.Precision.HIGHEST,
        preferred_element_type=F32,
    )
    row = lax.broadcasted_iota(jnp.int32, by_head.shape, 0)
    column = lax.broadcasted_iota(jnp.int32, by_head.shape, 1)
    table = jnp.sum(jnp.where(column // buckets == row, by_head, 0.0), axis=0, keepdims=True)
    small = [gain_sum, sums_ref[0:1, :], shift_sum, sums_ref[1:2, :]]
    for at, value in enumerate(small):
        small_ref[at : at + 1, :] = value
    small_ref[4:5, :BLOCK] = table
    if last_rows > rows_here:
        last_ref[:, rows_here:, :] = jnp.zeros_like(last_ref[:, rows_here:, :])
        for part in range(parts):
            for at, value in enumerate(small):
                last_ref[part, rows_here : rows_here + 1, at * rows_here : (at + 1) * rows_here] = value[
                    :, part * rows_here : (part + 1) * rows_here
                ].astype(BF16)
            per = parts // 4
            turned = table if part % per == 0 else pltpu.roll(table, BLOCK - part % per * (BLOCK // per), 1)
            turned = jnp.where(me_ref[0] == part // per, turned, 0.0)
            last_ref[part, rows_here : rows_here + 1, 4 * rows_here : 4 * rows_here + BLOCK] = turned.astype(BF16)


def norm_back_kernel(own_ref, near_ref, far_ref, tokens_ref, resid_ref, gain_ref, grad_ref):
    tok = own_ref.shape[0]
    upstream = own_ref[...] + near_ref[:tok, :].astype(F32) + far_ref[...].astype(F32)
    normed, inverse = layer_norm(tokens_ref[...].astype(F32))
    grad_ref[...] = resid_ref[...] + norm_back(upstream, normed, inverse, gain_ref[0:1, :])


def wide_feed_kernel(*refs):
    in_refs, down_refs, me_ref, in_ref, down_ref = refs[:4], refs[4:8], refs[8], refs[9], refs[10]
    rows = down_refs[0].shape[0]
    for step in range(4):
        down_ref[pl.ds(place(step, rows, me_ref), rows), :] = down_refs[step][...].astype(F32)
        for start in range(0, in_refs[step].shape[1], rows):
            at = pl.multiple_of(4 * start + (me_ref[0] ^ step) * rows, rows)
            in_ref[:, pl.ds(at, rows)] = in_refs[step][:, start : start + rows].astype(F32)


def wide_last_kernel(part, *refs):
    last_refs, me_ref, qkv_ref, out_ref, small_ref = refs[:4], refs[4], refs[5], refs[6], refs[7]
    rows = qkv_ref.shape[0]
    small = jnp.zeros(small_ref.shape, F32)
    for step, last in enumerate(last_refs):
        for third in range(3):
            at = pl.multiple_of(4 * third * part + (me_ref[0] ^ step) * part, part)
            qkv_ref[:, pl.ds(at, part)] = last[:rows, third * part : (third + 1) * part].astype(F32)
        out_ref[:, pl.ds(place(step, part, me_ref), part)] = last[:rows, 3 * part :].astype(F32)
        small += last[rows:, :].astype(F32)
    small_ref[...] = small


def stacked_sp(pieces):
    me = lax.axis_index("sp")
    whole = jnp.zeros((len(pieces),) + pieces[0].shape, pieces[0].dtype)
    for step, piece in enumerate(pieces):
        whole = lax.dynamic_update_index_in_dim(whole, piece, me ^ step, 0)
    return whole


def on_device(
    inputs,
    qkv_weight,
    out_weight,
    in_weight,
    down_weight,
    norm_gain,
    norm_shift,
    bias_table,
    segment_ids,
    bucket_index,
    cotangent,
):
    dp_count, sp_count = lax.axis_size("dp"), lax.axis_size("sp")
    me_sp = lax.axis_index("sp")
    me = me_sp.astype(jnp.int32).reshape(1)
    tok, width = inputs.shape[1:]
    head_total, bucket_count = bias_table.shape
    heads = head_total // sp_count
    scale = (width // head_total) ** (-0.5)
    seq_len = segment_ids.shape[1]
    rows_here = qkv_weight.shape[0]
    ff = in_weight.shape[1]
    ff_rows = ff // dp_count // sp_count
    ff_part = ff // sp_count
    part = width // sp_count
    diagonals = seq_len // BLOCK
    aligned = ff_rows % BLOCK == 0 and rows_here % BLOCK == 0

    if aligned:
        qkv_part = share(
            [qkv_weight], me, [(0, 1, third * width, part, part, third * part) for third in range(3)], rows_here
        )
        plan = [(0, 1, 0, part, part, 0)]
        plan += [
            (1, 1, index * sp_count * ff_rows, ff_rows, ff_rows, part + index * ff_rows)
            for index in range(dp_count)
        ]
        both_part = share([out_weight, in_weight], me, plan, rows_here)
    else:

        def own_sp(stacked, axis):
            return lax.dynamic_index_in_dim(stacked, me_sp, axis, keepdims=False)

        qkv_part = own_sp(qkv_weight.reshape(rows_here, 3, sp_count, part), 2).reshape(rows_here, 3 * part)
        out_part = own_sp(out_weight.reshape(rows_here, sp_count, part), 1)
        in_part = own_sp(in_weight.reshape(rows_here, dp_count, sp_count, ff_rows), 2)
        both_part = jnp.concatenate([out_part, in_part.reshape(rows_here, ff_part)], axis=1)
    down_part = lax.dynamic_slice_in_dim(down_weight, me_sp * ff_rows, ff_rows, 0)
    at_rows = gather_offsets(rows_here, dp_count)
    at_ff = gather_offsets(ff_rows, dp_count)
    qkv_pieces = gather_dp(qkv_part, dp_count)
    both_pieces = gather_dp(both_part, dp_count)
    down_pieces = gather_dp(down_part, dp_count)
    count = len(qkv_pieces)
    sems = pltpu.SemaphoreType.DMA((count,))

    table_here = lax.dynamic_slice_in_dim(bias_table, me_sp * heads, heads, 0)
    reversed_buckets = jnp.pad(bucket_index[::-1], (1, BLOCK - 1))[None]
    padded_buckets = jnp.pad(bucket_index, (BLOCK - 1, 1), constant_values=-1)[None]
    (bias,) = call(
        bias_kernel, [shaped((heads, diagonals, BLOCK, BLOCK), F32)], [table_here, reversed_buckets]
    )
    seg_row = segment_ids
    seg_col = segment_ids.reshape(seq_len, 1)

    tokens = inputs[0]
    token_pieces = gather_sp(tokens)
    up_pieces = gather_sp(cotangent[0])
    act_one, normed_one = call(
        norm_kernel,
        [shaped((seq_len, width), BF16)] * 2,
        [*token_pieces, norm_gain, norm_shift],
        (),
        [me],
        (),
        (20 * seq_len * width, 6 * seq_len * width),
    )
    qkv, attn, logs = call(
        functools.partial(attend_kernel, scale, count),
        [shaped((seq_len, 3 * part), BF16), shaped((seq_len, part), BF16), shaped((seq_len, BLOCK), F32)],
        [act_one, bias, seg_col, seg_row],
        qkv_pieces,
        [at_rows],
        [pltpu.VMEM((width, 3 * part), BF16), sems],
        (2 * seq_len * width * 3 * part, 8 * seq_len * width),
    )
    attn_pieces = gather_sp(attn)
    if count == 1:
        out_columns = both_pieces[0][:, :part]
    else:

        def assemble(*refs):
            finish(load(refs[:count], refs[count], refs[count + 1], refs[count + 2], slice(0, part)))

        (out_columns,) = call(
            assemble, [shaped((width, part), BF16)], [], both_pieces, [at_rows], [sems], (0, 4 * width * part)
        )
    out_pieces = gather_sp(out_columns)
    resid, act_two = call(
        branch_kernel,
        [shaped((tok, width), F32), shaped((tok, width), BF16)],
        [*attn_pieces, *out_pieces, tokens, norm_gain, norm_shift],
        (),
        [me],
        [pltpu.VMEM((tok, width), BF16)],
        (2 * tok * width * width, 4 * width * width),
    )
    act_pieces = gather_sp(act_two)
    fed, slope, grad_down = call(
        functools.partial(feed_kernel, count, part),
        [shaped((seq_len, ff_part), BF16), shaped((seq_len, ff_part), F32), shaped((ff_part, width), BF16)],
        [*act_pieces, *up_pieces],
        both_pieces,
        [at_rows],
        [pltpu.VMEM((width, ff_part), BF16), pltpu.VMEM((seq_len, width), BF16), sems],
        (4 * seq_len * width * ff_part, 12 * seq_len * width),
    )

    share_shapes = [shaped((tok, width), F32), shaped((tok, width), F32), shaped((2 * tok, width), BF16)]
    grad_hidden, own_two, far_two, send_two = call(
        functools.partial(feed_back_kernel, count, part),
        [shaped((seq_len, ff_part), BF16)] + share_shapes,
        [slope, *up_pieces],
        [*down_pieces, *both_pieces],
        [at_ff, at_rows],
        [pltpu.VMEM((ff_part, width), BF16), pltpu.VMEM((width, ff_part), BF16), sems, sems],
        (4 * seq_len * width * ff_part, 12 * seq_len * width),
    )
    near_two, last_two = reduce_sp(far_two, send_two)
    grad_in, own_out, far_out, send_out = call(
        functools.partial(feed_rest_kernel, count),
        [shaped((width, ff_part), BF16)] + share_shapes,
        [fed, grad_hidden, *act_pieces],
        down_pieces,
        [at_ff],
        [pltpu.VMEM((seq_len, width), BF16), pltpu.VMEM((ff_part, width), BF16), sems],
        (4 * seq_len * width * ff_part, 12 * seq_len * width),
    )
    near_out, last_out = reduce_sp(far_out, send_out)
    output = (resid + own_out + near_out[:tok].astype(F32) + last_out.astype(F32)).astype(BF16)

    grad_resid, sums_two, *sends = call(
        branch_back_kernel,
        [shaped((tok, width), F32), shaped((8, width), F32)] + [shaped((tok, 2 * part), BF16)] * 4,
        [own_two, near_two, last_two, resid, cotangent[0], norm_gain, *out_pieces],
        (),
        [me],
        [pltpu.VMEM((tok, width), BF16), pltpu.VMEM((tok, width), BF16)],
        (2 * tok * width * width, 4 * width * width),
    )
    grad_pieces = [sends[0]] + [swap(sends[step], step) for step in (1, 2, 3)]
    last_rows = rows_here + SMALL_ROWS if aligned else rows_here
    last, small, own_one, far_one, send_one = call(
        functools.partial(attend_back_kernel, scale, count),
        [shaped((dp_count, last_rows, 4 * part), BF16), shaped((8, width), F32)] + share_shapes,
        [qkv, logs, bias, seg_col, seg_row, act_one, normed_one, sums_two, padded_buckets]
        + [*attn_pieces, *grad_pieces],
        qkv_pieces,
        [at_rows, me],
        [
            pltpu.VMEM((width, 3 * part), BF16),
            pltpu.VMEM((seq_len, part), BF16),
            pltpu.VMEM((seq_len, part), BF16),
            pltpu.VMEM((seq_len, 3 * part), BF16),
            pltpu.VMEM((seq_len, part), F32),
            pltpu.VMEM((seq_len, part), F32),
            pltpu.VMEM((heads, diagonals, BLOCK, BLOCK), F32),
            pltpu.VMEM((heads, seq_len + BLOCK), F32),
            sems,
        ],
        (4 * seq_len * width * 4 * part, 16 * seq_len * width),
    )
    near_one, last_one = reduce_sp(far_one, send_one)
    (grad_input,) = call(
        norm_back_kernel,
        [shaped((tok, width), F32)],
        [own_one, near_one, last_one, tokens, grad_resid, norm_gain],
        cost=(20 * tok * width, 20 * tok * width),
    )

    sum_down = scatter_dp(grad_down.reshape(dp_count, ff_rows, width), dp_count)
    sum_in = scatter_dp(grad_in.reshape(dp_count, rows_here, ff_part), dp_count)
    if not aligned:
        table = jnp.zeros((head_total * bucket_count,), F32)
        table = lax.dynamic_update_slice_in_dim(table, small[4, :BLOCK], me_sp * BLOCK, 0)
        packed = [small[at].reshape(dp_count, -1) for at in range(4)] + [table.reshape(dp_count, -1)]
        packed = jnp.concatenate(packed, axis=1).astype(BF16)
        packed = jnp.pad(packed, ((0, 0), (0, 4 * part - packed.shape[1])))
        packed = jnp.pad(packed[:, None], ((0, 0), (0, SMALL_ROWS - 1), (0, 0)))
        last = jnp.concatenate([last, packed], axis=1)
    sum_last = scatter_dp(last, dp_count)
    in_pieces, down_sums, last_pieces = gather_sp(sum_in), gather_sp(sum_down), gather_sp(sum_last)
    if aligned:
        out_in, out_down = call(
            wide_feed_kernel,
            [shaped((rows_here, ff), F32), shaped((sp_count * ff_rows, width), F32)],
            [*in_pieces, *down_sums],
            (),
            [me],
            (),
            (0, 6 * rows_here * ff),
        )
        out_qkv, out_out, small_sum = call(
            functools.partial(wide_last_kernel, part),
            [
                shaped((rows_here, 3 * width), F32),
                shaped((rows_here, width), F32),
                shaped((SMALL_ROWS, 4 * part), F32),
            ],
            last_pieces,
            (),
            [me],
            (),
            (0, 24 * rows_here * width),
        )
    else:
        out_down = stacked_sp(down_sums).astype(F32).reshape(sp_count * ff_rows, width)
        all_in = stacked_sp(in_pieces).astype(F32).reshape(sp_count, rows_here, dp_count, ff_rows)
        out_in = jnp.moveaxis(all_in, 0, 2).reshape(rows_here, ff)
        all_last = stacked_sp(last_pieces).astype(F32)
        all_qkv = all_last[:, :rows_here, : 3 * part].reshape(sp_count, rows_here, 3, part)
        out_qkv = jnp.moveaxis(all_qkv, 0, 2).reshape(rows_here, 3 * width)
        out_out = jnp.moveaxis(all_last[:, :rows_here, 3 * part :], 0, 1).reshape(rows_here, width)
        small_sum = jnp.sum(all_last[:, rows_here:], axis=0)
    piece = width // dp_count
    small_row = small_sum[0]
    gains = small_row[: 2 * piece].reshape(2, piece)
    shifts = small_row[2 * piece : 4 * piece].reshape(2, piece)
    tables = small_row[4 * piece : 4 * piece + head_total * bucket_count // dp_count]
    return (output[None], grad_input[None], out_qkv, out_out, out_in, out_down, gains, shifts, tables)


def solution(mesh):
    in_specs = (
        P("dp", "sp", None),
        P("dp", None),
        P("dp", None),
        P("dp", None),
        P("dp", None),
        P(),
        P(),
        P(),
        P("dp", None),
        P(),
        P("dp", "sp", None),
    )
    out_specs = (
        P("dp", "sp", None),
        P("dp", "sp", None),
        P("dp", None),
        P("dp", None),
        P("dp", None),
        P("dp", None),
        P(None, "dp"),
        P(None, "dp"),
        P("dp"),
    )
    return jax.shard_map(
        on_device, mesh=mesh, in_specs=in_specs, out_specs=out_specs, check_vma=False
    )
```

time: 580 us -> 279 us (0.48); the launches traced: 572 us -> 278 us
  local copies, waits for them, and re-layouts: 346 us -> 19.2 us
  Pallas kernels: 12.6 us -> 76.2 us
  matrix products: 25.2 us -> 0 us
  waiting for transfers between devices: 84.1 us -> 101 us
  other arithmetic: 28.7 us -> 12.4 us
    dynamic_update_slice x56 -> x0, local copies, waits for them, and re-layouts: 265 us -> none  [the longest x3 219 us: gather_dp(): return lax.dynamic_update_slice(whole, down[None], (last, half, 0))]
    pallas_call x3 -> x15, Pallas kernels: 12.6 us -> 76.2 us  [call(): pl.pallas_call(kernel, out_shape=tuple(outs), in_specs=specs, out_specs=t...]
    dot_general x16 -> x0, matrix products: 25.2 us -> none  [the longest x15 25 us: dot(): lax.dot_general(left, right, (((left_dim,), (right_dim,)), ((), ())), pre...]
    broadcast_in_dim x25 -> x2, local copies, waits for them, and re-layouts: 23.5 us -> 1.15 us  [the longest x1 0.58 us: on_device(): reversed_buckets = jnp.pad(bucket_index[::-1], (1, BLOCK - 1))[None]]
    ppermute x9, waiting for transfers between devices: 4.66 us -> 22.5 us  [gather_dp(): up = lax.ppermute(up, 'dp', forward)]
    reshape x6 -> x0, local copies, waits for them, and re-layouts: 14.9 us -> none  [the longest x2 5.73 us: on_device(): jnp.moveaxis(all_in.reshape(sp_count, rows_here, dp_count, ff_rows), 0, 2)]
    gather x4 -> x0, local copies, waits for them, and re-layouts: 14.3 us -> none  [the longest x2 7.46 us: on_device(): sum_buckets = bucket_index[np.clip(summed, 0, seq_len - 1)]]
    ppermute x24, waiting for transfers between devices: 33.5 us -> 47.7 us  [the longest x9 32 us: scatter_dp(): lax.ppermute((for_down + down.astype(F32)).astype(BF16), 'dp', backward)]
  transfers between devices with their start and end apart: 87 -> 81, of which waited for: 29 -> 27; matrix products, arithmetic and copies ran while one was open for 66% -> 7% of each run, Pallas kernels for 2% -> 22%
where the time goes in v2:
time: 279 us; the launch traced here: 278 us
  waiting for transfers between devices  101 us (36%)
  Pallas kernels  76.2 us (27%)
  starting transfers between devices  67.8 us (24%)
  local copies, waits for them, and re-layouts  19.2 us (7%)
  other arithmetic  12.4 us (4%)
    pallas_call x15, Pallas kernels, call(): pl.pallas_call(kernel, out_shape=tuple(outs), in_specs=specs, out_specs=t...  76.2 us
    ppermute x9, waiting for transfers between devices, scatter_dp(): lax.ppermute((for_down + down.astype(F32)).astype(BF16), 'dp', backward)  32 us
    ppermute x33, waiting for transfers between devices, swap(): return lax.ppermute(values, 'sp', [(i, i ^ bit) for i in range(count)])  27 us
    ppermute x9, waiting for transfers between devices, gather_dp(): up = lax.ppermute(up, 'dp', forward)  22.5 us
    ppermute x33, starting transfers between devices, swap(): return lax.ppermute(values, 'sp', [(i, i ^ bit) for i in range(count)])  15.4 us
    ppermute x9, starting transfers between devices, gather_dp(): up = lax.ppermute(up, 'dp', forward)  15 us
    ppermute x9, starting transfers between devices, scatter_dp(): lax.ppermute((for_down + down.astype(F32)).astype(BF16), 'dp', backward)  12.3 us
    unnamed x132, local copies, waits for them, and re-layouts  8.34 us
  transfers between devices with their start and end apart: 81, of which 27 were waited for; matrix products, arithmetic and copies ran while one was open for 7% of the time, Pallas kernels for 22%

profile of v2, /device:TPU:0, one launch (start us, length us, event | category | flops | bytes accessed | tf_op | source)
XLA Modules:
  0.0 278.3 jit_solution(13708805180442834845)
XLA Ops:
  0.7 1.8 shard_map.182.refs_0_.refs_8_.refs_14_
  2.5 3.1 %collective-permute-start.14 = (bf16[128,1280]{1,0:T(8,128)(2,1)}, bf16[128,1280]{1,0:T(8,128)(2,1)S(1)}, u32[]{:S(2)}, u32[]{:S(2)}) collective-permute-start(bf16[128,1280]{1,0:T(8,128)(2,1)} %shard_map.182.refs_0_.refs_8_.refs_14_), channel_id=1, source_target_pairs={{0,8},{8,16},{16,24},{24,28},{28,20},{20,12},{12,4},{4,0},{1,9},{9... | collective-permute-start | bytes 983048 | tf_op jit(solution)/shard_map/ppermute | solution.py:95
  5.6 7.9 %collective-permute-done.14.refs_1_.refs_9_.refs_15_ = bf16[128,1280]{1,0:T(8,128)(2,1)S(1)} collective-permute-done((bf16[128,1280]{1,0:T(8,128)(2,1)}, bf16[128,1280]{1,0:T(8,128)(2,1)S(1)}, u32[]{:S(2)}, u32[]{:S(2)}) %collective-permute-start.14) | collective-permute-done | bytes 327712 | tf_op jit(solution)/shard_map/ppermute | solution.py:95
  13.5 1.8 collective-permute-start.16
  15.5 6.9 %collective-permute-done.16.refs_3_.refs_11_.refs_17_ = bf16[128,1280]{1,0:T(8,128)(2,1)S(1)} collective-permute-done((bf16[128,1280]{1,0:T(8,128)(2,1)S(1)}, bf16[128,1280]{1,0:T(8,128)(2,1)S(1)}, u32[]{:S(2)}, u32[]{:S(2)}) %collective-permute-start.16) | collective-permute-done | bytes 327712 | tf_op jit(solution)/shard_map/ppermute | solution.py:95
  22.4 1.5 collective-permute-start.18
  24.4 1.6 shard_map.180.refs_4_.refs_17_
  28.1 4.9 %collective-permute-done.18.refs_5_.refs_13_.refs_19_ = bf16[128,1280]{1,0:T(8,128)(2,1)S(1)} collective-permute-done((bf16[128,1280]{1,0:T(8,128)(2,1)S(1)}, bf16[128,1280]{1,0:T(8,128)(2,1)S(1)}, u32[]{:S(2)}, u32[]{:S(2)}) %collective-permute-start.18) | collective-permute-done | bytes 327712 | tf_op jit(solution)/shard_map/ppermute | solution.py:95
  33.0 1.5 collective-permute-start.20
  37.2 1.7 collective-permute-done.4.refs_6_.refs_19_
  41.5 2.6 shard_map.183.refs_4_.refs_6_
  44.1 1.6 collective-permute-start.23
  47.1 1.8 collective-permute-start.7
  52.3 2.2 shard_map.179.refs_1_.refs_2_
  54.9 1.8 collective-permute-start.9
  56.8 1.6 collective-permute-start.31
  59.1 3.3 %shard_map.178 = (bf16[512,1024]{1,0:T(8,128)(2,1)}, bf16[512,1024]{1,0:T(8,128)(2,1)}) custom-call(bf16[128,1024]{1,0:T(8,128)(2,1)} %bitcast.97, bf16[128,1024]{1,0:T(8,128)(2,1)} %copy-done.42, bf16[128,1024]{1,0:T(8,128)(2,1)} %collective-permute-done.1.refs_2_, bf16[128,1024]{1,0:T(8,128)(2,1)} %copy-done.43, f32[2,1024]{1,0:T(2,128)} %gain_ref.1, ...), custom_call_target="tpu_custom_call" | custom-call | flops 10485760 | bytes 3145728 | tf_op jit(solution)/shard_map/pallas_call | solution.py:48
  63.1 8.4 %shard_map.181 = (bf16[512,768]{1,0:T(8,128)(2,1)}, bf16[512,256]{1,0:T(8,128)(2,1)}, f32[512,128]{1,0:T(8,128)}) custom-call(bf16[512,1024]{1,0:T(8,128)(2,1)} %get-tuple-element.42.refs_0_.refs_5_, f32[4,4,128,128]{3,2,1,0:T(8,128)} %shard_map.179.refs_1_.refs_2_, s32[512,1]{1,0:T(8,128)} %copy.20.refs_2_.refs_3_, s32[1,512]{1,0:T(1,128)} %refs_4_.3, ...), custom_call_target="tpu_custom_call" | custom-call | flops 805306368 | bytes 4194304 | tf_op jit(solution)/shard_map/pallas_call | solution.py:48
  71.6 1.5 collective-permute-start.12
  73.6 1.6 collective-permute-start.33
  75.2 4.1 %collective-permute-done.12.refs_2_.refs_11_ = bf16[512,256]{1,0:T(8,128)(2,1)S(1)} collective-permute-done((bf16[512,256]{1,0:T(8,128)(2,1)}, bf16[512,256]{1,0:T(8,128)(2,1)S(1)}, u32[]{:S(2)}, u32[]{:S(2)}) %collective-permute-start.12) | collective-permute-done | bytes 262176 | tf_op jit(solution)/shard_map/ppermute | solution.py:128
  79.2 2.6 collective-permute-done.33.refs_8_.refs_9_
  82.9 1.6 collective-permute-start.35
  86.1 3.4 %shard_map.184 = (f32[128,1024]{1,0:T(8,128)}, bf16[128,1024]{1,0:T(8,128)(2,1)}) custom-call(bf16[512,256]{1,0:T(8,128)(2,1)} %get-tuple-element.43.refs_0_.refs_9_, bf16[512,256]{1,0:T(8,128)(2,1)} %copy-done.31, bf16[512,256]{1,0:T(8,128)(2,1)} %copy-done.30, bf16[512,256]{1,0:T(8,128)(2,1)} %copy-done.32, bf16[1024,256]{1,0:T(8,128)(2,1)} %shard_map.183.refs_4_.refs_6_, ...), custom_call_target="tpu_custom_call" | custom-call | flops 268435456 | bytes 4194304 | tf_op jit(solution)/shard_map/pallas_call | solution.py:48
  92.0 4.3 %collective-permute-done.26.refs_2_.refs_4_ = bf16[128,1024]{1,0:T(8,128)(2,1)S(1)} collective-permute-done((bf16[128,1024]{1,0:T(8,128)(2,1)}, bf16[128,1024]{1,0:T(8,128)(2,1)S(1)}, u32[]{:S(2)}, u32[]{:S(2)}) %collective-permute-start.26) | collective-permute-done | bytes 262176 | tf_op jit(solution)/shard_map/ppermute | solution.py:128
  97.3 1.6 collective-permute-start.37
  101.1 7.9 %shard_map.185 = (bf16[512,1024]{1,0:T(8,128)(2,1)}, f32[512,1024]{1,0:T(8,128)}, bf16[1024,1024]{1,0:T(8,128)(2,1)}) custom-call(bf16[128,1024]{1,0:T(8,128)(2,1)} %get-tuple-element.45.refs_0_.refs_2_, bf16[128,1024]{1,0:T(8,128)(2,1)} %copy-done.57, bf16[128,1024]{1,0:T(8,128)(2,1)} %copy-done.55, bf16[128,1024]{1,0:T(8,128)(2,1)} %copy-done.58, ...), custom_call_target="tpu_custom_call" | custom-call | flops 2147483648 | bytes 6291456 | tf_op jit(solution)/shard_map/pallas_call | solution.py:48
  109.7 10.6 %shard_map.186 = (bf16[512,1024]{1,0:T(8,128)(2,1)}, f32[128,1024]{1,0:T(8,128)}, f32[128,1024]{1,0:T(8,128)}, bf16[256,1024]{1,0:T(8,128)(2,1)}) custom-call(f32[512,1024]{1,0:T(8,128)} %get-tuple-element.47.refs_0_, bf16[128,1024]{1,0:T(8,128)(2,1)} %bitcast.118, bf16[128,1024]{1,0:T(8,128)(2,1)} %copy-done.59, bf16[128,1024]{1,0:T(8,128)(2,1)} %copy-done.56, ...), custom_call_target="tpu_custom_call" | custom-call | flops 2147483648 | bytes 6291456 | tf_op jit(solution)/shard_map/pallas_call | solution.py:48
  121.1 1.6 collective-permute-start.70
  122.7 5.6 %shard_map.187 = (bf16[1024,1024]{1,0:T(8,128)(2,1)}, f32[128,1024]{1,0:T(8,128)}, f32[128,1024]{1,0:T(8,128)}, bf16[256,1024]{1,0:T(8,128)(2,1)}) custom-call(bf16[512,1024]{1,0:T(8,128)(2,1)} %get-tuple-element.46.refs_0_, bf16[512,1024]{1,0:T(8,128)(2,1)} %get-tuple-element.48.refs_1_, bf16[128,1024]{1,0:T(8,128)(2,1)} %get-tuple-element.45.refs_0_.refs_2_, ...), custom_call_target="tpu_custom_call" | custom-call | flops 2147483648 | bytes 6291456 | tf_op jit(solution)/shard_map/pallas_call | solution.py:48
  128.3 1.7 dynamic-slice_bitcast_fusion.4
  130.0 1.5 collective-permute-start.59
  131.5 1.7 add_convert_fusion.1
  138.8 2.7 collective-permute-done.42.refs_2_
  142.2 4.3 %shard_map.188 = (f32[128,1024]{1,0:T(8,128)}, f32[8,1024]{1,0:T(8,128)}, bf16[128,512]{1,0:T(8,128)(2,1)}, bf16[128,512]{1,0:T(8,128)(2,1)}, bf16[128,512]{1,0:T(8,128)(2,1)}, /*index=5*/bf16[128,512]{1,0:T(8,128)(2,1)}) custom-call(f32[128,1024]{1,0:T(8,128)} %get-tuple-element.55.refs_0_, bf16[256,1024]{1,0:T(8,128)(2,1)} %collective-permute-done.41.refs_1_, ...), custom_call_target="tpu_custom_call" | custom-call | flops 268435456 | bytes 4194304 | tf_op jit(solution)/shard_map/pallas_call | solution.py:48
  148.4 1.7 fusion.12
  150.5 2.6 collective-permute-done.44.refs_15_
  156.3 15.1 %shard_map.189 = (bf16[8,144,1024]{2,1,0:T(8,128)(2,1)}, f32[8,1024]{1,0:T(8,128)}, f32[128,1024]{1,0:T(8,128)}, f32[128,1024]{1,0:T(8,128)}, bf16[256,1024]{1,0:T(8,128)(2,1)}) custom-call(bf16[512,768]{1,0:T(8,128)(2,1)} %get-tuple-element.52.refs_0_, f32[512,128]{1,0:T(8,128)} %get-tuple-element.53.refs_1_, ...), custom_call_target="tpu_custom_call" | custom-call | flops 2147483648 | bytes 8388608 | tf_op jit(solution)/shard_map/pallas_call | solution.py:48
  174.3 3.8 %collective-permute-done.48 = bf16[64,1024]{1,0:T(8,128)(2,1)S(1)} collective-permute-done((bf16[64,1024]{1,0:T(8,128)(2,1)S(1)}, bf16[64,1024]{1,0:T(8,128)(2,1)S(1)}, u32[]{:S(2)}, u32[]{:S(2)}) %collective-permute-start.48) | collective-permute-done | bytes 131104 | tf_op jit(solution)/shard_map/ppermute | solution.py:114
  183.2 1.6 collective-permute-start.75
  184.8 6.9 %collective-permute-done.49 = bf16[144,1024]{1,0:T(8,128)(2,1)S(1)} collective-permute-done((bf16[144,1024]{1,0:T(8,128)(2,1)S(1)}, bf16[144,1024]{1,0:T(8,128)(2,1)S(1)}, u32[]{:S(2)}, u32[]{:S(2)}) %collective-permute-start.49) | collective-permute-done | bytes 294944 | tf_op jit(solution)/shard_map/ppermute | solution.py:121
  193.7 1.5 collective-permute-start.52
  195.3 3.9 %collective-permute-done.52 = bf16[80,1024]{1,0:T(8,128)(2,1)S(1)} collective-permute-done((bf16[80,1024]{1,0:T(8,128)(2,1)S(1)}, bf16[80,1024]{1,0:T(8,128)(2,1)S(1)}, u32[]{:S(2)}, u32[]{:S(2)}) %collective-permute-start.52) | collective-permute-done | bytes 163872 | tf_op jit(solution)/shard_map/ppermute | solution.py:115
  199.2 1.5 collective-permute-start.64
  203.4 5.1 %collective-permute-done.64 = bf16[128,1024]{1,0:T(8,128)(2,1)S(1)} collective-permute-done((bf16[128,1024]{1,0:T(8,128)(2,1)S(1)}, bf16[128,1024]{1,0:T(8,128)(2,1)S(1)}, u32[]{:S(2)}, u32[]{:S(2)}) %collective-permute-start.64) | collective-permute-done | bytes 262176 | tf_op jit(solution)/shard_map/ppermute | solution.py:122
  208.5 1.6 collective-permute-start.65
  210.1 4.7 %collective-permute-done.53 = bf16[144,1024]{1,0:T(8,128)(2,1)S(1)} collective-permute-done((bf16[144,1024]{1,0:T(8,128)(2,1)S(1)}, bf16[144,1024]{1,0:T(8,128)(2,1)S(1)}, u32[]{:S(2)}, u32[]{:S(2)}) %collective-permute-start.53) | collective-permute-done | bytes 294944 | tf_op jit(solution)/shard_map/ppermute | solution.py:122
  214.9 5.5 %collective-permute-done.76 = bf16[128,1024]{1,0:T(8,128)(2,1)S(1)} collective-permute-done((bf16[128,1024]{1,0:T(8,128)(2,1)S(1)}, bf16[128,1024]{1,0:T(8,128)(2,1)S(1)}, u32[]{:S(2)}, u32[]{:S(2)}) %collective-permute-start.76) | collective-permute-done | bytes 262176 | tf_op jit(solution)/shard_map/ppermute | solution.py:122
  220.4 1.5 collective-permute-start.54
  222.0 4.0 %collective-permute-done.65 = bf16[128,1024]{1,0:T(8,128)(2,1)S(1)} collective-permute-done((bf16[128,1024]{1,0:T(8,128)(2,1)S(1)}, bf16[128,1024]{1,0:T(8,128)(2,1)S(1)}, u32[]{:S(2)}, u32[]{:S(2)}) %collective-permute-start.65) | collective-permute-done | bytes 262176 | tf_op jit(solution)/shard_map/ppermute | solution.py:122
  226.0 1.5 collective-permute-start.77
  227.6 4.7 %collective-permute-done.54 = bf16[144,1024]{1,0:T(8,128)(2,1)S(1)} collective-permute-done((bf16[144,1024]{1,0:T(8,128)(2,1)S(1)}, bf16[144,1024]{1,0:T(8,128)(2,1)S(1)}, u32[]{:S(2)}, u32[]{:S(2)}) %collective-permute-start.54) | collective-permute-done | bytes 294944 | tf_op jit(solution)/shard_map/ppermute | solution.py:122
  232.8 1.7 collective-permute-start.55
  235.0 3.0 %collective-permute-done.77 = bf16[128,1024]{1,0:T(8,128)(2,1)S(1)} collective-permute-done((bf16[128,1024]{1,0:T(8,128)(2,1)S(1)}, bf16[128,1024]{1,0:T(8,128)(2,1)S(1)}, u32[]{:S(2)}, u32[]{:S(2)}) %collective-permute-start.77) | collective-permute-done | bytes 262176 | tf_op jit(solution)/shard_map/ppermute | solution.py:122
  237.9 1.5 collective-permute-start.66
  240.3 3.0 %collective-permute-done.55 = bf16[144,1024]{1,0:T(8,128)(2,1)S(1)} collective-permute-done((bf16[144,1024]{1,0:T(8,128)(2,1)S(1)}, bf16[144,1024]{1,0:T(8,128)(2,1)S(1)}, u32[]{:S(2)}, u32[]{:S(2)}) %collective-permute-start.55) | collective-permute-done | bytes 294944 | tf_op jit(solution)/shard_map/ppermute | solution.py:122
  244.0 2.0 collective-permute-done.66
  246.7 1.6 collective-permute-start.68
  248.3 10.1 %collective-permute-done.57.refs_2_ = bf16[144,1024]{1,0:T(8,128)(2,1)S(1)} collective-permute-done((bf16[144,1024]{1,0:T(8,128)(2,1)S(1)}, bf16[144,1024]{1,0:T(8,128)(2,1)S(1)}, u32[]{:S(2)}, u32[]{:S(2)}) %collective-permute-start.57) | collective-permute-done | bytes 294944 | tf_op jit(solution)/shard_map/ppermute | solution.py:128
  259.0 2.5 collective-permute-done.68.refs_2_
  261.6 1.9 fusion.24
  263.4 2.7 shard_map.190
  267.7 3.9 %shard_map.192 = (f32[128,4096]{1,0:T(8,128)}, f32[512,1024]{1,0:T(8,128)}) custom-call(bf16[128,1024]{1,0:T(8,128)(2,1)} %copy-done.13, bf16[128,1024]{1,0:T(8,128)(2,1)} %copy-done.38, bf16[128,1024]{1,0:T(8,128)(2,1)} %copy-done.37, bf16[128,1024]{1,0:T(8,128)(2,1)} %copy-done.40, bf16[128,1024]{1,0:T(8,128)(2,1)} %copy-done.12, ...), custom_call_target="tpu_custom_call" | custom-call | bytes 3145728 | tf_op jit(solution)/shard_map/pallas_call | solution.py:48
  273.1 2.7 shard_map.191
  (288 shorter events, 58.6 us)
Async XLA Ops:
  2.5 10.9 %collective-permute-start.14 = (bf16[128,1280]{1,0:T(8,128)(2,1)}, bf16[128,1280]{1,0:T(8,128)(2,1)S(1)}, u32[]{:S(2)}, u32[]{:S(2)}) collective-permute-start(bf16[128,1280]{1,0:T(8,128)(2,1)} %shard_map.182.refs_0_.refs_8_.refs_14_), channel_id=1, source_target_pairs={{0,8},{8,16},{16,24},{24,28},{28,20},{20,12},{12,4},{4,0},{1,9},{9... | collective-permute-start | bytes 983048 | tf_op jit(solution)/shard_map/ppermute | solution.py:95
  5.6 9.7 %collective-permute-start.15 = (bf16[128,1280]{1,0:T(8,128)(2,1)}, bf16[128,1280]{1,0:T(8,128)(2,1)S(1)}, u32[]{:S(2)}, u32[]{:S(2)}) collective-permute-start(bf16[128,1280]{1,0:T(8,128)(2,1)} %shard_map.182.refs_0_.refs_8_.refs_14_), channel_id=1, source_target_pairs={{8,0},{16,8},{24,16},{28,24},{20,28},{12,20},{4,12},{0,4},{9,1},{1... | collective-permute-start | bytes 983048 | tf_op jit(solution)/shard_map/ppermute | solution.py:96
  13.5 8.9 %collective-permute-start.16 = (bf16[128,1280]{1,0:T(8,128)(2,1)S(1)}, bf16[128,1280]{1,0:T(8,128)(2,1)S(1)}, u32[]{:S(2)}, u32[]{:S(2)}) collective-permute-start(bf16[128,1280]{1,0:T(8,128)(2,1)S(1)} %collective-permute-done.14.refs_1_.refs_9_.refs_15_), channel_id=1, source_target_pairs={{0,8},{8,16},{16,24},{24,28},{28,20},{20,12},{12,4},{4,0},{1,9},{9... | collective-permute-start | bytes 983048 | tf_op jit(solution)/shard_map/ppermute | solution.py:95
  15.3 8.6 %collective-permute-start.17 = (bf16[128,1280]{1,0:T(8,128)(2,1)S(1)}, bf16[128,1280]{1,0:T(8,128)(2,1)S(1)}, u32[]{:S(2)}, u32[]{:S(2)}) collective-permute-start(bf16[128,1280]{1,0:T(8,128)(2,1)S(1)} %collective-permute-done.15.refs_2_.refs_10_.refs_16_), channel_id=1, source_target_pairs={{8,0},{16,8},{24,16},{28,24},{20,28},{12,20},{4,12},{0,4},{9,1},{1... | collective-permute-start | bytes 983048 | tf_op jit(solution)/shard_map/ppermute | solution.py:96
  22.4 10.6 %collective-permute-start.18 = (bf16[128,1280]{1,0:T(8,128)(2,1)S(1)}, bf16[128,1280]{1,0:T(8,128)(2,1)S(1)}, u32[]{:S(2)}, u32[]{:S(2)}) collective-permute-start(bf16[128,1280]{1,0:T(8,128)(2,1)S(1)} %collective-permute-done.16.refs_3_.refs_11_.refs_17_), channel_id=1, source_target_pairs={{0,8},{8,16},{16,24},{24,28},{28,20},{20,12},{12,4},{4,0},{1,9},{9... | collective-permute-start | bytes 983048 | tf_op jit(solution)/shard_map/ppermute | solution.py:95
  23.8 10.7 %collective-permute-start.19 = (bf16[128,1280]{1,0:T(8,128)(2,1)S(1)}, bf16[128,1280]{1,0:T(8,128)(2,1)S(1)}, u32[]{:S(2)}, u32[]{:S(2)}) collective-permute-start(bf16[128,1280]{1,0:T(8,128)(2,1)S(1)} %collective-permute-done.17.refs_4_.refs_12_.refs_18_), channel_id=1, source_target_pairs={{8,0},{16,8},{24,16},{28,24},{20,28},{12,20},{4,12},{0,4},{9,1},{1... | collective-permute-start | bytes 983048 | tf_op jit(solution)/shard_map/ppermute | solution.py:96
  26.0 12.8 %collective-permute-start.4 = (bf16[128,768]{1,0:T(8,128)(2,1)}, bf16[128,768]{1,0:T(8,128)(2,1)}, u32[]{:S(2)}, u32[]{:S(2)}) collective-permute-start(bf16[128,768]{1,0:T(8,128)(2,1)} %shard_map.180.refs_4_.refs_17_), channel_id=1, source_target_pairs={{8,0},{16,8},{24,16},{28,24},{20,28},{12,20},{4,12},{0,4},{9,1},{1... | collective-permute-start | bytes 589832 | tf_op jit(solution)/shard_map/ppermute | solution.py:96
  27.5 11.9 %collective-permute-start.3 = (bf16[128,768]{1,0:T(8,128)(2,1)}, bf16[128,768]{1,0:T(8,128)(2,1)}, u32[]{:S(2)}, u32[]{:S(2)}) collective-permute-start(bf16[128,768]{1,0:T(8,128)(2,1)} %shard_map.180.refs_4_.refs_17_), channel_id=1, source_target_pairs={{0,8},{8,16},{16,24},{24,28},{28,20},{20,12},{12,4},{4,0},{1,9},{9... | collective-permute-start | bytes 589832 | tf_op jit(solution)/shard_map/ppermute | solution.py:95
  33.0 8.4 %collective-permute-start.20 = (bf16[64,1280]{1,0:T(8,128)(2,1)S(1)}, bf16[64,1280]{1,0:T(8,128)(2,1)}, u32[]{:S(2)}, u32[]{:S(2)}) collective-permute-start(bf16[64,1280]{1,0:T(8,128)(2,1)S(1)} %slice.112), channel_id=1, source_target_pairs={{0,8},{8,16},{16,24},{24,28},{28,20},{20,12},{12,4},{4,0},{1,9},{9... | collective-permute-start | bytes 491528 | tf_op jit(solution)/shard_map/ppermute | solution.py:98
  35.8 13.1 %collective-permute-start.1 = (bf16[128,1024]{1,0:T(8,128)(2,1)S(1)}, bf16[128,1024]{1,0:T(8,128)(2,1)}, u32[]{:S(2)}, u32[]{:S(2)}) collective-permute-start(bf16[128,1024]{1,0:T(8,128)(2,1)S(1)} %bitcast.100), channel_id=1, source_target_pairs={{0,2},{1,3},{2,0},{3,1},{4,6},{5,7},{6,4},{7,5},{8,10},{9,11},{10,... | collective-permute-start | bytes 786440 | tf_op jit(solution)/shard_map/ppermute | solution.py:128
  38.8 8.1 %collective-permute-start.6 = (bf16[128,768]{1,0:T(8,128)(2,1)}, bf16[128,768]{1,0:T(8,128)(2,1)}, u32[]{:S(2)}, u32[]{:S(2)}) collective-permute-start(bf16[128,768]{1,0:T(8,128)(2,1)} %collective-permute-done.4.refs_6_.refs_19_), channel_id=1, source_target_pairs={{8,0},{16,8},{24,16},{28,24},{20,28},{12,20},{4,12},{0,4},{9,1},{1... | collective-permute-start | bytes 589832 | tf_op jit(solution)/shard_map/ppermute | solution.py:96
  39.4 7.8 %collective-permute-start.5 = (bf16[128,768]{1,0:T(8,128)(2,1)}, bf16[128,768]{1,0:T(8,128)(2,1)}, u32[]{:S(2)}, u32[]{:S(2)}) collective-permute-start(bf16[128,768]{1,0:T(8,128)(2,1)} %collective-permute-done.3.refs_5_.refs_18_), channel_id=1, source_target_pairs={{0,8},{8,16},{16,24},{24,28},{28,20},{20,12},{12,4},{4,0},{1,9},{9... | collective-permute-start | bytes 589832 | tf_op jit(solution)/shard_map/ppermute | solution.py:95
  44.1 29.0 %collective-permute-start.23 = (bf16[1024,256]{1,0:T(8,128)(2,1)}, bf16[1024,256]{1,0:T(8,128)(2,1)S(1)}, u32[]{:S(2)}, u32[]{:S(2)}) collective-permute-start(bf16[1024,256]{1,0:T(8,128)(2,1)} %shard_map.183.refs_4_.refs_6_), channel_id=1, source_target_pairs={{0,2},{1,3},{2,0},{3,1},{4,6},{5,7},{6,4},{7,5},{8,10},{9,11},{10,... | collective-permute-start | bytes 1572872 | tf_op jit(solution)/shard_map/ppermute | solution.py:128
  47.1 7.7 %collective-permute-start.7 = (bf16[128,768]{1,0:T(8,128)(2,1)}, bf16[128,768]{1,0:T(8,128)(2,1)S(1)}, u32[]{:S(2)}, u32[]{:S(2)}) collective-permute-start(bf16[128,768]{1,0:T(8,128)(2,1)} %collective-permute-done.5.refs_7_.refs_20_), channel_id=1, source_target_pairs={{0,8},{8,16},{16,24},{24,28},{28,20},{20,12},{12,4},{4,0},{1,9},{9... | collective-permute-start | bytes 589832 | tf_op jit(solution)/shard_map/ppermute | solution.py:95
  48.9 7.8 %collective-permute-start = (bf16[128,1024]{1,0:T(8,128)(2,1)S(1)}, bf16[128,1024]{1,0:T(8,128)(2,1)S(1)}, u32[]{:S(2)}, u32[]{:S(2)}) collective-permute-start(bf16[128,1024]{1,0:T(8,128)(2,1)S(1)} %bitcast.101), channel_id=1, source_target_pairs={{0,1},{1,0},{2,3},{3,2},{4,5},{5,4},{6,7},{7,6},{8,9},{9,8},{10,11... | collective-permute-start | bytes 786440 | tf_op jit(solution)/shard_map/ppermute | solution.py:128
  48.9 9.5 %collective-permute-start.2 = (bf16[128,1024]{1,0:T(8,128)(2,1)}, bf16[128,1024]{1,0:T(8,128)(2,1)S(1)}, u32[]{:S(2)}, u32[]{:S(2)}) collective-permute-start(bf16[128,1024]{1,0:T(8,128)(2,1)} %collective-permute-done.1.refs_2_), channel_id=1, source_target_pairs={{0,1},{1,0},{2,3},{3,2},{4,5},{5,4},{6,7},{7,6},{8,9},{9,8},{10,11... | collective-permute-start | bytes 786440 | tf_op jit(solution)/shard_map/ppermute | solution.py:128
  54.6 7.9 %collective-permute-start.10 = (bf16[64,768]{1,0:T(8,128)(2,1)S(1)}, bf16[64,768]{1,0:T(8,128)(2,1)S(1)}, u32[]{:S(2)}, u32[]{:S(2)}) collective-permute-start(bf16[64,768]{1,0:T(8,128)(2,1)S(1)} %slice.111), channel_id=1, source_target_pairs={{8,0},{16,8},{24,16},{28,24},{20,28},{12,20},{4,12},{0,4},{9,1},{1... | collective-permute-start | bytes 294920 | tf_op jit(solution)/shard_map/ppermute | solution.py:99
  56.8 16.8 %collective-permute-start.31 = (bf16[128,1024]{1,0:T(8,128)(2,1)S(1)}, bf16[128,1024]{1,0:T(8,128)(2,1)S(1)}, u32[]{:S(2)}, u32[]{:S(2)}) collective-permute-start(bf16[128,1024]{1,0:T(8,128)(2,1)S(1)} %constant_dynamic-slice_fusion.refs_5_.refs_6_), channel_id=1, source_target_pairs={{0,8},{8,16},{16,24},{24,28},{28,20},{20,12},{12,4},{4,0},{1,9},{9... | collective-permute-start | bytes 786440 | tf_op jit(solution)/shard_map/ppermute | solution.py:95
  58.4 16.8 %collective-permute-start.32 = (bf16[128,1024]{1,0:T(8,128)(2,1)S(1)}, bf16[128,1024]{1,0:T(8,128)(2,1)S(1)}, u32[]{:S(2)}, u32[]{:S(2)}) collective-permute-start(bf16[128,1024]{1,0:T(8,128)(2,1)S(1)} %constant_dynamic-slice_fusion.refs_5_.refs_6_), channel_id=1, source_target_pairs={{8,0},{16,8},{24,16},{28,24},{20,28},{12,20},{4,12},{0,4},{9,1},{1... | collective-permute-start | bytes 786440 | tf_op jit(solution)/shard_map/ppermute | solution.py:96
  73.1 11.5 %collective-permute-start.22 = (bf16[1024,256]{1,0:T(8,128)(2,1)S(1)}, bf16[1024,256]{1,0:T(8,128)(2,1)S(1)}, u32[]{:S(2)}, u32[]{:S(2)}) collective-permute-start(bf16[1024,256]{1,0:T(8,128)(2,1)S(1)} %copy-done.1), channel_id=1, source_target_pairs={{0,1},{1,0},{2,3},{3,2},{4,5},{5,4},{6,7},{7,6},{8,9},{9,8},{10,11... | collective-permute-start | bytes 1572872 | tf_op jit(solution)/shard_map/ppermute | solution.py:128
  73.1 11.5 %collective-permute-start.24 = (bf16[1024,256]{1,0:T(8,128)(2,1)S(1)}, bf16[1024,256]{1,0:T(8,128)(2,1)S(1)}, u32[]{:S(2)}, u32[]{:S(2)}) collective-permute-start(bf16[1024,256]{1,0:T(8,128)(2,1)S(1)} %collective-permute-done.23.refs_6_.refs_8_), channel_id=1, source_target_pairs={{0,1},{1,0},{2,3},{3,2},{4,5},{5,4},{6,7},{7,6},{8,9},{9,8},{10,11... | collective-permute-start | bytes 1572872 | tf_op jit(solution)/shard_map/ppermute | solution.py:128
  73.6 8.3 %collective-permute-start.33 = (bf16[128,1024]{1,0:T(8,128)(2,1)S(1)}, bf16[128,1024]{1,0:T(8,128)(2,1)S(1)}, u32[]{:S(2)}, u32[]{:S(2)}) collective-permute-start(bf16[128,1024]{1,0:T(8,128)(2,1)S(1)} %collective-permute-done.31.refs_6_.refs_7_), channel_id=1, source_target_pairs={{0,8},{8,16},{16,24},{24,28},{28,20},{20,12},{12,4},{4,0},{1,9},{9... | collective-permute-start | bytes 786440 | tf_op jit(solution)/shard_map/ppermute | solution.py:95
  81.9 9.5 %collective-permute-start.29 = (bf16[128,1024]{1,0:T(8,128)(2,1)S(1)}, bf16[128,1024]{1,0:T(8,128)(2,1)S(1)}, u32[]{:S(2)}, u32[]{:S(2)}) collective-permute-start(bf16[128,1024]{1,0:T(8,128)(2,1)S(1)} %bitcast.120), channel_id=1, source_target_pairs={{0,2},{1,3},{2,0},{3,1},{4,6},{5,7},{6,4},{7,5},{8,10},{9,11},{10,... | collective-permute-start | bytes 786440 | tf_op jit(solution)/shard_map/ppermute | solution.py:128
  82.5 8.4 %collective-permute-start.34 = (bf16[128,1024]{1,0:T(8,128)(2,1)S(1)}, bf16[128,1024]{1,0:T(8,128)(2,1)S(1)}, u32[]{:S(2)}, u32[]{:S(2)}) collective-permute-start(bf16[128,1024]{1,0:T(8,128)(2,1)S(1)} %collective-permute-done.32.refs_7_.refs_8_), channel_id=1, source_target_pairs={{8,0},{16,8},{24,16},{28,24},{20,28},{12,20},{4,12},{0,4},{9,1},{1... | collective-permute-start | bytes 786440 | tf_op jit(solution)/shard_map/ppermute | solution.py:96
  82.9 8.9 %collective-permute-start.35 = (bf16[128,1024]{1,0:T(8,128)(2,1)S(1)}, bf16[128,1024]{1,0:T(8,128)(2,1)S(1)}, u32[]{:S(2)}, u32[]{:S(2)}) collective-permute-start(bf16[128,1024]{1,0:T(8,128)(2,1)S(1)} %collective-permute-done.33.refs_8_.refs_9_), channel_id=1, source_target_pairs={{0,8},{8,16},{16,24},{24,28},{28,20},{20,12},{12,4},{4,0},{1,9},{9... | collective-permute-start | bytes 786440 | tf_op jit(solution)/shard_map/ppermute | solution.py:95
  91.4 8.2 %collective-permute-start.30 = (bf16[128,1024]{1,0:T(8,128)(2,1)S(1)}, bf16[128,1024]{1,0:T(8,128)(2,1)S(1)}, u32[]{:S(2)}, u32[]{:S(2)}) collective-permute-start(bf16[128,1024]{1,0:T(8,128)(2,1)S(1)} %collective-permute-done.29.refs_6_.refs_3_), channel_id=1, source_target_pairs={{0,1},{1,0},{2,3},{3,2},{4,5},{5,4},{6,7},{7,6},{8,9},{9,8},{10,11... | collective-permute-start | bytes 786440 | tf_op jit(solution)/shard_map/ppermute | solution.py:128
  91.9 7.7 %collective-permute-start.25 = (bf16[128,1024]{1,0:T(8,128)(2,1)}, bf16[128,1024]{1,0:T(8,128)(2,1)S(1)}, u32[]{:S(2)}, u32[]{:S(2)}) collective-permute-start(bf16[128,1024]{1,0:T(8,128)(2,1)} %get-tuple-element.45.refs_0_.refs_2_), channel_id=1, source_target_pairs={{0,1},{1,0},{2,3},{3,2},{4,5},{5,4},{6,7},{7,6},{8,9},{9,8},{10,11... | collective-permute-start | bytes 786440 | tf_op jit(solution)/shard_map/ppermute | solution.py:128
  97.3 11.7 %collective-permute-start.37 = (bf16[64,1024]{1,0:T(8,128)(2,1)S(1)}, bf16[64,1024]{1,0:T(8,128)(2,1)S(1)}, u32[]{:S(2)}, u32[]{:S(2)}) collective-permute-start(bf16[64,1024]{1,0:T(8,128)(2,1)S(1)} %slice.114), channel_id=1, source_target_pairs={{0,8},{8,16},{16,24},{24,28},{28,20},{20,12},{12,4},{4,0},{1,9},{9... | collective-permute-start | bytes 393224 | tf_op jit(solution)/shard_map/ppermute | solution.py:98
  98.9 10.1 %collective-permute-start.38 = (bf16[64,1024]{1,0:T(8,128)(2,1)S(1)}, bf16[64,1024]{1,0:T(8,128)(2,1)S(1)}, u32[]{:S(2)}, u32[]{:S(2)}) collective-permute-start(bf16[64,1024]{1,0:T(8,128)(2,1)S(1)} %slice.115), channel_id=1, source_target_pairs={{8,0},{16,8},{24,16},{28,24},{20,28},{12,20},{4,12},{0,4},{9,1},{1... | collective-permute-start | bytes 393224 | tf_op jit(solution)/shard_map/ppermute | solution.py:99
  120.4 11.2 %collective-permute-start.41 = (bf16[256,1024]{1,0:T(8,128)(2,1)}, bf16[256,1024]{1,0:T(8,128)(2,1)}, u32[]{:S(2)}, u32[]{:S(2)}) collective-permute-start(bf16[256,1024]{1,0:T(8,128)(2,1)} %get-tuple-element.56), channel_id=1, source_target_pairs={{0,1},{1,0},{2,3},{3,2},{4,5},{5,4},{6,7},{7,6},{8,9},{9,8},{10,11... | collective-permute-start | bytes 1572872 | tf_op jit(solution)/shard_map/ppermute | solution.py:128
  121.1 12.7 %collective-permute-start.70 = (bf16[64,1024]{1,0:T(8,128)(2,1)S(1)}, bf16[64,1024]{1,0:T(8,128)(2,1)S(1)}, u32[]{:S(2)}, u32[]{:S(2)}) collective-permute-start(bf16[64,1024]{1,0:T(8,128)(2,1)S(1)} %get-tuple-element.79), channel_id=1, source_target_pairs={{0,8},{8,16},{16,24},{24,28},{28,20},{20,12},{12,4},{4,0},{1,9},{9... | collective-permute-start | bytes 393224 | tf_op jit(solution)/shard_map/ppermute | solution.py:114
  130.0 7.8 %collective-permute-start.59 = (bf16[64,1024]{1,0:T(8,128)(2,1)}, bf16[64,1024]{1,0:T(8,128)(2,1)}, u32[]{:S(2)}, u32[]{:S(2)}) collective-permute-start(bf16[64,1024]{1,0:T(8,128)(2,1)} %get-tuple-element.83), channel_id=1, source_target_pairs={{0,8},{8,16},{16,24},{24,28},{28,20},{20,12},{12,4},{4,0},{1,9},{9... | collective-permute-start | bytes 393224 | tf_op jit(solution)/shard_map/ppermute | solution.py:114
  133.2 8.3 %collective-permute-start.42 = (bf16[128,1024]{1,0:T(8,128)(2,1)}, bf16[128,1024]{1,0:T(8,128)(2,1)S(1)}, u32[]{:S(2)}, u32[]{:S(2)}) collective-permute-start(bf16[128,1024]{1,0:T(8,128)(2,1)} %add_convert_fusion.1), channel_id=1, source_target_pairs={{0,2},{1,3},{2,0},{3,1},{4,6},{5,7},{6,4},{7,5},{8,10},{9,11},{10,... | collective-permute-start | bytes 786440 | tf_op jit(solution)/shard_map/ppermute | solution.py:128
  134.6 12.6 %collective-permute-start.71 = (bf16[128,1024]{1,0:T(8,128)(2,1)}, bf16[128,1024]{1,0:T(8,128)(2,1)}, u32[]{:S(2)}, u32[]{:S(2)}) collective-permute-start(bf16[128,1024]{1,0:T(8,128)(2,1)} %fusion.11), channel_id=1, source_target_pairs={{0,8},{8,16},{16,24},{24,28},{28,20},{20,12},{12,4},{4,0},{1,9},{9... | collective-permute-start | bytes 786440 | tf_op jit(solution)/shard_map/ppermute | solution.py:121
  136.6 45.0 %collective-permute-start.74 = (bf16[64,1024]{1,0:T(8,128)(2,1)}, bf16[64,1024]{1,0:T(8,128)(2,1)}, u32[]{:S(2)}, u32[]{:S(2)}) collective-permute-start(bf16[64,1024]{1,0:T(8,128)(2,1)} %get-tuple-element.80), channel_id=1, source_target_pairs={{8,0},{16,8},{24,16},{28,24},{20,28},{12,20},{4,12},{0,4},{9,1},{1... | collective-permute-start | bytes 393224 | tf_op jit(solution)/shard_map/ppermute | solution.py:115
  137.3 55.8 %collective-permute-start.63 = (bf16[64,1024]{1,0:T(8,128)(2,1)}, bf16[64,1024]{1,0:T(8,128)(2,1)S(1)}, u32[]{:S(2)}, u32[]{:S(2)}) collective-permute-start(bf16[64,1024]{1,0:T(8,128)(2,1)} %get-tuple-element.84), channel_id=1, source_target_pairs={{8,0},{16,8},{24,16},{28,24},{20,28},{12,20},{4,12},{0,4},{9,1},{1... | collective-permute-start | bytes 393224 | tf_op jit(solution)/shard_map/ppermute | solution.py:115
  147.2 7.8 %collective-permute-start.45 = (bf16[128,512]{1,0:T(8,128)(2,1)}, bf16[128,512]{1,0:T(8,128)(2,1)S(1)}, u32[]{:S(2)}, u32[]{:S(2)}) collective-permute-start(bf16[128,512]{1,0:T(8,128)(2,1)} %get-tuple-element.62), channel_id=1, source_target_pairs={{0,3},{1,2},{2,1},{3,0},{4,7},{5,6},{6,5},{7,4},{8,11},{9,10},{10,... | collective-permute-start | bytes 393224 | tf_op jit(solution)/shard_map/ppermute | solution.py:128
  150.1 29.8 %collective-permute-start.39 = (bf16[256,1024]{1,0:T(8,128)(2,1)}, bf16[256,1024]{1,0:T(8,128)(2,1)}, u32[]{:S(2)}, u32[]{:S(2)}) collective-permute-start(bf16[256,1024]{1,0:T(8,128)(2,1)} %get-tuple-element.50), channel_id=1, source_target_pairs={{0,1},{1,0},{2,3},{3,2},{4,5},{5,4},{6,7},{7,6},{8,9},{9,8},{10,11... | collective-permute-start | bytes 1572872 | tf_op jit(solution)/shard_map/ppermute | solution.py:128
  153.1 19.5 %collective-permute-start.60 = (bf16[128,1024]{1,0:T(8,128)(2,1)S(1)}, bf16[128,1024]{1,0:T(8,128)(2,1)}, u32[]{:S(2)}, u32[]{:S(2)}) collective-permute-start(bf16[128,1024]{1,0:T(8,128)(2,1)S(1)} %fusion.19), channel_id=1, source_target_pairs={{0,8},{8,16},{16,24},{24,28},{28,20},{20,12},{12,4},{4,0},{1,9},{9... | collective-permute-start | bytes 786440 | tf_op jit(solution)/shard_map/ppermute | solution.py:121
  155.0 27.1 %collective-permute-start.72 = (bf16[128,1024]{1,0:T(8,128)(2,1)}, bf16[128,1024]{1,0:T(8,128)(2,1)S(1)}, u32[]{:S(2)}, u32[]{:S(2)}) collective-permute-start(bf16[128,1024]{1,0:T(8,128)(2,1)} %fusion.12), channel_id=1, source_target_pairs={{0,8},{8,16},{16,24},{24,28},{28,20},{20,12},{12,4},{4,0},{1,9},{9... | collective-permute-start | bytes 786440 | tf_op jit(solution)/shard_map/ppermute | solution.py:121
  178.0 15.6 %collective-permute-start.61 = (bf16[128,1024]{1,0:T(8,128)(2,1)S(1)}, bf16[128,1024]{1,0:T(8,128)(2,1)S(1)}, u32[]{:S(2)}, u32[]{:S(2)}) collective-permute-start(bf16[128,1024]{1,0:T(8,128)(2,1)S(1)} %fusion.20), channel_id=1, source_target_pairs={{0,8},{8,16},{16,24},{24,28},{28,20},{20,12},{12,4},{4,0},{1,9},{9... | collective-permute-start | bytes 786440 | tf_op jit(solution)/shard_map/ppermute | solution.py:121
  179.9 11.8 %collective-permute-start.49 = (bf16[144,1024]{1,0:T(8,128)(2,1)S(1)}, bf16[144,1024]{1,0:T(8,128)(2,1)S(1)}, u32[]{:S(2)}, u32[]{:S(2)}) collective-permute-start(bf16[144,1024]{1,0:T(8,128)(2,1)S(1)} %fusion.3), channel_id=1, source_target_pairs={{0,8},{8,16},{16,24},{24,28},{28,20},{20,12},{12,4},{4,0},{1,9},{9... | collective-permute-start | bytes 884744 | tf_op jit(solution)/shard_map/ppermute | solution.py:121
  181.5 65.2 %collective-permute-start.40 = (bf16[128,1024]{1,0:T(8,128)(2,1)S(1)}, bf16[128,1024]{1,0:T(8,128)(2,1)S(1)}, u32[]{:S(2)}, u32[]{:S(2)}) collective-permute-start(bf16[128,1024]{1,0:T(8,128)(2,1)S(1)} %add_convert_fusion.3), channel_id=1, source_target_pairs={{0,2},{1,3},{2,0},{3,1},{4,6},{5,7},{6,4},{7,5},{8,10},{9,11},{10,... | collective-permute-start | bytes 786440 | tf_op jit(solution)/shard_map/ppermute | solution.py:128
  183.2 19.5 %collective-permute-start.75 = (bf16[128,1024]{1,0:T(8,128)(2,1)S(1)}, bf16[128,1024]{1,0:T(8,128)(2,1)S(1)}, u32[]{:S(2)}, u32[]{:S(2)}) collective-permute-start(bf16[128,1024]{1,0:T(8,128)(2,1)S(1)} %get-tuple-element.78), channel_id=1, source_target_pairs={{8,0},{16,8},{24,16},{28,24},{20,28},{12,20},{4,12},{0,4},{9,1},{1... | collective-permute-start | bytes 786440 | tf_op jit(solution)/shard_map/ppermute | solution.py:122
  191.8 10.0 %collective-permute-start.50 = (bf16[144,1024]{1,0:T(8,128)(2,1)S(1)}, bf16[144,1024]{1,0:T(8,128)(2,1)S(1)}, u32[]{:S(2)}, u32[]{:S(2)}) collective-permute-start(bf16[144,1024]{1,0:T(8,128)(2,1)S(1)} %fusion.4), channel_id=1, source_target_pairs={{0,8},{8,16},{16,24},{24,28},{28,20},{20,12},{12,4},{4,0},{1,9},{9... | collective-permute-start | bytes 884744 | tf_op jit(solution)/shard_map/ppermute | solution.py:121
  193.1 41.5 %collective-permute-start.73 = (bf16[128,1024]{1,0:T(8,128)(2,1)S(1)}, bf16[128,1024]{1,0:T(8,128)(2,1)S(1)}, u32[]{:S(2)}, u32[]{:S(2)}) collective-permute-start(bf16[128,1024]{1,0:T(8,128)(2,1)S(1)} %get-tuple-element.77), channel_id=1, source_target_pairs={{0,8},{8,16},{16,24},{24,28},{28,20},{20,12},{12,4},{4,0},{1,9},{9... | collective-permute-start | bytes 786440 | tf_op jit(solution)/shard_map/ppermute | solution.py:121
  199.2 9.2 %collective-permute-start.64 = (bf16[128,1024]{1,0:T(8,128)(2,1)S(1)}, bf16[128,1024]{1,0:T(8,128)(2,1)S(1)}, u32[]{:S(2)}, u32[]{:S(2)}) collective-permute-start(bf16[128,1024]{1,0:T(8,128)(2,1)S(1)} %get-tuple-element.82), channel_id=1, source_target_pairs={{8,0},{16,8},{24,16},{28,24},{20,28},{12,20},{4,12},{0,4},{9,1},{1... | collective-permute-start | bytes 786440 | tf_op jit(solution)/shard_map/ppermute | solution.py:122
  202.0 12.8 %collective-permute-start.53 = (bf16[144,1024]{1,0:T(8,128)(2,1)S(1)}, bf16[144,1024]{1,0:T(8,128)(2,1)S(1)}, u32[]{:S(2)}, u32[]{:S(2)}) collective-permute-start(bf16[144,1024]{1,0:T(8,128)(2,1)S(1)} %get-tuple-element.76), channel_id=1, source_target_pairs={{8,0},{16,8},{24,16},{28,24},{20,28},{12,20},{4,12},{0,4},{9,1},{1... | collective-permute-start | bytes 884744 | tf_op jit(solution)/shard_map/ppermute | solution.py:122
  202.8 17.6 %collective-permute-start.76 = (bf16[128,1024]{1,0:T(8,128)(2,1)S(1)}, bf16[128,1024]{1,0:T(8,128)(2,1)S(1)}, u32[]{:S(2)}, u32[]{:S(2)}) collective-permute-start(bf16[128,1024]{1,0:T(8,128)(2,1)S(1)} %fusion.9), channel_id=1, source_target_pairs={{8,0},{16,8},{24,16},{28,24},{20,28},{12,20},{4,12},{0,4},{9,1},{1... | collective-permute-start | bytes 786440 | tf_op jit(solution)/shard_map/ppermute | solution.py:122
  208.5 17.5 %collective-permute-start.65 = (bf16[128,1024]{1,0:T(8,128)(2,1)S(1)}, bf16[128,1024]{1,0:T(8,128)(2,1)S(1)}, u32[]{:S(2)}, u32[]{:S(2)}) collective-permute-start(bf16[128,1024]{1,0:T(8,128)(2,1)S(1)} %fusion.17), channel_id=1, source_target_pairs={{8,0},{16,8},{24,16},{28,24},{20,28},{12,20},{4,12},{0,4},{9,1},{1... | collective-permute-start | bytes 786440 | tf_op jit(solution)/shard_map/ppermute | solution.py:122
  214.8 18.0 %collective-permute-start.46 = (bf16[256,1024]{1,0:T(8,128)(2,1)S(1)}, bf16[256,1024]{1,0:T(8,128)(2,1)S(1)}, u32[]{:S(2)}, u32[]{:S(2)}) collective-permute-start(bf16[256,1024]{1,0:T(8,128)(2,1)S(1)} %copy-done.50), channel_id=1, source_target_pairs={{0,1},{1,0},{2,3},{3,2},{4,5},{5,4},{6,7},{7,6},{8,9},{9,8},{10,11... | collective-permute-start | bytes 1572872 | tf_op jit(solution)/shard_map/ppermute | solution.py:128
  220.4 11.9 %collective-permute-start.54 = (bf16[144,1024]{1,0:T(8,128)(2,1)S(1)}, bf16[144,1024]{1,0:T(8,128)(2,1)S(1)}, u32[]{:S(2)}, u32[]{:S(2)}) collective-permute-start(bf16[144,1024]{1,0:T(8,128)(2,1)S(1)} %fusion.1), channel_id=1, source_target_pairs={{8,0},{16,8},{24,16},{28,24},{20,28},{12,20},{4,12},{0,4},{9,1},{1... | collective-permute-start | bytes 884744 | tf_op jit(solution)/shard_map/ppermute | solution.py:122
  226.0 11.9 %collective-permute-start.77 = (bf16[128,1024]{1,0:T(8,128)(2,1)S(1)}, bf16[128,1024]{1,0:T(8,128)(2,1)S(1)}, u32[]{:S(2)}, u32[]{:S(2)}) collective-permute-start(bf16[128,1024]{1,0:T(8,128)(2,1)S(1)} %fusion.10), channel_id=1, source_target_pairs={{8,0},{16,8},{24,16},{28,24},{20,28},{12,20},{4,12},{0,4},{9,1},{1... | collective-permute-start | bytes 786440 | tf_op jit(solution)/shard_map/ppermute | solution.py:122
  232.8 10.5 %collective-permute-start.55 = (bf16[144,1024]{1,0:T(8,128)(2,1)S(1)}, bf16[144,1024]{1,0:T(8,128)(2,1)S(1)}, u32[]{:S(2)}, u32[]{:S(2)}) collective-permute-start(bf16[144,1024]{1,0:T(8,128)(2,1)S(1)} %fusion.2), channel_id=1, source_target_pairs={{8,0},{16,8},{24,16},{28,24},{20,28},{12,20},{4,12},{0,4},{9,1},{1... | collective-permute-start | bytes 884744 | tf_op jit(solution)/shard_map/ppermute | solution.py:122
  234.6 9.3 %collective-permute-start.62 = (bf16[128,1024]{1,0:T(8,128)(2,1)S(1)}, bf16[128,1024]{1,0:T(8,128)(2,1)S(1)}, u32[]{:S(2)}, u32[]{:S(2)}) collective-permute-start(bf16[128,1024]{1,0:T(8,128)(2,1)S(1)} %get-tuple-element.81), channel_id=1, source_target_pairs={{0,8},{8,16},{16,24},{24,28},{28,20},{20,12},{12,4},{4,0},{1,9},{9... | collective-permute-start | bytes 786440 | tf_op jit(solution)/shard_map/ppermute | solution.py:121
  237.9 8.1 %collective-permute-start.66 = (bf16[128,1024]{1,0:T(8,128)(2,1)S(1)}, bf16[128,1024]{1,0:T(8,128)(2,1)S(1)}, u32[]{:S(2)}, u32[]{:S(2)}) collective-permute-start(bf16[128,1024]{1,0:T(8,128)(2,1)S(1)} %fusion.18), channel_id=1, source_target_pairs={{8,0},{16,8},{24,16},{28,24},{20,28},{12,20},{4,12},{0,4},{9,1},{1... | collective-permute-start | bytes 786440 | tf_op jit(solution)/shard_map/ppermute | solution.py:122
  239.6 8.7 %collective-permute-start.47 = (bf16[128,1024]{1,0:T(8,128)(2,1)S(1)}, bf16[128,1024]{1,0:T(8,128)(2,1)S(1)}, u32[]{:S(2)}, u32[]{:S(2)}) collective-permute-start(bf16[128,1024]{1,0:T(8,128)(2,1)S(1)} %add_convert_fusion), channel_id=1, source_target_pairs={{0,2},{1,3},{2,0},{3,1},{4,6},{5,7},{6,4},{7,5},{8,10},{9,11},{10,... | collective-permute-start | bytes 786440 | tf_op jit(solution)/shard_map/ppermute | solution.py:128
  243.2 15.2 %collective-permute-start.79 = (bf16[128,1024]{1,0:T(8,128)(2,1)S(1)}, bf16[128,1024]{1,0:T(8,128)(2,1)S(1)}, u32[]{:S(2)}, u32[]{:S(2)}) collective-permute-start(bf16[128,1024]{1,0:T(8,128)(2,1)S(1)} %fusion.15.refs_4_), channel_id=1, source_target_pairs={{0,2},{1,3},{2,0},{3,1},{4,6},{5,7},{6,4},{7,5},{8,10},{9,11},{10,... | collective-permute-start | bytes 786440 | tf_op jit(solution)/shard_map/ppermute | solution.py:128
  243.9 15.0 %collective-permute-start.78 = (bf16[128,1024]{1,0:T(8,128)(2,1)S(1)}, bf16[128,1024]{1,0:T(8,128)(2,1)S(1)}, u32[]{:S(2)}, u32[]{:S(2)}) collective-permute-start(bf16[128,1024]{1,0:T(8,128)(2,1)S(1)} %fusion.15.refs_4_), channel_id=1, source_target_pairs={{0,1},{1,0},{2,3},{3,2},{4,5},{5,4},{6,7},{7,6},{8,9},{9,8},{10,11... | collective-permute-start | bytes 786440 | tf_op jit(solution)/shard_map/ppermute | solution.py:128
  246.0 12.4 %collective-permute-start.57 = (bf16[144,1024]{1,0:T(8,128)(2,1)S(1)}, bf16[144,1024]{1,0:T(8,128)(2,1)S(1)}, u32[]{:S(2)}, u32[]{:S(2)}) collective-permute-start(bf16[144,1024]{1,0:T(8,128)(2,1)S(1)} %fusion.7.refs_0_), channel_id=1, source_target_pairs={{0,2},{1,3},{2,0},{3,1},{4,6},{5,7},{6,4},{7,5},{8,10},{9,11},{10,... | collective-permute-start | bytes 884744 | tf_op jit(solution)/shard_map/ppermute | solution.py:128
  246.7 14.8 %collective-permute-start.68 = (bf16[128,1024]{1,0:T(8,128)(2,1)S(1)}, bf16[128,1024]{1,0:T(8,128)(2,1)S(1)}, u32[]{:S(2)}, u32[]{:S(2)}) collective-permute-start(bf16[128,1024]{1,0:T(8,128)(2,1)S(1)} %fusion.23.refs_0_), channel_id=1, source_target_pairs={{0,2},{1,3},{2,0},{3,1},{4,6},{5,7},{6,4},{7,5},{8,10},{9,11},{10,... | collective-permute-start | bytes 786440 | tf_op jit(solution)/shard_map/ppermute | solution.py:128
  248.3 23.4 %collective-permute-start.56 = (bf16[144,1024]{1,0:T(8,128)(2,1)S(1)}, bf16[144,1024]{1,0:T(8,128)(2,1)S(1)}, u32[]{:S(2)}, u32[]{:S(2)}) collective-permute-start(bf16[144,1024]{1,0:T(8,128)(2,1)S(1)} %fusion.7.refs_0_), channel_id=1, source_target_pairs={{0,1},{1,0},{2,3},{3,2},{4,5},{5,4},{6,7},{7,6},{8,9},{9,8},{10,11... | collective-permute-start | bytes 884744 | tf_op jit(solution)/shard_map/ppermute | solution.py:128
  258.4 13.3 %collective-permute-start.58 = (bf16[144,1024]{1,0:T(8,128)(2,1)S(1)}, bf16[144,1024]{1,0:T(8,128)(2,1)S(1)}, u32[]{:S(2)}, u32[]{:S(2)}) collective-permute-start(bf16[144,1024]{1,0:T(8,128)(2,1)S(1)} %collective-permute-done.57.refs_2_), channel_id=1, source_target_pairs={{0,1},{1,0},{2,3},{3,2},{4,5},{5,4},{6,7},{7,6},{8,9},{9,8},{10,11... | collective-permute-start | bytes 884744 | tf_op jit(solution)/shard_map/ppermute | solution.py:128
  258.4 7.8 %collective-permute-start.67 = (bf16[128,1024]{1,0:T(8,128)(2,1)S(1)}, bf16[128,1024]{1,0:T(8,128)(2,1)S(1)}, u32[]{:S(2)}, u32[]{:S(2)}) collective-permute-start(bf16[128,1024]{1,0:T(8,128)(2,1)S(1)} %fusion.23.refs_0_), channel_id=1, source_target_pairs={{0,1},{1,0},{2,3},{3,2},{4,5},{5,4},{6,7},{7,6},{8,9},{9,8},{10,11... | collective-permute-start | bytes 786440 | tf_op jit(solution)/shard_map/ppermute | solution.py:128
  (83 other events, 909.0 us)

commit v3 on v0

v3 whole, which is shorter than its diff:
```python
import functools

import jax
import jax.numpy as jnp
from jax import lax
from jax.experimental import pallas as pl
from jax.experimental.pallas import tpu as pltpu
from jax.sharding import PartitionSpec as P

BLOCK = 128
SMALL_ROWS = 16
NEG = -1e30
BF16 = jnp.bfloat16
F32 = jnp.float32
VMEM_LIMIT = 24 * 1024 * 1024
ROOT = 0.7978845608028654
CUBE = 0.044715


def dot(left, right, left_dim=1, right_dim=0):
    return lax.dot_general(
        left, right, (((left_dim,), (right_dim,)), ((), ())), preferred_element_type=F32
    )


def exact_dot(left, right, left_dim=1, right_dim=0):
    return lax.dot_general(
        left,
        right,
        (((left_dim,), (right_dim,)), ((), ())),
        precision=lax.Precision.HIGHEST,
        preferred_element_type=F32,
    )


def layer_norm(values):
    average = jnp.mean(values, axis=-1, keepdims=True)
    centred = values - average
    inverse = lax.rsqrt(jnp.mean(centred * centred, axis=-1, keepdims=True) + 1e-05)
    return centred * inverse, inverse


def norm_back(upstream, normed, inverse, gain):
    scaled = upstream * gain
    centre_term = jnp.mean(scaled, axis=-1, keepdims=True)
    slope_term = jnp.mean(scaled * normed, axis=-1, keepdims=True)
    return inverse * (scaled - centre_term - normed * slope_term)


def shaped(shape, dtype):
    return jax.ShapeDtypeStruct(tuple(shape), dtype)


def call(kernel, outs, args=(), hbm_args=(), smem_args=(), scratch=(), hbm_outs=(), micros=1):
    specs = [pl.BlockSpec(memory_space=pltpu.VMEM)] * len(args)
    specs += [pl.BlockSpec(memory_space=pltpu.HBM)] * len(hbm_args)
    specs += [pl.BlockSpec(memory_space=pltpu.SMEM)] * len(smem_args)
    out_specs = [pl.BlockSpec(memory_space=pltpu.VMEM)] * len(outs)
    out_specs += [pl.BlockSpec(memory_space=pltpu.HBM)] * len(hbm_outs)
    return pl.pallas_call(
        kernel,
        out_shape=(*outs, *hbm_outs),
        in_specs=specs,
        out_specs=tuple(out_specs),
        scratch_shapes=list(scratch),
        compiler_params=pltpu.CompilerParams(vmem_limit_bytes=VMEM_LIMIT),
        cost_estimate=pl.CostEstimate(flops=0, bytes_accessed=int(micros * 3.3e6), transcendentals=0),
    )(*args, *hbm_args, *smem_args)


def rank_at(position, count):
    position = lax.rem(position + 2 * count, count)
    return jnp.where(position < count // 2, 2 * position, 2 * (count - 1 - position) + 1)


def position_of(rank, count):
    return jnp.where(lax.rem(rank, 2) == 0, lax.div(rank, 2), count - 1 - lax.div(rank, 2))


def ring_pairs(count):
    order = list(range(0, count, 2)) + list(range(count - 1, 0, -2))
    forward = [(order[i], order[(i + 1) % count]) for i in range(count)]
    return forward, [(b, a) for a, b in forward]


def half_rows(rows):
    return rows // 2 // 16 * 16


def hold(value, *others):
    return lax.optimization_barrier((value, others))[0] if others else value


def halves(up, down):
    rows, columns = up.shape
    half = half_rows(rows)

    def kernel(up_ref, down_ref, upper_ref, lower_ref, sems):
        copies = [
            pltpu.make_async_copy(up_ref.at[:half, :], upper_ref, sems.at[0]),
            pltpu.make_async_copy(down_ref.at[half:, :], lower_ref, sems.at[1]),
        ]
        finish(start_all(copies))

    outs = [shaped((half, columns), up.dtype), shaped((rows - half, columns), up.dtype)]
    return call(kernel, outs, [], [up, down], scratch=[dma(2)])


class GatherRing:
    def __init__(self, shard, count):
        self.shard, self.count, self.at = shard, count, 0
        self.up = self.down = shard
        self.pieces, self.held = [shard], (shard, shard)

    def step(self, *others):
        self.at += 1
        if self.count != 8:
            if self.at == 1:
                self.up = self.down = lax.all_gather(self.shard, "dp", axis=0, tiled=True)
                self.pieces = [self.up]
            return
        forward, backward = ring_pairs(self.count)
        up, down = self.up, self.down
        if self.at == self.count // 2:
            up, down = halves(up, down)
        self.held = up, down
        up, down, *_ = lax.optimization_barrier((up, down, *others))
        self.up = lax.ppermute(up, "dp", forward)
        self.down = lax.ppermute(down, "dp", backward)
        self.pieces += [self.up, self.down]


def ring_add_kernel(count, step, *refs):
    parts, up_ref, down_ref, me_ref = refs[:4]
    *outs, mine, up, down, sems = refs[4:]
    rows = parts.shape[1]
    half = half_rows(rows)
    at = position_of(me_ref[1], count)
    up_rows, down_rows = (slice(0, half), slice(half, rows)) if step == 1 else (slice(0, rows),) * 2
    copies = [
        pltpu.make_async_copy(up_ref, up.at[up_rows, :], sems.at[0]),
        pltpu.make_async_copy(down_ref, down.at[down_rows, :], sems.at[1]),
        pltpu.make_async_copy(parts.at[rank_at(at + count // 2 - step, count)], mine.at[0], sems.at[2]),
    ]
    if step < count // 2:
        copies.append(
            pltpu.make_async_copy(parts.at[rank_at(at - count // 2 + step, count)], mine.at[1], sems.at[3])
        )
    finish(start_all(copies))
    if step == count // 2:
        total = mine[0].astype(F32) + up[...].astype(F32) + down[...].astype(F32)
        outs[0][...] = total.astype(BF16)
        return
    for target, own, arrived, where in zip(outs, (mine.at[0], mine.at[1]), (up, down), (up_rows, down_rows)):
        if step == 1:
            target[...] = own[...]
        target[where, :] = (own[where, :].astype(F32) + arrived[where, :].astype(F32)).astype(BF16)


class ScatterRing:
    def __init__(self, parts, me, count):
        self.parts, self.me, self.count, self.at = parts, me, count, 0
        self.total = None

    def step(self, *others):
        self.at += 1
        if self.count != 8:
            return
        forward, backward = ring_pairs(self.count)
        rows = self.parts.shape[1]
        half = half_rows(rows)
        if self.at == 1:
            me = position_of(lax.axis_index("dp"), self.count)
            far = rank_at(me + self.count // 2, self.count)
            far = lax.dynamic_index_in_dim(self.parts, far, 0, keepdims=False)
            up, down = far[:half], far[half:]
        else:
            up, down = self.add(self.at - 1, 2, *others)
        self.added = up, down
        self.up = lax.ppermute(up, "dp", forward)
        self.down = lax.ppermute(down, "dp", backward)

    def sent(self):
        return (self.up, self.down) if self.count == 8 else ()

    def sums(self):
        return self.added if self.count == 8 else ()

    def add(self, step, outs, *others):
        rows, columns = self.parts.shape[1:]
        up = hold(self.up, *others)
        return call(
            functools.partial(ring_add_kernel, self.count, step),
            [shaped((rows, columns), BF16)] * outs,
            [],
            [self.parts, up, self.down],
            [self.me],
            [pltpu.VMEM((2, rows, columns), BF16)] + [pltpu.VMEM((rows, columns), BF16)] * 2 + [dma(4)],
        )

    def finish(self, *others):
        if self.count != 8:
            return lax.psum_scatter(self.parts, "dp", scatter_dimension=0)
        return self.add(self.count // 2, 1, *others)[0]


def swap(values, bit):
    count = lax.axis_size("sp")
    return lax.ppermute(values, "sp", [(i, i ^ bit) for i in range(count)])


def gather_sp(piece):
    far = swap(piece, 2)
    near = swap(piece, 1)
    return [piece, near, far, swap(far, 1)]


def exchange_sp(sends):
    return [swap(send, step) for step, send in enumerate(sends, 1)]


def place(step, size, me_ref):
    return pl.multiple_of((me_ref[0] ^ step) * size, size)


def in_hbm(pieces):
    return [pltpu.with_memory_space_constraint(piece, pltpu.HBM) for piece in pieces]


def start_all(copies):
    for copy in copies:
        copy.start()
    return copies


def finish(copies):
    for copy in copies:
        copy.wait()


def load(pieces, me_ref, count, target, sems, lanes=slice(None)):
    if len(pieces) == 1:
        starts = [0]
    else:
        at = position_of(me_ref[1], count)
        rows = pieces[0].shape[0]
        starts = [rank_at(at + step, count) * rows for step in (0, -1, 1, -2, 2, -3, 3, 4)]
        starts.append(starts[-1] + half_rows(rows))
    copies = []
    for at, (start, piece) in enumerate(zip(starts, pieces)):
        rows = pl.ds(pl.multiple_of(start, 16), piece.shape[0])
        copies.append(pltpu.make_async_copy(piece.at[:, lanes], target.at[rows, :], sems.at[at]))
    return start_all(copies)


def load_rows(pieces, target, sems, me_ref=None, rows=slice(None), lanes=slice(None)):
    copies = []
    for step, piece in enumerate(pieces):
        block = piece.at[rows, lanes]
        size = block.shape[0]
        start = step * size if me_ref is None else place(step, size, me_ref)
        copies.append(pltpu.make_async_copy(block, target.at[pl.ds(start, size), :], sems.at[step]))
    return start_all(copies)


def dma(count):
    return pltpu.SemaphoreType.DMA((count,))


def share(sources, me, plan, rows):
    columns = sum(size for _, _, size, _ in plan)

    def kernel(*refs):
        *inputs, me_ref, target, sems = refs
        copies = []
        for at, (source, start, size, to) in enumerate(plan):
            if start is None:
                block = inputs[source].at[pl.ds(place(0, rows, me_ref), rows), :]
            else:
                block = inputs[source].at[:, pl.ds(start + place(0, size, me_ref), size)]
            copies.append(pltpu.make_async_copy(block, target.at[:, to : to + size], sems.at[at]))
        finish(start_all(copies))

    return call(
        kernel,
        [pltpu.VMEM((rows, columns), BF16)],
        [],
        [pltpu.with_memory_space_constraint(source, pltpu.HBM) for source in sources],
        [me],
        [dma(len(plan))],
    )[0]


def bias_kernel(table_ref, bucket_ref, seg_ref, me_ref, bias_ref, mask_ref):
    heads, diagonals = bias_ref.shape[:2]
    wide = bucket_ref.shape[1]
    bucket = lax.broadcasted_iota(jnp.int32, (table_ref.shape[1], wide), 0)
    chosen = (bucket == bucket_ref[...]).astype(F32)
    rows = exact_dot(table_ref[...], chosen)
    row = lax.broadcasted_iota(jnp.int32, rows.shape, 0)
    for head in range(heads):
        mine = jnp.sum(jnp.where(row == me_ref[0] * heads + head, rows, 0.0), axis=0, keepdims=True)
        for diagonal in range(diagonals):
            part = mine[:, diagonal * BLOCK : (diagonal + 2) * BLOCK]
            spread = jnp.broadcast_to(part, (BLOCK, 2 * BLOCK))
            rolled = pltpu.roll(spread, BLOCK, 1, stride=1, stride_axis=0)
            bias_ref[head, diagonal] = rolled[:, :BLOCK]
    segments = seg_ref[...].astype(F32)
    key = lax.broadcasted_iota(jnp.int32, (BLOCK, BLOCK), 0)
    query = lax.broadcasted_iota(jnp.int32, (BLOCK, BLOCK), 1)
    for block in range(diagonals):
        rows = slice(block * BLOCK, (block + 1) * BLOCK)
        keys = jnp.broadcast_to(segments[:, rows], (BLOCK, BLOCK)).T
        for index in range(block, diagonals):
            same = keys == segments[:, index * BLOCK : (index + 1) * BLOCK]
            if index == block:
                same = same & (query >= key)
            mask_ref[index, rows, :] = jnp.where(same, 0.0, NEG).astype(F32)


def norm_kernel(*refs):
    pieces, (gain_ref, shift_ref), me_ref = refs[2:6], refs[:2], refs[6]
    act_ref, normed_ref, up_ref, tokens, sems, up_sems = refs[7:]
    tok = up_ref.shape[0] // 4
    copies = load_rows(pieces, tokens, sems, me_ref, slice(0, tok))
    up_copies = load_rows(pieces, up_ref, up_sems, None, slice(tok, 2 * tok))
    finish(copies)
    for start in range(0, tokens.shape[0], BLOCK):
        rows = slice(start, start + BLOCK)
        normed, _ = layer_norm(tokens[rows, :].astype(F32))
        act_ref[rows, :] = (normed * gain_ref[0:1, :] + shift_ref[0:1, :]).astype(BF16)
        normed_ref[rows, :] = normed.astype(BF16)
    finish(up_copies)


def split_heads(rows):
    lane = lax.broadcasted_iota(jnp.int32, (1, BLOCK), 1)
    low = (lane < BLOCK // 2).astype(F32).astype(BF16)
    return jnp.concatenate([rows * low, rows * (1 - low)], axis=0)


def join_heads(both):
    half = BLOCK // 2
    return jnp.concatenate([both[:half, :BLOCK], both[half:, BLOCK:]], axis=0).T


def score_block(raw, bias_ref, mask_ref, pair, index, block):
    rows = slice(block * BLOCK, (block + 1) * BLOCK)
    mask = mask_ref[index, rows, :]
    return jnp.concatenate(
        [
            raw[rows, side * BLOCK : (side + 1) * BLOCK] + bias_ref[2 * pair + side, index - block] + mask
            for side in range(2)
        ],
        axis=1,
    )


def attend_kernel(scale, parts, count, *refs):
    act_ref, bias_ref, mask_ref = refs[:3]
    pieces, me_ref = refs[3 : 3 + count], refs[3 + count]
    qkv_ref, attn_ref, log_ref, weight, sems = refs[4 + count :]
    columns = attn_ref.shape[1]
    copies = load(pieces, me_ref, parts, weight, sems, slice(0, 3 * columns))
    finish(copies)
    for start in range(0, 3 * columns, columns):
        lanes = slice(start, start + columns)
        qkv_ref[:, lanes] = dot(act_ref[...], weight[:, lanes]).astype(BF16)
    for index in range(qkv_ref.shape[0] // BLOCK):
        rows = slice(index * BLOCK, (index + 1) * BLOCK)
        width = (index + 1) * BLOCK
        for pair in range(columns // BLOCK):
            lanes = slice(pair * BLOCK, (pair + 1) * BLOCK)
            queries = split_heads(qkv_ref[rows, lanes] * scale)
            keys = qkv_ref[:width, columns + pair * BLOCK : columns + (pair + 1) * BLOCK]
            values = qkv_ref[:width, 2 * columns + pair * BLOCK : 2 * columns + (pair + 1) * BLOCK]
            raw = dot(keys, queries, 1, 1)
            scores = [score_block(raw, bias_ref, mask_ref, pair, index, block) for block in range(index + 1)]
            largest = functools.reduce(
                jnp.maximum, [jnp.max(score, axis=0, keepdims=True) for score in scores]
            )
            weights = [jnp.exp(score - largest) for score in scores]
            total = functools.reduce(jnp.add, [jnp.sum(one, axis=0, keepdims=True) for one in weights])
            mixed = dot(values, jnp.concatenate([one.astype(BF16) for one in weights], axis=0), 0, 0)
            attn_ref[rows, lanes] = join_heads(mixed / total).astype(BF16)
            at = index * (columns // BLOCK) + pair
            log_ref[at : at + 1, :] = largest + jnp.log(total)


def branch_kernel(*refs):
    tokens_ref, gain_ref, shift_ref, attn_refs, weight_refs, me_ref = (*refs[:3], refs[3:7], refs[7:11], refs[11])
    resid_ref, act_ref, weight, own, sems, weight_sems = refs[12:]
    tok = tokens_ref.shape[0]
    part = weight_refs[0].shape[1]
    copies = []
    for step in range(4):
        columns = pl.ds(place(step, part, me_ref), part)
        rows = pl.ds(place(0, tok, me_ref), tok)
        copies.append(pltpu.make_async_copy(attn_refs[step].at[rows, :], own.at[:, columns], sems.at[step]))
        copies.append(pltpu.make_async_copy(weight_refs[step], weight.at[:, columns], weight_sems.at[step]))
    finish(start_all(copies))
    resid = tokens_ref[...].astype(F32) + dot(own[...], weight[...])
    resid_ref[...] = resid
    normed, _ = layer_norm(resid)
    act_ref[...] = (normed * gain_ref[1:2, :] + shift_ref[1:2, :]).astype(BF16)


def outer(left, right, grad_ref):
    parts, rows_here, _ = grad_ref.shape
    for start in range(0, parts * rows_here, 2 * BLOCK):
        block = dot(left[:, start : start + 2 * BLOCK], right[...], 0, 0).astype(BF16)
        for sub in range(2 * BLOCK // rows_here):
            grad_ref[start // rows_here + sub] = block[sub * rows_here : (sub + 1) * rows_here]


def store_shares(total, own_ref, send_refs, columns):
    tok = own_ref.shape[0]
    own_ref[:, columns] = total[:tok]
    for step, send in enumerate(send_refs, 1):
        send[:, columns] = total[step * tok : (step + 1) * tok].astype(BF16)


def feed_kernel(parts, count, *refs):
    up_from, act_refs, pieces, me_ref = refs[0], refs[1:5], refs[5 : 5 + count], refs[5 + count]
    fed_ref, grad_ref, own_ref, *send_refs = refs[6 + count : 12 + count]
    act, up_ref, weight, down, slope, hidden, act_sems, up_sems, sems, down_sems = refs[12 + count :]
    width = weight.shape[1]
    copies = load(pieces, me_ref, parts, weight, sems, slice(0, width)) + load_rows(act_refs, act, act_sems)
    late = load(pieces, me_ref, parts, down, down_sems, slice(width, None))
    late += start_all([pltpu.make_async_copy(up_from, up_ref, up_sems.at[0])])
    finish(copies)
    for start in range(0, width, 2 * BLOCK):
        columns = slice(start, start + 2 * BLOCK)
        units = dot(act[...], weight[:, columns])
        square = units * units
        bend = jnp.tanh(ROOT * units * (1.0 + CUBE * square))
        fed_ref[:, columns] = (0.5 * units * (1.0 + bend)).astype(BF16)
        slope[:, columns] = 0.5 * (1.0 + bend) + 0.5 * units * (1.0 - bend * bend) * ROOT * (
            1.0 + 3.0 * CUBE * square
        )
    finish(late)
    for start in range(0, width, 2 * BLOCK):
        rows = slice(start, start + 2 * BLOCK)
        hidden[:, rows] = (dot(up_ref[...], down[rows, :], 1, 1) * slope[:, rows]).astype(BF16)
    for start in range(0, weight.shape[0], 2 * BLOCK):
        rows = slice(start, start + 2 * BLOCK)
        store_shares(dot(hidden[...], weight[rows, :], 1, 1), own_ref, send_refs, rows)
    rows_here = grad_ref.shape[1]
    for at, (left, right) in enumerate([(act, hidden), (fed_ref, up_ref)]):
        lanes = slice(at * width, (at + 1) * width)
        for start in range(0, parts * rows_here, 2 * BLOCK):
            block = dot(left[:, start : start + 2 * BLOCK], right[...], 0, 0).astype(BF16)
            for sub in range(2 * BLOCK // rows_here):
                grad_ref[start // rows_here + sub, :, lanes] = block[sub * rows_here : (sub + 1) * rows_here]


def feed_out_kernel(parts, count, *refs):
    fed_ref, pieces, me_ref = refs[0], refs[1 : 1 + count], refs[1 + count]
    own_ref, *send_refs, down, sems = refs[2 + count :]
    width = down.shape[1]
    finish(load(pieces, me_ref, parts, down, sems, slice(width, None)))
    for start in range(0, width, 2 * BLOCK):
        columns = slice(start, start + 2 * BLOCK)
        store_shares(dot(fed_ref[...], down[:, columns]), own_ref, send_refs, columns)


def out_kernel(own_ref, resid_ref, *refs):
    sent, out_ref, rest, sems = refs[:3], refs[3], refs[4], refs[5]
    finish(load_rows(sent, rest, sems))
    tok = own_ref.shape[0]
    total = resid_ref[...] + own_ref[...]
    for step in range(3):
        total += rest[step * tok : (step + 1) * tok, :].astype(F32)
    out_ref[...] = total.astype(BF16)


def branch_back_kernel(*refs):
    own_ref, resid_ref, up_ref, gain_ref, sent, weight_refs, me_ref = (*refs[:4], refs[4:7], refs[7:11], refs[11])
    grad_ref, sums_ref, *send_refs, branch, grad_attn, rest, weight, sems, weight_sems = refs[12:]
    tok = up_ref.shape[0]
    part = send_refs[0].shape[1] // 2
    copies = load_rows(sent, rest, sems)
    late = []
    for step in range(4):
        columns = pl.ds(place(step, part, me_ref), part)
        late.append(pltpu.make_async_copy(weight_refs[step], weight.at[:, columns], weight_sems.at[step]))
    start_all(late)
    normed, inverse = layer_norm(resid_ref[...])
    finish(copies)
    upstream = own_ref[...]
    for step in range(3):
        upstream += rest[step * tok : (step + 1) * tok, :].astype(F32)
    sums_ref[0:1, :] = jnp.sum(upstream * normed, axis=0, keepdims=True)
    sums_ref[1:2, :] = jnp.sum(upstream, axis=0, keepdims=True)
    sums_ref[2:, :] = jnp.zeros_like(sums_ref[2:, :])
    grad = up_ref[...].astype(F32) + norm_back(upstream, normed, inverse, gain_ref[1:2, :])
    grad_ref[...] = grad
    branch[...] = grad.astype(BF16)
    finish(late)
    grad_attn[...] = dot(branch[...], weight[...], 1, 1).astype(BF16)
    for step, send in enumerate(send_refs):
        columns = pl.ds(place(step, part, me_ref), part)
        send[:, :part] = grad_attn[:, columns]
        send[:, part:] = branch[:, columns]


def attend_back_kernel(scale, dp_count, count, *refs):
    qkv_ref, log_ref, bias_ref, mask_ref, act_ref, normed_ref, sums_ref, bucket_ref = refs[:8]
    attn_refs, grad_refs, pieces, me_ref = refs[8:12], refs[12:16], refs[16 : 16 + count], refs[16 + count]
    last_ref, small_ref, own_ref, *send_refs = refs[17 + count : 23 + count]
    grads, branch, attn, grad_qkv, key_acc, value_acc, diagonal_acc, stacked, shares, weight_ref = refs[
        23 + count : 33 + count
    ]
    grad_sems, branch_sems, attn_sems, sems = refs[33 + count :]
    seq_len = qkv_ref.shape[0]
    columns = qkv_ref.shape[1] // 3
    heads, diagonals = bias_ref.shape[:2]
    tok = own_ref.shape[0]
    copies = load_rows(grad_refs, grads, grad_sems, me_ref, lanes=slice(0, columns))
    late = load_rows(grad_refs, branch, branch_sems, me_ref, lanes=slice(columns, 2 * columns))
    late += load_rows(attn_refs, attn, attn_sems)
    late += load(pieces, me_ref, dp_count, weight_ref, sems, slice(0, 3 * columns))
    key_acc[...] = jnp.zeros_like(key_acc)
    value_acc[...] = jnp.zeros_like(value_acc)
    diagonal_acc[...] = jnp.zeros_like(diagonal_acc)
    finish(copies)
    for pair in range(columns // BLOCK):
        lanes = slice(pair * BLOCK, (pair + 1) * BLOCK)
        all_keys = qkv_ref[:, columns + pair * BLOCK : columns + (pair + 1) * BLOCK]
        for index in range(seq_len // BLOCK):
            rows = slice(index * BLOCK, (index + 1) * BLOCK)
            width = (index + 1) * BLOCK
            queries = split_heads(qkv_ref[rows, lanes] * scale)
            grad_rows = split_heads(grads[rows, lanes])
            keys = all_keys[:width]
            values = qkv_ref[:width, 2 * columns + pair * BLOCK : 2 * columns + (pair + 1) * BLOCK]
            at = index * (columns // BLOCK) + pair
            logs = log_ref[at : at + 1, :]
            raw = dot(keys, queries, 1, 1)
            grad_probs = dot(values, grad_rows, 1, 1)
            probs = [
                jnp.exp(score_block(raw, bias_ref, mask_ref, pair, index, block) - logs)
                for block in range(index + 1)
            ]
            products = [
                one * grad_probs[block * BLOCK : (block + 1) * BLOCK] for block, one in enumerate(probs)
            ]
            row_term = functools.reduce(jnp.add, [jnp.sum(one, axis=0, keepdims=True) for one in products])
            grad_scores = [product - one * row_term for product, one in zip(products, probs)]
            for block, one in enumerate(grad_scores):
                diagonal_acc[pair, index - block] += one
            grad_raw = jnp.concatenate([one.astype(BF16) for one in grad_scores], axis=0)
            probs_all = jnp.concatenate([one.astype(BF16) for one in probs], axis=0)
            grad_qkv[rows, lanes] = (join_heads(dot(keys, grad_raw, 0, 0)) * scale).astype(BF16)
            key_acc[:width, lanes] += dot(grad_raw, queries)
            value_acc[:width, lanes] += dot(probs_all, grad_rows)
    grad_qkv[:, columns : 2 * columns] = key_acc[...].astype(BF16)
    grad_qkv[:, 2 * columns :] = value_acc[...].astype(BF16)

    parts, last_rows = last_ref.shape[:2]
    width = act_ref.shape[1]
    rows_here = width // parts
    for start in range(0, width, 2 * BLOCK):
        block = dot(act_ref[:, start : start + 2 * BLOCK], grad_qkv[...], 0, 0).astype(BF16)
        for sub in range(2 * BLOCK // rows_here):
            last_ref[start // rows_here + sub, :rows_here, : 3 * columns] = block[
                sub * rows_here : (sub + 1) * rows_here
            ]
    finish(late)
    for step in range(4):
        block = dot(attn[step * seq_len : (step + 1) * seq_len, :], branch[...], 0, 0).astype(BF16)
        for sub in range(columns // rows_here):
            part = (me_ref[0] ^ step) * (columns // rows_here) + sub
            last_ref[part, :rows_here, 3 * columns :] = block[sub * rows_here : (sub + 1) * rows_here]

    for start in range(0, width, 2 * BLOCK):
        lanes = slice(start, start + 2 * BLOCK)
        share_of = dot(grad_qkv[...], weight_ref[lanes, :], 1, 1)
        small_ref[0:1, lanes] = jnp.sum(share_of * normed_ref[:, lanes].astype(F32), axis=0, keepdims=True)
        small_ref[2:3, lanes] = jnp.sum(share_of, axis=0, keepdims=True)
        shares[:, lanes] = share_of
    for step, target in enumerate([own_ref, *send_refs]):
        rows = pl.ds(place(step, tok, me_ref), tok)
        target[...] = shares[rows, :].astype(target.dtype)
    small_ref[1:2, :] = sums_ref[0:1, :]
    small_ref[3:4, :] = sums_ref[1:2, :]

    row = lax.broadcasted_iota(jnp.int32, (BLOCK, BLOCK), 0)
    column = lax.broadcasted_iota(jnp.int32, (BLOCK, BLOCK), 1)
    flip = (row + column == BLOCK - 1).astype(F32)
    stacked[...] = jnp.zeros_like(stacked)
    for pair in range(heads // 2):
        for diagonal in range(diagonals):
            both = exact_dot(flip, diagonal_acc[pair, diagonal])
            at = slice(diagonal * BLOCK, (diagonal + 2) * BLOCK)
            for side in range(2):
                block = both[:, side * BLOCK : (side + 1) * BLOCK]
                wide = jnp.concatenate([block, jnp.zeros_like(block)], axis=1)
                rolled = pltpu.roll(wide, 1, 1, stride=1, stride_axis=0)
                head = 2 * pair + side
                stacked[head : head + 1, at] += jnp.sum(rolled, axis=0, keepdims=True)
    buckets = BLOCK // heads
    bucket = lax.rem(lax.broadcasted_iota(jnp.int32, (BLOCK, bucket_ref.shape[1]), 0), buckets)
    chosen = (bucket == bucket_ref[...]).astype(F32)
    by_head = exact_dot(stacked[...], chosen, 1, 1)
    row = lax.broadcasted_iota(jnp.int32, by_head.shape, 0)
    column = lax.broadcasted_iota(jnp.int32, by_head.shape, 1)
    table = jnp.sum(jnp.where(lax.div(column, buckets) == row, by_head, 0.0), axis=0, keepdims=True)
    small_ref[4:5, :BLOCK] = table
    if last_rows > rows_here:
        last_ref[:, rows_here:, :] = jnp.zeros_like(last_ref[:, rows_here:, :])
        per = parts // 4
        for part in range(parts):
            for at in range(4):
                last_ref[part, rows_here : rows_here + 1, at * rows_here : (at + 1) * rows_here] = small_ref[
                    at : at + 1, part * rows_here : (part + 1) * rows_here
                ].astype(BF16)
            turned = table if part % per == 0 else pltpu.roll(table, BLOCK - part % per * (BLOCK // per), 1)
            turned = jnp.where(me_ref[0] == part // per, turned, 0.0)
            last_ref[part, rows_here : rows_here + 1, 4 * rows_here : 4 * rows_here + BLOCK] = turned.astype(BF16)


def norm_back_kernel(own_ref, tokens_ref, resid_ref, gain_ref, *refs):
    sent, grad_ref, rest, sems = refs[:3], refs[3], refs[4], refs[5]
    copies = load_rows(sent, rest, sems)
    tok = own_ref.shape[0]
    normed, inverse = layer_norm(tokens_ref[...].astype(F32))
    finish(copies)
    upstream = own_ref[...]
    for step in range(3):
        upstream += rest[step * tok : (step + 1) * tok, :].astype(F32)
    grad_ref[...] = resid_ref[...] + norm_back(upstream, normed, inverse, gain_ref[0:1, :])


def wide_feed_kernel(*refs):
    pieces, me_ref, in_ref, down_ref, both, sems = refs[:4], refs[4], refs[5], refs[6], refs[7], refs[8]
    finish(load_rows(pieces, both, sems))
    rows = in_ref.shape[0]
    width = down_ref.shape[1]
    for step in range(4):
        mine = slice(step * rows, (step + 1) * rows)
        down_ref[pl.ds(place(step, rows, me_ref), rows), :] = both[mine, width:].astype(F32)
        for start in range(0, width, rows):
            at = pl.multiple_of(4 * start + (me_ref[0] ^ step) * rows, rows)
            in_ref[:, pl.ds(at, rows)] = both[mine, start : start + rows].astype(F32)


def wide_last_kernel(*refs):
    pieces, me_ref = refs[:4], refs[4]
    qkv_ref, out_ref, gain_ref, shift_ref, table_ref, last, sems = refs[5:]
    finish(load_rows(pieces, last, sems))
    rows, width = out_ref.shape
    part = width // 4
    whole = rows + SMALL_ROWS
    small = jnp.zeros((1, width), F32)
    for step in range(4):
        start = step * whole
        mine = slice(start, start + rows)
        for third in range(3):
            at = pl.multiple_of(third * width + (me_ref[0] ^ step) * part, part)
            qkv_ref[:, pl.ds(at, part)] = last[mine, third * part : (third + 1) * part].astype(F32)
        out_ref[:, pl.ds(place(step, part, me_ref), part)] = last[mine, 3 * part :].astype(F32)
        small += last[start + rows : start + whole, :].astype(F32)[0:1]
    for at in range(2):
        gain_ref[at : at + 1, :] = small[:, at * rows : (at + 1) * rows]
        shift_ref[at : at + 1, :] = small[:, (2 + at) * rows : (3 + at) * rows]
    table_ref[...] = small[:, 4 * rows : 4 * rows + table_ref.shape[1]]


def stacked_sp(pieces):
    me = lax.axis_index("sp")
    whole = jnp.zeros((len(pieces),) + pieces[0].shape, pieces[0].dtype)
    for step, piece in enumerate(pieces):
        whole = lax.dynamic_update_index_in_dim(whole, piece, me ^ step, 0)
    return whole


def on_device(
    inputs,
    qkv_weight,
    out_weight,
    in_weight,
    down_weight,
    norm_gain,
    norm_shift,
    bias_table,
    segment_ids,
    bucket_index,
    cotangent,
):
    dp_count, sp_count = lax.axis_size("dp"), lax.axis_size("sp")
    me_sp = lax.axis_index("sp")
    me = jnp.stack([me_sp, lax.axis_index("dp")]).astype(jnp.int32)
    tok, width = inputs.shape[1:]
    head_total, bucket_count = bias_table.shape
    heads = head_total // sp_count
    scale = (width // head_total) ** (-0.5)
    seq_len = segment_ids.shape[1]
    rows_here = qkv_weight.shape[0]
    ff = in_weight.shape[1]
    ff_rows = ff // dp_count // sp_count
    ff_part = ff // sp_count
    part = width // sp_count
    diagonals = seq_len // BLOCK
    aligned = ff_rows % BLOCK == 0 and rows_here % BLOCK == 0

    if aligned:
        plan = [(0, third * width, part, third * part) for third in range(3)] + [(1, 0, part, 3 * part)]
        first_part = share([qkv_weight, out_weight], me, plan, rows_here)
        step = sp_count * ff_rows
        plan = [(0, index * step, ff_rows, index * ff_rows) for index in range(dp_count)]
        plan.append((1, None, width, ff_part))
        rest_part = share([hold(in_weight, first_part), down_weight], me, plan, rows_here)
    else:

        def own_sp(stacked, axis):
            return lax.dynamic_index_in_dim(stacked, me_sp, axis, keepdims=False)

        first_part = own_sp(qkv_weight.reshape(rows_here, 3, sp_count, part), 2).reshape(rows_here, 3 * part)
        out_part = own_sp(out_weight.reshape(rows_here, sp_count, part), 1)
        first_part = jnp.concatenate([first_part, out_part], axis=1)
        in_part = own_sp(in_weight.reshape(rows_here, dp_count, sp_count, ff_rows), 2)
        in_part = in_part.reshape(rows_here, ff_part)
        down_part = lax.dynamic_slice_in_dim(down_weight, me_sp * ff_rows, ff_rows, 0)
        rest_part = jnp.concatenate([in_part, down_part], axis=1)
    first_ring = GatherRing(first_part, dp_count)
    rest_ring = GatherRing(rest_part, dp_count)

    tokens = inputs[0]
    first_ring.step()

    buckets = jnp.pad(bucket_index, (BLOCK, 0), constant_values=-1)[None]
    bias, mask = call(
        bias_kernel,
        [shaped((heads, diagonals, BLOCK, BLOCK), F32), shaped((diagonals, seq_len, BLOCK), F32)],
        [bias_table, hold(buckets, first_part), segment_ids],
        (),
        [me],
        micros=1.2,
    )
    both = jnp.concatenate([hold(tokens, bias), cotangent[0]], axis=0)
    token_far, token_near = swap(both, 2), swap(both, 1)
    first_ring.step(bias, rest_part)
    token_last = swap(token_far, 1)
    first_ring.step(token_far)
    act_one, normed_one, up_all = call(
        norm_kernel,
        [shaped((seq_len, width), BF16)] * 3,
        [hold(norm_gain, *first_ring.held), norm_shift],
        [both, token_near, token_far, token_last],
        [me],
        [pltpu.VMEM((seq_len, width), BF16), dma(4), dma(4)],
        micros=2.4,
    )
    first_ring.step()
    rest_ring.step(first_ring.up, first_ring.down)
    first_pieces = first_ring.pieces
    count = len(first_pieces)
    if count == 1:
        out_columns = first_pieces[0][:, 3 * part :]
    else:

        def assemble(*refs):
            *pieces, me_ref, target, sems = refs
            finish(load(pieces, me_ref, dp_count, target, sems, slice(3 * part, 4 * part)))

        (out_columns,) = call(
            assemble, [], [], first_pieces, [me], [dma(count)], [shaped((width, part), BF16)]
        )
    out_far, out_near = swap(out_columns, 2), swap(out_columns, 1)
    pairs = heads // 2
    qkv, attn, logs = call(
        functools.partial(attend_kernel, scale, dp_count, count),
        [
            shaped((seq_len, 3 * part), BF16),
            shaped((seq_len, part), BF16),
            shaped((diagonals * pairs, 2 * BLOCK), F32),
        ],
        [hold(act_one, out_columns), bias, mask],
        first_pieces,
        [me],
        [pltpu.VMEM((width, 3 * part), BF16), dma(count)],
        micros=5,
    )
    attn = hold(attn, rest_ring.up, rest_ring.down)
    attn_far, attn_near = swap(attn, 2), swap(attn, 1)
    rest_ring.step(attn)
    attn_last = swap(attn_far, 1)
    out_last = swap(out_far, 1)
    resid, act_two = call(
        branch_kernel,
        [shaped((tok, width), F32), shaped((tok, width), BF16)],
        [tokens, norm_gain, norm_shift],
        [attn, attn_near, attn_far, attn_last, out_columns, out_near, out_far, out_last],
        [me],
        [pltpu.VMEM((width, width), BF16), pltpu.VMEM((tok, width), BF16), dma(4), dma(4)],
        micros=2.4,
    )
    act_two = hold(act_two, rest_ring.up, rest_ring.down)
    act_far, act_near = swap(act_two, 2), swap(act_two, 1)
    rest_ring.step(act_two)
    act_last = swap(act_far, 1)
    rest_ring.step(act_last)
    shares = [shaped((tok, width), F32)] + [shaped((tok, width), BF16)] * 3
    fed, grad_feed, own_two, *sends = call(
        functools.partial(feed_kernel, dp_count, count),
        [shaped((seq_len, ff_part), BF16), shaped((dp_count, rows_here, 2 * width), BF16)] + shares,
        [],
        in_hbm([up_all, act_two, act_near, act_far, act_last, *rest_ring.pieces]),
        [me],
        [
            pltpu.VMEM((seq_len, width), BF16),
            pltpu.VMEM((seq_len, width), BF16),
            pltpu.VMEM((width, ff_part), BF16),
            pltpu.VMEM((ff_part, width), BF16),
            pltpu.VMEM((seq_len, ff_part), F32),
            pltpu.VMEM((seq_len, ff_part), BF16),
            dma(4),
            dma(1),
            dma(count),
            dma(count),
        ],
        micros=9,
    )

    sent_two = exchange_sp(sends)
    feed_grads = ScatterRing(grad_feed, me, dp_count)
    feed_grads.step()
    feed_grads.step(*sent_two)
    own_out, *out_sends = call(
        functools.partial(feed_out_kernel, dp_count, count),
        shares,
        [fed],
        in_hbm(rest_ring.pieces),
        [me],
        [pltpu.VMEM((ff_part, width), BF16), dma(count)],
        micros=3,
    )
    grad_resid, sums_two, *sends = call(
        branch_back_kernel,
        [shaped((tok, width), F32), shaped((8, width), F32)] + [shaped((tok, 2 * part), BF16)] * 4,
        [hold(own_two, own_out, *feed_grads.sums()), resid, cotangent[0], norm_gain],
        [*sent_two, out_columns, out_near, out_far, out_last],
        [me],
        [
            pltpu.VMEM((tok, width), BF16),
            pltpu.VMEM((tok, width), BF16),
            pltpu.VMEM((3 * tok, width), BF16),
            pltpu.VMEM((width, width), BF16),
            dma(3),
            dma(4),
        ],
        micros=2.5,
    )
    grad_pieces = [sends[0]] + exchange_sp(sends[1:])
    feed_grads.step(*grad_pieces[1:])
    last_rows = rows_here + SMALL_ROWS if aligned else rows_here
    last, small, own_one, *sends = call(
        functools.partial(attend_back_kernel, scale, dp_count, count),
        [shaped((dp_count, last_rows, 4 * part), BF16), shaped((8, width), F32)] + shares,
        [hold(qkv, *feed_grads.sums()), logs, bias, mask, act_one, normed_one, sums_two, buckets],
        [attn, attn_near, attn_far, attn_last, *grad_pieces, *first_pieces],
        [me],
        [
            pltpu.VMEM((seq_len, part), BF16),
            pltpu.VMEM((seq_len, part), BF16),
            pltpu.VMEM((4 * seq_len, part), BF16),
            pltpu.VMEM((seq_len, 3 * part), BF16),
            pltpu.VMEM((seq_len, part), F32),
            pltpu.VMEM((seq_len, part), F32),
            pltpu.VMEM((pairs, diagonals, BLOCK, 2 * BLOCK), F32),
            pltpu.VMEM((heads, seq_len + BLOCK), F32),
            pltpu.VMEM((seq_len, width), F32),
            pltpu.VMEM((width, 3 * part), BF16),
            dma(4),
            dma(4),
            dma(4),
            dma(count),
        ],
        micros=9.4,
    )
    if not aligned:
        table = jnp.zeros((head_total * bucket_count,), F32)
        table = lax.dynamic_update_slice_in_dim(table, small[4, :BLOCK], me_sp * BLOCK, 0)
        packed = [small[at].reshape(dp_count, -1) for at in range(4)] + [table.reshape(dp_count, -1)]
        packed = jnp.concatenate(packed, axis=1).astype(BF16)
        packed = jnp.pad(packed, ((0, 0), (0, 4 * part - packed.shape[1])))
        packed = jnp.pad(packed[:, None], ((0, 0), (0, SMALL_ROWS - 1), (0, 0)))
        last = jnp.concatenate([last, packed], axis=1)
    last_grads = ScatterRing(last, me, dp_count)
    last_grads.step()
    feed_grads.step(small)
    last_grads.step(*feed_grads.sums())
    sent_out = exchange_sp([hold(send, small) for send in out_sends])
    sent_one = exchange_sp([hold(send, *sent_out, *last_grads.sums()) for send in sends])
    last_grads.step()
    (grad_input,) = call(
        norm_back_kernel,
        [shaped((tok, width), F32)],
        [hold(own_one, *last_grads.sums()), tokens, grad_resid, norm_gain],
        sent_one,
        (),
        [pltpu.VMEM((3 * tok, width), BF16), dma(3)],
        micros=1.4,
    )

    sum_feed = feed_grads.finish(grad_input)
    last_grads.step(grad_input, sum_feed)
    feed_pieces = gather_sp(hold(sum_feed, *last_grads.sums()))
    (output,) = call(
        out_kernel,
        [shaped((tok, width), BF16)],
        [hold(own_out, *last_grads.sums()), resid],
        sent_out,
        (),
        [pltpu.VMEM((3 * tok, width), BF16), dma(3)],
    )

    sum_last = last_grads.finish()
    last_pieces = gather_sp(sum_last)
    piece = width // dp_count
    table_here = head_total * bucket_count // dp_count
    if aligned:
        out_in, out_down = call(
            wide_feed_kernel,
            [shaped((rows_here, ff), F32), shaped((sp_count * ff_rows, width), F32)],
            [],
            feed_pieces,
            [me],
            [pltpu.VMEM((sp_count * rows_here, 2 * width), BF16), dma(4)],
        micros=3,
    )
        out_qkv, out_out, gains, shifts, tables = call(
            wide_last_kernel,
            [
                shaped((rows_here, 3 * width), F32),
                shaped((rows_here, width), F32),
                shaped((2, piece), F32),
                shaped((2, piece), F32),
                shaped((1, table_here), F32),
            ],
            [],
            last_pieces,
            [me],
            [pltpu.VMEM((sp_count * (rows_here + SMALL_ROWS), width), BF16), dma(4)],
        micros=2.3,
    )
        tables = tables[0]
    else:
        all_feed = stacked_sp(feed_pieces).astype(F32)
        out_down = all_feed[:, :, width:].reshape(sp_count * ff_rows, width)
        all_in = all_feed[:, :, :width].reshape(sp_count, rows_here, dp_count, ff_rows)
        out_in = jnp.moveaxis(all_in, 0, 2).reshape(rows_here, ff)
        all_last = stacked_sp(last_pieces).astype(F32)
        all_qkv = all_last[:, :rows_here, : 3 * part].reshape(sp_count, rows_here, 3, part)
        out_qkv = jnp.moveaxis(all_qkv, 0, 2).reshape(rows_here, 3 * width)
        out_out = jnp.moveaxis(all_last[:, :rows_here, 3 * part :], 0, 1).reshape(rows_here, width)
        small_row = jnp.sum(all_last[:, rows_here:], axis=0)[0]
        gains = small_row[: 2 * piece].reshape(2, piece)
        shifts = small_row[2 * piece : 4 * piece].reshape(2, piece)
        tables = small_row[4 * piece : 4 * piece + table_here]
    return (output[None], grad_input[None], out_qkv, out_out, out_in, out_down, gains, shifts, tables)


def solution(mesh):
    in_specs = (
        P("dp", "sp", None),
        P("dp", None),
        P("dp", None),
        P("dp", None),
        P("dp", None),
        P(),
        P(),
        P(),
        P("dp", None),
        P(),
        P("dp", "sp", None),
    )
    out_specs = (
        P("dp", "sp", None),
        P("dp", "sp", None),
        P("dp", None),
        P("dp", None),
        P("dp", None),
        P("dp", None),
        P(None, "dp"),
        P(None, "dp"),
        P("dp"),
    )
    return jax.shard_map(
        on_device, mesh=mesh, in_specs=in_specs, out_specs=out_specs, check_vma=False
    )
```

time: 4180 us -> 211 us (0.05)
  local copies, waits for them, and re-layouts: 3720 us -> 4.2 us
  waiting for transfers between devices: 221 us -> 95.8 us
  matrix products: 120 us -> 0 us
  Pallas kernels: 0 us -> 56 us
  blocking collectives: 49.8 us -> 0 us
  starting transfers between devices: 8.31 us -> 50.9 us
    gather x3 -> x0, local copies, waits for them, and re-layouts: 3690 us -> none  [the longest x1 2750 us: bucket_sums(): bucket_block = jnp.take(bucket_index, distance, axis=0)]
    dot_general x23 -> x0, matrix products: 113 us -> none  [the longest x4 27.8 us: matmul_inner(): lax.dot_general(left, right, (((0,), (0,)), ((), ())), preferred_element_...]
    all_gather x4 -> x0, waiting for transfers between devices: 100 us -> none  [the longest x1 100 us: on_device(): lax.all_gather(qkv_weight, 'dp', axis=0, tiled=True)]
    ppermute x0 -> x62, waiting for transfers between devices: none -> 95.8 us  [the longest x30 52.7 us: swap(): return lax.ppermute(values, 'sp', [(i, i ^ bit) for i in range(count)])]
    psum x1 -> x0, waiting for transfers between devices: 63.1 us -> none  [on_device(): lax.psum(part_qkv.astype(jnp.bfloat16), 'sp').astype(jnp.float32)]
    pallas_call x0 -> x25, Pallas kernels: none -> 56 us  [call(): pl.pallas_call(kernel, out_shape=(*outs, *hbm_outs), in_specs=specs, out_...]
    unnamed x13 -> x0, waiting for transfers between devices: 51.9 us -> none
    ppermute x0 -> x62, starting transfers between devices: none -> 50.9 us  [the longest x16 18.3 us: step(): self.up = lax.ppermute(up, 'dp', forward)]
  transfers between devices with their start and end apart: 13 -> 62, of which waited for: 4 -> 34; matrix products, arithmetic and copies ran while one was open for 92% -> 1% of each run, Pallas kernels for 0% -> 18%
where the time goes in v3:
time: 211 us; the launch traced here: 210 us
  waiting for transfers between devices  95.8 us (45%)
  Pallas kernels  56 us (27%)
  starting transfers between devices  50.9 us (24%)
  local copies, waits for them, and re-layouts  4.2 us (2%)
    pallas_call x25, Pallas kernels, call(): pl.pallas_call(kernel, out_shape=(*outs, *hbm_outs), in_specs=specs, out_...  56 us
    ppermute x30, waiting for transfers between devices, swap(): return lax.ppermute(values, 'sp', [(i, i ^ bit) for i in range(count)])  52.7 us
    ppermute x16, waiting for transfers between devices, step(): self.up = lax.ppermute(up, 'dp', forward)  34.7 us
    ppermute x16, starting transfers between devices, step(): self.up = lax.ppermute(up, 'dp', forward)  18.3 us
    ppermute x30, starting transfers between devices, swap(): return lax.ppermute(values, 'sp', [(i, i ^ bit) for i in range(count)])  16.7 us
    ppermute x16, starting transfers between devices, step(): self.down = lax.ppermute(down, 'dp', backward)  15.9 us
    ppermute x16, waiting for transfers between devices, step(): self.down = lax.ppermute(down, 'dp', backward)  8.42 us
  transfers between devices with their start and end apart: 62, of which 34 were waited for; matrix products, arithmetic and copies ran while one was open for 1% of the time, Pallas kernels for 18%

profile of v3, /device:TPU:0, one launch (start us, length us, event | category | flops | bytes accessed | tf_op | source)
XLA Modules:
  0.0 210.2 jit_solution(3355536994589583848)
XLA Ops:
  0.7 1.5 shard_map.178.refs_0_.refs_3_.refs_16_
  2.2 3.1 %collective-permute-start = (bf16[128,1024]{1,0:T(8,128)(2,1)S(1)}, bf16[128,1024]{1,0:T(8,128)(2,1)S(1)}, u32[]{:S(2)}, u32[]{:S(2)}) collective-permute-start(bf16[128,1024]{1,0:T(8,128)(2,1)S(1)} %shard_map.178.refs_0_.refs_3_.refs_16_), channel_id=1, source_target_pairs={{0,8},{8,16},{16,24},{24,28},{28,20},{20,12},{12,4},{4,0},{1,9},{9... | collective-permute-start | bytes 786440 | tf_op jit(solution)/shard_map/ppermute | solution.py:128
  8.6 1.4 pad_maximum_fusion.refs_2_
  10.1 2.0 collective-permute-start.5
  12.1 1.7 shard_map.180.refs_5_.refs_1_
  13.9 1.6 collective-permute-start.2
  16.0 5.2 %collective-permute-done.2.refs_3_.refs_6_.refs_19_ = bf16[128,1024]{1,0:T(8,128)(2,1)S(1)} collective-permute-done((bf16[128,1024]{1,0:T(8,128)(2,1)S(1)}, bf16[128,1024]{1,0:T(8,128)(2,1)S(1)}, u32[]{:S(2)}, u32[]{:S(2)}) %collective-permute-start.2) | collective-permute-done | bytes 262176 | tf_op jit(solution)/shard_map/ppermute | solution.py:128
  21.1 1.3 collective-permute-done.3.refs_4_.refs_7_.refs_20_
  23.5 1.7 collective-permute-start.7
  25.6 4.8 %collective-permute-done.7.up_ref.refs_5_.refs_8_.refs_21_ = bf16[128,1024]{1,0:T(8,128)(2,1)S(1)} collective-permute-done((bf16[128,1024]{1,0:T(8,128)(2,1)S(1)}, bf16[128,1024]{1,0:T(8,128)(2,1)S(1)}, u32[]{:S(2)}, u32[]{:S(2)}) %collective-permute-start.7) | collective-permute-done | bytes 262176 | tf_op jit(solution)/shard_map/ppermute | solution.py:128
  30.4 1.3 collective-permute-done.8.down_ref.refs_6_.refs_9_.refs_22_
  32.0 1.6 collective-permute-start.9
  34.1 2.9 %collective-permute-done.9.refs_7_.refs_10_.refs_23_ = bf16[64,1024]{1,0:T(8,128)(2,1)S(1)} collective-permute-done((bf16[64,1024]{1,0:T(8,128)(2,1)S(1)}, bf16[64,1024]{1,0:T(8,128)(2,1)S(1)}, u32[]{:S(2)}, u32[]{:S(2)}) %collective-permute-start.9) | collective-permute-done | bytes 131104 | tf_op jit(solution)/shard_map/ppermute | solution.py:128
  37.0 1.6 collective-permute-done.10.refs_8_.refs_11_.refs_24_
  38.6 1.6 collective-permute-start.11
  41.4 1.6 collective-permute-start.17
  43.0 1.5 shard_map.181
  45.6 4.8 %shard_map.184 = (bf16[512,768]{1,0:T(8,128)(2,1)S(1)}, bf16[512,256]{1,0:T(8,128)(2,1)S(1)}, f32[8,256]{1,0:T(8,128)S(1)}) custom-call(bf16[512,1024]{1,0:T(8,128)(2,1)S(1)} %get-tuple-element.117.refs_0_.refs_4_, f32[4,4,128,128]{3,2,1,0:T(8,128)S(1)} %get-tuple-element.105.refs_1_.refs_2_, f32[4,512,128]{2,1,0:T(8,128)S(1)} %get-tuple-element.118.refs_2_.refs_3_, ...), custom_call_target="tpu_custom_call" | custom-call | bytes 16500000 | tf_op jit(solution)/shard_map/pallas_call | solution.py:60
  52.2 1.6 collective-permute-start.19
  54.2 5.9 %collective-permute-done.14.refs_5_.refs_10_ = bf16[512,256]{1,0:T(8,128)(2,1)S(1)} collective-permute-done((bf16[512,256]{1,0:T(8,128)(2,1)S(1)}, bf16[512,256]{1,0:T(8,128)(2,1)S(1)}, u32[]{:S(2)}, u32[]{:S(2)}) %collective-permute-start.14) | collective-permute-done | bytes 262176 | tf_op jit(solution)/shard_map/ppermute | solution.py:209
  60.1 1.5 collective-permute-done.15.refs_6_.refs_11_
  61.7 2.4 %shard_map.185 = (f32[128,1024]{1,0:T(8,128)S(1)}, bf16[128,1024]{1,0:T(8,128)(2,1)}) custom-call(bf16[128,1024]{1,0:T(8,128)(2,1)S(1)} %bitcast.16, f32[2,1024]{1,0:T(2,128)S(1)} %copy-done.43, f32[2,1024]{1,0:T(2,128)S(1)} %copy-done.44, bf16[512,256]{1,0:T(8,128)(2,1)S(1)} %get-tuple-element.122.refs_3_.refs_8_, ...), custom_call_target="tpu_custom_call" | custom-call | bytes 7920000 | tf_op jit(solution)/shard_map/pallas_call | solution.py:60
  64.0 2.3 %collective-permute-done.19.refs_8_.refs_4_ = bf16[128,2048]{1,0:T(8,128)(2,1)S(1)} collective-permute-done((bf16[128,2048]{1,0:T(8,128)(2,1)S(1)}, bf16[128,2048]{1,0:T(8,128)(2,1)S(1)}, u32[]{:S(2)}, u32[]{:S(2)}) %collective-permute-start.19) | collective-permute-done | bytes 524320 | tf_op jit(solution)/shard_map/ppermute | solution.py:128
  66.3 1.3 collective-permute-done.20.refs_9_.refs_5_
  67.6 1.5 collective-permute-start.24
  69.6 1.5 collective-permute-start.22
  71.1 5.5 %collective-permute-done.22.refs_3_ = bf16[128,1024]{1,0:T(8,128)(2,1)S(1)} collective-permute-done((bf16[128,1024]{1,0:T(8,128)(2,1)}, bf16[128,1024]{1,0:T(8,128)(2,1)S(1)}, u32[]{:S(2)}, u32[]{:S(2)}) %collective-permute-start.22) | collective-permute-done | bytes 262176 | tf_op jit(solution)/shard_map/ppermute | solution.py:209
  77.2 3.4 %collective-permute-done.24.up_ref.refs_10_.refs_6_ = bf16[128,2048]{1,0:T(8,128)(2,1)S(1)} collective-permute-done((bf16[128,2048]{1,0:T(8,128)(2,1)S(1)}, bf16[128,2048]{1,0:T(8,128)(2,1)S(1)}, u32[]{:S(2)}, u32[]{:S(2)}) %collective-permute-start.24) | collective-permute-done | bytes 524320 | tf_op jit(solution)/shard_map/ppermute | solution.py:128
  80.6 1.2 collective-permute-done.25.down_ref.refs_11_.refs_7_
  83.6 1.6 collective-permute-start.27
  85.2 4.4 %collective-permute-done.26.refs_12_.refs_8_ = bf16[64,2048]{1,0:T(8,128)(2,1)} collective-permute-done((bf16[64,2048]{1,0:T(8,128)(2,1)}, bf16[64,2048]{1,0:T(8,128)(2,1)}, u32[]{:S(2)}, u32[]{:S(2)}) %collective-permute-start.26) | collective-permute-done | bytes 262176 | tf_op jit(solution)/shard_map/ppermute | solution.py:128
  90.5 10.1 %shard_map.187 = (bf16[512,1024]{1,0:T(8,128)(2,1)S(1)}, bf16[8,128,2048]{2,1,0:T(8,128)(2,1)S(1)}, f32[128,1024]{1,0:T(8,128)S(1)}, bf16[128,1024]{1,0:T(8,128)...) custom-call(bf16[512,1024]{1,0:T(8,128)(2,1)} %copy-done.31, ...), custom_call_target="tpu_custom_call" | custom-call | bytes 29700000 | tf_op jit(solution)/shard_map/pallas_call | solution.py:60
  101.1 1.5 collective-permute-start.30
  103.0 1.6 collective-permute-start.32
  104.5 2.5 %collective-permute-done.28.refs_1_ = bf16[64,2048]{1,0:T(8,128)(2,1)S(1)} collective-permute-done((bf16[64,2048]{1,0:T(8,128)(2,1)S(1)}, bf16[64,2048]{1,0:T(8,128)(2,1)S(1)}, u32[]{:S(2)}, u32[]{:S(2)}) %collective-permute-start.28) | collective-permute-done | bytes 262176 | tf_op jit(solution)/shard_map/ppermute | solution.py:180
  107.0 3.2 %collective-permute-done.30.refs_5_ = bf16[128,1024]{1,0:T(8,128)(2,1)S(1)} collective-permute-done((bf16[128,1024]{1,0:T(8,128)(2,1)S(1)}, bf16[128,1024]{1,0:T(8,128)(2,1)S(1)}, u32[]{:S(2)}, u32[]{:S(2)}) %collective-permute-start.30) | collective-permute-done | bytes 262176 | tf_op jit(solution)/shard_map/ppermute | solution.py:209
  110.2 4.8 %collective-permute-done.31.refs_6_ = bf16[128,1024]{1,0:T(8,128)(2,1)S(1)} collective-permute-done((bf16[128,1024]{1,0:T(8,128)(2,1)S(1)}, bf16[128,1024]{1,0:T(8,128)(2,1)S(1)}, u32[]{:S(2)}, u32[]{:S(2)}) %collective-permute-start.31) | collective-permute-done | bytes 262176 | tf_op jit(solution)/shard_map/ppermute | solution.py:209
  116.5 1.5 collective-permute-start.37
  118.0 3.4 %shard_map.188 = (f32[128,1024]{1,0:T(8,128)S(1)}, bf16[128,1024]{1,0:T(8,128)(2,1)S(1)}, bf16[128,1024]{1,0:T(8,128)(2,1)S(1)}, bf16[128,1024]{1,0:T(8,128)(2,1)S(1)}) custom-call(bf16[512,1024]{1,0:T(8,128)(2,1)S(1)} %get-tuple-element.133.refs_0_, bf16[128,2048]{1,0:T(8,128)(2,1)} %copy-done.2, bf16[128,2048]{1,0:T(8,128)(2,1)} %copy-done.49, ...), custom_call_target="tpu_custom_call" | custom-call | bytes 9900000 | tf_op jit(solution)/shard_map/pallas_call | solution.py:60
  121.5 2.5 %shard_map.190 = (f32[128,1024]{1,0:T(8,128)S(1)}, f32[8,1024]{1,0:T(8,128)S(1)}, bf16[128,512]{1,0:T(8,128)(2,1)S(1)}, bf16[128,512]{1,0:T(8,128)(2,1)S(1)}, bf...) custom-call(f32[128,1024]{1,0:T(8,128)S(1)} %get-tuple-element.144.refs_0_, ...), custom_call_target="tpu_custom_call" | custom-call | bytes 8250000 | tf_op jit(solution)/shard_map/pallas_call | solution.py:60
  124.1 1.5 collective-permute-start.35
  126.1 4.3 %collective-permute-done.35.refs_14_ = bf16[128,512]{1,0:T(8,128)(2,1)S(1)} collective-permute-done((bf16[128,512]{1,0:T(8,128)(2,1)S(1)}, bf16[128,512]{1,0:T(8,128)(2,1)S(1)}, u32[]{:S(2)}, u32[]{:S(2)}) %collective-permute-start.35) | collective-permute-done | bytes 131104 | tf_op jit(solution)/shard_map/ppermute | solution.py:209
  130.5 1.9 collective-permute-done.36.refs_15_
  133.9 1.5 collective-permute-start.40
  135.6 9.4 %shard_map.192 = (bf16[8,144,1024]{2,1,0:T(8,128)(2,1)S(1)}, f32[8,1024]{1,0:T(8,128)}, f32[128,1024]{1,0:T(8,128)S(1)}, bf16[128,1024]{1,0:T(8,128)(2,1)S(1)}, ...) custom-call(bf16[512,768]{1,0:T(8,128)(2,1)S(1)} %copy-done.42, f32[8,256]{1,0:T(8,128)S(1)} %copy-done.47, ...), custom_call_target="tpu_custom_call" | custom-call | bytes 31020000 | tf_op jit(solution)/shard_map/pallas_call | solution.py:60
  145.1 1.6 collective-permute-start.41
  147.5 1.5 collective-permute-start.46
  150.1 1.6 collective-permute-done.38.refs_1_
  153.4 1.5 collective-permute-start.43
  155.0 1.7 collective-permute-done.46.refs_1_
  156.7 4.1 %collective-permute-done.47.refs_2_ = bf16[128,1024]{1,0:T(8,128)(2,1)S(1)} collective-permute-done((bf16[128,1024]{1,0:T(8,128)(2,1)S(1)}, bf16[128,1024]{1,0:T(8,128)(2,1)S(1)}, u32[]{:S(2)}, u32[]{:S(2)}) %collective-permute-start.47) | collective-permute-done | bytes 262176 | tf_op jit(solution)/shard_map/ppermute | solution.py:209
  161.4 1.4 collective-permute-start.49
  163.7 1.2 collective-permute-start.52
  167.9 1.7 collective-permute-done.49.refs_1_
  169.8 8.4 %collective-permute-done.50.refs_2_ = bf16[128,1024]{1,0:T(8,128)(2,1)S(1)} collective-permute-done((bf16[128,1024]{1,0:T(8,128)(2,1)S(1)}, bf16[128,1024]{1,0:T(8,128)(2,1)S(1)}, u32[]{:S(2)}, u32[]{:S(2)}) %collective-permute-start.50) | collective-permute-done | bytes 262176 | tf_op jit(solution)/shard_map/ppermute | solution.py:209
  178.2 1.4 shard_map.196
  180.6 2.1 %collective-permute-done.44.refs_1_ = bf16[144,1024]{1,0:T(8,128)(2,1)S(1)} collective-permute-done((bf16[144,1024]{1,0:T(8,128)(2,1)S(1)}, bf16[144,1024]{1,0:T(8,128)(2,1)S(1)}, u32[]{:S(2)}, u32[]{:S(2)}) %collective-permute-start.44) | collective-permute-done | bytes 294944 | tf_op jit(solution)/shard_map/ppermute | solution.py:180
  185.3 1.6 collective-permute-start.55
  186.8 5.1 %collective-permute-done.54.refs_1_ = bf16[144,1024]{1,0:T(8,128)(2,1)S(1)} collective-permute-done((bf16[144,1024]{1,0:T(8,128)(2,1)S(1)}, bf16[144,1024]{1,0:T(8,128)(2,1)S(1)}, u32[]{:S(2)}, u32[]{:S(2)}) %collective-permute-start.54) | collective-permute-done | bytes 294944 | tf_op jit(solution)/shard_map/ppermute | solution.py:180
  193.2 1.6 collective-permute-start.57
  194.7 4.4 %collective-permute-done.60.refs_2_ = bf16[128,2048]{1,0:T(8,128)(2,1)S(1)} collective-permute-done((bf16[128,2048]{1,0:T(8,128)(2,1)S(1)}, bf16[128,2048]{1,0:T(8,128)(2,1)S(1)}, u32[]{:S(2)}, u32[]{:S(2)}) %collective-permute-start.60) | collective-permute-done | bytes 524320 | tf_op jit(solution)/shard_map/ppermute | solution.py:209
  199.7 3.3 %collective-permute-done.57.refs_2_ = bf16[144,1024]{1,0:T(8,128)(2,1)S(1)} collective-permute-done((bf16[144,1024]{1,0:T(8,128)(2,1)S(1)}, bf16[144,1024]{1,0:T(8,128)(2,1)S(1)}, u32[]{:S(2)}, u32[]{:S(2)}) %collective-permute-start.57) | collective-permute-done | bytes 294944 | tf_op jit(solution)/shard_map/ppermute | solution.py:209
  204.5 2.3 %shard_map.201 = (f32[128,3072]{1,0:T(8,128)}, f32[128,1024]{1,0:T(8,128)}, f32[2,128]{1,0:T(2,128)}, f32[2,128]{1,0:T(2,128)}, f32[1,64]{1,0:T(1,128)}) custom-call(bf16[144,1024]{1,0:T(8,128)(2,1)S(1)} %shard_map.200.refs_0_, bf16[144,1024]{1,0:T(8,128)(2,1)S(1)} %collective-permute-done.56.refs_1_, bf16[144,1024]{1,0:T(8,128)(2,1)S(1)} %collective-permute-done.57.refs_2_, ...), custom_call_target="tpu_custom_call" | custom-call | bytes 7589999 | tf_op jit(solution)/shard_map/pallas_call | solution.py:60
  206.9 3.1 %shard_map.202 = (f32[128,4096]{1,0:T(8,128)}, f32[512,1024]{1,0:T(8,128)}) custom-call(bf16[128,2048]{1,0:T(8,128)(2,1)S(1)} %shard_map.197.refs_0_, bf16[128,2048]{1,0:T(8,128)(2,1)S(1)} %collective-permute-done.59.refs_1_, bf16[128,2048]{1,0:T(8,128)(2,1)S(1)} %collective-permute-done.60.refs_2_, bf16[128,2048]{1,0:T(8,128)(2,1)S(1)} %collective-permute-done.61.refs_3_, ...), custom_call_target="tpu_custom_call" | custom-call | bytes 9900000 | tf_op jit(solution)/shard_map/pallas_call | solution.py:60
  (202 shorter events, 33.5 us)
Async XLA Ops:
  2.2 11.6 %collective-permute-start = (bf16[128,1024]{1,0:T(8,128)(2,1)S(1)}, bf16[128,1024]{1,0:T(8,128)(2,1)S(1)}, u32[]{:S(2)}, u32[]{:S(2)}) collective-permute-start(bf16[128,1024]{1,0:T(8,128)(2,1)S(1)} %shard_map.178.refs_0_.refs_3_.refs_16_), channel_id=1, source_target_pairs={{0,8},{8,16},{16,24},{24,28},{28,20},{20,12},{12,4},{4,0},{1,9},{9... | collective-permute-start | bytes 786440 | tf_op jit(solution)/shard_map/ppermute | solution.py:128
  5.3 8.5 %collective-permute-start.1 = (bf16[128,1024]{1,0:T(8,128)(2,1)S(1)}, bf16[128,1024]{1,0:T(8,128)(2,1)S(1)}, u32[]{:S(2)}, u32[]{:S(2)}) collective-permute-start(bf16[128,1024]{1,0:T(8,128)(2,1)S(1)} %shard_map.178.refs_0_.refs_3_.refs_16_), channel_id=1, source_target_pairs={{8,0},{16,8},{24,16},{28,24},{20,28},{12,20},{4,12},{0,4},{9,1},{1... | collective-permute-start | bytes 786440 | tf_op jit(solution)/shard_map/ppermute | solution.py:129
  8.6 36.9 %copy-start.3 = (f32[4,512,128]{2,1,0:T(8,128)}, f32[4,512,128]{2,1,0:T(8,128)S(1)}, u32[]{:S(2)}) copy-start(f32[4,512,128]{2,1,0:T(8,128)S(1)} %get-tuple-element.118.refs_2_.refs_3_) | copy-start | bytes 3145732
  10.1 32.9 %copy-start.43 = (f32[2,1024]{1,0:T(2,128)S(1)}, f32[2,1024]{1,0:T(2,128)}, u32[]{:S(2)}) copy-start(f32[2,1024]{1,0:T(2,128)} %gain_ref.1) | copy-start | bytes 24580
  10.1 13.4 %collective-permute-start.5 = (bf16[256,1024]{1,0:T(8,128)(2,1)S(1)}, bf16[256,1024]{1,0:T(8,128)(2,1)S(1)}, u32[]{:S(2)}, u32[]{:S(2)}) collective-permute-start(bf16[256,1024]{1,0:T(8,128)(2,1)S(1)} %pad_maximum_fusion.refs_2_), channel_id=1, source_target_pairs={{0,2},{1,3},{2,0},{3,1},{4,6},{5,7},{6,4},{7,5},{8,10},{9,11},{10,... | collective-permute-start | bytes 1572872 | tf_op jit(solution)/shard_map/ppermute | solution.py:209
  13.9 7.3 %collective-permute-start.2 = (bf16[128,1024]{1,0:T(8,128)(2,1)S(1)}, bf16[128,1024]{1,0:T(8,128)(2,1)S(1)}, u32[]{:S(2)}, u32[]{:S(2)}) collective-permute-start(bf16[128,1024]{1,0:T(8,128)(2,1)S(1)} %collective-permute-done.refs_1_.refs_4_.refs_17_), channel_id=1, source_target_pairs={{0,8},{8,16},{16,24},{24,28},{28,20},{20,12},{12,4},{4,0},{1,9},{9... | collective-permute-start | bytes 786440 | tf_op jit(solution)/shard_map/ppermute | solution.py:128
  15.5 6.9 %collective-permute-start.3 = (bf16[128,1024]{1,0:T(8,128)(2,1)S(1)}, bf16[128,1024]{1,0:T(8,128)(2,1)S(1)}, u32[]{:S(2)}, u32[]{:S(2)}) collective-permute-start(bf16[128,1024]{1,0:T(8,128)(2,1)S(1)} %collective-permute-done.1.refs_2_.refs_5_.refs_18_), channel_id=1, source_target_pairs={{8,0},{16,8},{24,16},{28,24},{20,28},{12,20},{4,12},{0,4},{9,1},{1... | collective-permute-start | bytes 786440 | tf_op jit(solution)/shard_map/ppermute | solution.py:129
  23.5 6.9 %collective-permute-start.7 = (bf16[128,1024]{1,0:T(8,128)(2,1)S(1)}, bf16[128,1024]{1,0:T(8,128)(2,1)S(1)}, u32[]{:S(2)}, u32[]{:S(2)}) collective-permute-start(bf16[128,1024]{1,0:T(8,128)(2,1)S(1)} %collective-permute-done.2.refs_3_.refs_6_.refs_19_), channel_id=1, source_target_pairs={{0,8},{8,16},{16,24},{24,28},{28,20},{20,12},{12,4},{4,0},{1,9},{9... | collective-permute-start | bytes 786440 | tf_op jit(solution)/shard_map/ppermute | solution.py:128
  25.3 6.4 %collective-permute-start.8 = (bf16[128,1024]{1,0:T(8,128)(2,1)S(1)}, bf16[128,1024]{1,0:T(8,128)(2,1)S(1)}, u32[]{:S(2)}, u32[]{:S(2)}) collective-permute-start(bf16[128,1024]{1,0:T(8,128)(2,1)S(1)} %collective-permute-done.3.refs_4_.refs_7_.refs_20_), channel_id=1, source_target_pairs={{8,0},{16,8},{24,16},{28,24},{20,28},{12,20},{4,12},{0,4},{9,1},{1... | collective-permute-start | bytes 786440 | tf_op jit(solution)/shard_map/ppermute | solution.py:129
  25.6 17.4 %collective-permute-start.4 = (bf16[256,1024]{1,0:T(8,128)(2,1)S(1)}, bf16[256,1024]{1,0:T(8,128)(2,1)S(1)}, u32[]{:S(2)}, u32[]{:S(2)}) collective-permute-start(bf16[256,1024]{1,0:T(8,128)(2,1)S(1)} %pad_maximum_fusion.refs_2_), channel_id=1, source_target_pairs={{0,1},{1,0},{2,3},{3,2},{4,5},{5,4},{6,7},{7,6},{8,9},{9,8},{10,11... | collective-permute-start | bytes 1572872 | tf_op jit(solution)/shard_map/ppermute | solution.py:209
  32.0 5.0 %collective-permute-start.9 = (bf16[64,1024]{1,0:T(8,128)(2,1)S(1)}, bf16[64,1024]{1,0:T(8,128)(2,1)S(1)}, u32[]{:S(2)}, u32[]{:S(2)}) collective-permute-start(bf16[64,1024]{1,0:T(8,128)(2,1)S(1)} %get-tuple-element.115), channel_id=1, source_target_pairs={{0,8},{8,16},{16,24},{24,28},{28,20},{20,12},{12,4},{4,0},{1,9},{9... | collective-permute-start | bytes 393224 | tf_op jit(solution)/shard_map/ppermute | solution.py:128
  33.6 5.0 %collective-permute-start.10 = (bf16[64,1024]{1,0:T(8,128)(2,1)S(1)}, bf16[64,1024]{1,0:T(8,128)(2,1)S(1)}, u32[]{:S(2)}, u32[]{:S(2)}) collective-permute-start(bf16[64,1024]{1,0:T(8,128)(2,1)S(1)} %get-tuple-element.116), channel_id=1, source_target_pairs={{8,0},{16,8},{24,16},{28,24},{20,28},{12,20},{4,12},{0,4},{9,1},{1... | collective-permute-start | bytes 393224 | tf_op jit(solution)/shard_map/ppermute | solution.py:129
  34.1 8.9 %collective-permute-start.6 = (bf16[256,1024]{1,0:T(8,128)(2,1)S(1)}, bf16[256,1024]{1,0:T(8,128)(2,1)S(1)}, u32[]{:S(2)}, u32[]{:S(2)}) collective-permute-start(bf16[256,1024]{1,0:T(8,128)(2,1)S(1)} %collective-permute-done.5.refs_4_), channel_id=1, source_target_pairs={{0,1},{1,0},{2,3},{3,2},{4,5},{5,4},{6,7},{7,6},{8,9},{9,8},{10,11... | collective-permute-start | bytes 1572872 | tf_op jit(solution)/shard_map/ppermute | solution.py:209
  38.6 12.7 %collective-permute-start.11 = (bf16[128,2048]{1,0:T(8,128)(2,1)S(1)}, bf16[128,2048]{1,0:T(8,128)(2,1)S(1)}, u32[]{:S(2)}, u32[]{:S(2)}) collective-permute-start(bf16[128,2048]{1,0:T(8,128)(2,1)S(1)} %shard_map.180.refs_5_.refs_1_), channel_id=1, source_target_pairs={{0,8},{8,16},{16,24},{24,28},{28,20},{20,12},{12,4},{4,0},{1,9},{9... | collective-permute-start | bytes 1572872 | tf_op jit(solution)/shard_map/ppermute | solution.py:128
  40.2 11.1 %collective-permute-start.12 = (bf16[128,2048]{1,0:T(8,128)(2,1)S(1)}, bf16[128,2048]{1,0:T(8,128)(2,1)S(1)}, u32[]{:S(2)}, u32[]{:S(2)}) collective-permute-start(bf16[128,2048]{1,0:T(8,128)(2,1)S(1)} %shard_map.180.refs_5_.refs_1_), channel_id=1, source_target_pairs={{8,0},{16,8},{24,16},{28,24},{20,28},{12,20},{4,12},{0,4},{9,1},{1... | collective-permute-start | bytes 1572872 | tf_op jit(solution)/shard_map/ppermute | solution.py:129
  41.4 10.5 %collective-permute-start.17 = (bf16[1024,256]{1,0:T(8,128)(2,1)S(1)}, bf16[1024,256]{1,0:T(8,128)(2,1)S(1)}, u32[]{:S(2)}, u32[]{:S(2)}) collective-permute-start(bf16[1024,256]{1,0:T(8,128)(2,1)S(1)} %shard_map.183.refs_7_), channel_id=1, source_target_pairs={{0,2},{1,3},{2,0},{3,1},{4,6},{5,7},{6,4},{7,5},{8,10},{9,11},{10,... | collective-permute-start | bytes 1572872 | tf_op jit(solution)/shard_map/ppermute | solution.py:209
  43.0 11.2 %collective-permute-start.16 = (bf16[1024,256]{1,0:T(8,128)(2,1)S(1)}, bf16[1024,256]{1,0:T(8,128)(2,1)S(1)}, u32[]{:S(2)}, u32[]{:S(2)}) collective-permute-start(bf16[1024,256]{1,0:T(8,128)(2,1)S(1)} %shard_map.183.refs_7_), channel_id=1, source_target_pairs={{0,1},{1,0},{2,3},{3,2},{4,5},{5,4},{6,7},{7,6},{8,9},{9,8},{10,11... | collective-permute-start | bytes 1572872 | tf_op jit(solution)/shard_map/ppermute | solution.py:209
  51.3 8.8 %collective-permute-start.14 = (bf16[512,256]{1,0:T(8,128)(2,1)S(1)}, bf16[512,256]{1,0:T(8,128)(2,1)S(1)}, u32[]{:S(2)}, u32[]{:S(2)}) collective-permute-start(bf16[512,256]{1,0:T(8,128)(2,1)S(1)} %get-tuple-element.122.refs_3_.refs_8_), channel_id=1, source_target_pairs={{0,2},{1,3},{2,0},{3,1},{4,6},{5,7},{6,4},{7,5},{8,10},{9,11},{10,... | collective-permute-start | bytes 786440 | tf_op jit(solution)/shard_map/ppermute | solution.py:209
  51.9 9.7 %collective-permute-start.18 = (bf16[1024,256]{1,0:T(8,128)(2,1)S(1)}, bf16[1024,256]{1,0:T(8,128)(2,1)S(1)}, u32[]{:S(2)}, u32[]{:S(2)}) collective-permute-start(bf16[1024,256]{1,0:T(8,128)(2,1)S(1)} %collective-permute-done.17.refs_9_), channel_id=1, source_target_pairs={{0,1},{1,0},{2,3},{3,2},{4,5},{5,4},{6,7},{7,6},{8,9},{9,8},{10,11... | collective-permute-start | bytes 1572872 | tf_op jit(solution)/shard_map/ppermute | solution.py:209
  52.2 14.1 %collective-permute-start.19 = (bf16[128,2048]{1,0:T(8,128)(2,1)S(1)}, bf16[128,2048]{1,0:T(8,128)(2,1)S(1)}, u32[]{:S(2)}, u32[]{:S(2)}) collective-permute-start(bf16[128,2048]{1,0:T(8,128)(2,1)S(1)} %collective-permute-done.11.refs_6_.refs_2_), channel_id=1, source_target_pairs={{0,8},{8,16},{16,24},{24,28},{28,20},{20,12},{12,4},{4,0},{1,9},{9... | collective-permute-start | bytes 1572872 | tf_op jit(solution)/shard_map/ppermute | solution.py:128
  53.7 13.8 %collective-permute-start.20 = (bf16[128,2048]{1,0:T(8,128)(2,1)S(1)}, bf16[128,2048]{1,0:T(8,128)(2,1)S(1)}, u32[]{:S(2)}, u32[]{:S(2)}) collective-permute-start(bf16[128,2048]{1,0:T(8,128)(2,1)S(1)} %collective-permute-done.12.refs_7_.refs_3_), channel_id=1, source_target_pairs={{8,0},{16,8},{24,16},{28,24},{20,28},{12,20},{4,12},{0,4},{9,1},{1... | collective-permute-start | bytes 1572872 | tf_op jit(solution)/shard_map/ppermute | solution.py:129
  54.2 5.9 %collective-permute-start.13 = (bf16[512,256]{1,0:T(8,128)(2,1)S(1)}, bf16[512,256]{1,0:T(8,128)(2,1)S(1)}, u32[]{:S(2)}, u32[]{:S(2)}) collective-permute-start(bf16[512,256]{1,0:T(8,128)(2,1)S(1)} %get-tuple-element.122.refs_3_.refs_8_), channel_id=1, source_target_pairs={{0,1},{1,0},{2,3},{3,2},{4,5},{5,4},{6,7},{7,6},{8,9},{9,8},{10,11... | collective-permute-start | bytes 786440 | tf_op jit(solution)/shard_map/ppermute | solution.py:209
  60.1 1.5 collective-permute-start.15
  67.6 13.0 %collective-permute-start.24 = (bf16[128,2048]{1,0:T(8,128)(2,1)S(1)}, bf16[128,2048]{1,0:T(8,128)(2,1)S(1)}, u32[]{:S(2)}, u32[]{:S(2)}) collective-permute-start(bf16[128,2048]{1,0:T(8,128)(2,1)S(1)} %collective-permute-done.19.refs_8_.refs_4_), channel_id=1, source_target_pairs={{0,8},{8,16},{16,24},{24,28},{28,20},{20,12},{12,4},{4,0},{1,9},{9... | collective-permute-start | bytes 1572872 | tf_op jit(solution)/shard_map/ppermute | solution.py:128
  69.1 12.7 %collective-permute-start.25 = (bf16[128,2048]{1,0:T(8,128)(2,1)S(1)}, bf16[128,2048]{1,0:T(8,128)(2,1)S(1)}, u32[]{:S(2)}, u32[]{:S(2)}) collective-permute-start(bf16[128,2048]{1,0:T(8,128)(2,1)S(1)} %collective-permute-done.20.refs_9_.refs_5_), channel_id=1, source_target_pairs={{8,0},{16,8},{24,16},{28,24},{20,28},{12,20},{4,12},{0,4},{9,1},{1... | collective-permute-start | bytes 1572872 | tf_op jit(solution)/shard_map/ppermute | solution.py:129
  69.6 7.0 %collective-permute-start.22 = (bf16[128,1024]{1,0:T(8,128)(2,1)}, bf16[128,1024]{1,0:T(8,128)(2,1)S(1)}, u32[]{:S(2)}, u32[]{:S(2)}) collective-permute-start(bf16[128,1024]{1,0:T(8,128)(2,1)} %get-tuple-element.126.refs_1_), channel_id=1, source_target_pairs={{0,2},{1,3},{2,0},{3,1},{4,6},{5,7},{6,4},{7,5},{8,10},{9,11},{10,... | collective-permute-start | bytes 786440 | tf_op jit(solution)/shard_map/ppermute | solution.py:209
  76.6 6.1 %collective-permute-start.23 = (bf16[128,1024]{1,0:T(8,128)(2,1)S(1)}, bf16[128,1024]{1,0:T(8,128)(2,1)S(1)}, u32[]{:S(2)}, u32[]{:S(2)}) collective-permute-start(bf16[128,1024]{1,0:T(8,128)(2,1)S(1)} %collective-permute-done.22.refs_3_), channel_id=1, source_target_pairs={{0,1},{1,0},{2,3},{3,2},{4,5},{5,4},{6,7},{7,6},{8,9},{9,8},{10,11... | collective-permute-start | bytes 786440 | tf_op jit(solution)/shard_map/ppermute | solution.py:209
  76.6 8.5 %collective-permute-start.21 = (bf16[128,1024]{1,0:T(8,128)(2,1)}, bf16[128,1024]{1,0:T(8,128)(2,1)}, u32[]{:S(2)}, u32[]{:S(2)}) collective-permute-start(bf16[128,1024]{1,0:T(8,128)(2,1)} %get-tuple-element.126.refs_1_), channel_id=1, source_target_pairs={{0,1},{1,0},{2,3},{3,2},{4,5},{5,4},{6,7},{7,6},{8,9},{9,8},{10,11... | collective-permute-start | bytes 786440 | tf_op jit(solution)/shard_map/ppermute | solution.py:209
  82.8 6.7 %collective-permute-start.26 = (bf16[64,2048]{1,0:T(8,128)(2,1)}, bf16[64,2048]{1,0:T(8,128)(2,1)}, u32[]{:S(2)}, u32[]{:S(2)}) collective-permute-start(bf16[64,2048]{1,0:T(8,128)(2,1)} %get-tuple-element.131), channel_id=1, source_target_pairs={{0,8},{8,16},{16,24},{24,28},{28,20},{20,12},{12,4},{4,0},{1,9},{9... | collective-permute-start | bytes 786440 | tf_op jit(solution)/shard_map/ppermute | solution.py:128
  83.6 6.9 %collective-permute-start.27 = (bf16[64,2048]{1,0:T(8,128)(2,1)}, bf16[64,2048]{1,0:T(8,128)(2,1)}, u32[]{:S(2)}, u32[]{:S(2)}) collective-permute-start(bf16[64,2048]{1,0:T(8,128)(2,1)} %get-tuple-element.132), channel_id=1, source_target_pairs={{8,0},{16,8},{24,16},{28,24},{20,28},{12,20},{4,12},{0,4},{9,1},{1... | collective-permute-start | bytes 786440 | tf_op jit(solution)/shard_map/ppermute | solution.py:129
  100.6 6.4 %collective-permute-start.28 = (bf16[64,2048]{1,0:T(8,128)(2,1)S(1)}, bf16[64,2048]{1,0:T(8,128)(2,1)S(1)}, u32[]{:S(2)}, u32[]{:S(2)}) collective-permute-start(bf16[64,2048]{1,0:T(8,128)(2,1)S(1)} %get-tuple-element.196), channel_id=1, source_target_pairs={{0,8},{8,16},{16,24},{24,28},{28,20},{20,12},{12,4},{4,0},{1,9},{9... | collective-permute-start | bytes 786440 | tf_op jit(solution)/shard_map/ppermute | solution.py:180
  101.1 5.9 %collective-permute-start.29 = (bf16[128,1024]{1,0:T(8,128)(2,1)S(1)}, bf16[128,1024]{1,0:T(8,128)(2,1)S(1)}, u32[]{:S(2)}, u32[]{:S(2)}) collective-permute-start(bf16[128,1024]{1,0:T(8,128)(2,1)S(1)} %get-tuple-element.137), channel_id=1, source_target_pairs={{0,1},{1,0},{2,3},{3,2},{4,5},{5,4},{6,7},{7,6},{8,9},{9,8},{10,11... | collective-permute-start | bytes 786440 | tf_op jit(solution)/shard_map/ppermute | solution.py:209
  101.1 9.1 %collective-permute-start.30 = (bf16[128,1024]{1,0:T(8,128)(2,1)S(1)}, bf16[128,1024]{1,0:T(8,128)(2,1)S(1)}, u32[]{:S(2)}, u32[]{:S(2)}) collective-permute-start(bf16[128,1024]{1,0:T(8,128)(2,1)S(1)} %get-tuple-element.138), channel_id=1, source_target_pairs={{0,2},{1,3},{2,0},{3,1},{4,6},{5,7},{6,4},{7,5},{8,10},{9,11},{10,... | collective-permute-start | bytes 786440 | tf_op jit(solution)/shard_map/ppermute | solution.py:209
  102.6 12.5 %collective-permute-start.31 = (bf16[128,1024]{1,0:T(8,128)(2,1)S(1)}, bf16[128,1024]{1,0:T(8,128)(2,1)S(1)}, u32[]{:S(2)}, u32[]{:S(2)}) collective-permute-start(bf16[128,1024]{1,0:T(8,128)(2,1)S(1)} %get-tuple-element.139), channel_id=1, source_target_pairs={{0,3},{1,2},{2,1},{3,0},{4,7},{5,6},{6,5},{7,4},{8,11},{9,10},{10,... | collective-permute-start | bytes 786440 | tf_op jit(solution)/shard_map/ppermute | solution.py:209
  103.0 12.1 %collective-permute-start.32 = (bf16[64,2048]{1,0:T(8,128)(2,1)S(1)}, bf16[64,2048]{1,0:T(8,128)(2,1)S(1)}, u32[]{:S(2)}, u32[]{:S(2)}) collective-permute-start(bf16[64,2048]{1,0:T(8,128)(2,1)S(1)} %get-tuple-element.195), channel_id=1, source_target_pairs={{8,0},{16,8},{24,16},{28,24},{20,28},{12,20},{4,12},{0,4},{9,1},{1... | collective-permute-start | bytes 786440 | tf_op jit(solution)/shard_map/ppermute | solution.py:181
  115.9 16.4 %collective-permute-start.33 = (bf16[128,2048]{1,0:T(8,128)(2,1)S(1)}, bf16[128,2048]{1,0:T(8,128)(2,1)S(1)}, u32[]{:S(2)}, u32[]{:S(2)}) collective-permute-start(bf16[128,2048]{1,0:T(8,128)(2,1)S(1)} %get-tuple-element.141), channel_id=1, source_target_pairs={{0,8},{8,16},{16,24},{24,28},{28,20},{20,12},{12,4},{4,0},{1,9},{9... | collective-permute-start | bytes 1572872 | tf_op jit(solution)/shard_map/ppermute | solution.py:180
  116.5 15.9 %collective-permute-start.37 = (bf16[128,2048]{1,0:T(8,128)(2,1)S(1)}, bf16[128,2048]{1,0:T(8,128)(2,1)S(1)}, u32[]{:S(2)}, u32[]{:S(2)}) collective-permute-start(bf16[128,2048]{1,0:T(8,128)(2,1)S(1)} %get-tuple-element.143), channel_id=1, source_target_pairs={{8,0},{16,8},{24,16},{28,24},{20,28},{12,20},{4,12},{0,4},{9,1},{1... | collective-permute-start | bytes 1572872 | tf_op jit(solution)/shard_map/ppermute | solution.py:181
  124.0 2.1 collective-permute-start.34
  124.1 6.4 %collective-permute-start.35 = (bf16[128,512]{1,0:T(8,128)(2,1)S(1)}, bf16[128,512]{1,0:T(8,128)(2,1)S(1)}, u32[]{:S(2)}, u32[]{:S(2)}) collective-permute-start(bf16[128,512]{1,0:T(8,128)(2,1)S(1)} %get-tuple-element.147), channel_id=1, source_target_pairs={{0,2},{1,3},{2,0},{3,1},{4,6},{5,7},{6,4},{7,5},{8,10},{9,11},{10,... | collective-permute-start | bytes 393224 | tf_op jit(solution)/shard_map/ppermute | solution.py:209
  125.7 6.6 %collective-permute-start.36 = (bf16[128,512]{1,0:T(8,128)(2,1)S(1)}, bf16[128,512]{1,0:T(8,128)(2,1)S(1)}, u32[]{:S(2)}, u32[]{:S(2)}) collective-permute-start(bf16[128,512]{1,0:T(8,128)(2,1)S(1)} %get-tuple-element.148), channel_id=1, source_target_pairs={{0,3},{1,2},{2,1},{3,0},{4,7},{5,6},{6,5},{7,4},{8,11},{9,10},{10,... | collective-permute-start | bytes 393224 | tf_op jit(solution)/shard_map/ppermute | solution.py:209
  133.4 14.2 %collective-permute-start.39 = (bf16[128,2048]{1,0:T(8,128)(2,1)S(1)}, bf16[128,2048]{1,0:T(8,128)(2,1)S(1)}, u32[]{:S(2)}, u32[]{:S(2)}) collective-permute-start(bf16[128,2048]{1,0:T(8,128)(2,1)S(1)} %get-tuple-element.150), channel_id=1, source_target_pairs={{0,8},{8,16},{16,24},{24,28},{28,20},{20,12},{12,4},{4,0},{1,9},{9... | collective-permute-start | bytes 1572872 | tf_op jit(solution)/shard_map/ppermute | solution.py:180
  133.9 15.1 %collective-permute-start.40 = (bf16[128,2048]{1,0:T(8,128)(2,1)S(1)}, bf16[128,2048]{1,0:T(8,128)(2,1)S(1)}, u32[]{:S(2)}, u32[]{:S(2)}) collective-permute-start(bf16[128,2048]{1,0:T(8,128)(2,1)S(1)} %get-tuple-element.151), channel_id=1, source_target_pairs={{8,0},{16,8},{24,16},{28,24},{20,28},{12,20},{4,12},{0,4},{9,1},{1... | collective-permute-start | bytes 1572872 | tf_op jit(solution)/shard_map/ppermute | solution.py:181
  145.1 6.6 %collective-permute-start.41 = (bf16[80,1024]{1,0:T(8,128)(2,1)S(1)}, bf16[80,1024]{1,0:T(8,128)(2,1)S(1)}, u32[]{:S(2)}, u32[]{:S(2)}) collective-permute-start(bf16[80,1024]{1,0:T(8,128)(2,1)S(1)} %dynamic-slice_bitcast_fusion.2), channel_id=1, source_target_pairs={{8,0},{16,8},{24,16},{28,24},{20,28},{12,20},{4,12},{0,4},{9,1},{1... | collective-permute-start | bytes 491528 | tf_op jit(solution)/shard_map/ppermute | solution.py:181
  146.7 5.0 %collective-permute-start.38 = (bf16[64,1024]{1,0:T(8,128)(2,1)S(1)}, bf16[64,1024]{1,0:T(8,128)(2,1)S(1)}, u32[]{:S(2)}, u32[]{:S(2)}) collective-permute-start(bf16[64,1024]{1,0:T(8,128)(2,1)S(1)} %dynamic-slice_bitcast_fusion.3), channel_id=1, source_target_pairs={{0,8},{8,16},{16,24},{24,28},{28,20},{20,12},{12,4},{4,0},{1,9},{9... | collective-permute-start | bytes 393224 | tf_op jit(solution)/shard_map/ppermute | solution.py:180
  147.2 7.8 %collective-permute-start.45 = (bf16[128,1024]{1,0:T(8,128)(2,1)S(1)}, bf16[128,1024]{1,0:T(8,128)(2,1)S(1)}, u32[]{:S(2)}, u32[]{:S(2)}) collective-permute-start(bf16[128,1024]{1,0:T(8,128)(2,1)S(1)} %get-tuple-element.172), channel_id=1, source_target_pairs={{0,1},{1,0},{2,3},{3,2},{4,5},{5,4},{6,7},{7,6},{8,9},{9,8},{10,11... | collective-permute-start | bytes 786440 | tf_op jit(solution)/shard_map/ppermute | solution.py:209
  147.5 9.1 %collective-permute-start.46 = (bf16[128,1024]{1,0:T(8,128)(2,1)S(1)}, bf16[128,1024]{1,0:T(8,128)(2,1)S(1)}, u32[]{:S(2)}, u32[]{:S(2)}) collective-permute-start(bf16[128,1024]{1,0:T(8,128)(2,1)S(1)} %get-tuple-element.174), channel_id=1, source_target_pairs={{0,2},{1,3},{2,0},{3,1},{4,6},{5,7},{6,4},{7,5},{8,10},{9,11},{10,... | collective-permute-start | bytes 786440 | tf_op jit(solution)/shard_map/ppermute | solution.py:209
  149.0 11.8 %collective-permute-start.47 = (bf16[128,1024]{1,0:T(8,128)(2,1)S(1)}, bf16[128,1024]{1,0:T(8,128)(2,1)S(1)}, u32[]{:S(2)}, u32[]{:S(2)}) collective-permute-start(bf16[128,1024]{1,0:T(8,128)(2,1)S(1)} %get-tuple-element.176), channel_id=1, source_target_pairs={{0,3},{1,2},{2,1},{3,0},{4,7},{5,6},{6,5},{7,4},{8,11},{9,10},{10,... | collective-permute-start | bytes 786440 | tf_op jit(solution)/shard_map/ppermute | solution.py:209
  152.9 10.8 %collective-permute-start.42 = (bf16[144,1024]{1,0:T(8,128)(2,1)S(1)}, bf16[144,1024]{1,0:T(8,128)(2,1)S(1)}, u32[]{:S(2)}, u32[]{:S(2)}) collective-permute-start(bf16[144,1024]{1,0:T(8,128)(2,1)S(1)} %get-tuple-element.163), channel_id=1, source_target_pairs={{0,8},{8,16},{16,24},{24,28},{28,20},{20,12},{12,4},{4,0},{1,9},{9... | collective-permute-start | bytes 884744 | tf_op jit(solution)/shard_map/ppermute | solution.py:180
  153.4 11.5 %collective-permute-start.43 = (bf16[144,1024]{1,0:T(8,128)(2,1)S(1)}, bf16[144,1024]{1,0:T(8,128)(2,1)S(1)}, u32[]{:S(2)}, u32[]{:S(2)}) collective-permute-start(bf16[144,1024]{1,0:T(8,128)(2,1)S(1)} %get-tuple-element.164), channel_id=1, source_target_pairs={{8,0},{16,8},{24,16},{28,24},{20,28},{12,20},{4,12},{0,4},{9,1},{1... | collective-permute-start | bytes 884744 | tf_op jit(solution)/shard_map/ppermute | solution.py:181
  160.8 5.9 %collective-permute-start.48 = (bf16[128,1024]{1,0:T(8,128)(2,1)S(1)}, bf16[128,1024]{1,0:T(8,128)(2,1)S(1)}, u32[]{:S(2)}, u32[]{:S(2)}) collective-permute-start(bf16[128,1024]{1,0:T(8,128)(2,1)S(1)} %get-tuple-element.177), channel_id=1, source_target_pairs={{0,1},{1,0},{2,3},{3,2},{4,5},{5,4},{6,7},{7,6},{8,9},{9,8},{10,11... | collective-permute-start | bytes 786440 | tf_op jit(solution)/shard_map/ppermute | solution.py:209
  161.4 8.2 %collective-permute-start.49 = (bf16[128,1024]{1,0:T(8,128)(2,1)S(1)}, bf16[128,1024]{1,0:T(8,128)(2,1)S(1)}, u32[]{:S(2)}, u32[]{:S(2)}) collective-permute-start(bf16[128,1024]{1,0:T(8,128)(2,1)S(1)} %get-tuple-element.179), channel_id=1, source_target_pairs={{0,2},{1,3},{2,0},{3,1},{4,6},{5,7},{6,4},{7,5},{8,10},{9,11},{10,... | collective-permute-start | bytes 786440 | tf_op jit(solution)/shard_map/ppermute | solution.py:209
  162.8 16.8 %collective-permute-start.51 = (bf16[128,2048]{1,0:T(8,128)(2,1)S(1)}, bf16[128,2048]{1,0:T(8,128)(2,1)S(1)}, u32[]{:S(2)}, u32[]{:S(2)}) collective-permute-start(bf16[128,2048]{1,0:T(8,128)(2,1)S(1)} %get-tuple-element.160), channel_id=1, source_target_pairs={{0,8},{8,16},{16,24},{24,28},{28,20},{20,12},{12,4},{4,0},{1,9},{9... | collective-permute-start | bytes 1572872 | tf_op jit(solution)/shard_map/ppermute | solution.py:180
  163.7 16.0 %collective-permute-start.52 = (bf16[128,2048]{1,0:T(8,128)(2,1)S(1)}, bf16[128,2048]{1,0:T(8,128)(2,1)S(1)}, u32[]{:S(2)}, u32[]{:S(2)}) collective-permute-start(bf16[128,2048]{1,0:T(8,128)(2,1)S(1)} %get-tuple-element.161), channel_id=1, source_target_pairs={{8,0},{16,8},{24,16},{28,24},{20,28},{12,20},{4,12},{0,4},{9,1},{1... | collective-permute-start | bytes 1572872 | tf_op jit(solution)/shard_map/ppermute | solution.py:181
  165.9 16.9 %collective-permute-start.44 = (bf16[144,1024]{1,0:T(8,128)(2,1)S(1)}, bf16[144,1024]{1,0:T(8,128)(2,1)S(1)}, u32[]{:S(2)}, u32[]{:S(2)}) collective-permute-start(bf16[144,1024]{1,0:T(8,128)(2,1)S(1)} %get-tuple-element.165), channel_id=1, source_target_pairs={{0,8},{8,16},{16,24},{24,28},{28,20},{20,12},{12,4},{4,0},{1,9},{9... | collective-permute-start | bytes 884744 | tf_op jit(solution)/shard_map/ppermute | solution.py:180
  166.7 16.5 %collective-permute-start.53 = (bf16[144,1024]{1,0:T(8,128)(2,1)S(1)}, bf16[144,1024]{1,0:T(8,128)(2,1)S(1)}, u32[]{:S(2)}, u32[]{:S(2)}) collective-permute-start(bf16[144,1024]{1,0:T(8,128)(2,1)S(1)} %get-tuple-element.167), channel_id=1, source_target_pairs={{8,0},{16,8},{24,16},{28,24},{20,28},{12,20},{4,12},{0,4},{9,1},{1... | collective-permute-start | bytes 884744 | tf_op jit(solution)/shard_map/ppermute | solution.py:181
  169.6 8.6 %collective-permute-start.50 = (bf16[128,1024]{1,0:T(8,128)(2,1)S(1)}, bf16[128,1024]{1,0:T(8,128)(2,1)S(1)}, u32[]{:S(2)}, u32[]{:S(2)}) collective-permute-start(bf16[128,1024]{1,0:T(8,128)(2,1)S(1)} %get-tuple-element.181), channel_id=1, source_target_pairs={{0,3},{1,2},{2,1},{3,0},{4,7},{5,6},{6,5},{7,4},{8,11},{9,10},{10,... | collective-permute-start | bytes 786440 | tf_op jit(solution)/shard_map/ppermute | solution.py:209
  184.2 14.9 %collective-permute-start.60 = (bf16[128,2048]{1,0:T(8,128)(2,1)S(1)}, bf16[128,2048]{1,0:T(8,128)(2,1)S(1)}, u32[]{:S(2)}, u32[]{:S(2)}) collective-permute-start(bf16[128,2048]{1,0:T(8,128)(2,1)S(1)} %shard_map.197.refs_0_), channel_id=1, source_target_pairs={{0,2},{1,3},{2,0},{3,1},{4,6},{5,7},{6,4},{7,5},{8,10},{9,11},{10,... | collective-permute-start | bytes 1572872 | tf_op jit(solution)/shard_map/ppermute | solution.py:209
  184.8 7.2 %collective-permute-start.54 = (bf16[144,1024]{1,0:T(8,128)(2,1)S(1)}, bf16[144,1024]{1,0:T(8,128)(2,1)S(1)}, u32[]{:S(2)}, u32[]{:S(2)}) collective-permute-start(bf16[144,1024]{1,0:T(8,128)(2,1)S(1)} %get-tuple-element.184), channel_id=1, source_target_pairs={{0,8},{8,16},{16,24},{24,28},{28,20},{20,12},{12,4},{4,0},{1,9},{9... | collective-permute-start | bytes 884744 | tf_op jit(solution)/shard_map/ppermute | solution.py:180
  185.3 7.0 %collective-permute-start.55 = (bf16[144,1024]{1,0:T(8,128)(2,1)S(1)}, bf16[144,1024]{1,0:T(8,128)(2,1)S(1)}, u32[]{:S(2)}, u32[]{:S(2)}) collective-permute-start(bf16[144,1024]{1,0:T(8,128)(2,1)S(1)} %get-tuple-element.185), channel_id=1, source_target_pairs={{8,0},{16,8},{24,16},{28,24},{20,28},{12,20},{4,12},{0,4},{9,1},{1... | collective-permute-start | bytes 884744 | tf_op jit(solution)/shard_map/ppermute | solution.py:181
  193.2 9.8 %collective-permute-start.57 = (bf16[144,1024]{1,0:T(8,128)(2,1)S(1)}, bf16[144,1024]{1,0:T(8,128)(2,1)S(1)}, u32[]{:S(2)}, u32[]{:S(2)}) collective-permute-start(bf16[144,1024]{1,0:T(8,128)(2,1)S(1)} %shard_map.200.refs_0_), channel_id=1, source_target_pairs={{0,2},{1,3},{2,0},{3,1},{4,6},{5,7},{6,4},{7,5},{8,10},{9,11},{10,... | collective-permute-start | bytes 884744 | tf_op jit(solution)/shard_map/ppermute | solution.py:209
  194.7 12.1 %collective-permute-start.59 = (bf16[128,2048]{1,0:T(8,128)(2,1)S(1)}, bf16[128,2048]{1,0:T(8,128)(2,1)S(1)}, u32[]{:S(2)}, u32[]{:S(2)}) collective-permute-start(bf16[128,2048]{1,0:T(8,128)(2,1)S(1)} %shard_map.197.refs_0_), channel_id=1, source_target_pairs={{0,1},{1,0},{2,3},{3,2},{4,5},{5,4},{6,7},{7,6},{8,9},{9,8},{10,11... | collective-permute-start | bytes 1572872 | tf_op jit(solution)/shard_map/ppermute | solution.py:209
  199.2 7.7 %collective-permute-start.61 = (bf16[128,2048]{1,0:T(8,128)(2,1)S(1)}, bf16[128,2048]{1,0:T(8,128)(2,1)S(1)}, u32[]{:S(2)}, u32[]{:S(2)}) collective-permute-start(bf16[128,2048]{1,0:T(8,128)(2,1)S(1)} %collective-permute-done.60.refs_2_), channel_id=1, source_target_pairs={{0,1},{1,0},{2,3},{3,2},{4,5},{5,4},{6,7},{7,6},{8,9},{9,8},{10,11... | collective-permute-start | bytes 1572872 | tf_op jit(solution)/shard_map/ppermute | solution.py:209
  199.2 4.7 %collective-permute-start.56 = (bf16[144,1024]{1,0:T(8,128)(2,1)S(1)}, bf16[144,1024]{1,0:T(8,128)(2,1)S(1)}, u32[]{:S(2)}, u32[]{:S(2)}) collective-permute-start(bf16[144,1024]{1,0:T(8,128)(2,1)S(1)} %shard_map.200.refs_0_), channel_id=1, source_target_pairs={{0,1},{1,0},{2,3},{3,2},{4,5},{5,4},{6,7},{7,6},{8,9},{9,8},{10,11... | collective-permute-start | bytes 884744 | tf_op jit(solution)/shard_map/ppermute | solution.py:209
  203.0 1.6 collective-permute-start.58
  (53 other events, 779.9 us)

commit v4 on v3

--- a/solution.py
+++ b/solution.py
@@ -130,53 +130,83 @@
         self.pieces += [self.up, self.down]
 
 
+def target_rows(parts, me_ref, count, step):
+    at = position_of(me_ref[1], count)
+    near, far = count // 2 - step, count // 2 + 1 - step
+    middle = parts.shape[2] // 2
+    left, right = slice(0, middle), slice(middle, 2 * middle)
+    up = parts.at[rank_at(at + far, count), :, left], parts.at[rank_at(at + near, count), :, right]
+    down = parts.at[rank_at(at - near, count), :, left], parts.at[rank_at(at - far, count), :, right]
+    return up, down
+
+
+def store_first(parts, me_ref, up_ref, down_ref):
+    middle = parts.shape[2] // 2
+    for target, (left, right) in zip((up_ref, down_ref), target_rows(parts, me_ref, parts.shape[0], 1)):
+        target[:, :middle] = left[...]
+        target[:, middle:] = right[...]
+
+
 def ring_add_kernel(count, step, *refs):
     parts, up_ref, down_ref, me_ref = refs[:4]
-    *outs, mine, up, down, sems = refs[4:]
-    rows = parts.shape[1]
-    half = half_rows(rows)
-    at = position_of(me_ref[1], count)
-    up_rows, down_rows = (slice(0, half), slice(half, rows)) if step == 1 else (slice(0, rows),) * 2
+    up_out, down_out, mine, up, down, sems = refs[4:]
+    middle = parts.shape[2] // 2
+    left, right = slice(0, middle), slice(middle, 2 * middle)
+    (up_left, up_right), (down_left, down_right) = target_rows(parts, me_ref, count, step)
+    last = step == count // 2
     copies = [
-        pltpu.make_async_copy(up_ref, up.at[up_rows, :], sems.at[0]),
-        pltpu.make_async_copy(down_ref, down.at[down_rows, :], sems.at[1]),
-        pltpu.make_async_copy(parts.at[rank_at(at + count // 2 - step, count)], mine.at[0], sems.at[2]),
+        pltpu.make_async_copy(up_ref.at[:, left if last else slice(None)], up.at[:, left if last else slice(None)], sems.at[0]),
+        pltpu.make_async_copy(down_ref.at[:, right if last else slice(None)], down.at[:, right if last else slice(None)], sems.at[1]),
+        pltpu.make_async_copy(up_left, mine.at[0, :, left], sems.at[2]),
+        pltpu.make_async_copy(down_right, mine.at[1, :, right], sems.at[3]),
     ]
-    if step < count // 2:
-        copies.append(
-            pltpu.make_async_copy(parts.at[rank_at(at - count // 2 + step, count)], mine.at[1], sems.at[3])
-        )
+    if not last:
+        copies.append(pltpu.make_async_copy(up_right, mine.at[0, :, right], sems.at[4]))
+        copies.append(pltpu.make_async_copy(down_left, mine.at[1, :, left], sems.at[5]))
     finish(start_all(copies))
-    if step == count // 2:
-        total = mine[0].astype(F32) + up[...].astype(F32) + down[...].astype(F32)
-        outs[0][...] = total.astype(BF16)
-        return
-    for target, own, arrived, where in zip(outs, (mine.at[0], mine.at[1]), (up, down), (up_rows, down_rows)):
-        if step == 1:
-            target[...] = own[...]
-        target[where, :] = (own[where, :].astype(F32) + arrived[where, :].astype(F32)).astype(BF16)
+    up_lanes, down_lanes = (left, right) if last else (slice(None), slice(None))
+    up_out[...] = (mine[0, :, up_lanes].astype(F32) + up[:, up_lanes].astype(F32)).astype(BF16)
+    down_out[...] = (mine[1, :, down_lanes].astype(F32) + down[:, down_lanes].astype(F32)).astype(BF16)
+
+
+def ring_total_kernel(count, parts, up_ref, down_ref, last_up_ref, last_down_ref, me_ref, out_ref, mine, first, last, sems):
+    middle = parts.shape[2] // 2
+    left, right = slice(0, middle), slice(middle, 2 * middle)
+    copies = [
+        pltpu.make_async_copy(parts.at[me_ref[1]], mine, sems.at[0]),
+        pltpu.make_async_copy(down_ref.at[:, left], first.at[:, left], sems.at[1]),
+        pltpu.make_async_copy(up_ref.at[:, right], first.at[:, right], sems.at[2]),
+        pltpu.make_async_copy(last_up_ref, last.at[:, left], sems.at[3]),
+        pltpu.make_async_copy(last_down_ref, last.at[:, right], sems.at[4]),
+    ]
+    finish(start_all(copies))
+    total = mine[...].astype(F32) + first[...].astype(F32) + last[...].astype(F32)
+    out_ref[...] = total.astype(BF16)
 
 
 class ScatterRing:
-    def __init__(self, parts, me, count):
+    def __init__(self, parts, first, me, count):
         self.parts, self.me, self.count, self.at = parts, me, count, 0
-        self.total = None
+        self.added = first
 
     def step(self, *others):
         self.at += 1
         if self.count != 8:
             return
         forward, backward = ring_pairs(self.count)
-        rows = self.parts.shape[1]
-        half = half_rows(rows)
-        if self.at == 1:
-            me = position_of(lax.axis_index("dp"), self.count)
-            far = rank_at(me + self.count // 2, self.count)
-            far = lax.dynamic_index_in_dim(self.parts, far, 0, keepdims=False)
-            up, down = far[:half], far[half:]
-        else:
-            up, down = self.add(self.at - 1, 2, *others)
-        self.added = up, down
+        rows, columns = self.parts.shape[1:]
+        if self.at > 1:
+            width = columns // 2 if self.at == self.count // 2 else columns
+            self.before = self.up, self.down
+            self.added = call(
+                functools.partial(ring_add_kernel, self.count, self.at),
+                [shaped((rows, width), BF16)] * 2,
+                [],
+                [self.parts, hold(self.up, *others), self.down],
+                [self.me],
+                [pltpu.VMEM((2, rows, columns), BF16)] + [pltpu.VMEM((rows, columns), BF16)] * 2 + [dma(6)],
+            )
+        up, down = self.added
         self.up = lax.ppermute(up, "dp", forward)
         self.down = lax.ppermute(down, "dp", backward)
 
@@ -184,24 +214,20 @@
         return (self.up, self.down) if self.count == 8 else ()
 
     def sums(self):
-        return self.added if self.count == 8 else ()
-
-    def add(self, step, outs, *others):
-        rows, columns = self.parts.shape[1:]
-        up = hold(self.up, *others)
-        return call(
-            functools.partial(ring_add_kernel, self.count, step),
-            [shaped((rows, columns), BF16)] * outs,
-            [],
-            [self.parts, up, self.down],
-            [self.me],
-            [pltpu.VMEM((2, rows, columns), BF16)] + [pltpu.VMEM((rows, columns), BF16)] * 2 + [dma(4)],
-        )
+        return tuple(self.added) if self.count == 8 else ()
 
     def finish(self, *others):
         if self.count != 8:
             return lax.psum_scatter(self.parts, "dp", scatter_dimension=0)
-        return self.add(self.count // 2, 1, *others)[0]
+        rows, columns = self.parts.shape[1:]
+        return call(
+            functools.partial(ring_total_kernel, self.count),
+            [shaped((rows, columns), BF16)],
+            [],
+            [self.parts, *self.before, hold(self.up, *others), self.down],
+            [self.me],
+            [pltpu.VMEM((rows, columns), BF16)] * 3 + [dma(5)],
+        )[0]
 
 
 def swap(values, bit):
@@ -213,6 +239,22 @@
     far = swap(piece, 2)
     near = swap(piece, 1)
     return [piece, near, far, swap(far, 1)]
+
+
+def far_kernel(far_ref, near_ref, out_ref, near, sems):
+    finish(start_all([pltpu.make_async_copy(near_ref.at[far_ref.shape[0] :, :], near, sems.at[0])]))
+    out_ref[...] = (far_ref[...] + near[...].astype(F32)).astype(BF16)
+
+
+def add_far(far, near):
+    return call(
+        far_kernel,
+        [shaped(far.shape, BF16)],
+        [far],
+        [near],
+        (),
+        [pltpu.VMEM(far.shape, BF16), dma(1)],
+    )[0]
 
 
 def exchange_sp(sends):
@@ -291,11 +333,15 @@
     )[0]
 
 
+def padded(bucket_ref):
+    return jnp.concatenate([jnp.full((1, BLOCK), -1, jnp.int32), bucket_ref[...]], axis=1)
+
+
 def bias_kernel(table_ref, bucket_ref, seg_ref, me_ref, bias_ref, mask_ref):
     heads, diagonals = bias_ref.shape[:2]
-    wide = bucket_ref.shape[1]
-    bucket = lax.broadcasted_iota(jnp.int32, (table_ref.shape[1], wide), 0)
-    chosen = (bucket == bucket_ref[...]).astype(F32)
+    buckets = padded(bucket_ref)
+    bucket = lax.broadcasted_iota(jnp.int32, (table_ref.shape[1], buckets.shape[1]), 0)
+    chosen = (bucket == buckets).astype(F32)
     rows = exact_dot(table_ref[...], chosen)
     row = lax.broadcasted_iota(jnp.int32, rows.shape, 0)
     for head in range(heads):
@@ -420,10 +466,20 @@
         send[:, columns] = total[step * tok : (step + 1) * tok].astype(BF16)
 
 
+def store_pairs(total, own_ref, far_ref, send_ref, columns):
+    tok = own_ref.shape[0]
+    own_ref[:, columns] = total[:tok]
+    far_ref[:, columns] = total[2 * tok : 3 * tok].astype(far_ref.dtype)
+    send_ref[:tok, columns] = total[tok : 2 * tok].astype(BF16)
+    send_ref[tok:, columns] = total[3 * tok :].astype(BF16)
+
+
 def feed_kernel(parts, count, *refs):
     up_from, act_refs, pieces, me_ref = refs[0], refs[1:5], refs[5 : 5 + count], refs[5 + count]
-    fed_ref, grad_ref, own_ref, *send_refs = refs[6 + count : 12 + count]
-    act, up_ref, weight, down, slope, hidden, act_sems, up_sems, sems, down_sems = refs[12 + count :]
+    grad_ref, up_first, down_first, own_ref, *send_refs, own_out_ref, far_out_ref, send_out_ref = refs[
+        6 + count : 16 + count
+    ]
+    act, up_ref, weight, down, slope, hidden, fed_ref, act_sems, up_sems, sems, down_sems = refs[16 + count :]
     width = weight.shape[1]
     copies = load(pieces, me_ref, parts, weight, sems, slice(0, width)) + load_rows(act_refs, act, act_sems)
     late = load(pieces, me_ref, parts, down, down_sems, slice(width, None))
@@ -445,6 +501,9 @@
     for start in range(0, weight.shape[0], 2 * BLOCK):
         rows = slice(start, start + 2 * BLOCK)
         store_shares(dot(hidden[...], weight[rows, :], 1, 1), own_ref, send_refs, rows)
+    for start in range(0, down.shape[1], 2 * BLOCK):
+        columns = slice(start, start + 2 * BLOCK)
+        store_pairs(dot(fed_ref[...], down[:, columns]), own_out_ref, far_out_ref, send_out_ref, columns)
     rows_here = grad_ref.shape[1]
     for at, (left, right) in enumerate([(act, hidden), (fed_ref, up_ref)]):
         lanes = slice(at * width, (at + 1) * width)
@@ -452,26 +511,8 @@
             block = dot(left[:, start : start + 2 * BLOCK], right[...], 0, 0).astype(BF16)
             for sub in range(2 * BLOCK // rows_here):
                 grad_ref[start // rows_here + sub, :, lanes] = block[sub * rows_here : (sub + 1) * rows_here]
-
-
-def feed_out_kernel(parts, count, *refs):
-    fed_ref, pieces, me_ref = refs[0], refs[1 : 1 + count], refs[1 + count]
-    own_ref, *send_refs, down, sems = refs[2 + count :]
-    width = down.shape[1]
-    finish(load(pieces, me_ref, parts, down, sems, slice(width, None)))
-    for start in range(0, width, 2 * BLOCK):
-        columns = slice(start, start + 2 * BLOCK)
-        store_shares(dot(fed_ref[...], down[:, columns]), own_ref, send_refs, columns)
-
-
-def out_kernel(own_ref, resid_ref, *refs):
-    sent, out_ref, rest, sems = refs[:3], refs[3], refs[4], refs[5]
-    finish(load_rows(sent, rest, sems))
-    tok = own_ref.shape[0]
-    total = resid_ref[...] + own_ref[...]
-    for step in range(3):
-        total += rest[step * tok : (step + 1) * tok, :].astype(F32)
-    out_ref[...] = total.astype(BF16)
+    if parts == 8:
+        store_first(grad_ref, me_ref, up_first, down_first)
 
 
 def branch_back_kernel(*refs):
@@ -506,12 +547,13 @@
 
 def attend_back_kernel(scale, dp_count, count, *refs):
     qkv_ref, log_ref, bias_ref, mask_ref, act_ref, normed_ref, sums_ref, bucket_ref = refs[:8]
-    attn_refs, grad_refs, pieces, me_ref = refs[8:12], refs[12:16], refs[16 : 16 + count], refs[16 + count]
-    last_ref, small_ref, own_ref, *send_refs = refs[17 + count : 23 + count]
+    far_out_ref, send_out_ref, attn_refs, grad_refs = refs[8], refs[9], refs[10:14], refs[14:18]
+    pieces, me_ref = refs[18 : 18 + count], refs[18 + count]
+    last_ref, up_first, down_first, small_ref, own_ref, far_ref, send_ref = refs[19 + count : 26 + count]
     grads, branch, attn, grad_qkv, key_acc, value_acc, diagonal_acc, stacked, shares, weight_ref = refs[
-        23 + count : 33 + count
+        26 + count : 36 + count
     ]
-    grad_sems, branch_sems, attn_sems, sems = refs[33 + count :]
+    grad_sems, branch_sems, attn_sems, sems, out_sems = refs[36 + count :]
     seq_len = qkv_ref.shape[0]
     columns = qkv_ref.shape[1] // 3
     heads, diagonals = bias_ref.shape[:2]
@@ -520,6 +562,13 @@
     late = load_rows(grad_refs, branch, branch_sems, me_ref, lanes=slice(columns, 2 * columns))
     late += load_rows(attn_refs, attn, attn_sems)
     late += load(pieces, me_ref, dp_count, weight_ref, sems, slice(0, 3 * columns))
+    late += start_all(
+        [
+            pltpu.make_async_copy(far_out_ref, far_ref.at[tok:, :], out_sems.at[0]),
+            pltpu.make_async_copy(send_out_ref.at[:tok, :], send_ref.at[tok : 2 * tok, :], out_sems.at[1]),
+            pltpu.make_async_copy(send_out_ref.at[tok:, :], send_ref.at[3 * tok :, :], out_sems.at[2]),
+        ]
+    )
     key_acc[...] = jnp.zeros_like(key_acc)
     value_acc[...] = jnp.zeros_like(value_acc)
     diagonal_acc[...] = jnp.zeros_like(diagonal_acc)
@@ -579,9 +628,9 @@
         small_ref[0:1, lanes] = jnp.sum(share_of * normed_ref[:, lanes].astype(F32), axis=0, keepdims=True)
         small_ref[2:3, lanes] = jnp.sum(share_of, axis=0, keepdims=True)
         shares[:, lanes] = share_of
-    for step, target in enumerate([own_ref, *send_refs]):
+    for step, (target, to) in enumerate([(own_ref, 0), (send_ref, 0), (far_ref, 0), (send_ref, 2 * tok)]):
         rows = pl.ds(place(step, tok, me_ref), tok)
-        target[...] = shares[rows, :].astype(target.dtype)
+        target[to : to + tok, :] = shares[rows, :].astype(target.dtype)
     small_ref[1:2, :] = sums_ref[0:1, :]
     small_ref[3:4, :] = sums_ref[1:2, :]
 
@@ -600,8 +649,9 @@
                 head = 2 * pair + side
                 stacked[head : head + 1, at] += jnp.sum(rolled, axis=0, keepdims=True)
     buckets = BLOCK // heads
-    bucket = lax.rem(lax.broadcasted_iota(jnp.int32, (BLOCK, bucket_ref.shape[1]), 0), buckets)
-    chosen = (bucket == bucket_ref[...]).astype(F32)
+    distances = padded(bucket_ref)
+    bucket = lax.rem(lax.broadcasted_iota(jnp.int32, (BLOCK, distances.shape[1]), 0), buckets)
+    chosen = (bucket == distances).astype(F32)
     by_head = exact_dot(stacked[...], chosen, 1, 1)
     row = lax.broadcasted_iota(jnp.int32, by_head.shape, 0)
     column = lax.broadcasted_iota(jnp.int32, by_head.shape, 1)
@@ -618,18 +668,25 @@
             turned = table if part % per == 0 else pltpu.roll(table, BLOCK - part % per * (BLOCK // per), 1)
             turned = jnp.where(me_ref[0] == part // per, turned, 0.0)
             last_ref[part, rows_here : rows_here + 1, 4 * rows_here : 4 * rows_here + BLOCK] = turned.astype(BF16)
-
-
-def norm_back_kernel(own_ref, tokens_ref, resid_ref, gain_ref, *refs):
-    sent, grad_ref, rest, sems = refs[:3], refs[3], refs[4], refs[5]
-    copies = load_rows(sent, rest, sems)
+    if parts == 8:
+        store_first(last_ref, me_ref, up_first, down_first)
+
+
+def ends_kernel(own_ref, tokens_ref, grad_resid_ref, gain_ref, own_out_ref, resid_ref, *refs):
+    near_ref, far_ref, grad_ref, out_ref, near, far, sems = refs
+    copies = start_all(
+        [
+            pltpu.make_async_copy(near_ref.at[: near.shape[0], :], near, sems.at[0]),
+            pltpu.make_async_copy(far_ref, far, sems.at[1]),
+        ]
+    )
     tok = own_ref.shape[0]
     normed, inverse = layer_norm(tokens_ref[...].astype(F32))
     finish(copies)
-    upstream = own_ref[...]
-    for step in range(3):
-        upstream += rest[step * tok : (step + 1) * tok, :].astype(F32)
-    grad_ref[...] = resid_ref[...] + norm_back(upstream, normed, inverse, gain_ref[0:1, :])
+    upstream = own_ref[...] + near[:tok, :].astype(F32) + far[:tok, :].astype(F32)
+    grad_ref[...] = grad_resid_ref[...] + norm_back(upstream, normed, inverse, gain_ref[0:1, :])
+    total = resid_ref[...] + own_out_ref[...] + near[tok:, :].astype(F32) + far[tok:, :].astype(F32)
+    out_ref[...] = total.astype(BF16)
 
 
 def wide_feed_kernel(*refs):
@@ -729,7 +786,7 @@
     tokens = inputs[0]
     first_ring.step()
 
-    buckets = jnp.pad(bucket_index, (BLOCK, 0), constant_values=-1)[None]
+    buckets = bucket_index[None]
     bias, mask = call(
         bias_kernel,
         [shaped((heads, diagonals, BLOCK, BLOCK), F32), shaped((diagonals, seq_len, BLOCK), F32)],
@@ -738,7 +795,7 @@
         [me],
         micros=1.2,
     )
-    both = jnp.concatenate([hold(tokens, bias), cotangent[0]], axis=0)
+    both = jnp.concatenate([hold(tokens, first_part), cotangent[0]], axis=0)
     token_far, token_near = swap(both, 2), swap(both, 1)
     first_ring.step(bias, rest_part)
     token_last = swap(token_far, 1)
@@ -802,9 +859,11 @@
     act_last = swap(act_far, 1)
     rest_ring.step(act_last)
     shares = [shaped((tok, width), F32)] + [shaped((tok, width), BF16)] * 3
-    fed, grad_feed, own_two, *sends = call(
+    pair_shares = [shaped((tok, width), F32), shaped((tok, width), BF16), shaped((2 * tok, width), BF16)]
+    grad_feed, up_first, down_first, own_two, *sends, own_out, far_out, send_out = call(
         functools.partial(feed_kernel, dp_count, count),
-        [shaped((seq_len, ff_part), BF16), shaped((dp_count, rows_here, 2 * width), BF16)] + shares,
+        [shaped((dp_count, rows_here, 2 * width), BF16)] + [shaped((rows_here, 2 * width), BF16)] * 2
+        + shares + pair_shares,
         [],
         in_hbm([up_all, act_two, act_near, act_far, act_last, *rest_ring.pieces]),
         [me],
@@ -815,6 +874,7 @@
             pltpu.VMEM((ff_part, width), BF16),
             pltpu.VMEM((seq_len, ff_part), F32),
             pltpu.VMEM((seq_len, ff_part), BF16),
+            pltpu.VMEM((seq_len, ff_part), BF16),
             dma(4),
             dma(1),
             dma(count),
@@ -824,22 +884,13 @@
     )
 
     sent_two = exchange_sp(sends)
-    feed_grads = ScatterRing(grad_feed, me, dp_count)
+    feed_grads = ScatterRing(grad_feed, (up_first, down_first), me, dp_count)
     feed_grads.step()
     feed_grads.step(*sent_two)
-    own_out, *out_sends = call(
-        functools.partial(feed_out_kernel, dp_count, count),
-        shares,
-        [fed],
-        in_hbm(rest_ring.pieces),
-        [me],
-        [pltpu.VMEM((ff_part, width), BF16), dma(count)],
-        micros=3,
-    )
     grad_resid, sums_two, *sends = call(
         branch_back_kernel,
         [shaped((tok, width), F32), shaped((8, width), F32)] + [shaped((tok, 2 * part), BF16)] * 4,
-        [hold(own_two, own_out, *feed_grads.sums()), resid, cotangent[0], norm_gain],
+        [hold(own_two, *feed_grads.sums()), resid, cotangent[0], norm_gain],
         [*sent_two, out_columns, out_near, out_far, out_last],
         [me],
         [
@@ -855,11 +906,13 @@
     grad_pieces = [sends[0]] + exchange_sp(sends[1:])
     feed_grads.step(*grad_pieces[1:])
     last_rows = rows_here + SMALL_ROWS if aligned else rows_here
-    last, small, own_one, *sends = call(
+    last, up_first, down_first, small, own_one, far_both, send_both = call(
         functools.partial(attend_back_kernel, scale, dp_count, count),
-        [shaped((dp_count, last_rows, 4 * part), BF16), shaped((8, width), F32)] + shares,
+        [shaped((dp_count, last_rows, 4 * part), BF16)] + [shaped((last_rows, 4 * part), BF16)] * 2
+        + [shaped((8, width), F32)]
+        + [shaped((tok, width), F32), shaped((2 * tok, width), BF16), shaped((4 * tok, width), BF16)],
         [hold(qkv, *feed_grads.sums()), logs, bias, mask, act_one, normed_one, sums_two, buckets],
-        [attn, attn_near, attn_far, attn_last, *grad_pieces, *first_pieces],
+        [far_out, send_out, attn, attn_near, attn_far, attn_last, *grad_pieces, *first_pieces],
         [me],
         [
             pltpu.VMEM((seq_len, part), BF16),
@@ -876,6 +929,7 @@
             dma(4),
             dma(4),
             dma(count),
+            dma(3),
         ],
         micros=9.4,
     )
@@ -887,37 +941,31 @@
         packed = jnp.pad(packed, ((0, 0), (0, 4 * part - packed.shape[1])))
         packed = jnp.pad(packed[:, None], ((0, 0), (0, SMALL_ROWS - 1), (0, 0)))
         last = jnp.concatenate([last, packed], axis=1)
-    last_grads = ScatterRing(last, me, dp_count)
+    last_grads = ScatterRing(last, hold((up_first, down_first), *feed_grads.sent()), me, dp_count)
     last_grads.step()
+    near_both = swap(hold(send_both, *feed_grads.sent()), 1)
     feed_grads.step(small)
-    last_grads.step(*feed_grads.sums())
-    sent_out = exchange_sp([hold(send, small) for send in out_sends])
-    sent_one = exchange_sp([hold(send, *sent_out, *last_grads.sums()) for send in sends])
-    last_grads.step()
-    (grad_input,) = call(
-        norm_back_kernel,
-        [shaped((tok, width), F32)],
-        [hold(own_one, *last_grads.sums()), tokens, grad_resid, norm_gain],
-        sent_one,
+    last_grads.step(*feed_grads.sums(), near_both)
+    sent_both = add_far(hold(far_both, *last_grads.sums()), near_both)
+    last_both = swap(sent_both, 2)
+    sum_feed = feed_grads.finish(sent_both)
+    feed_far, feed_near = swap(sum_feed, 2), swap(sum_feed, 1)
+    last_grads.step(sum_feed)
+    last_grads.step(last_both)
+    sum_last = last_grads.finish()
+    grad_input, output = call(
+        ends_kernel,
+        [shaped((tok, width), F32), shaped((tok, width), BF16)],
+        [hold(own_one, sum_last), tokens, grad_resid, norm_gain, own_out, resid],
+        [near_both, last_both],
         (),
-        [pltpu.VMEM((3 * tok, width), BF16), dma(3)],
-        micros=1.4,
-    )
-
-    sum_feed = feed_grads.finish(grad_input)
-    last_grads.step(grad_input, sum_feed)
-    feed_pieces = gather_sp(hold(sum_feed, *last_grads.sums()))
-    (output,) = call(
-        out_kernel,
-        [shaped((tok, width), BF16)],
-        [hold(own_out, *last_grads.sums()), resid],
-        sent_out,
-        (),
-        [pltpu.VMEM((3 * tok, width), BF16), dma(3)],
-    )
-
-    sum_last = last_grads.finish()
-    last_pieces = gather_sp(sum_last)
+        [pltpu.VMEM((2 * tok, width), BF16)] * 2 + [dma(2)],
+        micros=1.6,
+    )
+
+    feed_last = swap(hold(feed_far, sum_last), 1)
+    feed_pieces = [sum_feed, feed_near, feed_far, feed_last]
+    last_far, last_near = swap(sum_last, 2), swap(sum_last, 1)
     piece = width // dp_count
     table_here = head_total * bucket_count // dp_count
     if aligned:
@@ -925,11 +973,12 @@
             wide_feed_kernel,
             [shaped((rows_here, ff), F32), shaped((sp_count * ff_rows, width), F32)],
             [],
-            feed_pieces,
+            [hold(feed_pieces[0], sum_last)] + feed_pieces[1:],
             [me],
             [pltpu.VMEM((sp_count * rows_here, 2 * width), BF16), dma(4)],
         micros=3,
     )
+        last_pieces = [sum_last, last_near, last_far, swap(hold(last_far, out_in, grad_input), 1)]
         out_qkv, out_out, gains, shifts, tables = call(
             wide_last_kernel,
             [
@@ -951,7 +1000,7 @@
         out_down = all_feed[:, :, width:].reshape(sp_count * ff_rows, width)
         all_in = all_feed[:, :, :width].reshape(sp_count, rows_here, dp_count, ff_rows)
         out_in = jnp.moveaxis(all_in, 0, 2).reshape(rows_here, ff)
-        all_last = stacked_sp(last_pieces).astype(F32)
+        all_last = stacked_sp([sum_last, last_near, last_far, swap(last_far, 1)]).astype(F32)
         all_qkv = all_last[:, :rows_here, : 3 * part].reshape(sp_count, rows_here, 3, part)
         out_qkv = jnp.moveaxis(all_qkv, 0, 2).reshape(rows_here, 3 * width)
         out_out = jnp.moveaxis(all_last[:, :rows_here, 3 * part :], 0, 1).reshape(rows_here, width)

time: 211 us -> 198 us (0.938)
  Pallas kernels: 56 us -> 51 us
  local copies, waits for them, and re-layouts: 4.2 us -> 0.72 us
  starting transfers between devices: 50.9 us -> 48.6 us
    ppermute x30 -> x26, waiting for transfers between devices: 52.7 us -> 44.4 us  [swap(): return lax.ppermute(values, 'sp', [(i, i ^ bit) for i in range(count)])]
    ppermute x16, waiting for transfers between devices: 8.42 us -> 14.7 us  [step(): self.down = lax.ppermute(down, 'dp', backward)]
    pallas_call x25 -> x24, Pallas kernels: 56 us -> 51 us  [call(): pl.pallas_call(kernel, out_shape=(*outs, *hbm_outs), in_specs=specs, out_...]
    unnamed x110 -> x42, local copies, waits for them, and re-layouts: 3.42 us -> 0.72 us
    ppermute x16, starting transfers between devices: 15.9 us -> 13.8 us  [step(): self.down = lax.ppermute(down, 'dp', backward)]
    ppermute x30 -> x26, starting transfers between devices: 16.7 us -> 14.7 us  [swap(): return lax.ppermute(values, 'sp', [(i, i ^ bit) for i in range(count)])]
  transfers between devices with their start and end apart: 62 -> 58, of which waited for: 34 -> 40; matrix products, arithmetic and copies ran while one was open for 1% -> 1% of each run, Pallas kernels for 18% -> 17%
where the time goes in v4:
time: 198 us; the launch traced here: 197 us
  waiting for transfers between devices  94.6 us (48%)
  Pallas kernels  51 us (26%)
  starting transfers between devices  48.6 us (25%)
    pallas_call x24, Pallas kernels, call(): pl.pallas_call(kernel, out_shape=(*outs, *hbm_outs), in_specs=specs, out_...  51 us
    ppermute x26, waiting for transfers between devices, swap(): return lax.ppermute(values, 'sp', [(i, i ^ bit) for i in range(count)])  44.4 us
    ppermute x16, waiting for transfers between devices, step(): self.up = lax.ppermute(up, 'dp', forward)  35.4 us
    ppermute x16, starting transfers between devices, step(): self.up = lax.ppermute(up, 'dp', forward)  20.1 us
    ppermute x16, waiting for transfers between devices, step(): self.down = lax.ppermute(down, 'dp', backward)  14.7 us
    ppermute x26, starting transfers between devices, swap(): return lax.ppermute(values, 'sp', [(i, i ^ bit) for i in range(count)])  14.7 us
    ppermute x16, starting transfers between devices, step(): self.down = lax.ppermute(down, 'dp', backward)  13.8 us
  transfers between devices with their start and end apart: 58, of which 40 were waited for; matrix products, arithmetic and copies ran while one was open for 1% of the time, Pallas kernels for 17%

profile of v4, /device:TPU:0, one launch (start us, length us, event | category | flops | bytes accessed | tf_op | source)
XLA Modules:
  0.0 197.4 jit_solution(8179163768079807998)
XLA Ops:
  0.7 1.5 shard_map.178.refs_0_.refs_3_.refs_18_
  2.3 3.1 %collective-permute-start = (bf16[128,1024]{1,0:T(8,128)(2,1)S(1)}, bf16[128,1024]{1,0:T(8,128)(2,1)S(1)}, u32[]{:S(2)}, u32[]{:S(2)}) collective-permute-start(bf16[128,1024]{1,0:T(8,128)(2,1)S(1)} %shard_map.178.refs_0_.refs_3_.refs_18_), channel_id=1, source_target_pairs={{0,8},{8,16},{16,24},{24,28},{28,20},{20,12},{12,4},{4,0},{1,9},{9... | collective-permute-start | bytes 786440 | tf_op jit(solution)/shard_map/ppermute | solution.py:128
  5.4 1.1 pad_maximum_fusion.refs_2_
  6.4 2.0 %collective-permute-start.5 = (bf16[256,1024]{1,0:T(8,128)(2,1)S(1)}, bf16[256,1024]{1,0:T(8,128)(2,1)S(1)}, u32[]{:S(2)}, u32[]{:S(2)}) collective-permute-start(bf16[256,1024]{1,0:T(8,128)(2,1)S(1)} %pad_maximum_fusion.refs_2_), channel_id=1, source_target_pairs={{0,2},{1,3},{2,0},{3,1},{4,6},{5,7},{6,4},{7,5},{8,10},{9,11},{10,... | collective-permute-start | bytes 1572872 | tf_op jit(solution)/shard_map/ppermute | solution.py:235
  8.4 1.7 shard_map.180.refs_5_
  10.2 1.2 shard_map.179
  11.6 1.5 collective-permute-done.1.refs_2_.refs_5_.refs_20_
  13.1 1.6 collective-permute-start.2
  15.2 4.7 %collective-permute-done.5.refs_4_ = bf16[256,1024]{1,0:T(8,128)(2,1)S(1)} collective-permute-done((bf16[256,1024]{1,0:T(8,128)(2,1)S(1)}, bf16[256,1024]{1,0:T(8,128)(2,1)S(1)}, u32[]{:S(2)}, u32[]{:S(2)}) %collective-permute-start.5) | collective-permute-done | bytes 524320 | tf_op jit(solution)/shard_map/ppermute | solution.py:235
  20.0 1.3 collective-permute-done.3.refs_4_.refs_7_.refs_22_
  21.3 1.6 collective-permute-start.7
  23.3 4.3 %collective-permute-done.7.up_ref.refs_5_.refs_8_.refs_23_ = bf16[128,1024]{1,0:T(8,128)(2,1)S(1)} collective-permute-done((bf16[128,1024]{1,0:T(8,128)(2,1)S(1)}, bf16[128,1024]{1,0:T(8,128)(2,1)S(1)}, u32[]{:S(2)}, u32[]{:S(2)}) %collective-permute-start.7) | collective-permute-done | bytes 262176 | tf_op jit(solution)/shard_map/ppermute | solution.py:128
  27.7 1.6 collective-permute-done.8.down_ref.refs_6_.refs_9_.refs_24_
  29.6 1.6 collective-permute-start.9
  31.6 2.9 %collective-permute-done.9.refs_7_.refs_10_.refs_25_ = bf16[64,1024]{1,0:T(8,128)(2,1)S(1)} collective-permute-done((bf16[64,1024]{1,0:T(8,128)(2,1)S(1)}, bf16[64,1024]{1,0:T(8,128)(2,1)S(1)}, u32[]{:S(2)}, u32[]{:S(2)}) %collective-permute-start.9) | collective-permute-done | bytes 131104 | tf_op jit(solution)/shard_map/ppermute | solution.py:128
  34.6 1.6 collective-permute-done.10.refs_8_.refs_11_.refs_26_
  36.8 1.4 collective-permute-start.12
  39.0 1.6 collective-permute-start.17
  40.6 1.5 shard_map.181
  42.1 4.8 %shard_map.184 = (bf16[512,768]{1,0:T(8,128)(2,1)S(1)}, bf16[512,256]{1,0:T(8,128)(2,1)S(1)}, f32[8,256]{1,0:T(8,128)S(1)}) custom-call(bf16[512,1024]{1,0:T(8,128)(2,1)S(1)} %get-tuple-element.117.refs_0_.refs_4_, f32[4,4,128,128]{3,2,1,0:T(8,128)S(1)} %get-tuple-element.106.refs_1_.refs_2_, f32[4,512,128]{2,1,0:T(8,128)S(1)} %get-tuple-element.118.refs_2_.refs_3_, ...), custom_call_target="tpu_custom_call" | custom-call | bytes 16500000 | tf_op jit(solution)/shard_map/pallas_call | solution.py:60
  47.3 1.5 collective-permute-start.14
  50.9 4.9 %collective-permute-done.14.refs_5_.refs_12_ = bf16[512,256]{1,0:T(8,128)(2,1)S(1)} collective-permute-done((bf16[512,256]{1,0:T(8,128)(2,1)S(1)}, bf16[512,256]{1,0:T(8,128)(2,1)S(1)}, u32[]{:S(2)}, u32[]{:S(2)}) %collective-permute-start.14) | collective-permute-done | bytes 262176 | tf_op jit(solution)/shard_map/ppermute | solution.py:235
  55.8 1.5 collective-permute-done.15.refs_6_.refs_13_
  57.3 1.6 shard_map.185
  59.0 4.2 %collective-permute-done.19.refs_8_ = bf16[128,2048]{1,0:T(8,128)(2,1)S(1)} collective-permute-done((bf16[128,2048]{1,0:T(8,128)(2,1)S(1)}, bf16[128,2048]{1,0:T(8,128)(2,1)S(1)}, u32[]{:S(2)}, u32[]{:S(2)}) %collective-permute-start.19) | collective-permute-done | bytes 524320 | tf_op jit(solution)/shard_map/ppermute | solution.py:128
  64.8 1.1 collective-permute-start.25
  65.9 1.5 collective-permute-start.22
  67.4 5.6 %collective-permute-done.22.refs_3_ = bf16[128,1024]{1,0:T(8,128)(2,1)S(1)} collective-permute-done((bf16[128,1024]{1,0:T(8,128)(2,1)S(1)}, bf16[128,1024]{1,0:T(8,128)(2,1)S(1)}, u32[]{:S(2)}, u32[]{:S(2)}) %collective-permute-start.22) | collective-permute-done | bytes 262176 | tf_op jit(solution)/shard_map/ppermute | solution.py:235
  73.5 3.6 %collective-permute-done.24.up_ref.refs_10_ = bf16[128,2048]{1,0:T(8,128)(2,1)S(1)} collective-permute-done((bf16[128,2048]{1,0:T(8,128)(2,1)S(1)}, bf16[128,2048]{1,0:T(8,128)(2,1)S(1)}, u32[]{:S(2)}, u32[]{:S(2)}) %collective-permute-start.24) | collective-permute-done | bytes 524320 | tf_op jit(solution)/shard_map/ppermute | solution.py:128
  78.9 1.1 collective-permute-start.27
  80.0 4.4 %collective-permute-done.26.refs_12_ = bf16[64,2048]{1,0:T(8,128)(2,1)S(1)} collective-permute-done((bf16[64,2048]{1,0:T(8,128)(2,1)S(1)}, bf16[64,2048]{1,0:T(8,128)(2,1)S(1)}, u32[]{:S(2)}, u32[]{:S(2)}) %collective-permute-start.26) | collective-permute-done | bytes 262176 | tf_op jit(solution)/shard_map/ppermute | solution.py:128
  86.0 11.1 %shard_map.187 = (bf16[8,128,2048]{2,1,0:T(8,128)(2,1)S(1)}, bf16[128,2048]{1,0:T(8,128)(2,1)S(1)}, bf16[128,2048]{1,0:T(8,128)(2,1)S(1)}, f32[128,1024]{1,0:T(8...) custom-call(bf16[512,1024]{1,0:T(8,128)(2,1)} %copy-done.4, ...), custom_call_target="tpu_custom_call" | custom-call | bytes 29700000 | tf_op jit(solution)/shard_map/pallas_call | solution.py:60
  97.8 1.4 collective-permute-start.32
  99.2 1.6 collective-permute-start.30
  101.1 7.2 %collective-permute-done.30.refs_5_ = bf16[128,1024]{1,0:T(8,128)(2,1)S(1)} collective-permute-done((bf16[128,1024]{1,0:T(8,128)(2,1)S(1)}, bf16[128,1024]{1,0:T(8,128)(2,1)S(1)}, u32[]{:S(2)}, u32[]{:S(2)}) %collective-permute-start.30) | collective-permute-done | bytes 262176 | tf_op jit(solution)/shard_map/ppermute | solution.py:235
  108.3 4.8 %collective-permute-done.31.refs_6_ = bf16[128,1024]{1,0:T(8,128)(2,1)S(1)} collective-permute-done((bf16[128,1024]{1,0:T(8,128)(2,1)S(1)}, bf16[128,1024]{1,0:T(8,128)(2,1)S(1)}, u32[]{:S(2)}, u32[]{:S(2)}) %collective-permute-start.31) | collective-permute-done | bytes 262176 | tf_op jit(solution)/shard_map/ppermute | solution.py:235
  114.9 1.4 collective-permute-start.37
  116.3 2.5 %shard_map.189 = (f32[128,1024]{1,0:T(8,128)S(1)}, f32[8,1024]{1,0:T(8,128)S(1)}, bf16[128,512]{1,0:T(8,128)(2,1)S(1)}, bf16[128,512]{1,0:T(8,128)(2,1)S(1)}, bf...) custom-call(f32[128,1024]{1,0:T(8,128)S(1)} %get-tuple-element.145.refs_0_, ...), custom_call_target="tpu_custom_call" | custom-call | bytes 8250000 | tf_op jit(solution)/shard_map/pallas_call | solution.py:60
  118.9 1.7 collective-permute-start.35
  120.7 4.5 %collective-permute-done.35.refs_16_ = bf16[128,512]{1,0:T(8,128)(2,1)S(1)} collective-permute-done((bf16[128,512]{1,0:T(8,128)(2,1)S(1)}, bf16[128,512]{1,0:T(8,128)(2,1)S(1)}, u32[]{:S(2)}, u32[]{:S(2)}) %collective-permute-start.35) | collective-permute-done | bytes 131104 | tf_op jit(solution)/shard_map/ppermute | solution.py:235
  125.2 1.9 collective-permute-done.36.refs_17_
  127.1 1.2 collective-permute-done.33.refs_1_
  130.3 1.5 collective-permute-start.39
  131.8 9.4 %shard_map.191 = (bf16[8,144,1024]{2,1,0:T(8,128)(2,1)S(1)}, bf16[144,1024]{1,0:T(8,128)(2,1)S(1)}, bf16[144,1024]{1,0:T(8,128)(2,1)S(1)}, f32[8,1024]{1,0:T(8,1...) custom-call(bf16[512,768]{1,0:T(8,128)(2,1)S(1)} %get-tuple-element.153.refs_0_, ...), custom_call_target="tpu_custom_call" | custom-call | bytes 31020000 | tf_op jit(solution)/shard_map/pallas_call | solution.py:60
  141.2 1.5 collective-permute-done.38.refs_1_.up_ref
  143.8 1.2 collective-permute-start.42
  146.7 1.2 collective-permute-start.45
  147.9 4.9 %collective-permute-done.40.refs_1_ = bf16[144,1024]{1,0:T(8,128)(2,1)S(1)} collective-permute-done((bf16[144,1024]{1,0:T(8,128)(2,1)S(1)}, bf16[144,1024]{1,0:T(8,128)(2,1)S(1)}, u32[]{:S(2)}, u32[]{:S(2)}) %collective-permute-start.40) | collective-permute-done | bytes 294944 | tf_op jit(solution)/shard_map/ppermute | solution.py:210
  154.6 1.6 collective-permute-start.43
  156.9 1.4 collective-permute-start.49
  160.2 1.4 collective-permute-start.55
  161.6 2.7 %collective-permute-done.43.refs_1_ = bf16[144,1024]{1,0:T(8,128)(2,1)S(1)} collective-permute-done((bf16[144,1024]{1,0:T(8,128)(2,1)S(1)}, bf16[144,1024]{1,0:T(8,128)(2,1)S(1)}, u32[]{:S(2)}, u32[]{:S(2)}) %collective-permute-start.43) | collective-permute-done | bytes 294944 | tf_op jit(solution)/shard_map/ppermute | solution.py:210
  165.9 1.6 collective-permute-start.47
  167.9 3.9 %collective-permute-done.49.refs_1_ = bf16[256,1024]{1,0:T(8,128)(2,1)S(1)} collective-permute-done((bf16[256,1024]{1,0:T(8,128)(2,1)S(1)}, bf16[256,1024]{1,0:T(8,128)(2,1)S(1)}, u32[]{:S(2)}, u32[]{:S(2)}) %collective-permute-start.49) | collective-permute-done | bytes 524320 | tf_op jit(solution)/shard_map/ppermute | solution.py:235
  171.8 2.2 %collective-permute-done.47.refs_1_.up_ref = bf16[144,1024]{1,0:T(8,128)(2,1)S(1)} collective-permute-done((bf16[144,1024]{1,0:T(8,128)(2,1)S(1)}, bf16[144,1024]{1,0:T(8,128)(2,1)S(1)}, u32[]{:S(2)}, u32[]{:S(2)}) %collective-permute-start.47) | collective-permute-done | bytes 294944 | tf_op jit(solution)/shard_map/ppermute | solution.py:210
  174.0 1.3 collective-permute-done.48.refs_2_.down_ref
  176.1 1.8 collective-permute-start.50
  178.2 3.1 %collective-permute-done.50.last_up_ref = bf16[144,512]{1,0:T(8,128)(2,1)S(1)} collective-permute-done((bf16[144,512]{1,0:T(8,128)(2,1)S(1)}, bf16[144,512]{1,0:T(8,128)(2,1)S(1)}, u32[]{:S(2)}, u32[]{:S(2)}) %collective-permute-start.50) | collective-permute-done | bytes 147488 | tf_op jit(solution)/shard_map/ppermute | solution.py:210
  181.3 1.7 collective-permute-done.51.last_down_ref
  184.9 1.5 shard_map.199
  186.5 3.1 %shard_map.200 = (f32[128,4096]{1,0:T(8,128)}, f32[512,1024]{1,0:T(8,128)}) custom-call(bf16[128,2048]{1,0:T(8,128)(2,1)S(1)} %shard_map.195.refs_0_, bf16[128,2048]{1,0:T(8,128)(2,1)S(1)} %collective-permute-done.54.refs_1_, bf16[128,2048]{1,0:T(8,128)(2,1)S(1)} %collective-permute-done.55.refs_2_, bf16[128,2048]{1,0:T(8,128)(2,1)S(1)} %collective-permute-done.56.refs_3_, ...), custom_call_target="tpu_custom_call" | custom-call | bytes 9900000 | tf_op jit(solution)/shard_map/pallas_call | solution.py:60
  189.6 3.8 %collective-permute-done.53.refs_2_ = bf16[144,1024]{1,0:T(8,128)(2,1)S(1)} collective-permute-done((bf16[144,1024]{1,0:T(8,128)(2,1)S(1)}, bf16[144,1024]{1,0:T(8,128)(2,1)S(1)}, u32[]{:S(2)}, u32[]{:S(2)}) %collective-permute-start.53) | collective-permute-done | bytes 294944 | tf_op jit(solution)/shard_map/ppermute | solution.py:235
  193.4 1.6 collective-permute-done.57.refs_3_
  195.0 2.3 %shard_map.201 = (f32[128,3072]{1,0:T(8,128)}, f32[128,1024]{1,0:T(8,128)}, f32[2,128]{1,0:T(2,128)}, f32[2,128]{1,0:T(2,128)}, f32[1,64]{1,0:T(1,128)}) custom-call(bf16[144,1024]{1,0:T(8,128)(2,1)S(1)} %shard_map.198.refs_0_, bf16[144,1024]{1,0:T(8,128)(2,1)S(1)} %collective-permute-done.52.refs_1_, bf16[144,1024]{1,0:T(8,128)(2,1)S(1)} %collective-permute-done.53.refs_2_, ...), custom_call_target="tpu_custom_call" | custom-call | bytes 7589999 | tf_op jit(solution)/shard_map/pallas_call | solution.py:60
  (120 shorter events, 28.5 us)
Async XLA Ops:
  2.3 9.3 %collective-permute-start = (bf16[128,1024]{1,0:T(8,128)(2,1)S(1)}, bf16[128,1024]{1,0:T(8,128)(2,1)S(1)}, u32[]{:S(2)}, u32[]{:S(2)}) collective-permute-start(bf16[128,1024]{1,0:T(8,128)(2,1)S(1)} %shard_map.178.refs_0_.refs_3_.refs_18_), channel_id=1, source_target_pairs={{0,8},{8,16},{16,24},{24,28},{28,20},{20,12},{12,4},{4,0},{1,9},{9... | collective-permute-start | bytes 786440 | tf_op jit(solution)/shard_map/ppermute | solution.py:128
  5.4 7.8 %collective-permute-start.1 = (bf16[128,1024]{1,0:T(8,128)(2,1)S(1)}, bf16[128,1024]{1,0:T(8,128)(2,1)S(1)}, u32[]{:S(2)}, u32[]{:S(2)}) collective-permute-start(bf16[128,1024]{1,0:T(8,128)(2,1)S(1)} %shard_map.178.refs_0_.refs_3_.refs_18_), channel_id=1, source_target_pairs={{8,0},{16,8},{24,16},{28,24},{20,28},{12,20},{4,12},{0,4},{9,1},{1... | collective-permute-start | bytes 786440 | tf_op jit(solution)/shard_map/ppermute | solution.py:129
  6.4 13.4 %collective-permute-start.5 = (bf16[256,1024]{1,0:T(8,128)(2,1)S(1)}, bf16[256,1024]{1,0:T(8,128)(2,1)S(1)}, u32[]{:S(2)}, u32[]{:S(2)}) collective-permute-start(bf16[256,1024]{1,0:T(8,128)(2,1)S(1)} %pad_maximum_fusion.refs_2_), channel_id=1, source_target_pairs={{0,2},{1,3},{2,0},{3,1},{4,6},{5,7},{6,4},{7,5},{8,10},{9,11},{10,... | collective-permute-start | bytes 1572872 | tf_op jit(solution)/shard_map/ppermute | solution.py:235
  10.2 31.9 %copy-start.3 = (bf16[128,2048]{1,0:T(8,128)(2,1)}, bf16[128,2048]{1,0:T(8,128)(2,1)S(1)}, u32[]{:S(2)}) copy-start(bf16[128,2048]{1,0:T(8,128)(2,1)S(1)} %shard_map.180.refs_5_) | copy-start | bytes 1572868
  10.2 30.3 %copy-start.7 = (f32[2,1024]{1,0:T(2,128)S(1)}, f32[2,1024]{1,0:T(2,128)}, u32[]{:S(2)}) copy-start(f32[2,1024]{1,0:T(2,128)} %gain_ref.1) | copy-start | bytes 24580
  10.2 30.3 %copy-start.8 = (f32[2,1024]{1,0:T(2,128)S(1)}, f32[2,1024]{1,0:T(2,128)}, u32[]{:S(2)}) copy-start(f32[2,1024]{1,0:T(2,128)} %refs_2_.1) | copy-start | bytes 24580
  13.1 6.9 %collective-permute-start.2 = (bf16[128,1024]{1,0:T(8,128)(2,1)S(1)}, bf16[128,1024]{1,0:T(8,128)(2,1)S(1)}, u32[]{:S(2)}, u32[]{:S(2)}) collective-permute-start(bf16[128,1024]{1,0:T(8,128)(2,1)S(1)} %collective-permute-done.refs_1_.refs_4_.refs_19_), channel_id=1, source_target_pairs={{0,8},{8,16},{16,24},{24,28},{28,20},{20,12},{12,4},{4,0},{1,9},{9... | collective-permute-start | bytes 786440 | tf_op jit(solution)/shard_map/ppermute | solution.py:128
  14.7 6.6 %collective-permute-start.3 = (bf16[128,1024]{1,0:T(8,128)(2,1)S(1)}, bf16[128,1024]{1,0:T(8,128)(2,1)S(1)}, u32[]{:S(2)}, u32[]{:S(2)}) collective-permute-start(bf16[128,1024]{1,0:T(8,128)(2,1)S(1)} %collective-permute-done.1.refs_2_.refs_5_.refs_20_), channel_id=1, source_target_pairs={{8,0},{16,8},{24,16},{28,24},{20,28},{12,20},{4,12},{0,4},{9,1},{1... | collective-permute-start | bytes 786440 | tf_op jit(solution)/shard_map/ppermute | solution.py:129
  21.3 6.4 %collective-permute-start.7 = (bf16[128,1024]{1,0:T(8,128)(2,1)S(1)}, bf16[128,1024]{1,0:T(8,128)(2,1)S(1)}, u32[]{:S(2)}, u32[]{:S(2)}) collective-permute-start(bf16[128,1024]{1,0:T(8,128)(2,1)S(1)} %collective-permute-done.2.refs_3_.refs_6_.refs_21_), channel_id=1, source_target_pairs={{0,8},{8,16},{16,24},{24,28},{28,20},{20,12},{12,4},{4,0},{1,9},{9... | collective-permute-start | bytes 786440 | tf_op jit(solution)/shard_map/ppermute | solution.py:128
  22.9 6.4 %collective-permute-start.8 = (bf16[128,1024]{1,0:T(8,128)(2,1)S(1)}, bf16[128,1024]{1,0:T(8,128)(2,1)S(1)}, u32[]{:S(2)}, u32[]{:S(2)}) collective-permute-start(bf16[128,1024]{1,0:T(8,128)(2,1)S(1)} %collective-permute-done.3.refs_4_.refs_7_.refs_22_), channel_id=1, source_target_pairs={{8,0},{16,8},{24,16},{28,24},{20,28},{12,20},{4,12},{0,4},{9,1},{1... | collective-permute-start | bytes 786440 | tf_op jit(solution)/shard_map/ppermute | solution.py:129
  23.3 17.2 %collective-permute-start.4 = (bf16[256,1024]{1,0:T(8,128)(2,1)S(1)}, bf16[256,1024]{1,0:T(8,128)(2,1)S(1)}, u32[]{:S(2)}, u32[]{:S(2)}) collective-permute-start(bf16[256,1024]{1,0:T(8,128)(2,1)S(1)} %pad_maximum_fusion.refs_2_), channel_id=1, source_target_pairs={{0,1},{1,0},{2,3},{3,2},{4,5},{5,4},{6,7},{7,6},{8,9},{9,8},{10,11... | collective-permute-start | bytes 1572872 | tf_op jit(solution)/shard_map/ppermute | solution.py:235
  29.6 5.0 %collective-permute-start.9 = (bf16[64,1024]{1,0:T(8,128)(2,1)S(1)}, bf16[64,1024]{1,0:T(8,128)(2,1)S(1)}, u32[]{:S(2)}, u32[]{:S(2)}) collective-permute-start(bf16[64,1024]{1,0:T(8,128)(2,1)S(1)} %get-tuple-element.115), channel_id=1, source_target_pairs={{0,8},{8,16},{16,24},{24,28},{28,20},{20,12},{12,4},{4,0},{1,9},{9... | collective-permute-start | bytes 393224 | tf_op jit(solution)/shard_map/ppermute | solution.py:128
  31.1 5.0 %collective-permute-start.10 = (bf16[64,1024]{1,0:T(8,128)(2,1)S(1)}, bf16[64,1024]{1,0:T(8,128)(2,1)S(1)}, u32[]{:S(2)}, u32[]{:S(2)}) collective-permute-start(bf16[64,1024]{1,0:T(8,128)(2,1)S(1)} %get-tuple-element.116), channel_id=1, source_target_pairs={{8,0},{16,8},{24,16},{28,24},{20,28},{12,20},{4,12},{0,4},{9,1},{1... | collective-permute-start | bytes 393224 | tf_op jit(solution)/shard_map/ppermute | solution.py:129
  31.6 8.9 %collective-permute-start.6 = (bf16[256,1024]{1,0:T(8,128)(2,1)S(1)}, bf16[256,1024]{1,0:T(8,128)(2,1)S(1)}, u32[]{:S(2)}, u32[]{:S(2)}) collective-permute-start(bf16[256,1024]{1,0:T(8,128)(2,1)S(1)} %collective-permute-done.5.refs_4_), channel_id=1, source_target_pairs={{0,1},{1,0},{2,3},{3,2},{4,5},{5,4},{6,7},{7,6},{8,9},{9,8},{10,11... | collective-permute-start | bytes 1572872 | tf_op jit(solution)/shard_map/ppermute | solution.py:235
  36.2 10.8 %collective-permute-start.11 = (bf16[128,2048]{1,0:T(8,128)(2,1)S(1)}, bf16[128,2048]{1,0:T(8,128)(2,1)S(1)}, u32[]{:S(2)}, u32[]{:S(2)}) collective-permute-start(bf16[128,2048]{1,0:T(8,128)(2,1)S(1)} %shard_map.180.refs_5_), channel_id=1, source_target_pairs={{0,8},{8,16},{16,24},{24,28},{28,20},{20,12},{12,4},{4,0},{1,9},{9... | collective-permute-start | bytes 1572872 | tf_op jit(solution)/shard_map/ppermute | solution.py:128
  36.8 10.6 %collective-permute-start.12 = (bf16[128,2048]{1,0:T(8,128)(2,1)S(1)}, bf16[128,2048]{1,0:T(8,128)(2,1)S(1)}, u32[]{:S(2)}, u32[]{:S(2)}) collective-permute-start(bf16[128,2048]{1,0:T(8,128)(2,1)S(1)} %shard_map.180.refs_5_), channel_id=1, source_target_pairs={{8,0},{16,8},{24,16},{28,24},{20,28},{12,20},{4,12},{0,4},{9,1},{1... | collective-permute-start | bytes 1572872 | tf_op jit(solution)/shard_map/ppermute | solution.py:129
  39.0 9.9 %collective-permute-start.17 = (bf16[1024,256]{1,0:T(8,128)(2,1)S(1)}, bf16[1024,256]{1,0:T(8,128)(2,1)S(1)}, u32[]{:S(2)}, u32[]{:S(2)}) collective-permute-start(bf16[1024,256]{1,0:T(8,128)(2,1)S(1)} %shard_map.183.refs_7_), channel_id=1, source_target_pairs={{0,2},{1,3},{2,0},{3,1},{4,6},{5,7},{6,4},{7,5},{8,10},{9,11},{10,... | collective-permute-start | bytes 1572872 | tf_op jit(solution)/shard_map/ppermute | solution.py:235
  40.5 10.3 %collective-permute-start.16 = (bf16[1024,256]{1,0:T(8,128)(2,1)S(1)}, bf16[1024,256]{1,0:T(8,128)(2,1)S(1)}, u32[]{:S(2)}, u32[]{:S(2)}) collective-permute-start(bf16[1024,256]{1,0:T(8,128)(2,1)S(1)} %shard_map.183.refs_7_), channel_id=1, source_target_pairs={{0,1},{1,0},{2,3},{3,2},{4,5},{5,4},{6,7},{7,6},{8,9},{9,8},{10,11... | collective-permute-start | bytes 1572872 | tf_op jit(solution)/shard_map/ppermute | solution.py:235
  46.9 30.9 %copy-start.12 = (bf16[128,2048]{1,0:T(8,128)(2,1)}, bf16[128,2048]{1,0:T(8,128)(2,1)S(1)}, u32[]{:S(2)}) copy-start(bf16[128,2048]{1,0:T(8,128)(2,1)S(1)} %collective-permute-done.11.refs_6_) | copy-start | bytes 1572868
  47.3 30.5 %copy-start.13 = (bf16[128,2048]{1,0:T(8,128)(2,1)}, bf16[128,2048]{1,0:T(8,128)(2,1)S(1)}, u32[]{:S(2)}) copy-start(bf16[128,2048]{1,0:T(8,128)(2,1)S(1)} %collective-permute-done.12.refs_7_) | copy-start | bytes 1572868
  47.3 8.4 %collective-permute-start.14 = (bf16[512,256]{1,0:T(8,128)(2,1)S(1)}, bf16[512,256]{1,0:T(8,128)(2,1)S(1)}, u32[]{:S(2)}, u32[]{:S(2)}) collective-permute-start(bf16[512,256]{1,0:T(8,128)(2,1)S(1)} %get-tuple-element.124.refs_3_.refs_10_), channel_id=1, source_target_pairs={{0,2},{1,3},{2,0},{3,1},{4,6},{5,7},{6,4},{7,5},{8,10},{9,11},{10,... | collective-permute-start | bytes 786440 | tf_op jit(solution)/shard_map/ppermute | solution.py:235
  48.8 8.5 %collective-permute-start.18 = (bf16[1024,256]{1,0:T(8,128)(2,1)S(1)}, bf16[1024,256]{1,0:T(8,128)(2,1)S(1)}, u32[]{:S(2)}, u32[]{:S(2)}) collective-permute-start(bf16[1024,256]{1,0:T(8,128)(2,1)S(1)} %collective-permute-done.17.refs_9_), channel_id=1, source_target_pairs={{0,1},{1,0},{2,3},{3,2},{4,5},{5,4},{6,7},{7,6},{8,9},{9,8},{10,11... | collective-permute-start | bytes 1572872 | tf_op jit(solution)/shard_map/ppermute | solution.py:235
  48.8 14.3 %collective-permute-start.19 = (bf16[128,2048]{1,0:T(8,128)(2,1)S(1)}, bf16[128,2048]{1,0:T(8,128)(2,1)S(1)}, u32[]{:S(2)}, u32[]{:S(2)}) collective-permute-start(bf16[128,2048]{1,0:T(8,128)(2,1)S(1)} %collective-permute-done.11.refs_6_), channel_id=1, source_target_pairs={{0,8},{8,16},{16,24},{24,28},{28,20},{20,12},{12,4},{4,0},{1,9},{9... | collective-permute-start | bytes 1572872 | tf_op jit(solution)/shard_map/ppermute | solution.py:128
  49.8 14.1 %collective-permute-start.20 = (bf16[128,2048]{1,0:T(8,128)(2,1)S(1)}, bf16[128,2048]{1,0:T(8,128)(2,1)S(1)}, u32[]{:S(2)}, u32[]{:S(2)}) collective-permute-start(bf16[128,2048]{1,0:T(8,128)(2,1)S(1)} %collective-permute-done.12.refs_7_), channel_id=1, source_target_pairs={{8,0},{16,8},{24,16},{28,24},{20,28},{12,20},{4,12},{0,4},{9,1},{1... | collective-permute-start | bytes 1572872 | tf_op jit(solution)/shard_map/ppermute | solution.py:129
  50.9 4.9 %collective-permute-start.13 = (bf16[512,256]{1,0:T(8,128)(2,1)S(1)}, bf16[512,256]{1,0:T(8,128)(2,1)S(1)}, u32[]{:S(2)}, u32[]{:S(2)}) collective-permute-start(bf16[512,256]{1,0:T(8,128)(2,1)S(1)} %get-tuple-element.124.refs_3_.refs_10_), channel_id=1, source_target_pairs={{0,1},{1,0},{2,3},{3,2},{4,5},{5,4},{6,7},{7,6},{8,9},{9,8},{10,11... | collective-permute-start | bytes 786440 | tf_op jit(solution)/shard_map/ppermute | solution.py:235
  55.8 1.5 collective-permute-start.15
  58.9 26.4 %copy-start.6 = (bf16[128,1024]{1,0:T(8,128)(2,1)}, bf16[128,1024]{1,0:T(8,128)(2,1)S(1)}, u32[]{:S(2)}) copy-start(bf16[128,1024]{1,0:T(8,128)(2,1)S(1)} %get-tuple-element.128.refs_1_) | copy-start | bytes 786436
  63.9 13.2 %collective-permute-start.24 = (bf16[128,2048]{1,0:T(8,128)(2,1)S(1)}, bf16[128,2048]{1,0:T(8,128)(2,1)S(1)}, u32[]{:S(2)}, u32[]{:S(2)}) collective-permute-start(bf16[128,2048]{1,0:T(8,128)(2,1)S(1)} %collective-permute-done.19.refs_8_), channel_id=1, source_target_pairs={{0,8},{8,16},{16,24},{24,28},{28,20},{20,12},{12,4},{4,0},{1,9},{9... | collective-permute-start | bytes 1572872 | tf_op jit(solution)/shard_map/ppermute | solution.py:128
  64.8 13.0 %collective-permute-start.25 = (bf16[128,2048]{1,0:T(8,128)(2,1)S(1)}, bf16[128,2048]{1,0:T(8,128)(2,1)S(1)}, u32[]{:S(2)}, u32[]{:S(2)}) collective-permute-start(bf16[128,2048]{1,0:T(8,128)(2,1)S(1)} %collective-permute-done.20.refs_9_), channel_id=1, source_target_pairs={{8,0},{16,8},{24,16},{28,24},{20,28},{12,20},{4,12},{0,4},{9,1},{1... | collective-permute-start | bytes 1572872 | tf_op jit(solution)/shard_map/ppermute | solution.py:129
  65.9 7.1 %collective-permute-start.22 = (bf16[128,1024]{1,0:T(8,128)(2,1)S(1)}, bf16[128,1024]{1,0:T(8,128)(2,1)S(1)}, u32[]{:S(2)}, u32[]{:S(2)}) collective-permute-start(bf16[128,1024]{1,0:T(8,128)(2,1)S(1)} %get-tuple-element.128.refs_1_), channel_id=1, source_target_pairs={{0,2},{1,3},{2,0},{3,1},{4,6},{5,7},{6,4},{7,5},{8,10},{9,11},{10,... | collective-permute-start | bytes 786440 | tf_op jit(solution)/shard_map/ppermute | solution.py:235
  73.0 4.9 %collective-permute-start.23 = (bf16[128,1024]{1,0:T(8,128)(2,1)S(1)}, bf16[128,1024]{1,0:T(8,128)(2,1)S(1)}, u32[]{:S(2)}, u32[]{:S(2)}) collective-permute-start(bf16[128,1024]{1,0:T(8,128)(2,1)S(1)} %collective-permute-done.22.refs_3_), channel_id=1, source_target_pairs={{0,1},{1,0},{2,3},{3,2},{4,5},{5,4},{6,7},{7,6},{8,9},{9,8},{10,11... | collective-permute-start | bytes 786440 | tf_op jit(solution)/shard_map/ppermute | solution.py:235
  73.0 7.0 %collective-permute-start.21 = (bf16[128,1024]{1,0:T(8,128)(2,1)S(1)}, bf16[128,1024]{1,0:T(8,128)(2,1)S(1)}, u32[]{:S(2)}, u32[]{:S(2)}) collective-permute-start(bf16[128,1024]{1,0:T(8,128)(2,1)S(1)} %get-tuple-element.128.refs_1_), channel_id=1, source_target_pairs={{0,1},{1,0},{2,3},{3,2},{4,5},{5,4},{6,7},{7,6},{8,9},{9,8},{10,11... | collective-permute-start | bytes 786440 | tf_op jit(solution)/shard_map/ppermute | solution.py:235
  77.9 6.5 %collective-permute-start.26 = (bf16[64,2048]{1,0:T(8,128)(2,1)S(1)}, bf16[64,2048]{1,0:T(8,128)(2,1)S(1)}, u32[]{:S(2)}, u32[]{:S(2)}) collective-permute-start(bf16[64,2048]{1,0:T(8,128)(2,1)S(1)} %get-tuple-element.133), channel_id=1, source_target_pairs={{0,8},{8,16},{16,24},{24,28},{28,20},{20,12},{12,4},{4,0},{1,9},{9... | collective-permute-start | bytes 786440 | tf_op jit(solution)/shard_map/ppermute | solution.py:128
  78.9 6.4 %collective-permute-start.27 = (bf16[64,2048]{1,0:T(8,128)(2,1)S(1)}, bf16[64,2048]{1,0:T(8,128)(2,1)S(1)}, u32[]{:S(2)}, u32[]{:S(2)}) collective-permute-start(bf16[64,2048]{1,0:T(8,128)(2,1)S(1)} %get-tuple-element.134), channel_id=1, source_target_pairs={{8,0},{16,8},{24,16},{28,24},{20,28},{12,20},{4,12},{0,4},{9,1},{1... | collective-permute-start | bytes 786440 | tf_op jit(solution)/shard_map/ppermute | solution.py:129
  97.1 16.0 %collective-permute-start.28 = (bf16[128,2048]{1,0:T(8,128)(2,1)S(1)}, bf16[128,2048]{1,0:T(8,128)(2,1)S(1)}, u32[]{:S(2)}, u32[]{:S(2)}) collective-permute-start(bf16[128,2048]{1,0:T(8,128)(2,1)S(1)} %get-tuple-element.136), channel_id=1, source_target_pairs={{0,8},{8,16},{16,24},{24,28},{28,20},{20,12},{12,4},{4,0},{1,9},{9... | collective-permute-start | bytes 1572872 | tf_op jit(solution)/shard_map/ppermute | solution.py:210
  97.8 15.3 %collective-permute-start.32 = (bf16[128,2048]{1,0:T(8,128)(2,1)S(1)}, bf16[128,2048]{1,0:T(8,128)(2,1)S(1)}, u32[]{:S(2)}, u32[]{:S(2)}) collective-permute-start(bf16[128,2048]{1,0:T(8,128)(2,1)S(1)} %get-tuple-element.141), channel_id=1, source_target_pairs={{8,0},{16,8},{24,16},{28,24},{20,28},{12,20},{4,12},{0,4},{9,1},{1... | collective-permute-start | bytes 1572872 | tf_op jit(solution)/shard_map/ppermute | solution.py:211
  99.2 1.9 collective-permute-start.29
  99.2 9.1 %collective-permute-start.30 = (bf16[128,1024]{1,0:T(8,128)(2,1)S(1)}, bf16[128,1024]{1,0:T(8,128)(2,1)S(1)}, u32[]{:S(2)}, u32[]{:S(2)}) collective-permute-start(bf16[128,1024]{1,0:T(8,128)(2,1)S(1)} %get-tuple-element.138), channel_id=1, source_target_pairs={{0,2},{1,3},{2,0},{3,1},{4,6},{5,7},{6,4},{7,5},{8,10},{9,11},{10,... | collective-permute-start | bytes 786440 | tf_op jit(solution)/shard_map/ppermute | solution.py:235
  100.8 12.3 %collective-permute-start.31 = (bf16[128,1024]{1,0:T(8,128)(2,1)S(1)}, bf16[128,1024]{1,0:T(8,128)(2,1)S(1)}, u32[]{:S(2)}, u32[]{:S(2)}) collective-permute-start(bf16[128,1024]{1,0:T(8,128)(2,1)S(1)} %get-tuple-element.139), channel_id=1, source_target_pairs={{0,3},{1,2},{2,1},{3,0},{4,7},{5,6},{6,5},{7,4},{8,11},{9,10},{10,... | collective-permute-start | bytes 786440 | tf_op jit(solution)/shard_map/ppermute | solution.py:235
  114.2 14.1 %collective-permute-start.33 = (bf16[128,2048]{1,0:T(8,128)(2,1)S(1)}, bf16[128,2048]{1,0:T(8,128)(2,1)S(1)}, u32[]{:S(2)}, u32[]{:S(2)}) collective-permute-start(bf16[128,2048]{1,0:T(8,128)(2,1)S(1)} %get-tuple-element.142), channel_id=1, source_target_pairs={{0,8},{8,16},{16,24},{24,28},{28,20},{20,12},{12,4},{4,0},{1,9},{9... | collective-permute-start | bytes 1572872 | tf_op jit(solution)/shard_map/ppermute | solution.py:210
  114.9 13.8 %collective-permute-start.37 = (bf16[128,2048]{1,0:T(8,128)(2,1)S(1)}, bf16[128,2048]{1,0:T(8,128)(2,1)S(1)}, u32[]{:S(2)}, u32[]{:S(2)}) collective-permute-start(bf16[128,2048]{1,0:T(8,128)(2,1)S(1)} %get-tuple-element.144), channel_id=1, source_target_pairs={{8,0},{16,8},{24,16},{28,24},{20,28},{12,20},{4,12},{0,4},{9,1},{1... | collective-permute-start | bytes 1572872 | tf_op jit(solution)/shard_map/ppermute | solution.py:211
  118.8 1.9 collective-permute-start.34
  118.9 6.4 %collective-permute-start.35 = (bf16[128,512]{1,0:T(8,128)(2,1)S(1)}, bf16[128,512]{1,0:T(8,128)(2,1)S(1)}, u32[]{:S(2)}, u32[]{:S(2)}) collective-permute-start(bf16[128,512]{1,0:T(8,128)(2,1)S(1)} %get-tuple-element.148), channel_id=1, source_target_pairs={{0,2},{1,3},{2,0},{3,1},{4,6},{5,7},{6,4},{7,5},{8,10},{9,11},{10,... | collective-permute-start | bytes 393224 | tf_op jit(solution)/shard_map/ppermute | solution.py:235
  120.5 6.6 %collective-permute-start.36 = (bf16[128,512]{1,0:T(8,128)(2,1)S(1)}, bf16[128,512]{1,0:T(8,128)(2,1)S(1)}, u32[]{:S(2)}, u32[]{:S(2)}) collective-permute-start(bf16[128,512]{1,0:T(8,128)(2,1)S(1)} %get-tuple-element.149), channel_id=1, source_target_pairs={{0,3},{1,2},{2,1},{3,0},{4,7},{5,6},{6,5},{7,4},{8,11},{9,10},{10,... | collective-permute-start | bytes 393224 | tf_op jit(solution)/shard_map/ppermute | solution.py:235
  129.7 12.9 %collective-permute-start.38 = (bf16[128,2048]{1,0:T(8,128)(2,1)S(1)}, bf16[128,2048]{1,0:T(8,128)(2,1)S(1)}, u32[]{:S(2)}, u32[]{:S(2)}) collective-permute-start(bf16[128,2048]{1,0:T(8,128)(2,1)S(1)} %get-tuple-element.151), channel_id=1, source_target_pairs={{0,8},{8,16},{16,24},{24,28},{28,20},{20,12},{12,4},{4,0},{1,9},{9... | collective-permute-start | bytes 1572872 | tf_op jit(solution)/shard_map/ppermute | solution.py:210
  130.3 12.7 %collective-permute-start.39 = (bf16[128,2048]{1,0:T(8,128)(2,1)S(1)}, bf16[128,2048]{1,0:T(8,128)(2,1)S(1)}, u32[]{:S(2)}, u32[]{:S(2)}) collective-permute-start(bf16[128,2048]{1,0:T(8,128)(2,1)S(1)} %get-tuple-element.152), channel_id=1, source_target_pairs={{8,0},{16,8},{24,16},{28,24},{20,28},{12,20},{4,12},{0,4},{9,1},{1... | collective-permute-start | bytes 1572872 | tf_op jit(solution)/shard_map/ppermute | solution.py:211
  143.0 9.8 %collective-permute-start.41 = (bf16[512,1024]{1,0:T(8,128)(2,1)S(1)}, bf16[512,1024]{1,0:T(8,128)(2,1)S(1)}, u32[]{:S(2)}, u32[]{:S(2)}) collective-permute-start(bf16[512,1024]{1,0:T(8,128)(2,1)S(1)} %get-tuple-element.168), channel_id=1, source_target_pairs={{0,1},{1,0},{2,3},{3,2},{4,5},{5,4},{6,7},{7,6},{8,9},{9,8},{10,11... | collective-permute-start | bytes 3145736 | tf_op jit(solution)/shard_map/ppermute | solution.py:235
  143.0 9.8 %collective-permute-start.40 = (bf16[144,1024]{1,0:T(8,128)(2,1)S(1)}, bf16[144,1024]{1,0:T(8,128)(2,1)S(1)}, u32[]{:S(2)}, u32[]{:S(2)}) collective-permute-start(bf16[144,1024]{1,0:T(8,128)(2,1)S(1)} %get-tuple-element.164), channel_id=1, source_target_pairs={{0,8},{8,16},{16,24},{24,28},{28,20},{20,12},{12,4},{4,0},{1,9},{9... | collective-permute-start | bytes 884744 | tf_op jit(solution)/shard_map/ppermute | solution.py:210
  143.8 9.8 %collective-permute-start.42 = (bf16[144,1024]{1,0:T(8,128)(2,1)S(1)}, bf16[144,1024]{1,0:T(8,128)(2,1)S(1)}, u32[]{:S(2)}, u32[]{:S(2)}) collective-permute-start(bf16[144,1024]{1,0:T(8,128)(2,1)S(1)} %get-tuple-element.170), channel_id=1, source_target_pairs={{8,0},{16,8},{24,16},{28,24},{20,28},{12,20},{4,12},{0,4},{9,1},{1... | collective-permute-start | bytes 884744 | tf_op jit(solution)/shard_map/ppermute | solution.py:211
  145.8 12.6 %collective-permute-start.44 = (bf16[128,1024]{1,0:T(8,128)(2,1)S(1)}, bf16[128,1024]{1,0:T(8,128)(2,1)S(1)}, u32[]{:S(2)}, u32[]{:S(2)}) collective-permute-start(bf16[128,1024]{1,0:T(8,128)(2,1)S(1)} %get-tuple-element.165), channel_id=1, source_target_pairs={{0,8},{8,16},{16,24},{24,28},{28,20},{20,12},{12,4},{4,0},{1,9},{9... | collective-permute-start | bytes 786440 | tf_op jit(solution)/shard_map/ppermute | solution.py:210
  146.7 12.6 %collective-permute-start.45 = (bf16[128,1024]{1,0:T(8,128)(2,1)S(1)}, bf16[128,1024]{1,0:T(8,128)(2,1)S(1)}, u32[]{:S(2)}, u32[]{:S(2)}) collective-permute-start(bf16[128,1024]{1,0:T(8,128)(2,1)S(1)} %get-tuple-element.166), channel_id=1, source_target_pairs={{8,0},{16,8},{24,16},{28,24},{20,28},{12,20},{4,12},{0,4},{9,1},{1... | collective-permute-start | bytes 786440 | tf_op jit(solution)/shard_map/ppermute | solution.py:211
  154.6 9.7 %collective-permute-start.43 = (bf16[144,1024]{1,0:T(8,128)(2,1)S(1)}, bf16[144,1024]{1,0:T(8,128)(2,1)S(1)}, u32[]{:S(2)}, u32[]{:S(2)}) collective-permute-start(bf16[144,1024]{1,0:T(8,128)(2,1)S(1)} %get-tuple-element.171), channel_id=1, source_target_pairs={{0,8},{8,16},{16,24},{24,28},{28,20},{20,12},{12,4},{4,0},{1,9},{9... | collective-permute-start | bytes 884744 | tf_op jit(solution)/shard_map/ppermute | solution.py:210
  156.2 8.6 %collective-permute-start.46 = (bf16[144,1024]{1,0:T(8,128)(2,1)S(1)}, bf16[144,1024]{1,0:T(8,128)(2,1)S(1)}, u32[]{:S(2)}, u32[]{:S(2)}) collective-permute-start(bf16[144,1024]{1,0:T(8,128)(2,1)S(1)} %get-tuple-element.173), channel_id=1, source_target_pairs={{8,0},{16,8},{24,16},{28,24},{20,28},{12,20},{4,12},{0,4},{9,1},{1... | collective-permute-start | bytes 884744 | tf_op jit(solution)/shard_map/ppermute | solution.py:211
  156.9 14.9 %collective-permute-start.49 = (bf16[256,1024]{1,0:T(8,128)(2,1)S(1)}, bf16[256,1024]{1,0:T(8,128)(2,1)S(1)}, u32[]{:S(2)}, u32[]{:S(2)}) collective-permute-start(bf16[256,1024]{1,0:T(8,128)(2,1)S(1)} %shard_map.194), channel_id=1, source_target_pairs={{0,2},{1,3},{2,0},{3,1},{4,6},{5,7},{6,4},{7,5},{8,10},{9,11},{10,... | collective-permute-start | bytes 1572872 | tf_op jit(solution)/shard_map/ppermute | solution.py:235
  160.2 23.7 %collective-permute-start.55 = (bf16[128,2048]{1,0:T(8,128)(2,1)S(1)}, bf16[128,2048]{1,0:T(8,128)(2,1)S(1)}, u32[]{:S(2)}, u32[]{:S(2)}) collective-permute-start(bf16[128,2048]{1,0:T(8,128)(2,1)S(1)} %shard_map.195.refs_0_), channel_id=1, source_target_pairs={{0,2},{1,3},{2,0},{3,1},{4,6},{5,7},{6,4},{7,5},{8,10},{9,11},{10,... | collective-permute-start | bytes 1572872 | tf_op jit(solution)/shard_map/ppermute | solution.py:235
  165.9 8.1 %collective-permute-start.47 = (bf16[144,1024]{1,0:T(8,128)(2,1)S(1)}, bf16[144,1024]{1,0:T(8,128)(2,1)S(1)}, u32[]{:S(2)}, u32[]{:S(2)}) collective-permute-start(bf16[144,1024]{1,0:T(8,128)(2,1)S(1)} %get-tuple-element.177), channel_id=1, source_target_pairs={{0,8},{8,16},{16,24},{24,28},{28,20},{20,12},{12,4},{4,0},{1,9},{9... | collective-permute-start | bytes 884744 | tf_op jit(solution)/shard_map/ppermute | solution.py:210
  167.5 7.8 %collective-permute-start.48 = (bf16[144,1024]{1,0:T(8,128)(2,1)S(1)}, bf16[144,1024]{1,0:T(8,128)(2,1)S(1)}, u32[]{:S(2)}, u32[]{:S(2)}) collective-permute-start(bf16[144,1024]{1,0:T(8,128)(2,1)S(1)} %get-tuple-element.178), channel_id=1, source_target_pairs={{8,0},{16,8},{24,16},{28,24},{20,28},{12,20},{4,12},{0,4},{9,1},{1... | collective-permute-start | bytes 884744 | tf_op jit(solution)/shard_map/ppermute | solution.py:211
  176.1 5.2 %collective-permute-start.50 = (bf16[144,512]{1,0:T(8,128)(2,1)S(1)}, bf16[144,512]{1,0:T(8,128)(2,1)S(1)}, u32[]{:S(2)}, u32[]{:S(2)}) collective-permute-start(bf16[144,512]{1,0:T(8,128)(2,1)S(1)} %get-tuple-element.180), channel_id=1, source_target_pairs={{0,8},{8,16},{16,24},{24,28},{28,20},{20,12},{12,4},{4,0},{1,9},{9... | collective-permute-start | bytes 442376 | tf_op jit(solution)/shard_map/ppermute | solution.py:210
  177.9 5.1 %collective-permute-start.51 = (bf16[144,512]{1,0:T(8,128)(2,1)S(1)}, bf16[144,512]{1,0:T(8,128)(2,1)S(1)}, u32[]{:S(2)}, u32[]{:S(2)}) collective-permute-start(bf16[144,512]{1,0:T(8,128)(2,1)S(1)} %get-tuple-element.181), channel_id=1, source_target_pairs={{8,0},{16,8},{24,16},{28,24},{20,28},{12,20},{4,12},{0,4},{9,1},{1... | collective-permute-start | bytes 442376 | tf_op jit(solution)/shard_map/ppermute | solution.py:211
  178.2 8.3 %collective-permute-start.54 = (bf16[128,2048]{1,0:T(8,128)(2,1)S(1)}, bf16[128,2048]{1,0:T(8,128)(2,1)S(1)}, u32[]{:S(2)}, u32[]{:S(2)}) collective-permute-start(bf16[128,2048]{1,0:T(8,128)(2,1)S(1)} %shard_map.195.refs_0_), channel_id=1, source_target_pairs={{0,1},{1,0},{2,3},{3,2},{4,5},{5,4},{6,7},{7,6},{8,9},{9,8},{10,11... | collective-permute-start | bytes 1572872 | tf_op jit(solution)/shard_map/ppermute | solution.py:235
  183.9 2.6 %collective-permute-start.56 = (bf16[128,2048]{1,0:T(8,128)(2,1)S(1)}, bf16[128,2048]{1,0:T(8,128)(2,1)S(1)}, u32[]{:S(2)}, u32[]{:S(2)}) collective-permute-start(bf16[128,2048]{1,0:T(8,128)(2,1)S(1)} %collective-permute-done.55.refs_2_), channel_id=1, source_target_pairs={{0,1},{1,0},{2,3},{3,2},{4,5},{5,4},{6,7},{7,6},{8,9},{9,8},{10,11... | collective-permute-start | bytes 1572872 | tf_op jit(solution)/shard_map/ppermute | solution.py:235
  184.0 9.4 %collective-permute-start.53 = (bf16[144,1024]{1,0:T(8,128)(2,1)S(1)}, bf16[144,1024]{1,0:T(8,128)(2,1)S(1)}, u32[]{:S(2)}, u32[]{:S(2)}) collective-permute-start(bf16[144,1024]{1,0:T(8,128)(2,1)S(1)} %shard_map.198.refs_0_), channel_id=1, source_target_pairs={{0,2},{1,3},{2,0},{3,1},{4,6},{5,7},{6,4},{7,5},{8,10},{9,11},{10,... | collective-permute-start | bytes 884744 | tf_op jit(solution)/shard_map/ppermute | solution.py:235
  184.7 8.6 %collective-permute-start.52 = (bf16[144,1024]{1,0:T(8,128)(2,1)S(1)}, bf16[144,1024]{1,0:T(8,128)(2,1)S(1)}, u32[]{:S(2)}, u32[]{:S(2)}) collective-permute-start(bf16[144,1024]{1,0:T(8,128)(2,1)S(1)} %shard_map.198.refs_0_), channel_id=1, source_target_pairs={{0,1},{1,0},{2,3},{3,2},{4,5},{5,4},{6,7},{7,6},{8,9},{9,8},{10,11... | collective-permute-start | bytes 884744 | tf_op jit(solution)/shard_map/ppermute | solution.py:235
  193.4 1.6 collective-permute-start.57
  (15 other events, 133.1 us)

commit v5 on v4

--- a/solution.py
+++ b/solution.py
@@ -459,32 +459,16 @@
             grad_ref[start // rows_here + sub] = block[sub * rows_here : (sub + 1) * rows_here]
 
 
-def store_shares(total, own_ref, send_refs, columns):
-    tok = own_ref.shape[0]
-    own_ref[:, columns] = total[:tok]
-    for step, send in enumerate(send_refs, 1):
-        send[:, columns] = total[step * tok : (step + 1) * tok].astype(BF16)
-
-
-def store_pairs(total, own_ref, far_ref, send_ref, columns):
-    tok = own_ref.shape[0]
-    own_ref[:, columns] = total[:tok]
-    far_ref[:, columns] = total[2 * tok : 3 * tok].astype(far_ref.dtype)
-    send_ref[:tok, columns] = total[tok : 2 * tok].astype(BF16)
-    send_ref[tok:, columns] = total[3 * tok :].astype(BF16)
-
-
 def feed_kernel(parts, count, *refs):
     up_from, act_refs, pieces, me_ref = refs[0], refs[1:5], refs[5 : 5 + count], refs[5 + count]
-    grad_ref, up_first, down_first, own_ref, *send_refs, own_out_ref, far_out_ref, send_out_ref = refs[
-        6 + count : 16 + count
-    ]
-    act, up_ref, weight, down, slope, hidden, fed_ref, act_sems, up_sems, sems, down_sems = refs[16 + count :]
+    grad_ref, up_first, down_first, own_ref, far_ref, send_ref, fed_ref = refs[6 + count : 13 + count]
+    act, up_ref, weight, down, slope, hidden, act_sems, up_sems, sems, down_sems = refs[13 + count :]
+    tok = own_ref.shape[0]
     width = weight.shape[1]
     copies = load(pieces, me_ref, parts, weight, sems, slice(0, width)) + load_rows(act_refs, act, act_sems)
+    finish(copies)
     late = load(pieces, me_ref, parts, down, down_sems, slice(width, None))
     late += start_all([pltpu.make_async_copy(up_from, up_ref, up_sems.at[0])])
-    finish(copies)
     for start in range(0, width, 2 * BLOCK):
         columns = slice(start, start + 2 * BLOCK)
         units = dot(act[...], weight[:, columns])
@@ -500,10 +484,11 @@
         hidden[:, rows] = (dot(up_ref[...], down[rows, :], 1, 1) * slope[:, rows]).astype(BF16)
     for start in range(0, weight.shape[0], 2 * BLOCK):
         rows = slice(start, start + 2 * BLOCK)
-        store_shares(dot(hidden[...], weight[rows, :], 1, 1), own_ref, send_refs, rows)
-    for start in range(0, down.shape[1], 2 * BLOCK):
-        columns = slice(start, start + 2 * BLOCK)
-        store_pairs(dot(fed_ref[...], down[:, columns]), own_out_ref, far_out_ref, send_out_ref, columns)
+        share_of = dot(hidden[...], weight[rows, :], 1, 1)
+        own_ref[:, rows] = share_of[:tok]
+        far_ref[:, rows] = share_of[2 * tok : 3 * tok]
+        send_ref[:tok, rows] = share_of[tok : 2 * tok].astype(BF16)
+        send_ref[tok:, rows] = share_of[3 * tok :].astype(BF16)
     rows_here = grad_ref.shape[1]
     for at, (left, right) in enumerate([(act, hidden), (fed_ref, up_ref)]):
         lanes = slice(at * width, (at + 1) * width)
@@ -516,11 +501,16 @@
 
 
 def branch_back_kernel(*refs):
-    own_ref, resid_ref, up_ref, gain_ref, sent, weight_refs, me_ref = (*refs[:4], refs[4:7], refs[7:11], refs[11])
-    grad_ref, sums_ref, *send_refs, branch, grad_attn, rest, weight, sems, weight_sems = refs[12:]
+    own_ref, resid_ref, up_ref, gain_ref, near_ref, far_ref, weight_refs, me_ref = (*refs[:6], refs[6:10], refs[10])
+    grad_ref, sums_ref, *send_refs, branch, grad_attn, near, far, weight, sems, weight_sems = refs[11:]
     tok = up_ref.shape[0]
     part = send_refs[0].shape[1] // 2
-    copies = load_rows(sent, rest, sems)
+    copies = start_all(
+        [
+            pltpu.make_async_copy(near_ref.at[:tok, :], near, sems.at[0]),
+            pltpu.make_async_copy(far_ref, far, sems.at[1]),
+        ]
+    )
     late = []
     for step in range(4):
         columns = pl.ds(place(step, part, me_ref), part)
@@ -528,9 +518,7 @@
     start_all(late)
     normed, inverse = layer_norm(resid_ref[...])
     finish(copies)
-    upstream = own_ref[...]
-    for step in range(3):
-        upstream += rest[step * tok : (step + 1) * tok, :].astype(F32)
+    upstream = own_ref[...] + near[...].astype(F32) + far[...].astype(F32)
     sums_ref[0:1, :] = jnp.sum(upstream * normed, axis=0, keepdims=True)
     sums_ref[1:2, :] = jnp.sum(upstream, axis=0, keepdims=True)
     sums_ref[2:, :] = jnp.zeros_like(sums_ref[2:, :])
@@ -545,15 +533,15 @@
         send[:, part:] = branch[:, columns]
 
 
-def attend_back_kernel(scale, dp_count, count, *refs):
+def attend_back_kernel(scale, dp_count, count, rest_count, *refs):
     qkv_ref, log_ref, bias_ref, mask_ref, act_ref, normed_ref, sums_ref, bucket_ref = refs[:8]
-    far_out_ref, send_out_ref, attn_refs, grad_refs = refs[8], refs[9], refs[10:14], refs[14:18]
-    pieces, me_ref = refs[18 : 18 + count], refs[18 + count]
-    last_ref, up_first, down_first, small_ref, own_ref, far_ref, send_ref = refs[19 + count : 26 + count]
-    grads, branch, attn, grad_qkv, key_acc, value_acc, diagonal_acc, stacked, shares, weight_ref = refs[
-        26 + count : 36 + count
+    fed_from, attn_refs, grad_refs, pieces = refs[8], refs[9:13], refs[13:17], refs[17 : 17 + count]
+    down_refs, me_ref, refs = refs[17 + count : 17 + count + rest_count], refs[17 + count + rest_count], refs[18 + count + rest_count :]
+    last_ref, up_first, down_first, small_ref, own_ref, own_out_ref, far_ref, send_ref = refs[:8]
+    grads, branch, attn, grad_qkv, key_acc, value_acc, diagonal_acc, stacked, rolled, rolled_high, shares, weight_ref, fed_ref, down = refs[
+        8:22
     ]
-    grad_sems, branch_sems, attn_sems, sems, out_sems = refs[36 + count :]
+    grad_sems, branch_sems, attn_sems, sems, fed_sems, down_sems = refs[22:]
     seq_len = qkv_ref.shape[0]
     columns = qkv_ref.shape[1] // 3
     heads, diagonals = bias_ref.shape[:2]
@@ -562,13 +550,8 @@
     late = load_rows(grad_refs, branch, branch_sems, me_ref, lanes=slice(columns, 2 * columns))
     late += load_rows(attn_refs, attn, attn_sems)
     late += load(pieces, me_ref, dp_count, weight_ref, sems, slice(0, 3 * columns))
-    late += start_all(
-        [
-            pltpu.make_async_copy(far_out_ref, far_ref.at[tok:, :], out_sems.at[0]),
-            pltpu.make_async_copy(send_out_ref.at[:tok, :], send_ref.at[tok : 2 * tok, :], out_sems.at[1]),
-            pltpu.make_async_copy(send_out_ref.at[tok:, :], send_ref.at[3 * tok :, :], out_sems.at[2]),
-        ]
-    )
+    late += load(down_refs, me_ref, dp_count, down, down_sems, slice(act_ref.shape[1], None))
+    late += start_all([pltpu.make_async_copy(fed_from, fed_ref, fed_sems.at[0])])
     key_acc[...] = jnp.zeros_like(key_acc)
     value_acc[...] = jnp.zeros_like(value_acc)
     diagonal_acc[...] = jnp.zeros_like(diagonal_acc)
@@ -628,26 +611,40 @@
         small_ref[0:1, lanes] = jnp.sum(share_of * normed_ref[:, lanes].astype(F32), axis=0, keepdims=True)
         small_ref[2:3, lanes] = jnp.sum(share_of, axis=0, keepdims=True)
         shares[:, lanes] = share_of
+    for start in range(0, width, 2 * BLOCK):
+        lanes = slice(start, start + 2 * BLOCK)
+        share_of = dot(fed_ref[...], down[:, lanes])
+        own_out_ref[:, lanes] = share_of[:tok]
+        send_ref[tok : 2 * tok, lanes] = share_of[tok : 2 * tok].astype(BF16)
+        far_ref[tok:, lanes] = share_of[2 * tok : 3 * tok].astype(BF16)
+        send_ref[3 * tok :, lanes] = share_of[3 * tok :].astype(BF16)
     for step, (target, to) in enumerate([(own_ref, 0), (send_ref, 0), (far_ref, 0), (send_ref, 2 * tok)]):
         rows = pl.ds(place(step, tok, me_ref), tok)
         target[to : to + tok, :] = shares[rows, :].astype(target.dtype)
     small_ref[1:2, :] = sums_ref[0:1, :]
     small_ref[3:4, :] = sums_ref[1:2, :]
 
-    row = lax.broadcasted_iota(jnp.int32, (BLOCK, BLOCK), 0)
-    column = lax.broadcasted_iota(jnp.int32, (BLOCK, BLOCK), 1)
-    flip = (row + column == BLOCK - 1).astype(F32)
-    stacked[...] = jnp.zeros_like(stacked)
     for pair in range(heads // 2):
         for diagonal in range(diagonals):
-            both = exact_dot(flip, diagonal_acc[pair, diagonal])
-            at = slice(diagonal * BLOCK, (diagonal + 2) * BLOCK)
             for side in range(2):
-                block = both[:, side * BLOCK : (side + 1) * BLOCK]
-                wide = jnp.concatenate([block, jnp.zeros_like(block)], axis=1)
-                rolled = pltpu.roll(wide, 1, 1, stride=1, stride_axis=0)
-                head = 2 * pair + side
-                stacked[head : head + 1, at] += jnp.sum(rolled, axis=0, keepdims=True)
+                total = jnp.zeros((8, 2 * BLOCK), F32)
+                for start in range(0, BLOCK, 8):
+                    some = diagonal_acc[pair, diagonal, start : start + 8, side * BLOCK : (side + 1) * BLOCK]
+                    wide = jnp.concatenate([some, jnp.zeros_like(some)], axis=1)
+                    total += wide if start == 0 else pltpu.roll(wide, 2 * BLOCK - start, 1)
+                at = ((2 * pair + side) * diagonals + diagonal) * 8
+                rolled[at : at + 8, :] = total[:, :BLOCK]
+                rolled_high[at : at + 8, :] = total[:, BLOCK:]
+    turned = jnp.zeros((heads * diagonals, 2 * BLOCK), F32)
+    for start in range(8):
+        rows = pl.ds(start, heads * diagonals, stride=8)
+        both = jnp.concatenate([rolled[rows, :], rolled_high[rows, :]], axis=1)
+        turned += pltpu.roll(both, BLOCK - start, 1)
+    stacked[...] = jnp.zeros_like(stacked)
+    for head in range(heads):
+        for diagonal in range(diagonals):
+            at = head * diagonals + diagonal
+            stacked[head : head + 1, diagonal * BLOCK : (diagonal + 2) * BLOCK] += turned[at : at + 1, :]
     buckets = BLOCK // heads
     distances = padded(bucket_ref)
     bucket = lax.rem(lax.broadcasted_iota(jnp.int32, (BLOCK, distances.shape[1]), 0), buckets)
@@ -858,12 +855,11 @@
     rest_ring.step(act_two)
     act_last = swap(act_far, 1)
     rest_ring.step(act_last)
-    shares = [shaped((tok, width), F32)] + [shaped((tok, width), BF16)] * 3
-    pair_shares = [shaped((tok, width), F32), shaped((tok, width), BF16), shaped((2 * tok, width), BF16)]
-    grad_feed, up_first, down_first, own_two, *sends, own_out, far_out, send_out = call(
+    grad_feed, up_first, down_first, own_two, far_two, send_two, fed = call(
         functools.partial(feed_kernel, dp_count, count),
         [shaped((dp_count, rows_here, 2 * width), BF16)] + [shaped((rows_here, 2 * width), BF16)] * 2
-        + shares + pair_shares,
+        + [shaped((tok, width), F32)] * 2
+        + [shaped((2 * tok, width), BF16), shaped((seq_len, ff_part), BF16)],
         [],
         in_hbm([up_all, act_two, act_near, act_far, act_last, *rest_ring.pieces]),
         [me],
@@ -874,7 +870,6 @@
             pltpu.VMEM((ff_part, width), BF16),
             pltpu.VMEM((seq_len, ff_part), F32),
             pltpu.VMEM((seq_len, ff_part), BF16),
-            pltpu.VMEM((seq_len, ff_part), BF16),
             dma(4),
             dma(1),
             dma(count),
@@ -883,22 +878,21 @@
         micros=9,
     )
 
-    sent_two = exchange_sp(sends)
+    near_two = swap(send_two, 1)
+    last_two = swap(add_far(far_two, near_two), 2)
     feed_grads = ScatterRing(grad_feed, (up_first, down_first), me, dp_count)
     feed_grads.step()
-    feed_grads.step(*sent_two)
+    feed_grads.step(last_two)
     grad_resid, sums_two, *sends = call(
         branch_back_kernel,
         [shaped((tok, width), F32), shaped((8, width), F32)] + [shaped((tok, 2 * part), BF16)] * 4,
         [hold(own_two, *feed_grads.sums()), resid, cotangent[0], norm_gain],
-        [*sent_two, out_columns, out_near, out_far, out_last],
+        [near_two, last_two, out_columns, out_near, out_far, out_last],
         [me],
         [
-            pltpu.VMEM((tok, width), BF16),
-            pltpu.VMEM((tok, width), BF16),
-            pltpu.VMEM((3 * tok, width), BF16),
+            *[pltpu.VMEM((tok, width), BF16)] * 4,
             pltpu.VMEM((width, width), BF16),
-            dma(3),
+            dma(2),
             dma(4),
         ],
         micros=2.5,
@@ -906,13 +900,14 @@
     grad_pieces = [sends[0]] + exchange_sp(sends[1:])
     feed_grads.step(*grad_pieces[1:])
     last_rows = rows_here + SMALL_ROWS if aligned else rows_here
-    last, up_first, down_first, small, own_one, far_both, send_both = call(
-        functools.partial(attend_back_kernel, scale, dp_count, count),
+    last, up_first, down_first, small, own_one, own_out, far_both, send_both = call(
+        functools.partial(attend_back_kernel, scale, dp_count, count, len(rest_ring.pieces)),
         [shaped((dp_count, last_rows, 4 * part), BF16)] + [shaped((last_rows, 4 * part), BF16)] * 2
         + [shaped((8, width), F32)]
-        + [shaped((tok, width), F32), shaped((2 * tok, width), BF16), shaped((4 * tok, width), BF16)],
+        + [shaped((tok, width), F32)] * 2
+        + [shaped((2 * tok, width), BF16), shaped((4 * tok, width), BF16)],
         [hold(qkv, *feed_grads.sums()), logs, bias, mask, act_one, normed_one, sums_two, buckets],
-        [far_out, send_out, attn, attn_near, attn_far, attn_last, *grad_pieces, *first_pieces],
+        [fed, attn, attn_near, attn_far, attn_last, *grad_pieces, *first_pieces, *in_hbm(rest_ring.pieces)],
         [me],
         [
             pltpu.VMEM((seq_len, part), BF16),
@@ -923,13 +918,18 @@
             pltpu.VMEM((seq_len, part), F32),
             pltpu.VMEM((pairs, diagonals, BLOCK, 2 * BLOCK), F32),
             pltpu.VMEM((heads, seq_len + BLOCK), F32),
+            pltpu.VMEM((8 * heads * diagonals, BLOCK), F32),
+            pltpu.VMEM((8 * heads * diagonals, BLOCK), F32),
             pltpu.VMEM((seq_len, width), F32),
             pltpu.VMEM((width, 3 * part), BF16),
+            pltpu.VMEM((seq_len, ff_part), BF16),
+            pltpu.VMEM((ff_part, width), BF16),
             dma(4),
             dma(4),
             dma(4),
             dma(count),
-            dma(3),
+            dma(1),
+            dma(count),
         ],
         micros=9.4,
     )

time: 198 us -> 195 us (0.985)
    ppermute x26 -> x25, waiting for transfers between devices: 44.4 us -> 33.3 us  [swap(): return lax.ppermute(values, 'sp', [(i, i ^ bit) for i in range(count)])]
    ppermute x16, waiting for transfers between devices: 35.4 us -> 45.1 us  [step(): self.up = lax.ppermute(up, 'dp', forward)]
    pallas_call x24 -> x25, Pallas kernels: 51 us -> 49.7 us  [call(): pl.pallas_call(kernel, out_shape=(*outs, *hbm_outs), in_specs=specs, out_...]
    ppermute x26 -> x25, starting transfers between devices: 14.7 us -> 13.5 us  [swap(): return lax.ppermute(values, 'sp', [(i, i ^ bit) for i in range(count)])]
  transfers between devices with their start and end apart: 58 -> 57, of which waited for: 40 -> 39; matrix products, arithmetic and copies ran while one was open for 1% -> 1% of each run, Pallas kernels for 17% -> 18%
where the time goes in v5:
time: 195 us; the launch traced here: 194 us
  waiting for transfers between devices  93.1 us (48%)
  Pallas kernels  49.7 us (25%)
  starting transfers between devices  47.5 us (24%)
    pallas_call x25, Pallas kernels, call(): pl.pallas_call(kernel, out_shape=(*outs, *hbm_outs), in_specs=specs, out_...  49.7 us
    ppermute x16, waiting for transfers between devices, step(): self.up = lax.ppermute(up, 'dp', forward)  45.1 us
    ppermute x25, waiting for transfers between devices, swap(): return lax.ppermute(values, 'sp', [(i, i ^ bit) for i in range(count)])  33.3 us
    ppermute x16, starting transfers between devices, step(): self.up = lax.ppermute(up, 'dp', forward)  20.4 us
    ppermute x16, waiting for transfers between devices, step(): self.down = lax.ppermute(down, 'dp', backward)  14.8 us
    ppermute x16, starting transfers between devices, step(): self.down = lax.ppermute(down, 'dp', backward)  13.5 us
    ppermute x25, starting transfers between devices, swap(): return lax.ppermute(values, 'sp', [(i, i ^ bit) for i in range(count)])  13.5 us
  transfers between devices with their start and end apart: 57, of which 39 were waited for; matrix products, arithmetic and copies ran while one was open for 1% of the time, Pallas kernels for 18%

profile of v5, /device:TPU:0, one launch (start us, length us, event | category | flops | bytes accessed | tf_op | source)
XLA Modules:
  0.0 194.5 jit_solution(11409890626647498124)
XLA Ops:
  0.7 1.5 shard_map.178.refs_0_.refs_3_.refs_17_
  2.3 3.1 %collective-permute-start = (bf16[128,1024]{1,0:T(8,128)(2,1)S(1)}, bf16[128,1024]{1,0:T(8,128)(2,1)S(1)}, u32[]{:S(2)}, u32[]{:S(2)}) collective-permute-start(bf16[128,1024]{1,0:T(8,128)(2,1)S(1)} %shard_map.178.refs_0_.refs_3_.refs_17_), channel_id=1, source_target_pairs={{0,8},{8,16},{16,24},{24,28},{28,20},{20,12},{12,4},{4,0},{1,9},{9... | collective-permute-start | bytes 786440 | tf_op jit(solution)/shard_map/ppermute | solution.py:128
  5.4 1.1 pad_maximum_fusion.refs_2_
  6.4 2.0 %collective-permute-start.5 = (bf16[256,1024]{1,0:T(8,128)(2,1)S(1)}, bf16[256,1024]{1,0:T(8,128)(2,1)S(1)}, u32[]{:S(2)}, u32[]{:S(2)}) collective-permute-start(bf16[256,1024]{1,0:T(8,128)(2,1)S(1)} %pad_maximum_fusion.refs_2_), channel_id=1, source_target_pairs={{0,2},{1,3},{2,0},{3,1},{4,6},{5,7},{6,4},{7,5},{8,10},{9,11},{10,... | collective-permute-start | bytes 1572872 | tf_op jit(solution)/shard_map/ppermute | solution.py:235
  8.4 1.7 shard_map.180.refs_5_.refs_26_
  10.2 1.2 shard_map.179
  11.6 1.5 collective-permute-done.1.refs_2_.refs_5_.refs_19_
  13.1 1.6 collective-permute-start.2
  15.2 4.7 %collective-permute-done.5.refs_4_ = bf16[256,1024]{1,0:T(8,128)(2,1)S(1)} collective-permute-done((bf16[256,1024]{1,0:T(8,128)(2,1)S(1)}, bf16[256,1024]{1,0:T(8,128)(2,1)S(1)}, u32[]{:S(2)}, u32[]{:S(2)}) %collective-permute-start.5) | collective-permute-done | bytes 524320 | tf_op jit(solution)/shard_map/ppermute | solution.py:235
  20.0 1.3 collective-permute-done.3.refs_4_.refs_7_.refs_21_
  21.3 1.6 collective-permute-start.7
  23.3 4.3 %collective-permute-done.7.up_ref.refs_5_.refs_8_.refs_22_ = bf16[128,1024]{1,0:T(8,128)(2,1)S(1)} collective-permute-done((bf16[128,1024]{1,0:T(8,128)(2,1)S(1)}, bf16[128,1024]{1,0:T(8,128)(2,1)S(1)}, u32[]{:S(2)}, u32[]{:S(2)}) %collective-permute-start.7) | collective-permute-done | bytes 262176 | tf_op jit(solution)/shard_map/ppermute | solution.py:128
  27.7 1.6 collective-permute-done.8.down_ref.refs_6_.refs_9_.refs_23_
  29.6 1.6 collective-permute-start.9
  31.6 2.9 %collective-permute-done.9.refs_7_.refs_10_.refs_24_ = bf16[64,1024]{1,0:T(8,128)(2,1)S(1)} collective-permute-done((bf16[64,1024]{1,0:T(8,128)(2,1)S(1)}, bf16[64,1024]{1,0:T(8,128)(2,1)S(1)}, u32[]{:S(2)}, u32[]{:S(2)}) %collective-permute-start.9) | collective-permute-done | bytes 131104 | tf_op jit(solution)/shard_map/ppermute | solution.py:128
  34.6 1.6 collective-permute-done.10.refs_8_.refs_11_.refs_25_
  36.8 1.4 collective-permute-start.12
  39.0 1.6 collective-permute-start.17
  40.6 1.5 shard_map.181
  43.1 4.8 %shard_map.184 = (bf16[512,768]{1,0:T(8,128)(2,1)S(1)}, bf16[512,256]{1,0:T(8,128)(2,1)S(1)}, f32[8,256]{1,0:T(8,128)S(1)}) custom-call(bf16[512,1024]{1,0:T(8,128)(2,1)S(1)} %get-tuple-element.115.refs_0_.refs_4_, f32[4,4,128,128]{3,2,1,0:T(8,128)S(1)} %get-tuple-element.104.refs_1_.refs_2_, f32[4,512,128]{2,1,0:T(8,128)S(1)} %get-tuple-element.116.refs_2_.refs_3_, ...), custom_call_target="tpu_custom_call" | custom-call | bytes 16500000 | tf_op jit(solution)/shard_map/pallas_call | solution.py:60
  49.8 1.1 collective-permute-start.20
  50.9 5.8 %collective-permute-done.14.refs_5_.refs_11_ = bf16[512,256]{1,0:T(8,128)(2,1)S(1)} collective-permute-done((bf16[512,256]{1,0:T(8,128)(2,1)S(1)}, bf16[512,256]{1,0:T(8,128)(2,1)S(1)}, u32[]{:S(2)}, u32[]{:S(2)}) %collective-permute-start.14) | collective-permute-done | bytes 262176 | tf_op jit(solution)/shard_map/ppermute | solution.py:235
  56.7 1.5 collective-permute-done.15.refs_6_.refs_12_
  58.2 1.6 shard_map.185
  59.9 3.3 %collective-permute-done.19.refs_8_.refs_29_ = bf16[128,2048]{1,0:T(8,128)(2,1)S(1)} collective-permute-done((bf16[128,2048]{1,0:T(8,128)(2,1)S(1)}, bf16[128,2048]{1,0:T(8,128)(2,1)S(1)}, u32[]{:S(2)}, u32[]{:S(2)}) %collective-permute-start.19) | collective-permute-done | bytes 524320 | tf_op jit(solution)/shard_map/ppermute | solution.py:128
  64.8 1.1 collective-permute-start.25
  65.9 1.5 collective-permute-start.22
  67.4 5.6 %collective-permute-done.22.refs_3_ = bf16[128,1024]{1,0:T(8,128)(2,1)S(1)} collective-permute-done((bf16[128,1024]{1,0:T(8,128)(2,1)S(1)}, bf16[128,1024]{1,0:T(8,128)(2,1)S(1)}, u32[]{:S(2)}, u32[]{:S(2)}) %collective-permute-start.22) | collective-permute-done | bytes 262176 | tf_op jit(solution)/shard_map/ppermute | solution.py:235
  73.5 3.6 %collective-permute-done.24.up_ref.refs_10_.refs_31_ = bf16[128,2048]{1,0:T(8,128)(2,1)S(1)} collective-permute-done((bf16[128,2048]{1,0:T(8,128)(2,1)S(1)}, bf16[128,2048]{1,0:T(8,128)(2,1)S(1)}, u32[]{:S(2)}, u32[]{:S(2)}) %collective-permute-start.24) | collective-permute-done | bytes 524320 | tf_op jit(solution)/shard_map/ppermute | solution.py:128
  77.9 1.0 collective-permute-start.26
  78.9 1.1 collective-permute-start.27
  80.0 4.4 %collective-permute-done.26.refs_12_.refs_33_ = bf16[64,2048]{1,0:T(8,128)(2,1)S(1)} collective-permute-done((bf16[64,2048]{1,0:T(8,128)(2,1)S(1)}, bf16[64,2048]{1,0:T(8,128)(2,1)S(1)}, u32[]{:S(2)}, u32[]{:S(2)}) %collective-permute-start.26) | collective-permute-done | bytes 262176 | tf_op jit(solution)/shard_map/ppermute | solution.py:128
  86.0 9.5 %shard_map.187 = (bf16[8,128,2048]{2,1,0:T(8,128)(2,1)S(1)}, bf16[128,2048]{1,0:T(8,128)(2,1)S(1)}, bf16[128,2048]{1,0:T(8,128)(2,1)S(1)}, f32[128,1024]{1,0:T(8...) custom-call(bf16[512,1024]{1,0:T(8,128)(2,1)} %copy-done.4, ...), custom_call_target="tpu_custom_call" | custom-call | bytes 29700000 | tf_op jit(solution)/shard_map/pallas_call | solution.py:60
  96.3 1.4 collective-permute-start.31
  97.8 1.6 collective-permute-start.30
  99.3 10.6 %collective-permute-done.28.refs_1_ = bf16[128,2048]{1,0:T(8,128)(2,1)S(1)} collective-permute-done((bf16[128,2048]{1,0:T(8,128)(2,1)S(1)}, bf16[128,2048]{1,0:T(8,128)(2,1)S(1)}, u32[]{:S(2)}, u32[]{:S(2)}) %collective-permute-start.28) | collective-permute-done | bytes 524320 | tf_op jit(solution)/shard_map/ppermute | solution.py:210
  110.3 1.0 shard_map.189
  111.9 1.5 collective-permute-start.36
  113.4 2.4 %shard_map.190 = (f32[128,1024]{1,0:T(8,128)S(1)}, f32[8,1024]{1,0:T(8,128)S(1)}, bf16[128,512]{1,0:T(8,128)(2,1)S(1)}, bf16[128,512]{1,0:T(8,128)(2,1)S(1)}, bf...) custom-call(f32[128,1024]{1,0:T(8,128)S(1)} %get-tuple-element.142.refs_0_, ...), custom_call_target="tpu_custom_call" | custom-call | bytes 8250000 | tf_op jit(solution)/shard_map/pallas_call | solution.py:60
  115.9 1.6 collective-permute-start.34
  117.8 4.5 %collective-permute-done.34.refs_15_ = bf16[128,512]{1,0:T(8,128)(2,1)S(1)} collective-permute-done((bf16[128,512]{1,0:T(8,128)(2,1)S(1)}, bf16[128,512]{1,0:T(8,128)(2,1)S(1)}, u32[]{:S(2)}, u32[]{:S(2)}) %collective-permute-start.34) | collective-permute-done | bytes 131104 | tf_op jit(solution)/shard_map/ppermute | solution.py:235
  122.3 1.9 collective-permute-done.35.refs_16_
  126.8 1.2 collective-permute-start.38
  128.0 9.7 %shard_map.192 = (bf16[8,144,1024]{2,1,0:T(8,128)(2,1)S(1)}, bf16[144,1024]{1,0:T(8,128)(2,1)S(1)}, bf16[144,1024]{1,0:T(8,128)(2,1)S(1)}, f32[8,1024]{1,0:T(8,1...) custom-call(bf16[512,768]{1,0:T(8,128)(2,1)S(1)} %get-tuple-element., ...), custom_call_target="tpu_custom_call" | custom-call | bytes 31020000 | tf_op jit(solution)/shard_map/pallas_call | solution.py:60
  137.7 1.9 collective-permute-done.37.refs_1_.up_ref
  140.8 1.1 collective-permute-start.41
  143.7 1.1 collective-permute-start.44
  144.9 4.9 %collective-permute-done.39.refs_1_ = bf16[144,1024]{1,0:T(8,128)(2,1)S(1)} collective-permute-done((bf16[144,1024]{1,0:T(8,128)(2,1)S(1)}, bf16[144,1024]{1,0:T(8,128)(2,1)S(1)}, u32[]{:S(2)}, u32[]{:S(2)}) %collective-permute-start.39) | collective-permute-done | bytes 294944 | tf_op jit(solution)/shard_map/ppermute | solution.py:210
  151.6 1.6 collective-permute-start.42
  153.9 1.2 collective-permute-start.48
  157.2 1.2 collective-permute-start.54
  158.4 2.9 %collective-permute-done.42.refs_1_ = bf16[144,1024]{1,0:T(8,128)(2,1)S(1)} collective-permute-done((bf16[144,1024]{1,0:T(8,128)(2,1)S(1)}, bf16[144,1024]{1,0:T(8,128)(2,1)S(1)}, u32[]{:S(2)}, u32[]{:S(2)}) %collective-permute-start.42) | collective-permute-done | bytes 294944 | tf_op jit(solution)/shard_map/ppermute | solution.py:210
  162.9 1.6 collective-permute-start.46
  165.0 3.9 %collective-permute-done.48.refs_1_ = bf16[256,1024]{1,0:T(8,128)(2,1)S(1)} collective-permute-done((bf16[256,1024]{1,0:T(8,128)(2,1)S(1)}, bf16[256,1024]{1,0:T(8,128)(2,1)S(1)}, u32[]{:S(2)}, u32[]{:S(2)}) %collective-permute-start.48) | collective-permute-done | bytes 524320 | tf_op jit(solution)/shard_map/ppermute | solution.py:235
  168.8 2.2 %collective-permute-done.46.refs_1_.up_ref = bf16[144,1024]{1,0:T(8,128)(2,1)S(1)} collective-permute-done((bf16[144,1024]{1,0:T(8,128)(2,1)S(1)}, bf16[144,1024]{1,0:T(8,128)(2,1)S(1)}, u32[]{:S(2)}, u32[]{:S(2)}) %collective-permute-start.46) | collective-permute-done | bytes 294944 | tf_op jit(solution)/shard_map/ppermute | solution.py:210
  171.0 1.4 collective-permute-done.47.refs_2_.down_ref
  173.1 1.8 collective-permute-start.49
  175.2 3.1 %collective-permute-done.49.last_up_ref = bf16[144,512]{1,0:T(8,128)(2,1)S(1)} collective-permute-done((bf16[144,512]{1,0:T(8,128)(2,1)S(1)}, bf16[144,512]{1,0:T(8,128)(2,1)S(1)}, u32[]{:S(2)}, u32[]{:S(2)}) %collective-permute-start.49) | collective-permute-done | bytes 147488 | tf_op jit(solution)/shard_map/ppermute | solution.py:210
  178.3 1.7 collective-permute-done.50.last_down_ref
  181.9 1.5 shard_map.200
  183.5 3.1 %shard_map.201 = (f32[128,4096]{1,0:T(8,128)}, f32[512,1024]{1,0:T(8,128)}) custom-call(bf16[128,2048]{1,0:T(8,128)(2,1)S(1)} %shard_map.196.refs_0_, bf16[128,2048]{1,0:T(8,128)(2,1)S(1)} %collective-permute-done.53.refs_1_, bf16[128,2048]{1,0:T(8,128)(2,1)S(1)} %collective-permute-done.54.refs_2_, bf16[128,2048]{1,0:T(8,128)(2,1)S(1)} %collective-permute-done.55.refs_3_, ...), custom_call_target="tpu_custom_call" | custom-call | bytes 9900000 | tf_op jit(solution)/shard_map/pallas_call | solution.py:60
  186.7 3.8 %collective-permute-done.52.refs_2_ = bf16[144,1024]{1,0:T(8,128)(2,1)S(1)} collective-permute-done((bf16[144,1024]{1,0:T(8,128)(2,1)S(1)}, bf16[144,1024]{1,0:T(8,128)(2,1)S(1)}, u32[]{:S(2)}, u32[]{:S(2)}) %collective-permute-start.52) | collective-permute-done | bytes 294944 | tf_op jit(solution)/shard_map/ppermute | solution.py:235
  190.4 1.6 collective-permute-done.56.refs_3_
  192.0 2.3 %shard_map.202 = (f32[128,3072]{1,0:T(8,128)}, f32[128,1024]{1,0:T(8,128)}, f32[2,128]{1,0:T(2,128)}, f32[2,128]{1,0:T(2,128)}, f32[1,64]{1,0:T(1,128)}) custom-call(bf16[144,1024]{1,0:T(8,128)(2,1)S(1)} %shard_map.199.refs_0_, bf16[144,1024]{1,0:T(8,128)(2,1)S(1)} %collective-permute-done.51.refs_1_, bf16[144,1024]{1,0:T(8,128)(2,1)S(1)} %collective-permute-done.52.refs_2_, ...), custom_call_target="tpu_custom_call" | custom-call | bytes 7589999 | tf_op jit(solution)/shard_map/pallas_call | solution.py:60
  (119 shorter events, 28.1 us)
Async XLA Ops:
  2.3 9.3 %collective-permute-start = (bf16[128,1024]{1,0:T(8,128)(2,1)S(1)}, bf16[128,1024]{1,0:T(8,128)(2,1)S(1)}, u32[]{:S(2)}, u32[]{:S(2)}) collective-permute-start(bf16[128,1024]{1,0:T(8,128)(2,1)S(1)} %shard_map.178.refs_0_.refs_3_.refs_17_), channel_id=1, source_target_pairs={{0,8},{8,16},{16,24},{24,28},{28,20},{20,12},{12,4},{4,0},{1,9},{9... | collective-permute-start | bytes 786440 | tf_op jit(solution)/shard_map/ppermute | solution.py:128
  5.4 7.8 %collective-permute-start.1 = (bf16[128,1024]{1,0:T(8,128)(2,1)S(1)}, bf16[128,1024]{1,0:T(8,128)(2,1)S(1)}, u32[]{:S(2)}, u32[]{:S(2)}) collective-permute-start(bf16[128,1024]{1,0:T(8,128)(2,1)S(1)} %shard_map.178.refs_0_.refs_3_.refs_17_), channel_id=1, source_target_pairs={{8,0},{16,8},{24,16},{28,24},{20,28},{12,20},{4,12},{0,4},{9,1},{1... | collective-permute-start | bytes 786440 | tf_op jit(solution)/shard_map/ppermute | solution.py:129
  6.4 13.4 %collective-permute-start.5 = (bf16[256,1024]{1,0:T(8,128)(2,1)S(1)}, bf16[256,1024]{1,0:T(8,128)(2,1)S(1)}, u32[]{:S(2)}, u32[]{:S(2)}) collective-permute-start(bf16[256,1024]{1,0:T(8,128)(2,1)S(1)} %pad_maximum_fusion.refs_2_), channel_id=1, source_target_pairs={{0,2},{1,3},{2,0},{3,1},{4,6},{5,7},{6,4},{7,5},{8,10},{9,11},{10,... | collective-permute-start | bytes 1572872 | tf_op jit(solution)/shard_map/ppermute | solution.py:235
  10.2 31.9 %copy-start.2 = (bf16[128,2048]{1,0:T(8,128)(2,1)}, bf16[128,2048]{1,0:T(8,128)(2,1)S(1)}, u32[]{:S(2)}) copy-start(bf16[128,2048]{1,0:T(8,128)(2,1)S(1)} %shard_map.180.refs_5_.refs_26_) | copy-start | bytes 1572868
  10.2 30.3 %copy-start.7 = (f32[2,1024]{1,0:T(2,128)S(1)}, f32[2,1024]{1,0:T(2,128)}, u32[]{:S(2)}) copy-start(f32[2,1024]{1,0:T(2,128)} %gain_ref.1) | copy-start | bytes 24580
  10.2 30.3 %copy-start.8 = (f32[2,1024]{1,0:T(2,128)S(1)}, f32[2,1024]{1,0:T(2,128)}, u32[]{:S(2)}) copy-start(f32[2,1024]{1,0:T(2,128)} %refs_2_.1) | copy-start | bytes 24580
  13.1 6.9 %collective-permute-start.2 = (bf16[128,1024]{1,0:T(8,128)(2,1)S(1)}, bf16[128,1024]{1,0:T(8,128)(2,1)S(1)}, u32[]{:S(2)}, u32[]{:S(2)}) collective-permute-start(bf16[128,1024]{1,0:T(8,128)(2,1)S(1)} %collective-permute-done.refs_1_.refs_4_.refs_18_), channel_id=1, source_target_pairs={{0,8},{8,16},{16,24},{24,28},{28,20},{20,12},{12,4},{4,0},{1,9},{9... | collective-permute-start | bytes 786440 | tf_op jit(solution)/shard_map/ppermute | solution.py:128
  14.7 6.6 %collective-permute-start.3 = (bf16[128,1024]{1,0:T(8,128)(2,1)S(1)}, bf16[128,1024]{1,0:T(8,128)(2,1)S(1)}, u32[]{:S(2)}, u32[]{:S(2)}) collective-permute-start(bf16[128,1024]{1,0:T(8,128)(2,1)S(1)} %collective-permute-done.1.refs_2_.refs_5_.refs_19_), channel_id=1, source_target_pairs={{8,0},{16,8},{24,16},{28,24},{20,28},{12,20},{4,12},{0,4},{9,1},{1... | collective-permute-start | bytes 786440 | tf_op jit(solution)/shard_map/ppermute | solution.py:129
  21.3 6.4 %collective-permute-start.7 = (bf16[128,1024]{1,0:T(8,128)(2,1)S(1)}, bf16[128,1024]{1,0:T(8,128)(2,1)S(1)}, u32[]{:S(2)}, u32[]{:S(2)}) collective-permute-start(bf16[128,1024]{1,0:T(8,128)(2,1)S(1)} %collective-permute-done.2.refs_3_.refs_6_.refs_20_), channel_id=1, source_target_pairs={{0,8},{8,16},{16,24},{24,28},{28,20},{20,12},{12,4},{4,0},{1,9},{9... | collective-permute-start | bytes 786440 | tf_op jit(solution)/shard_map/ppermute | solution.py:128
  22.9 6.4 %collective-permute-start.8 = (bf16[128,1024]{1,0:T(8,128)(2,1)S(1)}, bf16[128,1024]{1,0:T(8,128)(2,1)S(1)}, u32[]{:S(2)}, u32[]{:S(2)}) collective-permute-start(bf16[128,1024]{1,0:T(8,128)(2,1)S(1)} %collective-permute-done.3.refs_4_.refs_7_.refs_21_), channel_id=1, source_target_pairs={{8,0},{16,8},{24,16},{28,24},{20,28},{12,20},{4,12},{0,4},{9,1},{1... | collective-permute-start | bytes 786440 | tf_op jit(solution)/shard_map/ppermute | solution.py:129
  23.3 17.2 %collective-permute-start.4 = (bf16[256,1024]{1,0:T(8,128)(2,1)S(1)}, bf16[256,1024]{1,0:T(8,128)(2,1)S(1)}, u32[]{:S(2)}, u32[]{:S(2)}) collective-permute-start(bf16[256,1024]{1,0:T(8,128)(2,1)S(1)} %pad_maximum_fusion.refs_2_), channel_id=1, source_target_pairs={{0,1},{1,0},{2,3},{3,2},{4,5},{5,4},{6,7},{7,6},{8,9},{9,8},{10,11... | collective-permute-start | bytes 1572872 | tf_op jit(solution)/shard_map/ppermute | solution.py:235
  29.6 5.0 %collective-permute-start.9 = (bf16[64,1024]{1,0:T(8,128)(2,1)S(1)}, bf16[64,1024]{1,0:T(8,128)(2,1)S(1)}, u32[]{:S(2)}, u32[]{:S(2)}) collective-permute-start(bf16[64,1024]{1,0:T(8,128)(2,1)S(1)} %get-tuple-element.113), channel_id=1, source_target_pairs={{0,8},{8,16},{16,24},{24,28},{28,20},{20,12},{12,4},{4,0},{1,9},{9... | collective-permute-start | bytes 393224 | tf_op jit(solution)/shard_map/ppermute | solution.py:128
  31.1 5.0 %collective-permute-start.10 = (bf16[64,1024]{1,0:T(8,128)(2,1)S(1)}, bf16[64,1024]{1,0:T(8,128)(2,1)S(1)}, u32[]{:S(2)}, u32[]{:S(2)}) collective-permute-start(bf16[64,1024]{1,0:T(8,128)(2,1)S(1)} %get-tuple-element.114), channel_id=1, source_target_pairs={{8,0},{16,8},{24,16},{28,24},{20,28},{12,20},{4,12},{0,4},{9,1},{1... | collective-permute-start | bytes 393224 | tf_op jit(solution)/shard_map/ppermute | solution.py:129
  31.6 8.9 %collective-permute-start.6 = (bf16[256,1024]{1,0:T(8,128)(2,1)S(1)}, bf16[256,1024]{1,0:T(8,128)(2,1)S(1)}, u32[]{:S(2)}, u32[]{:S(2)}) collective-permute-start(bf16[256,1024]{1,0:T(8,128)(2,1)S(1)} %collective-permute-done.5.refs_4_), channel_id=1, source_target_pairs={{0,1},{1,0},{2,3},{3,2},{4,5},{5,4},{6,7},{7,6},{8,9},{9,8},{10,11... | collective-permute-start | bytes 1572872 | tf_op jit(solution)/shard_map/ppermute | solution.py:235
  36.2 11.7 %collective-permute-start.11 = (bf16[128,2048]{1,0:T(8,128)(2,1)S(1)}, bf16[128,2048]{1,0:T(8,128)(2,1)S(1)}, u32[]{:S(2)}, u32[]{:S(2)}) collective-permute-start(bf16[128,2048]{1,0:T(8,128)(2,1)S(1)} %shard_map.180.refs_5_.refs_26_), channel_id=1, source_target_pairs={{0,8},{8,16},{16,24},{24,28},{28,20},{20,12},{12,4},{4,0},{1,9},{9... | collective-permute-start | bytes 1572872 | tf_op jit(solution)/shard_map/ppermute | solution.py:128
  36.8 11.1 %collective-permute-start.12 = (bf16[128,2048]{1,0:T(8,128)(2,1)S(1)}, bf16[128,2048]{1,0:T(8,128)(2,1)S(1)}, u32[]{:S(2)}, u32[]{:S(2)}) collective-permute-start(bf16[128,2048]{1,0:T(8,128)(2,1)S(1)} %shard_map.180.refs_5_.refs_26_), channel_id=1, source_target_pairs={{8,0},{16,8},{24,16},{28,24},{20,28},{12,20},{4,12},{0,4},{9,1},{1... | collective-permute-start | bytes 1572872 | tf_op jit(solution)/shard_map/ppermute | solution.py:129
  39.0 9.9 %collective-permute-start.17 = (bf16[1024,256]{1,0:T(8,128)(2,1)S(1)}, bf16[1024,256]{1,0:T(8,128)(2,1)S(1)}, u32[]{:S(2)}, u32[]{:S(2)}) collective-permute-start(bf16[1024,256]{1,0:T(8,128)(2,1)S(1)} %shard_map.183.refs_7_.refs_6_), channel_id=1, source_target_pairs={{0,2},{1,3},{2,0},{3,1},{4,6},{5,7},{6,4},{7,5},{8,10},{9,11},{10,... | collective-permute-start | bytes 1572872 | tf_op jit(solution)/shard_map/ppermute | solution.py:235
  40.5 10.3 %collective-permute-start.16 = (bf16[1024,256]{1,0:T(8,128)(2,1)S(1)}, bf16[1024,256]{1,0:T(8,128)(2,1)S(1)}, u32[]{:S(2)}, u32[]{:S(2)}) collective-permute-start(bf16[1024,256]{1,0:T(8,128)(2,1)S(1)} %shard_map.183.refs_7_.refs_6_), channel_id=1, source_target_pairs={{0,1},{1,0},{2,3},{3,2},{4,5},{5,4},{6,7},{7,6},{8,9},{9,8},{10,11... | collective-permute-start | bytes 1572872 | tf_op jit(solution)/shard_map/ppermute | solution.py:235
  47.9 30.0 %copy-start.12 = (bf16[128,2048]{1,0:T(8,128)(2,1)}, bf16[128,2048]{1,0:T(8,128)(2,1)S(1)}, u32[]{:S(2)}) copy-start(bf16[128,2048]{1,0:T(8,128)(2,1)S(1)} %collective-permute-done.11.refs_6_.refs_27_) | copy-start | bytes 1572868
  47.9 30.0 %copy-start.13 = (bf16[128,2048]{1,0:T(8,128)(2,1)}, bf16[128,2048]{1,0:T(8,128)(2,1)S(1)}, u32[]{:S(2)}) copy-start(bf16[128,2048]{1,0:T(8,128)(2,1)S(1)} %collective-permute-done.12.refs_7_.refs_28_) | copy-start | bytes 1572868
  47.9 8.8 %collective-permute-start.14 = (bf16[512,256]{1,0:T(8,128)(2,1)S(1)}, bf16[512,256]{1,0:T(8,128)(2,1)S(1)}, u32[]{:S(2)}, u32[]{:S(2)}) collective-permute-start(bf16[512,256]{1,0:T(8,128)(2,1)S(1)} %get-tuple-element.122.refs_3_.refs_9_), channel_id=1, source_target_pairs={{0,2},{1,3},{2,0},{3,1},{4,6},{5,7},{6,4},{7,5},{8,10},{9,11},{10,... | collective-permute-start | bytes 786440 | tf_op jit(solution)/shard_map/ppermute | solution.py:235
  48.8 9.4 %collective-permute-start.18 = (bf16[1024,256]{1,0:T(8,128)(2,1)S(1)}, bf16[1024,256]{1,0:T(8,128)(2,1)S(1)}, u32[]{:S(2)}, u32[]{:S(2)}) collective-permute-start(bf16[1024,256]{1,0:T(8,128)(2,1)S(1)} %collective-permute-done.17.refs_9_.refs_8_), channel_id=1, source_target_pairs={{0,1},{1,0},{2,3},{3,2},{4,5},{5,4},{6,7},{7,6},{8,9},{9,8},{10,11... | collective-permute-start | bytes 1572872 | tf_op jit(solution)/shard_map/ppermute | solution.py:235
  48.8 14.3 %collective-permute-start.19 = (bf16[128,2048]{1,0:T(8,128)(2,1)S(1)}, bf16[128,2048]{1,0:T(8,128)(2,1)S(1)}, u32[]{:S(2)}, u32[]{:S(2)}) collective-permute-start(bf16[128,2048]{1,0:T(8,128)(2,1)S(1)} %collective-permute-done.11.refs_6_.refs_27_), channel_id=1, source_target_pairs={{0,8},{8,16},{16,24},{24,28},{28,20},{20,12},{12,4},{4,0},{1,9},{9... | collective-permute-start | bytes 1572872 | tf_op jit(solution)/shard_map/ppermute | solution.py:128
  49.8 14.1 %collective-permute-start.20 = (bf16[128,2048]{1,0:T(8,128)(2,1)S(1)}, bf16[128,2048]{1,0:T(8,128)(2,1)S(1)}, u32[]{:S(2)}, u32[]{:S(2)}) collective-permute-start(bf16[128,2048]{1,0:T(8,128)(2,1)S(1)} %collective-permute-done.12.refs_7_.refs_28_), channel_id=1, source_target_pairs={{8,0},{16,8},{24,16},{28,24},{20,28},{12,20},{4,12},{0,4},{9,1},{1... | collective-permute-start | bytes 1572872 | tf_op jit(solution)/shard_map/ppermute | solution.py:129
  50.9 5.8 %collective-permute-start.13 = (bf16[512,256]{1,0:T(8,128)(2,1)S(1)}, bf16[512,256]{1,0:T(8,128)(2,1)S(1)}, u32[]{:S(2)}, u32[]{:S(2)}) collective-permute-start(bf16[512,256]{1,0:T(8,128)(2,1)S(1)} %get-tuple-element.122.refs_3_.refs_9_), channel_id=1, source_target_pairs={{0,1},{1,0},{2,3},{3,2},{4,5},{5,4},{6,7},{7,6},{8,9},{9,8},{10,11... | collective-permute-start | bytes 786440 | tf_op jit(solution)/shard_map/ppermute | solution.py:235
  56.7 1.5 collective-permute-start.15
  59.9 25.4 %copy-start.6 = (bf16[128,1024]{1,0:T(8,128)(2,1)}, bf16[128,1024]{1,0:T(8,128)(2,1)S(1)}, u32[]{:S(2)}) copy-start(bf16[128,1024]{1,0:T(8,128)(2,1)S(1)} %get-tuple-element.126.refs_1_) | copy-start | bytes 786436
  63.2 22.1 %copy-start.14 = (bf16[128,2048]{1,0:T(8,128)(2,1)}, bf16[128,2048]{1,0:T(8,128)(2,1)S(1)}, u32[]{:S(2)}) copy-start(bf16[128,2048]{1,0:T(8,128)(2,1)S(1)} %collective-permute-done.19.refs_8_.refs_29_) | copy-start | bytes 1572868
  63.9 13.2 %collective-permute-start.24 = (bf16[128,2048]{1,0:T(8,128)(2,1)S(1)}, bf16[128,2048]{1,0:T(8,128)(2,1)S(1)}, u32[]{:S(2)}, u32[]{:S(2)}) collective-permute-start(bf16[128,2048]{1,0:T(8,128)(2,1)S(1)} %collective-permute-done.19.refs_8_.refs_29_), channel_id=1, source_target_pairs={{0,8},{8,16},{16,24},{24,28},{28,20},{20,12},{12,4},{4,0},{1,9},{9... | collective-permute-start | bytes 1572872 | tf_op jit(solution)/shard_map/ppermute | solution.py:128
  64.8 13.0 %collective-permute-start.25 = (bf16[128,2048]{1,0:T(8,128)(2,1)S(1)}, bf16[128,2048]{1,0:T(8,128)(2,1)S(1)}, u32[]{:S(2)}, u32[]{:S(2)}) collective-permute-start(bf16[128,2048]{1,0:T(8,128)(2,1)S(1)} %collective-permute-done.20.refs_9_.refs_30_), channel_id=1, source_target_pairs={{8,0},{16,8},{24,16},{28,24},{20,28},{12,20},{4,12},{0,4},{9,1},{1... | collective-permute-start | bytes 1572872 | tf_op jit(solution)/shard_map/ppermute | solution.py:129
  65.9 7.1 %collective-permute-start.22 = (bf16[128,1024]{1,0:T(8,128)(2,1)S(1)}, bf16[128,1024]{1,0:T(8,128)(2,1)S(1)}, u32[]{:S(2)}, u32[]{:S(2)}) collective-permute-start(bf16[128,1024]{1,0:T(8,128)(2,1)S(1)} %get-tuple-element.126.refs_1_), channel_id=1, source_target_pairs={{0,2},{1,3},{2,0},{3,1},{4,6},{5,7},{6,4},{7,5},{8,10},{9,11},{10,... | collective-permute-start | bytes 786440 | tf_op jit(solution)/shard_map/ppermute | solution.py:235
  73.0 4.9 %collective-permute-start.23 = (bf16[128,1024]{1,0:T(8,128)(2,1)S(1)}, bf16[128,1024]{1,0:T(8,128)(2,1)S(1)}, u32[]{:S(2)}, u32[]{:S(2)}) collective-permute-start(bf16[128,1024]{1,0:T(8,128)(2,1)S(1)} %collective-permute-done.22.refs_3_), channel_id=1, source_target_pairs={{0,1},{1,0},{2,3},{3,2},{4,5},{5,4},{6,7},{7,6},{8,9},{9,8},{10,11... | collective-permute-start | bytes 786440 | tf_op jit(solution)/shard_map/ppermute | solution.py:235
  73.0 7.0 %collective-permute-start.21 = (bf16[128,1024]{1,0:T(8,128)(2,1)S(1)}, bf16[128,1024]{1,0:T(8,128)(2,1)S(1)}, u32[]{:S(2)}, u32[]{:S(2)}) collective-permute-start(bf16[128,1024]{1,0:T(8,128)(2,1)S(1)} %get-tuple-element.126.refs_1_), channel_id=1, source_target_pairs={{0,1},{1,0},{2,3},{3,2},{4,5},{5,4},{6,7},{7,6},{8,9},{9,8},{10,11... | collective-permute-start | bytes 786440 | tf_op jit(solution)/shard_map/ppermute | solution.py:235
  77.9 6.5 %collective-permute-start.26 = (bf16[64,2048]{1,0:T(8,128)(2,1)S(1)}, bf16[64,2048]{1,0:T(8,128)(2,1)S(1)}, u32[]{:S(2)}, u32[]{:S(2)}) collective-permute-start(bf16[64,2048]{1,0:T(8,128)(2,1)S(1)} %get-tuple-element.131), channel_id=1, source_target_pairs={{0,8},{8,16},{16,24},{24,28},{28,20},{20,12},{12,4},{4,0},{1,9},{9... | collective-permute-start | bytes 786440 | tf_op jit(solution)/shard_map/ppermute | solution.py:128
  78.9 6.4 %collective-permute-start.27 = (bf16[64,2048]{1,0:T(8,128)(2,1)S(1)}, bf16[64,2048]{1,0:T(8,128)(2,1)S(1)}, u32[]{:S(2)}, u32[]{:S(2)}) collective-permute-start(bf16[64,2048]{1,0:T(8,128)(2,1)S(1)} %get-tuple-element.132), channel_id=1, source_target_pairs={{8,0},{16,8},{24,16},{28,24},{20,28},{12,20},{4,12},{0,4},{9,1},{1... | collective-permute-start | bytes 786440 | tf_op jit(solution)/shard_map/ppermute | solution.py:129
  95.5 2.2 %collective-permute-start.29 = (bf16[256,1024]{1,0:T(8,128)(2,1)S(1)}, bf16[256,1024]{1,0:T(8,128)(2,1)S(1)}, u32[]{:S(2)}, u32[]{:S(2)}) collective-permute-start(bf16[256,1024]{1,0:T(8,128)(2,1)S(1)} %get-tuple-element.136), channel_id=1, source_target_pairs={{0,1},{1,0},{2,3},{3,2},{4,5},{5,4},{6,7},{7,6},{8,9},{9,8},{10,11... | collective-permute-start | bytes 1572872 | tf_op jit(solution)/shard_map/ppermute | solution.py:235
  95.6 14.3 %collective-permute-start.28 = (bf16[128,2048]{1,0:T(8,128)(2,1)S(1)}, bf16[128,2048]{1,0:T(8,128)(2,1)S(1)}, u32[]{:S(2)}, u32[]{:S(2)}) collective-permute-start(bf16[128,2048]{1,0:T(8,128)(2,1)S(1)} %get-tuple-element.134), channel_id=1, source_target_pairs={{0,8},{8,16},{16,24},{24,28},{28,20},{20,12},{12,4},{4,0},{1,9},{9... | collective-permute-start | bytes 1572872 | tf_op jit(solution)/shard_map/ppermute | solution.py:210
  96.3 14.0 %collective-permute-start.31 = (bf16[128,2048]{1,0:T(8,128)(2,1)S(1)}, bf16[128,2048]{1,0:T(8,128)(2,1)S(1)}, u32[]{:S(2)}, u32[]{:S(2)}) collective-permute-start(bf16[128,2048]{1,0:T(8,128)(2,1)S(1)} %get-tuple-element.138), channel_id=1, source_target_pairs={{8,0},{16,8},{24,16},{28,24},{20,28},{12,20},{4,12},{0,4},{9,1},{1... | collective-permute-start | bytes 1572872 | tf_op jit(solution)/shard_map/ppermute | solution.py:211
  97.8 12.2 %collective-permute-start.30 = (bf16[128,1024]{1,0:T(8,128)(2,1)S(1)}, bf16[128,1024]{1,0:T(8,128)(2,1)S(1)}, u32[]{:S(2)}, u32[]{:S(2)}) collective-permute-start(bf16[128,1024]{1,0:T(8,128)(2,1)S(1)} %shard_map.188), channel_id=1, source_target_pairs={{0,2},{1,3},{2,0},{3,1},{4,6},{5,7},{6,4},{7,5},{8,10},{9,11},{10,... | collective-permute-start | bytes 786440 | tf_op jit(solution)/shard_map/ppermute | solution.py:235
  111.3 13.2 %collective-permute-start.32 = (bf16[128,2048]{1,0:T(8,128)(2,1)S(1)}, bf16[128,2048]{1,0:T(8,128)(2,1)S(1)}, u32[]{:S(2)}, u32[]{:S(2)}) collective-permute-start(bf16[128,2048]{1,0:T(8,128)(2,1)S(1)} %get-tuple-element.139), channel_id=1, source_target_pairs={{0,8},{8,16},{16,24},{24,28},{28,20},{20,12},{12,4},{4,0},{1,9},{9... | collective-permute-start | bytes 1572872 | tf_op jit(solution)/shard_map/ppermute | solution.py:210
  111.9 13.0 %collective-permute-start.36 = (bf16[128,2048]{1,0:T(8,128)(2,1)S(1)}, bf16[128,2048]{1,0:T(8,128)(2,1)S(1)}, u32[]{:S(2)}, u32[]{:S(2)}) collective-permute-start(bf16[128,2048]{1,0:T(8,128)(2,1)S(1)} %get-tuple-element.141), channel_id=1, source_target_pairs={{8,0},{16,8},{24,16},{28,24},{20,28},{12,20},{4,12},{0,4},{9,1},{1... | collective-permute-start | bytes 1572872 | tf_op jit(solution)/shard_map/ppermute | solution.py:211
  115.8 1.9 collective-permute-start.33
  115.9 6.4 %collective-permute-start.34 = (bf16[128,512]{1,0:T(8,128)(2,1)S(1)}, bf16[128,512]{1,0:T(8,128)(2,1)S(1)}, u32[]{:S(2)}, u32[]{:S(2)}) collective-permute-start(bf16[128,512]{1,0:T(8,128)(2,1)S(1)} %get-tuple-element.145), channel_id=1, source_target_pairs={{0,2},{1,3},{2,0},{3,1},{4,6},{5,7},{6,4},{7,5},{8,10},{9,11},{10,... | collective-permute-start | bytes 393224 | tf_op jit(solution)/shard_map/ppermute | solution.py:235
  117.5 6.7 %collective-permute-start.35 = (bf16[128,512]{1,0:T(8,128)(2,1)S(1)}, bf16[128,512]{1,0:T(8,128)(2,1)S(1)}, u32[]{:S(2)}, u32[]{:S(2)}) collective-permute-start(bf16[128,512]{1,0:T(8,128)(2,1)S(1)} %get-tuple-element.146), channel_id=1, source_target_pairs={{0,3},{1,2},{2,1},{3,0},{4,7},{5,6},{6,5},{7,4},{8,11},{9,10},{10,... | collective-permute-start | bytes 393224 | tf_op jit(solution)/shard_map/ppermute | solution.py:235
  125.9 13.8 %collective-permute-start.37 = (bf16[128,2048]{1,0:T(8,128)(2,1)S(1)}, bf16[128,2048]{1,0:T(8,128)(2,1)S(1)}, u32[]{:S(2)}, u32[]{:S(2)}) collective-permute-start(bf16[128,2048]{1,0:T(8,128)(2,1)S(1)} %get-tuple-element.148), channel_id=1, source_target_pairs={{0,8},{8,16},{16,24},{24,28},{28,20},{20,12},{12,4},{4,0},{1,9},{9... | collective-permute-start | bytes 1572872 | tf_op jit(solution)/shard_map/ppermute | solution.py:210
  126.8 13.2 %collective-permute-start.38 = (bf16[128,2048]{1,0:T(8,128)(2,1)S(1)}, bf16[128,2048]{1,0:T(8,128)(2,1)S(1)}, u32[]{:S(2)}, u32[]{:S(2)}) collective-permute-start(bf16[128,2048]{1,0:T(8,128)(2,1)S(1)} %get-tuple-element.149), channel_id=1, source_target_pairs={{8,0},{16,8},{24,16},{28,24},{20,28},{12,20},{4,12},{0,4},{9,1},{1... | collective-permute-start | bytes 1572872 | tf_op jit(solution)/shard_map/ppermute | solution.py:211
  139.9 9.8 %collective-permute-start.40 = (bf16[512,1024]{1,0:T(8,128)(2,1)S(1)}, bf16[512,1024]{1,0:T(8,128)(2,1)S(1)}, u32[]{:S(2)}, u32[]{:S(2)}) collective-permute-start(bf16[512,1024]{1,0:T(8,128)(2,1)S(1)} %get-tuple-element.164), channel_id=1, source_target_pairs={{0,1},{1,0},{2,3},{3,2},{4,5},{5,4},{6,7},{7,6},{8,9},{9,8},{10,11... | collective-permute-start | bytes 3145736 | tf_op jit(solution)/shard_map/ppermute | solution.py:235
  139.9 9.8 %collective-permute-start.39 = (bf16[144,1024]{1,0:T(8,128)(2,1)S(1)}, bf16[144,1024]{1,0:T(8,128)(2,1)S(1)}, u32[]{:S(2)}, u32[]{:S(2)}) collective-permute-start(bf16[144,1024]{1,0:T(8,128)(2,1)S(1)} %get-tuple-element.160), channel_id=1, source_target_pairs={{0,8},{8,16},{16,24},{24,28},{28,20},{20,12},{12,4},{4,0},{1,9},{9... | collective-permute-start | bytes 884744 | tf_op jit(solution)/shard_map/ppermute | solution.py:210
  140.8 9.8 %collective-permute-start.41 = (bf16[144,1024]{1,0:T(8,128)(2,1)S(1)}, bf16[144,1024]{1,0:T(8,128)(2,1)S(1)}, u32[]{:S(2)}, u32[]{:S(2)}) collective-permute-start(bf16[144,1024]{1,0:T(8,128)(2,1)S(1)} %get-tuple-element.166), channel_id=1, source_target_pairs={{8,0},{16,8},{24,16},{28,24},{20,28},{12,20},{4,12},{0,4},{9,1},{1... | collective-permute-start | bytes 884744 | tf_op jit(solution)/shard_map/ppermute | solution.py:211
  142.8 12.6 %collective-permute-start.43 = (bf16[128,1024]{1,0:T(8,128)(2,1)S(1)}, bf16[128,1024]{1,0:T(8,128)(2,1)S(1)}, u32[]{:S(2)}, u32[]{:S(2)}) collective-permute-start(bf16[128,1024]{1,0:T(8,128)(2,1)S(1)} %get-tuple-element.161), channel_id=1, source_target_pairs={{0,8},{8,16},{16,24},{24,28},{28,20},{20,12},{12,4},{4,0},{1,9},{9... | collective-permute-start | bytes 786440 | tf_op jit(solution)/shard_map/ppermute | solution.py:210
  143.7 12.6 %collective-permute-start.44 = (bf16[128,1024]{1,0:T(8,128)(2,1)S(1)}, bf16[128,1024]{1,0:T(8,128)(2,1)S(1)}, u32[]{:S(2)}, u32[]{:S(2)}) collective-permute-start(bf16[128,1024]{1,0:T(8,128)(2,1)S(1)} %get-tuple-element.162), channel_id=1, source_target_pairs={{8,0},{16,8},{24,16},{28,24},{20,28},{12,20},{4,12},{0,4},{9,1},{1... | collective-permute-start | bytes 786440 | tf_op jit(solution)/shard_map/ppermute | solution.py:211
  151.6 9.7 %collective-permute-start.42 = (bf16[144,1024]{1,0:T(8,128)(2,1)S(1)}, bf16[144,1024]{1,0:T(8,128)(2,1)S(1)}, u32[]{:S(2)}, u32[]{:S(2)}) collective-permute-start(bf16[144,1024]{1,0:T(8,128)(2,1)S(1)} %get-tuple-element.167), channel_id=1, source_target_pairs={{0,8},{8,16},{16,24},{24,28},{28,20},{20,12},{12,4},{4,0},{1,9},{9... | collective-permute-start | bytes 884744 | tf_op jit(solution)/shard_map/ppermute | solution.py:210
  153.3 8.6 %collective-permute-start.45 = (bf16[144,1024]{1,0:T(8,128)(2,1)S(1)}, bf16[144,1024]{1,0:T(8,128)(2,1)S(1)}, u32[]{:S(2)}, u32[]{:S(2)}) collective-permute-start(bf16[144,1024]{1,0:T(8,128)(2,1)S(1)} %get-tuple-element.169), channel_id=1, source_target_pairs={{8,0},{16,8},{24,16},{28,24},{20,28},{12,20},{4,12},{0,4},{9,1},{1... | collective-permute-start | bytes 884744 | tf_op jit(solution)/shard_map/ppermute | solution.py:211
  153.9 14.9 %collective-permute-start.48 = (bf16[256,1024]{1,0:T(8,128)(2,1)S(1)}, bf16[256,1024]{1,0:T(8,128)(2,1)S(1)}, u32[]{:S(2)}, u32[]{:S(2)}) collective-permute-start(bf16[256,1024]{1,0:T(8,128)(2,1)S(1)} %shard_map.195), channel_id=1, source_target_pairs={{0,2},{1,3},{2,0},{3,1},{4,6},{5,7},{6,4},{7,5},{8,10},{9,11},{10,... | collective-permute-start | bytes 1572872 | tf_op jit(solution)/shard_map/ppermute | solution.py:235
  157.2 23.7 %collective-permute-start.54 = (bf16[128,2048]{1,0:T(8,128)(2,1)S(1)}, bf16[128,2048]{1,0:T(8,128)(2,1)S(1)}, u32[]{:S(2)}, u32[]{:S(2)}) collective-permute-start(bf16[128,2048]{1,0:T(8,128)(2,1)S(1)} %shard_map.196.refs_0_), channel_id=1, source_target_pairs={{0,2},{1,3},{2,0},{3,1},{4,6},{5,7},{6,4},{7,5},{8,10},{9,11},{10,... | collective-permute-start | bytes 1572872 | tf_op jit(solution)/shard_map/ppermute | solution.py:235
  162.9 8.1 %collective-permute-start.46 = (bf16[144,1024]{1,0:T(8,128)(2,1)S(1)}, bf16[144,1024]{1,0:T(8,128)(2,1)S(1)}, u32[]{:S(2)}, u32[]{:S(2)}) collective-permute-start(bf16[144,1024]{1,0:T(8,128)(2,1)S(1)} %get-tuple-element.173), channel_id=1, source_target_pairs={{0,8},{8,16},{16,24},{24,28},{28,20},{20,12},{12,4},{4,0},{1,9},{9... | collective-permute-start | bytes 884744 | tf_op jit(solution)/shard_map/ppermute | solution.py:210
  164.5 7.8 %collective-permute-start.47 = (bf16[144,1024]{1,0:T(8,128)(2,1)S(1)}, bf16[144,1024]{1,0:T(8,128)(2,1)S(1)}, u32[]{:S(2)}, u32[]{:S(2)}) collective-permute-start(bf16[144,1024]{1,0:T(8,128)(2,1)S(1)} %get-tuple-element.174), channel_id=1, source_target_pairs={{8,0},{16,8},{24,16},{28,24},{20,28},{12,20},{4,12},{0,4},{9,1},{1... | collective-permute-start | bytes 884744 | tf_op jit(solution)/shard_map/ppermute | solution.py:211
  173.1 5.2 %collective-permute-start.49 = (bf16[144,512]{1,0:T(8,128)(2,1)S(1)}, bf16[144,512]{1,0:T(8,128)(2,1)S(1)}, u32[]{:S(2)}, u32[]{:S(2)}) collective-permute-start(bf16[144,512]{1,0:T(8,128)(2,1)S(1)} %get-tuple-element.176), channel_id=1, source_target_pairs={{0,8},{8,16},{16,24},{24,28},{28,20},{20,12},{12,4},{4,0},{1,9},{9... | collective-permute-start | bytes 442376 | tf_op jit(solution)/shard_map/ppermute | solution.py:210
  174.9 5.1 %collective-permute-start.50 = (bf16[144,512]{1,0:T(8,128)(2,1)S(1)}, bf16[144,512]{1,0:T(8,128)(2,1)S(1)}, u32[]{:S(2)}, u32[]{:S(2)}) collective-permute-start(bf16[144,512]{1,0:T(8,128)(2,1)S(1)} %get-tuple-element.177), channel_id=1, source_target_pairs={{8,0},{16,8},{24,16},{28,24},{20,28},{12,20},{4,12},{0,4},{9,1},{1... | collective-permute-start | bytes 442376 | tf_op jit(solution)/shard_map/ppermute | solution.py:211
  175.2 8.3 %collective-permute-start.53 = (bf16[128,2048]{1,0:T(8,128)(2,1)S(1)}, bf16[128,2048]{1,0:T(8,128)(2,1)S(1)}, u32[]{:S(2)}, u32[]{:S(2)}) collective-permute-start(bf16[128,2048]{1,0:T(8,128)(2,1)S(1)} %shard_map.196.refs_0_), channel_id=1, source_target_pairs={{0,1},{1,0},{2,3},{3,2},{4,5},{5,4},{6,7},{7,6},{8,9},{9,8},{10,11... | collective-permute-start | bytes 1572872 | tf_op jit(solution)/shard_map/ppermute | solution.py:235
  180.9 2.6 %collective-permute-start.55 = (bf16[128,2048]{1,0:T(8,128)(2,1)S(1)}, bf16[128,2048]{1,0:T(8,128)(2,1)S(1)}, u32[]{:S(2)}, u32[]{:S(2)}) collective-permute-start(bf16[128,2048]{1,0:T(8,128)(2,1)S(1)} %collective-permute-done.54.refs_2_), channel_id=1, source_target_pairs={{0,1},{1,0},{2,3},{3,2},{4,5},{5,4},{6,7},{7,6},{8,9},{9,8},{10,11... | collective-permute-start | bytes 1572872 | tf_op jit(solution)/shard_map/ppermute | solution.py:235
  181.0 9.4 %collective-permute-start.52 = (bf16[144,1024]{1,0:T(8,128)(2,1)S(1)}, bf16[144,1024]{1,0:T(8,128)(2,1)S(1)}, u32[]{:S(2)}, u32[]{:S(2)}) collective-permute-start(bf16[144,1024]{1,0:T(8,128)(2,1)S(1)} %shard_map.199.refs_0_), channel_id=1, source_target_pairs={{0,2},{1,3},{2,0},{3,1},{4,6},{5,7},{6,4},{7,5},{8,10},{9,11},{10,... | collective-permute-start | bytes 884744 | tf_op jit(solution)/shard_map/ppermute | solution.py:235
  181.8 8.6 %collective-permute-start.51 = (bf16[144,1024]{1,0:T(8,128)(2,1)S(1)}, bf16[144,1024]{1,0:T(8,128)(2,1)S(1)}, u32[]{:S(2)}, u32[]{:S(2)}) collective-permute-start(bf16[144,1024]{1,0:T(8,128)(2,1)S(1)} %shard_map.199.refs_0_), channel_id=1, source_target_pairs={{0,1},{1,0},{2,3},{3,2},{4,5},{5,4},{6,7},{7,6},{8,9},{9,8},{10,11... | collective-permute-start | bytes 884744 | tf_op jit(solution)/shard_map/ppermute | solution.py:235
  190.4 1.6 collective-permute-start.56
  (14 other events, 107.1 us)

commit v6 on v5

--- a/solution.py
+++ b/solution.py
@@ -461,8 +461,8 @@
 
 def feed_kernel(parts, count, *refs):
     up_from, act_refs, pieces, me_ref = refs[0], refs[1:5], refs[5 : 5 + count], refs[5 + count]
-    grad_ref, up_first, down_first, own_ref, far_ref, send_ref, fed_ref = refs[6 + count : 13 + count]
-    act, up_ref, weight, down, slope, hidden, act_sems, up_sems, sems, down_sems = refs[13 + count :]
+    up_first, down_first, own_ref, far_ref, send_ref, fed_ref, hidden = refs[6 + count : 13 + count]
+    act, up_ref, weight, down, slope, act_sems, up_sems, sems, down_sems = refs[13 + count :]
     tok = own_ref.shape[0]
     width = weight.shape[1]
     copies = load(pieces, me_ref, parts, weight, sems, slice(0, width)) + load_rows(act_refs, act, act_sems)
@@ -489,15 +489,37 @@
         far_ref[:, rows] = share_of[2 * tok : 3 * tok]
         send_ref[:tok, rows] = share_of[tok : 2 * tok].astype(BF16)
         send_ref[tok:, rows] = share_of[3 * tok :].astype(BF16)
-    rows_here = grad_ref.shape[1]
-    for at, (left, right) in enumerate([(act, hidden), (fed_ref, up_ref)]):
-        lanes = slice(at * width, (at + 1) * width)
+    if parts == 8:
+        rows_here = up_first.shape[0]
+        at = position_of(me_ref[1], parts)
+        far, near = parts // 2, parts // 2 - 1
+        for side, (left, right, up_to, down_to) in enumerate(
+            [(act, hidden, at + far, at - near), (fed_ref, up_ref, at + near, at - far)]
+        ):
+            some = [
+                left[:, pl.ds(pl.multiple_of(rank_at(target, parts) * rows_here, rows_here), rows_here)]
+                for target in (up_to, down_to)
+            ]
+            block = dot(jnp.concatenate(some, axis=1), right[...], 0, 0).astype(BF16)
+            up_first[:, side * width : (side + 1) * width] = block[:rows_here]
+            down_first[:, side * width : (side + 1) * width] = block[rows_here:]
+
+
+def feed_grad_kernel(*refs):
+    hidden_ref, fed_ref, up_from, act_refs, grad_ref, act, up_ref, act_sems, up_sems = (
+        *refs[:3],
+        refs[3:7],
+        *refs[7:],
+    )
+    late = start_all([pltpu.make_async_copy(up_from, up_ref, up_sems.at[0])])
+    finish(load_rows(act_refs, act, act_sems) + late)
+    parts, rows_here, wide = grad_ref.shape
+    for at, (left, right) in enumerate([(act, hidden_ref), (fed_ref, up_ref)]):
+        lanes = slice(at * wide // 2, (at + 1) * wide // 2)
         for start in range(0, parts * rows_here, 2 * BLOCK):
             block = dot(left[:, start : start + 2 * BLOCK], right[...], 0, 0).astype(BF16)
             for sub in range(2 * BLOCK // rows_here):
                 grad_ref[start // rows_here + sub, :, lanes] = block[sub * rows_here : (sub + 1) * rows_here]
-    if parts == 8:
-        store_first(grad_ref, me_ref, up_first, down_first)
 
 
 def branch_back_kernel(*refs):
@@ -850,16 +872,16 @@
         [pltpu.VMEM((width, width), BF16), pltpu.VMEM((tok, width), BF16), dma(4), dma(4)],
         micros=2.4,
     )
-    act_two = hold(act_two, rest_ring.up, rest_ring.down)
     act_far, act_near = swap(act_two, 2), swap(act_two, 1)
     rest_ring.step(act_two)
     act_last = swap(act_far, 1)
     rest_ring.step(act_last)
-    grad_feed, up_first, down_first, own_two, far_two, send_two, fed = call(
+    up_first, down_first, own_two, far_two, send_two, fed, grad_hidden = call(
         functools.partial(feed_kernel, dp_count, count),
-        [shaped((dp_count, rows_here, 2 * width), BF16)] + [shaped((rows_here, 2 * width), BF16)] * 2
+        [shaped((rows_here, 2 * width), BF16)] * 2
         + [shaped((tok, width), F32)] * 2
-        + [shaped((2 * tok, width), BF16), shaped((seq_len, ff_part), BF16)],
+        + [shaped((2 * tok, width), BF16)]
+        + [shaped((seq_len, ff_part), BF16)] * 2,
         [],
         in_hbm([up_all, act_two, act_near, act_far, act_last, *rest_ring.pieces]),
         [me],
@@ -869,16 +891,24 @@
             pltpu.VMEM((width, ff_part), BF16),
             pltpu.VMEM((ff_part, width), BF16),
             pltpu.VMEM((seq_len, ff_part), F32),
-            pltpu.VMEM((seq_len, ff_part), BF16),
             dma(4),
             dma(1),
             dma(count),
             dma(count),
         ],
-        micros=9,
+        micros=7,
     )
 
     near_two = swap(send_two, 1)
+    (grad_feed,) = call(
+        feed_grad_kernel,
+        [shaped((dp_count, rows_here, 2 * width), BF16)],
+        [grad_hidden, fed],
+        in_hbm([up_all, act_two, act_near, act_far, act_last]),
+        (),
+        [pltpu.VMEM((seq_len, width), BF16)] * 2 + [dma(4), dma(1)],
+        micros=3,
+    )
     last_two = swap(add_far(far_two, near_two), 2)
     feed_grads = ScatterRing(grad_feed, (up_first, down_first), me, dp_count)
     feed_grads.step()

time: 195 us -> 193 us (0.990)
  waiting for transfers between devices: 93.1 us -> 89.2 us
  Pallas kernels: 49.7 us -> 51.9 us
    ppermute x16, waiting for transfers between devices: 45.1 us -> 41.1 us  [step(): self.up = lax.ppermute(up, 'dp', forward)]
    pallas_call x25 -> x26, Pallas kernels: 49.7 us -> 51.9 us  [call(): pl.pallas_call(kernel, out_shape=(*outs, *hbm_outs), in_specs=specs, out_...]
  transfers between devices with their start and end apart: 57 -> 57, of which waited for: 39 -> 39; matrix products, arithmetic and copies ran while one was open for 1% -> 1% of each run, Pallas kernels for 18% -> 20%
where the time goes in v6:
time: 193 us
  waiting for transfers between devices  89.2 us (46%)
  Pallas kernels  51.9 us (27%)
  starting transfers between devices  47.4 us (25%)
    pallas_call x26, Pallas kernels, call(): pl.pallas_call(kernel, out_shape=(*outs, *hbm_outs), in_specs=specs, out_...  51.9 us
    ppermute x16, waiting for transfers between devices, step(): self.up = lax.ppermute(up, 'dp', forward)  41.1 us
    ppermute x25, waiting for transfers between devices, swap(): return lax.ppermute(values, 'sp', [(i, i ^ bit) for i in range(count)])  33.3 us
    ppermute x16, starting transfers between devices, step(): self.up = lax.ppermute(up, 'dp', forward)  20.4 us
    ppermute x16, waiting for transfers between devices, step(): self.down = lax.ppermute(down, 'dp', backward)  14.8 us
    ppermute x16, starting transfers between devices, step(): self.down = lax.ppermute(down, 'dp', backward)  13.5 us
    ppermute x25, starting transfers between devices, swap(): return lax.ppermute(values, 'sp', [(i, i ^ bit) for i in range(count)])  13.5 us
  transfers between devices with their start and end apart: 57, of which 39 were waited for; matrix products, arithmetic and copies ran while one was open for 1% of the time, Pallas kernels for 20%

profile of v6, /device:TPU:0, one launch (start us, length us, event | category | flops | bytes accessed | tf_op | source)
XLA Modules:
  0.0 192.8 jit_solution(8827594495757244455)
XLA Ops:
  0.7 1.5 shard_map.178.refs_0_.refs_3_.refs_17_
  2.3 3.1 %collective-permute-start = (bf16[128,1024]{1,0:T(8,128)(2,1)S(1)}, bf16[128,1024]{1,0:T(8,128)(2,1)S(1)}, u32[]{:S(2)}, u32[]{:S(2)}) collective-permute-start(bf16[128,1024]{1,0:T(8,128)(2,1)S(1)} %shard_map.178.refs_0_.refs_3_.refs_17_), channel_id=1, source_target_pairs={{0,8},{8,16},{16,24},{24,28},{28,20},{20,12},{12,4},{4,0},{1,9},{9... | collective-permute-start | bytes 786440 | tf_op jit(solution)/shard_map/ppermute | solution.py:128
  5.4 1.1 pad_maximum_fusion.refs_2_
  6.4 2.0 %collective-permute-start.5 = (bf16[256,1024]{1,0:T(8,128)(2,1)S(1)}, bf16[256,1024]{1,0:T(8,128)(2,1)S(1)}, u32[]{:S(2)}, u32[]{:S(2)}) collective-permute-start(bf16[256,1024]{1,0:T(8,128)(2,1)S(1)} %pad_maximum_fusion.refs_2_), channel_id=1, source_target_pairs={{0,2},{1,3},{2,0},{3,1},{4,6},{5,7},{6,4},{7,5},{8,10},{9,11},{10,... | collective-permute-start | bytes 1572872 | tf_op jit(solution)/shard_map/ppermute | solution.py:235
  8.4 1.7 shard_map.180.refs_5_.refs_26_
  10.2 1.2 shard_map.179
  11.6 1.5 collective-permute-done.1.refs_2_.refs_5_.refs_19_
  13.1 1.6 collective-permute-start.2
  15.2 4.7 %collective-permute-done.5.refs_4_ = bf16[256,1024]{1,0:T(8,128)(2,1)S(1)} collective-permute-done((bf16[256,1024]{1,0:T(8,128)(2,1)S(1)}, bf16[256,1024]{1,0:T(8,128)(2,1)S(1)}, u32[]{:S(2)}, u32[]{:S(2)}) %collective-permute-start.5) | collective-permute-done | bytes 524320 | tf_op jit(solution)/shard_map/ppermute | solution.py:235
  20.0 1.3 collective-permute-done.3.refs_4_.refs_7_.refs_21_
  21.3 1.6 collective-permute-start.7
  23.3 4.3 %collective-permute-done.7.up_ref.refs_5_.refs_8_.refs_22_ = bf16[128,1024]{1,0:T(8,128)(2,1)S(1)} collective-permute-done((bf16[128,1024]{1,0:T(8,128)(2,1)S(1)}, bf16[128,1024]{1,0:T(8,128)(2,1)S(1)}, u32[]{:S(2)}, u32[]{:S(2)}) %collective-permute-start.7) | collective-permute-done | bytes 262176 | tf_op jit(solution)/shard_map/ppermute | solution.py:128
  27.7 1.6 collective-permute-done.8.down_ref.refs_6_.refs_9_.refs_23_
  29.6 1.6 collective-permute-start.9
  31.6 2.9 %collective-permute-done.9.refs_7_.refs_10_.refs_24_ = bf16[64,1024]{1,0:T(8,128)(2,1)S(1)} collective-permute-done((bf16[64,1024]{1,0:T(8,128)(2,1)S(1)}, bf16[64,1024]{1,0:T(8,128)(2,1)S(1)}, u32[]{:S(2)}, u32[]{:S(2)}) %collective-permute-start.9) | collective-permute-done | bytes 131104 | tf_op jit(solution)/shard_map/ppermute | solution.py:128
  34.6 1.6 collective-permute-done.10.refs_8_.refs_11_.refs_25_
  36.8 1.4 collective-permute-start.12
  39.0 1.6 collective-permute-start.17
  40.6 1.5 shard_map.181
  43.1 4.8 %shard_map.184 = (bf16[512,768]{1,0:T(8,128)(2,1)S(1)}, bf16[512,256]{1,0:T(8,128)(2,1)S(1)}, f32[8,256]{1,0:T(8,128)S(1)}) custom-call(bf16[512,1024]{1,0:T(8,128)(2,1)S(1)} %get-tuple-element.114.refs_0_.refs_4_, f32[4,4,128,128]{3,2,1,0:T(8,128)S(1)} %get-tuple-element.103.refs_1_.refs_2_, f32[4,512,128]{2,1,0:T(8,128)S(1)} %get-tuple-element.115.refs_2_.refs_3_, ...), custom_call_target="tpu_custom_call" | custom-call | bytes 16500000 | tf_op jit(solution)/shard_map/pallas_call | solution.py:60
  49.8 1.1 collective-permute-start.23
  50.9 5.8 %collective-permute-done.14.refs_5_.refs_11_ = bf16[512,256]{1,0:T(8,128)(2,1)S(1)} collective-permute-done((bf16[512,256]{1,0:T(8,128)(2,1)S(1)}, bf16[512,256]{1,0:T(8,128)(2,1)S(1)}, u32[]{:S(2)}, u32[]{:S(2)}) %collective-permute-start.14) | collective-permute-done | bytes 262176 | tf_op jit(solution)/shard_map/ppermute | solution.py:235
  56.7 1.5 collective-permute-done.15.refs_6_.refs_12_
  58.2 1.6 shard_map.185
  59.9 3.3 %collective-permute-done.22.refs_8_.refs_29_ = bf16[128,2048]{1,0:T(8,128)(2,1)S(1)} collective-permute-done((bf16[128,2048]{1,0:T(8,128)(2,1)S(1)}, bf16[128,2048]{1,0:T(8,128)(2,1)S(1)}, u32[]{:S(2)}, u32[]{:S(2)}) %collective-permute-start.22) | collective-permute-done | bytes 524320 | tf_op jit(solution)/shard_map/ppermute | solution.py:128
  64.8 1.1 collective-permute-start.25
  65.9 1.5 collective-permute-start.20
  67.4 5.6 %collective-permute-done.20.refs_3_.refs_5_ = bf16[128,1024]{1,0:T(8,128)(2,1)S(1)} collective-permute-done((bf16[128,1024]{1,0:T(8,128)(2,1)S(1)}, bf16[128,1024]{1,0:T(8,128)(2,1)S(1)}, u32[]{:S(2)}, u32[]{:S(2)}) %collective-permute-start.20) | collective-permute-done | bytes 262176 | tf_op jit(solution)/shard_map/ppermute | solution.py:235
  73.5 3.6 %collective-permute-done.24.up_ref.refs_10_.refs_31_ = bf16[128,2048]{1,0:T(8,128)(2,1)S(1)} collective-permute-done((bf16[128,2048]{1,0:T(8,128)(2,1)S(1)}, bf16[128,2048]{1,0:T(8,128)(2,1)S(1)}, u32[]{:S(2)}, u32[]{:S(2)}) %collective-permute-start.24) | collective-permute-done | bytes 524320 | tf_op jit(solution)/shard_map/ppermute | solution.py:128
  77.9 1.0 collective-permute-start.26
  78.9 1.1 collective-permute-start.27
  80.0 4.4 %collective-permute-done.26.refs_12_.refs_33_ = bf16[64,2048]{1,0:T(8,128)(2,1)S(1)} collective-permute-done((bf16[64,2048]{1,0:T(8,128)(2,1)S(1)}, bf16[64,2048]{1,0:T(8,128)(2,1)S(1)}, u32[]{:S(2)}, u32[]{:S(2)}) %collective-permute-start.26) | collective-permute-done | bytes 262176 | tf_op jit(solution)/shard_map/ppermute | solution.py:128
  86.0 7.8 %shard_map.187 = (bf16[128,2048]{1,0:T(8,128)(2,1)S(1)}, bf16[128,2048]{1,0:T(8,128)(2,1)S(1)}, f32[128,1024]{1,0:T(8,128)S(1)}, f32[128,1024]{1,0:T(8,128)S(1)}...) custom-call(bf16[512,1024]{1,0:T(8,128)(2,1)} %copy-done.3, ...), custom_call_target="tpu_custom_call" | custom-call | bytes 23100000 | tf_op jit(solution)/shard_map/pallas_call | solution.py:60
  94.6 1.4 collective-permute-start.31
  96.1 1.6 collective-permute-start.30
  97.6 4.0 %shard_map.188.refs_0_.parts = bf16[8,128,2048]{2,1,0:T(8,128)(2,1)S(1)} custom-call(bf16[512,1024]{1,0:T(8,128)(2,1)S(1)} %get-tuple-element.131.refs_0_, bf16[512,1024]{1,0:T(8,128)(2,1)S(1)} %get-tuple-element.132.refs_1_.refs_8_, bf16[512,1024]{1,0:T(8,128)(2,1)} %copy-done.3, bf16[128,1024]{1,0:T(8,128)(2,1)} %copy-done.5, ...), custom_call_target="tpu_custom_call" | custom-call | bytes 9900000 | tf_op jit(solution)/shard_map/pallas_call | solution.py:60
  101.6 6.6 %collective-permute-done.28.refs_1_ = bf16[128,2048]{1,0:T(8,128)(2,1)S(1)} collective-permute-done((bf16[128,2048]{1,0:T(8,128)(2,1)S(1)}, bf16[128,2048]{1,0:T(8,128)(2,1)S(1)}, u32[]{:S(2)}, u32[]{:S(2)}) %collective-permute-start.28) | collective-permute-done | bytes 524320 | tf_op jit(solution)/shard_map/ppermute | solution.py:210
  110.2 1.5 collective-permute-start.36
  111.7 2.4 %shard_map.191 = (f32[128,1024]{1,0:T(8,128)S(1)}, f32[8,1024]{1,0:T(8,128)S(1)}, bf16[128,512]{1,0:T(8,128)(2,1)S(1)}, bf16[128,512]{1,0:T(8,128)(2,1)S(1)}, bf...) custom-call(f32[128,1024]{1,0:T(8,128)S(1)} %get-tuple-element.141.refs_0_, ...), custom_call_target="tpu_custom_call" | custom-call | bytes 8250000 | tf_op jit(solution)/shard_map/pallas_call | solution.py:60
  114.2 1.6 collective-permute-start.34
  116.1 4.5 %collective-permute-done.34.refs_15_ = bf16[128,512]{1,0:T(8,128)(2,1)S(1)} collective-permute-done((bf16[128,512]{1,0:T(8,128)(2,1)S(1)}, bf16[128,512]{1,0:T(8,128)(2,1)S(1)}, u32[]{:S(2)}, u32[]{:S(2)}) %collective-permute-start.34) | collective-permute-done | bytes 131104 | tf_op jit(solution)/shard_map/ppermute | solution.py:235
  120.6 1.9 collective-permute-done.35.refs_16_
  125.1 1.2 collective-permute-start.38
  126.3 9.7 %shard_map.193 = (bf16[8,144,1024]{2,1,0:T(8,128)(2,1)S(1)}, bf16[144,1024]{1,0:T(8,128)(2,1)S(1)}, bf16[144,1024]{1,0:T(8,128)(2,1)S(1)}, f32[8,1024]{1,0:T(8,1...) custom-call(bf16[512,768]{1,0:T(8,128)(2,1)S(1)} %get-tuple-element., ...), custom_call_target="tpu_custom_call" | custom-call | bytes 31020000 | tf_op jit(solution)/shard_map/pallas_call | solution.py:60
  136.0 1.9 %collective-permute-done.37.refs_1_.up_ref = bf16[128,2048]{1,0:T(8,128)(2,1)S(1)} collective-permute-done((bf16[128,2048]{1,0:T(8,128)(2,1)S(1)}, bf16[128,2048]{1,0:T(8,128)(2,1)S(1)}, u32[]{:S(2)}, u32[]{:S(2)}) %collective-permute-start.37) | collective-permute-done | bytes 524320 | tf_op jit(solution)/shard_map/ppermute | solution.py:210
  139.1 1.1 collective-permute-start.41
  142.0 1.1 collective-permute-start.44
  143.2 4.9 %collective-permute-done.39.refs_1_ = bf16[144,1024]{1,0:T(8,128)(2,1)S(1)} collective-permute-done((bf16[144,1024]{1,0:T(8,128)(2,1)S(1)}, bf16[144,1024]{1,0:T(8,128)(2,1)S(1)}, u32[]{:S(2)}, u32[]{:S(2)}) %collective-permute-start.39) | collective-permute-done | bytes 294944 | tf_op jit(solution)/shard_map/ppermute | solution.py:210
  150.0 1.6 collective-permute-start.42
  152.2 1.2 collective-permute-start.48
  155.5 1.2 collective-permute-start.54
  156.7 2.9 %collective-permute-done.42.refs_1_ = bf16[144,1024]{1,0:T(8,128)(2,1)S(1)} collective-permute-done((bf16[144,1024]{1,0:T(8,128)(2,1)S(1)}, bf16[144,1024]{1,0:T(8,128)(2,1)S(1)}, u32[]{:S(2)}, u32[]{:S(2)}) %collective-permute-start.42) | collective-permute-done | bytes 294944 | tf_op jit(solution)/shard_map/ppermute | solution.py:210
  161.2 1.6 collective-permute-start.46
  163.3 3.9 %collective-permute-done.48.refs_1_ = bf16[256,1024]{1,0:T(8,128)(2,1)S(1)} collective-permute-done((bf16[256,1024]{1,0:T(8,128)(2,1)S(1)}, bf16[256,1024]{1,0:T(8,128)(2,1)S(1)}, u32[]{:S(2)}, u32[]{:S(2)}) %collective-permute-start.48) | collective-permute-done | bytes 524320 | tf_op jit(solution)/shard_map/ppermute | solution.py:235
  167.1 2.1 %collective-permute-done.46.refs_1_.up_ref = bf16[144,1024]{1,0:T(8,128)(2,1)S(1)} collective-permute-done((bf16[144,1024]{1,0:T(8,128)(2,1)S(1)}, bf16[144,1024]{1,0:T(8,128)(2,1)S(1)}, u32[]{:S(2)}, u32[]{:S(2)}) %collective-permute-start.46) | collective-permute-done | bytes 294944 | tf_op jit(solution)/shard_map/ppermute | solution.py:210
  169.3 1.4 collective-permute-done.47.refs_2_.down_ref
  171.4 1.8 collective-permute-start.49
  173.5 3.1 %collective-permute-done.49.last_up_ref = bf16[144,512]{1,0:T(8,128)(2,1)S(1)} collective-permute-done((bf16[144,512]{1,0:T(8,128)(2,1)S(1)}, bf16[144,512]{1,0:T(8,128)(2,1)S(1)}, u32[]{:S(2)}, u32[]{:S(2)}) %collective-permute-start.49) | collective-permute-done | bytes 147488 | tf_op jit(solution)/shard_map/ppermute | solution.py:210
  176.6 1.7 collective-permute-done.50.last_down_ref
  180.3 1.5 shard_map.201
  181.8 3.1 %shard_map.202 = (f32[128,4096]{1,0:T(8,128)}, f32[512,1024]{1,0:T(8,128)}) custom-call(bf16[128,2048]{1,0:T(8,128)(2,1)S(1)} %shard_map.197.refs_0_, bf16[128,2048]{1,0:T(8,128)(2,1)S(1)} %collective-permute-done.53.refs_1_, bf16[128,2048]{1,0:T(8,128)(2,1)S(1)} %collective-permute-done.54.refs_2_, bf16[128,2048]{1,0:T(8,128)(2,1)S(1)} %collective-permute-done.55.refs_3_, ...), custom_call_target="tpu_custom_call" | custom-call | bytes 9900000 | tf_op jit(solution)/shard_map/pallas_call | solution.py:60
  185.0 3.8 %collective-permute-done.52.refs_2_ = bf16[144,1024]{1,0:T(8,128)(2,1)S(1)} collective-permute-done((bf16[144,1024]{1,0:T(8,128)(2,1)S(1)}, bf16[144,1024]{1,0:T(8,128)(2,1)S(1)}, u32[]{:S(2)}, u32[]{:S(2)}) %collective-permute-start.52) | collective-permute-done | bytes 294944 | tf_op jit(solution)/shard_map/ppermute | solution.py:235
  188.7 1.6 collective-permute-done.56.refs_3_
  190.3 2.3 %shard_map.203 = (f32[128,3072]{1,0:T(8,128)}, f32[128,1024]{1,0:T(8,128)}, f32[2,128]{1,0:T(2,128)}, f32[2,128]{1,0:T(2,128)}, f32[1,64]{1,0:T(1,128)}) custom-call(bf16[144,1024]{1,0:T(8,128)(2,1)S(1)} %shard_map.200.refs_0_, bf16[144,1024]{1,0:T(8,128)(2,1)S(1)} %collective-permute-done.51.refs_1_, bf16[144,1024]{1,0:T(8,128)(2,1)S(1)} %collective-permute-done.52.refs_2_, ...), custom_call_target="tpu_custom_call" | custom-call | bytes 7589999 | tf_op jit(solution)/shard_map/pallas_call | solution.py:60
  (120 shorter events, 29.2 us)
Async XLA Ops:
  2.3 9.3 %collective-permute-start = (bf16[128,1024]{1,0:T(8,128)(2,1)S(1)}, bf16[128,1024]{1,0:T(8,128)(2,1)S(1)}, u32[]{:S(2)}, u32[]{:S(2)}) collective-permute-start(bf16[128,1024]{1,0:T(8,128)(2,1)S(1)} %shard_map.178.refs_0_.refs_3_.refs_17_), channel_id=1, source_target_pairs={{0,8},{8,16},{16,24},{24,28},{28,20},{20,12},{12,4},{4,0},{1,9},{9... | collective-permute-start | bytes 786440 | tf_op jit(solution)/shard_map/ppermute | solution.py:128
  5.4 7.8 %collective-permute-start.1 = (bf16[128,1024]{1,0:T(8,128)(2,1)S(1)}, bf16[128,1024]{1,0:T(8,128)(2,1)S(1)}, u32[]{:S(2)}, u32[]{:S(2)}) collective-permute-start(bf16[128,1024]{1,0:T(8,128)(2,1)S(1)} %shard_map.178.refs_0_.refs_3_.refs_17_), channel_id=1, source_target_pairs={{8,0},{16,8},{24,16},{28,24},{20,28},{12,20},{4,12},{0,4},{9,1},{1... | collective-permute-start | bytes 786440 | tf_op jit(solution)/shard_map/ppermute | solution.py:129
  6.4 13.4 %collective-permute-start.5 = (bf16[256,1024]{1,0:T(8,128)(2,1)S(1)}, bf16[256,1024]{1,0:T(8,128)(2,1)S(1)}, u32[]{:S(2)}, u32[]{:S(2)}) collective-permute-start(bf16[256,1024]{1,0:T(8,128)(2,1)S(1)} %pad_maximum_fusion.refs_2_), channel_id=1, source_target_pairs={{0,2},{1,3},{2,0},{3,1},{4,6},{5,7},{6,4},{7,5},{8,10},{9,11},{10,... | collective-permute-start | bytes 1572872 | tf_op jit(solution)/shard_map/ppermute | solution.py:235
  10.2 31.9 %copy-start.2 = (bf16[128,2048]{1,0:T(8,128)(2,1)}, bf16[128,2048]{1,0:T(8,128)(2,1)S(1)}, u32[]{:S(2)}) copy-start(bf16[128,2048]{1,0:T(8,128)(2,1)S(1)} %shard_map.180.refs_5_.refs_26_) | copy-start | bytes 1572868
  10.2 30.3 %copy-start.7 = (f32[2,1024]{1,0:T(2,128)S(1)}, f32[2,1024]{1,0:T(2,128)}, u32[]{:S(2)}) copy-start(f32[2,1024]{1,0:T(2,128)} %gain_ref.1) | copy-start | bytes 24580
  10.2 30.3 %copy-start.8 = (f32[2,1024]{1,0:T(2,128)S(1)}, f32[2,1024]{1,0:T(2,128)}, u32[]{:S(2)}) copy-start(f32[2,1024]{1,0:T(2,128)} %refs_2_.1) | copy-start | bytes 24580
  13.1 6.9 %collective-permute-start.2 = (bf16[128,1024]{1,0:T(8,128)(2,1)S(1)}, bf16[128,1024]{1,0:T(8,128)(2,1)S(1)}, u32[]{:S(2)}, u32[]{:S(2)}) collective-permute-start(bf16[128,1024]{1,0:T(8,128)(2,1)S(1)} %collective-permute-done.refs_1_.refs_4_.refs_18_), channel_id=1, source_target_pairs={{0,8},{8,16},{16,24},{24,28},{28,20},{20,12},{12,4},{4,0},{1,9},{9... | collective-permute-start | bytes 786440 | tf_op jit(solution)/shard_map/ppermute | solution.py:128
  14.7 6.6 %collective-permute-start.3 = (bf16[128,1024]{1,0:T(8,128)(2,1)S(1)}, bf16[128,1024]{1,0:T(8,128)(2,1)S(1)}, u32[]{:S(2)}, u32[]{:S(2)}) collective-permute-start(bf16[128,1024]{1,0:T(8,128)(2,1)S(1)} %collective-permute-done.1.refs_2_.refs_5_.refs_19_), channel_id=1, source_target_pairs={{8,0},{16,8},{24,16},{28,24},{20,28},{12,20},{4,12},{0,4},{9,1},{1... | collective-permute-start | bytes 786440 | tf_op jit(solution)/shard_map/ppermute | solution.py:129
  21.3 6.4 %collective-permute-start.7 = (bf16[128,1024]{1,0:T(8,128)(2,1)S(1)}, bf16[128,1024]{1,0:T(8,128)(2,1)S(1)}, u32[]{:S(2)}, u32[]{:S(2)}) collective-permute-start(bf16[128,1024]{1,0:T(8,128)(2,1)S(1)} %collective-permute-done.2.refs_3_.refs_6_.refs_20_), channel_id=1, source_target_pairs={{0,8},{8,16},{16,24},{24,28},{28,20},{20,12},{12,4},{4,0},{1,9},{9... | collective-permute-start | bytes 786440 | tf_op jit(solution)/shard_map/ppermute | solution.py:128
  22.9 6.4 %collective-permute-start.8 = (bf16[128,1024]{1,0:T(8,128)(2,1)S(1)}, bf16[128,1024]{1,0:T(8,128)(2,1)S(1)}, u32[]{:S(2)}, u32[]{:S(2)}) collective-permute-start(bf16[128,1024]{1,0:T(8,128)(2,1)S(1)} %collective-permute-done.3.refs_4_.refs_7_.refs_21_), channel_id=1, source_target_pairs={{8,0},{16,8},{24,16},{28,24},{20,28},{12,20},{4,12},{0,4},{9,1},{1... | collective-permute-start | bytes 786440 | tf_op jit(solution)/shard_map/ppermute | solution.py:129
  23.3 17.2 %collective-permute-start.4 = (bf16[256,1024]{1,0:T(8,128)(2,1)S(1)}, bf16[256,1024]{1,0:T(8,128)(2,1)S(1)}, u32[]{:S(2)}, u32[]{:S(2)}) collective-permute-start(bf16[256,1024]{1,0:T(8,128)(2,1)S(1)} %pad_maximum_fusion.refs_2_), channel_id=1, source_target_pairs={{0,1},{1,0},{2,3},{3,2},{4,5},{5,4},{6,7},{7,6},{8,9},{9,8},{10,11... | collective-permute-start | bytes 1572872 | tf_op jit(solution)/shard_map/ppermute | solution.py:235
  29.6 5.0 %collective-permute-start.9 = (bf16[64,1024]{1,0:T(8,128)(2,1)S(1)}, bf16[64,1024]{1,0:T(8,128)(2,1)S(1)}, u32[]{:S(2)}, u32[]{:S(2)}) collective-permute-start(bf16[64,1024]{1,0:T(8,128)(2,1)S(1)} %get-tuple-element.112), channel_id=1, source_target_pairs={{0,8},{8,16},{16,24},{24,28},{28,20},{20,12},{12,4},{4,0},{1,9},{9... | collective-permute-start | bytes 393224 | tf_op jit(solution)/shard_map/ppermute | solution.py:128
  31.1 5.0 %collective-permute-start.10 = (bf16[64,1024]{1,0:T(8,128)(2,1)S(1)}, bf16[64,1024]{1,0:T(8,128)(2,1)S(1)}, u32[]{:S(2)}, u32[]{:S(2)}) collective-permute-start(bf16[64,1024]{1,0:T(8,128)(2,1)S(1)} %get-tuple-element.113), channel_id=1, source_target_pairs={{8,0},{16,8},{24,16},{28,24},{20,28},{12,20},{4,12},{0,4},{9,1},{1... | collective-permute-start | bytes 393224 | tf_op jit(solution)/shard_map/ppermute | solution.py:129
  31.6 8.9 %collective-permute-start.6 = (bf16[256,1024]{1,0:T(8,128)(2,1)S(1)}, bf16[256,1024]{1,0:T(8,128)(2,1)S(1)}, u32[]{:S(2)}, u32[]{:S(2)}) collective-permute-start(bf16[256,1024]{1,0:T(8,128)(2,1)S(1)} %collective-permute-done.5.refs_4_), channel_id=1, source_target_pairs={{0,1},{1,0},{2,3},{3,2},{4,5},{5,4},{6,7},{7,6},{8,9},{9,8},{10,11... | collective-permute-start | bytes 1572872 | tf_op jit(solution)/shard_map/ppermute | solution.py:235
  36.2 11.7 %collective-permute-start.11 = (bf16[128,2048]{1,0:T(8,128)(2,1)S(1)}, bf16[128,2048]{1,0:T(8,128)(2,1)S(1)}, u32[]{:S(2)}, u32[]{:S(2)}) collective-permute-start(bf16[128,2048]{1,0:T(8,128)(2,1)S(1)} %shard_map.180.refs_5_.refs_26_), channel_id=1, source_target_pairs={{0,8},{8,16},{16,24},{24,28},{28,20},{20,12},{12,4},{4,0},{1,9},{9... | collective-permute-start | bytes 1572872 | tf_op jit(solution)/shard_map/ppermute | solution.py:128
  36.8 11.1 %collective-permute-start.12 = (bf16[128,2048]{1,0:T(8,128)(2,1)S(1)}, bf16[128,2048]{1,0:T(8,128)(2,1)S(1)}, u32[]{:S(2)}, u32[]{:S(2)}) collective-permute-start(bf16[128,2048]{1,0:T(8,128)(2,1)S(1)} %shard_map.180.refs_5_.refs_26_), channel_id=1, source_target_pairs={{8,0},{16,8},{24,16},{28,24},{20,28},{12,20},{4,12},{0,4},{9,1},{1... | collective-permute-start | bytes 1572872 | tf_op jit(solution)/shard_map/ppermute | solution.py:129
  39.0 9.9 %collective-permute-start.17 = (bf16[1024,256]{1,0:T(8,128)(2,1)S(1)}, bf16[1024,256]{1,0:T(8,128)(2,1)S(1)}, u32[]{:S(2)}, u32[]{:S(2)}) collective-permute-start(bf16[1024,256]{1,0:T(8,128)(2,1)S(1)} %shard_map.183.refs_7_.refs_6_), channel_id=1, source_target_pairs={{0,2},{1,3},{2,0},{3,1},{4,6},{5,7},{6,4},{7,5},{8,10},{9,11},{10,... | collective-permute-start | bytes 1572872 | tf_op jit(solution)/shard_map/ppermute | solution.py:235
  40.5 10.3 %collective-permute-start.16 = (bf16[1024,256]{1,0:T(8,128)(2,1)S(1)}, bf16[1024,256]{1,0:T(8,128)(2,1)S(1)}, u32[]{:S(2)}, u32[]{:S(2)}) collective-permute-start(bf16[1024,256]{1,0:T(8,128)(2,1)S(1)} %shard_map.183.refs_7_.refs_6_), channel_id=1, source_target_pairs={{0,1},{1,0},{2,3},{3,2},{4,5},{5,4},{6,7},{7,6},{8,9},{9,8},{10,11... | collective-permute-start | bytes 1572872 | tf_op jit(solution)/shard_map/ppermute | solution.py:235
  47.9 30.0 %copy-start.12 = (bf16[128,2048]{1,0:T(8,128)(2,1)}, bf16[128,2048]{1,0:T(8,128)(2,1)S(1)}, u32[]{:S(2)}) copy-start(bf16[128,2048]{1,0:T(8,128)(2,1)S(1)} %collective-permute-done.11.refs_6_.refs_27_) | copy-start | bytes 1572868
  47.9 30.0 %copy-start.13 = (bf16[128,2048]{1,0:T(8,128)(2,1)}, bf16[128,2048]{1,0:T(8,128)(2,1)S(1)}, u32[]{:S(2)}) copy-start(bf16[128,2048]{1,0:T(8,128)(2,1)S(1)} %collective-permute-done.12.refs_7_.refs_28_) | copy-start | bytes 1572868
  47.9 8.8 %collective-permute-start.14 = (bf16[512,256]{1,0:T(8,128)(2,1)S(1)}, bf16[512,256]{1,0:T(8,128)(2,1)S(1)}, u32[]{:S(2)}, u32[]{:S(2)}) collective-permute-start(bf16[512,256]{1,0:T(8,128)(2,1)S(1)} %get-tuple-element.121.refs_3_.refs_9_), channel_id=1, source_target_pairs={{0,2},{1,3},{2,0},{3,1},{4,6},{5,7},{6,4},{7,5},{8,10},{9,11},{10,... | collective-permute-start | bytes 786440 | tf_op jit(solution)/shard_map/ppermute | solution.py:235
  48.8 9.4 %collective-permute-start.18 = (bf16[1024,256]{1,0:T(8,128)(2,1)S(1)}, bf16[1024,256]{1,0:T(8,128)(2,1)S(1)}, u32[]{:S(2)}, u32[]{:S(2)}) collective-permute-start(bf16[1024,256]{1,0:T(8,128)(2,1)S(1)} %collective-permute-done.17.refs_9_.refs_8_), channel_id=1, source_target_pairs={{0,1},{1,0},{2,3},{3,2},{4,5},{5,4},{6,7},{7,6},{8,9},{9,8},{10,11... | collective-permute-start | bytes 1572872 | tf_op jit(solution)/shard_map/ppermute | solution.py:235
  48.8 14.3 %collective-permute-start.22 = (bf16[128,2048]{1,0:T(8,128)(2,1)S(1)}, bf16[128,2048]{1,0:T(8,128)(2,1)S(1)}, u32[]{:S(2)}, u32[]{:S(2)}) collective-permute-start(bf16[128,2048]{1,0:T(8,128)(2,1)S(1)} %collective-permute-done.11.refs_6_.refs_27_), channel_id=1, source_target_pairs={{0,8},{8,16},{16,24},{24,28},{28,20},{20,12},{12,4},{4,0},{1,9},{9... | collective-permute-start | bytes 1572872 | tf_op jit(solution)/shard_map/ppermute | solution.py:128
  49.8 14.1 %collective-permute-start.23 = (bf16[128,2048]{1,0:T(8,128)(2,1)S(1)}, bf16[128,2048]{1,0:T(8,128)(2,1)S(1)}, u32[]{:S(2)}, u32[]{:S(2)}) collective-permute-start(bf16[128,2048]{1,0:T(8,128)(2,1)S(1)} %collective-permute-done.12.refs_7_.refs_28_), channel_id=1, source_target_pairs={{8,0},{16,8},{24,16},{28,24},{20,28},{12,20},{4,12},{0,4},{9,1},{1... | collective-permute-start | bytes 1572872 | tf_op jit(solution)/shard_map/ppermute | solution.py:129
  50.9 5.8 %collective-permute-start.13 = (bf16[512,256]{1,0:T(8,128)(2,1)S(1)}, bf16[512,256]{1,0:T(8,128)(2,1)S(1)}, u32[]{:S(2)}, u32[]{:S(2)}) collective-permute-start(bf16[512,256]{1,0:T(8,128)(2,1)S(1)} %get-tuple-element.121.refs_3_.refs_9_), channel_id=1, source_target_pairs={{0,1},{1,0},{2,3},{3,2},{4,5},{5,4},{6,7},{7,6},{8,9},{9,8},{10,11... | collective-permute-start | bytes 786440 | tf_op jit(solution)/shard_map/ppermute | solution.py:235
  56.7 1.5 collective-permute-start.15
  59.9 25.4 %copy-start.5 = (bf16[128,1024]{1,0:T(8,128)(2,1)}, bf16[128,1024]{1,0:T(8,128)(2,1)S(1)}, u32[]{:S(2)}) copy-start(bf16[128,1024]{1,0:T(8,128)(2,1)S(1)} %get-tuple-element.122.refs_1_.refs_3_) | copy-start | bytes 786436
  63.2 22.1 %copy-start.14 = (bf16[128,2048]{1,0:T(8,128)(2,1)}, bf16[128,2048]{1,0:T(8,128)(2,1)S(1)}, u32[]{:S(2)}) copy-start(bf16[128,2048]{1,0:T(8,128)(2,1)S(1)} %collective-permute-done.22.refs_8_.refs_29_) | copy-start | bytes 1572868
  63.9 13.2 %collective-permute-start.24 = (bf16[128,2048]{1,0:T(8,128)(2,1)S(1)}, bf16[128,2048]{1,0:T(8,128)(2,1)S(1)}, u32[]{:S(2)}, u32[]{:S(2)}) collective-permute-start(bf16[128,2048]{1,0:T(8,128)(2,1)S(1)} %collective-permute-done.22.refs_8_.refs_29_), channel_id=1, source_target_pairs={{0,8},{8,16},{16,24},{24,28},{28,20},{20,12},{12,4},{4,0},{1,9},{9... | collective-permute-start | bytes 1572872 | tf_op jit(solution)/shard_map/ppermute | solution.py:128
  64.8 13.0 %collective-permute-start.25 = (bf16[128,2048]{1,0:T(8,128)(2,1)S(1)}, bf16[128,2048]{1,0:T(8,128)(2,1)S(1)}, u32[]{:S(2)}, u32[]{:S(2)}) collective-permute-start(bf16[128,2048]{1,0:T(8,128)(2,1)S(1)} %collective-permute-done.23.refs_9_.refs_30_), channel_id=1, source_target_pairs={{8,0},{16,8},{24,16},{28,24},{20,28},{12,20},{4,12},{0,4},{9,1},{1... | collective-permute-start | bytes 1572872 | tf_op jit(solution)/shard_map/ppermute | solution.py:129
  65.9 7.1 %collective-permute-start.20 = (bf16[128,1024]{1,0:T(8,128)(2,1)S(1)}, bf16[128,1024]{1,0:T(8,128)(2,1)S(1)}, u32[]{:S(2)}, u32[]{:S(2)}) collective-permute-start(bf16[128,1024]{1,0:T(8,128)(2,1)S(1)} %get-tuple-element.122.refs_1_.refs_3_), channel_id=1, source_target_pairs={{0,2},{1,3},{2,0},{3,1},{4,6},{5,7},{6,4},{7,5},{8,10},{9,11},{10,... | collective-permute-start | bytes 786440 | tf_op jit(solution)/shard_map/ppermute | solution.py:235
  73.0 4.9 %collective-permute-start.21 = (bf16[128,1024]{1,0:T(8,128)(2,1)S(1)}, bf16[128,1024]{1,0:T(8,128)(2,1)S(1)}, u32[]{:S(2)}, u32[]{:S(2)}) collective-permute-start(bf16[128,1024]{1,0:T(8,128)(2,1)S(1)} %collective-permute-done.20.refs_3_.refs_5_), channel_id=1, source_target_pairs={{0,1},{1,0},{2,3},{3,2},{4,5},{5,4},{6,7},{7,6},{8,9},{9,8},{10,11... | collective-permute-start | bytes 786440 | tf_op jit(solution)/shard_map/ppermute | solution.py:235
  73.0 7.0 %collective-permute-start.19 = (bf16[128,1024]{1,0:T(8,128)(2,1)S(1)}, bf16[128,1024]{1,0:T(8,128)(2,1)S(1)}, u32[]{:S(2)}, u32[]{:S(2)}) collective-permute-start(bf16[128,1024]{1,0:T(8,128)(2,1)S(1)} %get-tuple-element.122.refs_1_.refs_3_), channel_id=1, source_target_pairs={{0,1},{1,0},{2,3},{3,2},{4,5},{5,4},{6,7},{7,6},{8,9},{9,8},{10,11... | collective-permute-start | bytes 786440 | tf_op jit(solution)/shard_map/ppermute | solution.py:235
  77.9 6.5 %collective-permute-start.26 = (bf16[64,2048]{1,0:T(8,128)(2,1)S(1)}, bf16[64,2048]{1,0:T(8,128)(2,1)S(1)}, u32[]{:S(2)}, u32[]{:S(2)}) collective-permute-start(bf16[64,2048]{1,0:T(8,128)(2,1)S(1)} %get-tuple-element.129), channel_id=1, source_target_pairs={{0,8},{8,16},{16,24},{24,28},{28,20},{20,12},{12,4},{4,0},{1,9},{9... | collective-permute-start | bytes 786440 | tf_op jit(solution)/shard_map/ppermute | solution.py:128
  78.9 6.4 %collective-permute-start.27 = (bf16[64,2048]{1,0:T(8,128)(2,1)S(1)}, bf16[64,2048]{1,0:T(8,128)(2,1)S(1)}, u32[]{:S(2)}, u32[]{:S(2)}) collective-permute-start(bf16[64,2048]{1,0:T(8,128)(2,1)S(1)} %get-tuple-element.130), channel_id=1, source_target_pairs={{8,0},{16,8},{24,16},{28,24},{20,28},{12,20},{4,12},{0,4},{9,1},{1... | collective-permute-start | bytes 786440 | tf_op jit(solution)/shard_map/ppermute | solution.py:129
  93.8 2.2 %collective-permute-start.29 = (bf16[256,1024]{1,0:T(8,128)(2,1)S(1)}, bf16[256,1024]{1,0:T(8,128)(2,1)S(1)}, u32[]{:S(2)}, u32[]{:S(2)}) collective-permute-start(bf16[256,1024]{1,0:T(8,128)(2,1)S(1)} %get-tuple-element.135), channel_id=1, source_target_pairs={{0,1},{1,0},{2,3},{3,2},{4,5},{5,4},{6,7},{7,6},{8,9},{9,8},{10,11... | collective-permute-start | bytes 1572872 | tf_op jit(solution)/shard_map/ppermute | solution.py:235
  93.9 14.3 %collective-permute-start.28 = (bf16[128,2048]{1,0:T(8,128)(2,1)S(1)}, bf16[128,2048]{1,0:T(8,128)(2,1)S(1)}, u32[]{:S(2)}, u32[]{:S(2)}) collective-permute-start(bf16[128,2048]{1,0:T(8,128)(2,1)S(1)} %get-tuple-element.133), channel_id=1, source_target_pairs={{0,8},{8,16},{16,24},{24,28},{28,20},{20,12},{12,4},{4,0},{1,9},{9... | collective-permute-start | bytes 1572872 | tf_op jit(solution)/shard_map/ppermute | solution.py:210
  94.6 14.0 %collective-permute-start.31 = (bf16[128,2048]{1,0:T(8,128)(2,1)S(1)}, bf16[128,2048]{1,0:T(8,128)(2,1)S(1)}, u32[]{:S(2)}, u32[]{:S(2)}) collective-permute-start(bf16[128,2048]{1,0:T(8,128)(2,1)S(1)} %get-tuple-element.137), channel_id=1, source_target_pairs={{8,0},{16,8},{24,16},{28,24},{20,28},{12,20},{4,12},{0,4},{9,1},{1... | collective-permute-start | bytes 1572872 | tf_op jit(solution)/shard_map/ppermute | solution.py:211
  96.1 12.2 %collective-permute-start.30 = (bf16[128,1024]{1,0:T(8,128)(2,1)S(1)}, bf16[128,1024]{1,0:T(8,128)(2,1)S(1)}, u32[]{:S(2)}, u32[]{:S(2)}) collective-permute-start(bf16[128,1024]{1,0:T(8,128)(2,1)S(1)} %shard_map.189), channel_id=1, source_target_pairs={{0,2},{1,3},{2,0},{3,1},{4,6},{5,7},{6,4},{7,5},{8,10},{9,11},{10,... | collective-permute-start | bytes 786440 | tf_op jit(solution)/shard_map/ppermute | solution.py:235
  109.6 13.2 %collective-permute-start.32 = (bf16[128,2048]{1,0:T(8,128)(2,1)S(1)}, bf16[128,2048]{1,0:T(8,128)(2,1)S(1)}, u32[]{:S(2)}, u32[]{:S(2)}) collective-permute-start(bf16[128,2048]{1,0:T(8,128)(2,1)S(1)} %get-tuple-element.138), channel_id=1, source_target_pairs={{0,8},{8,16},{16,24},{24,28},{28,20},{20,12},{12,4},{4,0},{1,9},{9... | collective-permute-start | bytes 1572872 | tf_op jit(solution)/shard_map/ppermute | solution.py:210
  110.2 13.0 %collective-permute-start.36 = (bf16[128,2048]{1,0:T(8,128)(2,1)S(1)}, bf16[128,2048]{1,0:T(8,128)(2,1)S(1)}, u32[]{:S(2)}, u32[]{:S(2)}) collective-permute-start(bf16[128,2048]{1,0:T(8,128)(2,1)S(1)} %get-tuple-element.140), channel_id=1, source_target_pairs={{8,0},{16,8},{24,16},{28,24},{20,28},{12,20},{4,12},{0,4},{9,1},{1... | collective-permute-start | bytes 1572872 | tf_op jit(solution)/shard_map/ppermute | solution.py:211
  114.1 1.9 %collective-permute-start.33 = (bf16[128,512]{1,0:T(8,128)(2,1)S(1)}, bf16[128,512]{1,0:T(8,128)(2,1)S(1)}, u32[]{:S(2)}, u32[]{:S(2)}) collective-permute-start(bf16[128,512]{1,0:T(8,128)(2,1)S(1)} %get-tuple-element.143), channel_id=1, source_target_pairs={{0,1},{1,0},{2,3},{3,2},{4,5},{5,4},{6,7},{7,6},{8,9},{9,8},{10,11... | collective-permute-start | bytes 393224 | tf_op jit(solution)/shard_map/ppermute | solution.py:235
  114.2 6.4 %collective-permute-start.34 = (bf16[128,512]{1,0:T(8,128)(2,1)S(1)}, bf16[128,512]{1,0:T(8,128)(2,1)S(1)}, u32[]{:S(2)}, u32[]{:S(2)}) collective-permute-start(bf16[128,512]{1,0:T(8,128)(2,1)S(1)} %get-tuple-element.144), channel_id=1, source_target_pairs={{0,2},{1,3},{2,0},{3,1},{4,6},{5,7},{6,4},{7,5},{8,10},{9,11},{10,... | collective-permute-start | bytes 393224 | tf_op jit(solution)/shard_map/ppermute | solution.py:235
  115.8 6.7 %collective-permute-start.35 = (bf16[128,512]{1,0:T(8,128)(2,1)S(1)}, bf16[128,512]{1,0:T(8,128)(2,1)S(1)}, u32[]{:S(2)}, u32[]{:S(2)}) collective-permute-start(bf16[128,512]{1,0:T(8,128)(2,1)S(1)} %get-tuple-element.145), channel_id=1, source_target_pairs={{0,3},{1,2},{2,1},{3,0},{4,7},{5,6},{6,5},{7,4},{8,11},{9,10},{10,... | collective-permute-start | bytes 393224 | tf_op jit(solution)/shard_map/ppermute | solution.py:235
  124.2 13.8 %collective-permute-start.37 = (bf16[128,2048]{1,0:T(8,128)(2,1)S(1)}, bf16[128,2048]{1,0:T(8,128)(2,1)S(1)}, u32[]{:S(2)}, u32[]{:S(2)}) collective-permute-start(bf16[128,2048]{1,0:T(8,128)(2,1)S(1)} %get-tuple-element.147), channel_id=1, source_target_pairs={{0,8},{8,16},{16,24},{24,28},{28,20},{20,12},{12,4},{4,0},{1,9},{9... | collective-permute-start | bytes 1572872 | tf_op jit(solution)/shard_map/ppermute | solution.py:210
  125.1 13.1 %collective-permute-start.38 = (bf16[128,2048]{1,0:T(8,128)(2,1)S(1)}, bf16[128,2048]{1,0:T(8,128)(2,1)S(1)}, u32[]{:S(2)}, u32[]{:S(2)}) collective-permute-start(bf16[128,2048]{1,0:T(8,128)(2,1)S(1)} %get-tuple-element.148), channel_id=1, source_target_pairs={{8,0},{16,8},{24,16},{28,24},{20,28},{12,20},{4,12},{0,4},{9,1},{1... | collective-permute-start | bytes 1572872 | tf_op jit(solution)/shard_map/ppermute | solution.py:211
  138.3 9.8 %collective-permute-start.40 = (bf16[512,1024]{1,0:T(8,128)(2,1)S(1)}, bf16[512,1024]{1,0:T(8,128)(2,1)S(1)}, u32[]{:S(2)}, u32[]{:S(2)}) collective-permute-start(bf16[512,1024]{1,0:T(8,128)(2,1)S(1)} %get-tuple-element.162), channel_id=1, source_target_pairs={{0,1},{1,0},{2,3},{3,2},{4,5},{5,4},{6,7},{7,6},{8,9},{9,8},{10,11... | collective-permute-start | bytes 3145736 | tf_op jit(solution)/shard_map/ppermute | solution.py:235
  138.3 9.8 %collective-permute-start.39 = (bf16[144,1024]{1,0:T(8,128)(2,1)S(1)}, bf16[144,1024]{1,0:T(8,128)(2,1)S(1)}, u32[]{:S(2)}, u32[]{:S(2)}) collective-permute-start(bf16[144,1024]{1,0:T(8,128)(2,1)S(1)} %get-tuple-element.158), channel_id=1, source_target_pairs={{0,8},{8,16},{16,24},{24,28},{28,20},{20,12},{12,4},{4,0},{1,9},{9... | collective-permute-start | bytes 884744 | tf_op jit(solution)/shard_map/ppermute | solution.py:210
  139.1 9.8 %collective-permute-start.41 = (bf16[144,1024]{1,0:T(8,128)(2,1)S(1)}, bf16[144,1024]{1,0:T(8,128)(2,1)S(1)}, u32[]{:S(2)}, u32[]{:S(2)}) collective-permute-start(bf16[144,1024]{1,0:T(8,128)(2,1)S(1)} %get-tuple-element.164), channel_id=1, source_target_pairs={{8,0},{16,8},{24,16},{28,24},{20,28},{12,20},{4,12},{0,4},{9,1},{1... | collective-permute-start | bytes 884744 | tf_op jit(solution)/shard_map/ppermute | solution.py:211
  141.1 12.6 %collective-permute-start.43 = (bf16[128,1024]{1,0:T(8,128)(2,1)S(1)}, bf16[128,1024]{1,0:T(8,128)(2,1)S(1)}, u32[]{:S(2)}, u32[]{:S(2)}) collective-permute-start(bf16[128,1024]{1,0:T(8,128)(2,1)S(1)} %get-tuple-element.159), channel_id=1, source_target_pairs={{0,8},{8,16},{16,24},{24,28},{28,20},{20,12},{12,4},{4,0},{1,9},{9... | collective-permute-start | bytes 786440 | tf_op jit(solution)/shard_map/ppermute | solution.py:210
  142.0 12.6 %collective-permute-start.44 = (bf16[128,1024]{1,0:T(8,128)(2,1)S(1)}, bf16[128,1024]{1,0:T(8,128)(2,1)S(1)}, u32[]{:S(2)}, u32[]{:S(2)}) collective-permute-start(bf16[128,1024]{1,0:T(8,128)(2,1)S(1)} %get-tuple-element.160), channel_id=1, source_target_pairs={{8,0},{16,8},{24,16},{28,24},{20,28},{12,20},{4,12},{0,4},{9,1},{1... | collective-permute-start | bytes 786440 | tf_op jit(solution)/shard_map/ppermute | solution.py:211
  150.0 9.6 %collective-permute-start.42 = (bf16[144,1024]{1,0:T(8,128)(2,1)S(1)}, bf16[144,1024]{1,0:T(8,128)(2,1)S(1)}, u32[]{:S(2)}, u32[]{:S(2)}) collective-permute-start(bf16[144,1024]{1,0:T(8,128)(2,1)S(1)} %get-tuple-element.165), channel_id=1, source_target_pairs={{0,8},{8,16},{16,24},{24,28},{28,20},{20,12},{12,4},{4,0},{1,9},{9... | collective-permute-start | bytes 884744 | tf_op jit(solution)/shard_map/ppermute | solution.py:210
  151.6 8.6 %collective-permute-start.45 = (bf16[144,1024]{1,0:T(8,128)(2,1)S(1)}, bf16[144,1024]{1,0:T(8,128)(2,1)S(1)}, u32[]{:S(2)}, u32[]{:S(2)}) collective-permute-start(bf16[144,1024]{1,0:T(8,128)(2,1)S(1)} %get-tuple-element.167), channel_id=1, source_target_pairs={{8,0},{16,8},{24,16},{28,24},{20,28},{12,20},{4,12},{0,4},{9,1},{1... | collective-permute-start | bytes 884744 | tf_op jit(solution)/shard_map/ppermute | solution.py:211
  152.2 14.9 %collective-permute-start.48 = (bf16[256,1024]{1,0:T(8,128)(2,1)S(1)}, bf16[256,1024]{1,0:T(8,128)(2,1)S(1)}, u32[]{:S(2)}, u32[]{:S(2)}) collective-permute-start(bf16[256,1024]{1,0:T(8,128)(2,1)S(1)} %shard_map.196), channel_id=1, source_target_pairs={{0,2},{1,3},{2,0},{3,1},{4,6},{5,7},{6,4},{7,5},{8,10},{9,11},{10,... | collective-permute-start | bytes 1572872 | tf_op jit(solution)/shard_map/ppermute | solution.py:235
  155.5 23.7 %collective-permute-start.54 = (bf16[128,2048]{1,0:T(8,128)(2,1)S(1)}, bf16[128,2048]{1,0:T(8,128)(2,1)S(1)}, u32[]{:S(2)}, u32[]{:S(2)}) collective-permute-start(bf16[128,2048]{1,0:T(8,128)(2,1)S(1)} %shard_map.197.refs_0_), channel_id=1, source_target_pairs={{0,2},{1,3},{2,0},{3,1},{4,6},{5,7},{6,4},{7,5},{8,10},{9,11},{10,... | collective-permute-start | bytes 1572872 | tf_op jit(solution)/shard_map/ppermute | solution.py:235
  161.2 8.1 %collective-permute-start.46 = (bf16[144,1024]{1,0:T(8,128)(2,1)S(1)}, bf16[144,1024]{1,0:T(8,128)(2,1)S(1)}, u32[]{:S(2)}, u32[]{:S(2)}) collective-permute-start(bf16[144,1024]{1,0:T(8,128)(2,1)S(1)} %get-tuple-element.171), channel_id=1, source_target_pairs={{0,8},{8,16},{16,24},{24,28},{28,20},{20,12},{12,4},{4,0},{1,9},{9... | collective-permute-start | bytes 884744 | tf_op jit(solution)/shard_map/ppermute | solution.py:210
  162.8 7.8 %collective-permute-start.47 = (bf16[144,1024]{1,0:T(8,128)(2,1)S(1)}, bf16[144,1024]{1,0:T(8,128)(2,1)S(1)}, u32[]{:S(2)}, u32[]{:S(2)}) collective-permute-start(bf16[144,1024]{1,0:T(8,128)(2,1)S(1)} %get-tuple-element.172), channel_id=1, source_target_pairs={{8,0},{16,8},{24,16},{28,24},{20,28},{12,20},{4,12},{0,4},{9,1},{1... | collective-permute-start | bytes 884744 | tf_op jit(solution)/shard_map/ppermute | solution.py:211
  171.4 5.2 %collective-permute-start.49 = (bf16[144,512]{1,0:T(8,128)(2,1)S(1)}, bf16[144,512]{1,0:T(8,128)(2,1)S(1)}, u32[]{:S(2)}, u32[]{:S(2)}) collective-permute-start(bf16[144,512]{1,0:T(8,128)(2,1)S(1)} %get-tuple-element.174), channel_id=1, source_target_pairs={{0,8},{8,16},{16,24},{24,28},{28,20},{20,12},{12,4},{4,0},{1,9},{9... | collective-permute-start | bytes 442376 | tf_op jit(solution)/shard_map/ppermute | solution.py:210
  173.2 5.1 %collective-permute-start.50 = (bf16[144,512]{1,0:T(8,128)(2,1)S(1)}, bf16[144,512]{1,0:T(8,128)(2,1)S(1)}, u32[]{:S(2)}, u32[]{:S(2)}) collective-permute-start(bf16[144,512]{1,0:T(8,128)(2,1)S(1)} %get-tuple-element.175), channel_id=1, source_target_pairs={{8,0},{16,8},{24,16},{28,24},{20,28},{12,20},{4,12},{0,4},{9,1},{1... | collective-permute-start | bytes 442376 | tf_op jit(solution)/shard_map/ppermute | solution.py:211
  173.5 8.3 %collective-permute-start.53 = (bf16[128,2048]{1,0:T(8,128)(2,1)S(1)}, bf16[128,2048]{1,0:T(8,128)(2,1)S(1)}, u32[]{:S(2)}, u32[]{:S(2)}) collective-permute-start(bf16[128,2048]{1,0:T(8,128)(2,1)S(1)} %shard_map.197.refs_0_), channel_id=1, source_target_pairs={{0,1},{1,0},{2,3},{3,2},{4,5},{5,4},{6,7},{7,6},{8,9},{9,8},{10,11... | collective-permute-start | bytes 1572872 | tf_op jit(solution)/shard_map/ppermute | solution.py:235
  179.2 2.6 %collective-permute-start.55 = (bf16[128,2048]{1,0:T(8,128)(2,1)S(1)}, bf16[128,2048]{1,0:T(8,128)(2,1)S(1)}, u32[]{:S(2)}, u32[]{:S(2)}) collective-permute-start(bf16[128,2048]{1,0:T(8,128)(2,1)S(1)} %collective-permute-done.54.refs_2_), channel_id=1, source_target_pairs={{0,1},{1,0},{2,3},{3,2},{4,5},{5,4},{6,7},{7,6},{8,9},{9,8},{10,11... | collective-permute-start | bytes 1572872 | tf_op jit(solution)/shard_map/ppermute | solution.py:235
  179.3 9.4 %collective-permute-start.52 = (bf16[144,1024]{1,0:T(8,128)(2,1)S(1)}, bf16[144,1024]{1,0:T(8,128)(2,1)S(1)}, u32[]{:S(2)}, u32[]{:S(2)}) collective-permute-start(bf16[144,1024]{1,0:T(8,128)(2,1)S(1)} %shard_map.200.refs_0_), channel_id=1, source_target_pairs={{0,2},{1,3},{2,0},{3,1},{4,6},{5,7},{6,4},{7,5},{8,10},{9,11},{10,... | collective-permute-start | bytes 884744 | tf_op jit(solution)/shard_map/ppermute | solution.py:235
  180.1 8.6 %collective-permute-start.51 = (bf16[144,1024]{1,0:T(8,128)(2,1)S(1)}, bf16[144,1024]{1,0:T(8,128)(2,1)S(1)}, u32[]{:S(2)}, u32[]{:S(2)}) collective-permute-start(bf16[144,1024]{1,0:T(8,128)(2,1)S(1)} %shard_map.200.refs_0_), channel_id=1, source_target_pairs={{0,1},{1,0},{2,3},{3,2},{4,5},{5,4},{6,7},{7,6},{8,9},{9,8},{10,11... | collective-permute-start | bytes 884744 | tf_op jit(solution)/shard_map/ppermute | solution.py:235
  188.7 1.6 collective-permute-start.56
  (14 other events, 114.1 us)

commit v7 on v6

--- a/solution.py
+++ b/solution.py
@@ -147,41 +147,31 @@
         target[:, middle:] = right[...]
 
 
-def ring_add_kernel(count, step, *refs):
-    parts, up_ref, down_ref, me_ref = refs[:4]
-    up_out, down_out, mine, up, down, sems = refs[4:]
+def ring_add_kernel(count, step, up_ref, down_ref, parts, me_ref, up_out, down_out, mine, sems):
     middle = parts.shape[2] // 2
     left, right = slice(0, middle), slice(middle, 2 * middle)
     (up_left, up_right), (down_left, down_right) = target_rows(parts, me_ref, count, step)
-    last = step == count // 2
     copies = [
-        pltpu.make_async_copy(up_ref.at[:, left if last else slice(None)], up.at[:, left if last else slice(None)], sems.at[0]),
-        pltpu.make_async_copy(down_ref.at[:, right if last else slice(None)], down.at[:, right if last else slice(None)], sems.at[1]),
-        pltpu.make_async_copy(up_left, mine.at[0, :, left], sems.at[2]),
-        pltpu.make_async_copy(down_right, mine.at[1, :, right], sems.at[3]),
+        pltpu.make_async_copy(up_left, mine.at[0, :, left], sems.at[0]),
+        pltpu.make_async_copy(down_right, mine.at[1, :, right], sems.at[1]),
     ]
-    if not last:
-        copies.append(pltpu.make_async_copy(up_right, mine.at[0, :, right], sems.at[4]))
-        copies.append(pltpu.make_async_copy(down_left, mine.at[1, :, left], sems.at[5]))
+    up_lanes, down_lanes = left, right
+    if step < count // 2:
+        copies.append(pltpu.make_async_copy(up_right, mine.at[0, :, right], sems.at[2]))
+        copies.append(pltpu.make_async_copy(down_left, mine.at[1, :, left], sems.at[3]))
+        up_lanes = down_lanes = slice(0, 2 * middle)
     finish(start_all(copies))
-    up_lanes, down_lanes = (left, right) if last else (slice(None), slice(None))
-    up_out[...] = (mine[0, :, up_lanes].astype(F32) + up[:, up_lanes].astype(F32)).astype(BF16)
-    down_out[...] = (mine[1, :, down_lanes].astype(F32) + down[:, down_lanes].astype(F32)).astype(BF16)
-
-
-def ring_total_kernel(count, parts, up_ref, down_ref, last_up_ref, last_down_ref, me_ref, out_ref, mine, first, last, sems):
+    up_out[...] = (mine[0, :, up_lanes].astype(F32) + up_ref[:, up_lanes].astype(F32)).astype(BF16)
+    down_out[...] = (mine[1, :, down_lanes].astype(F32) + down_ref[:, down_lanes].astype(F32)).astype(BF16)
+
+
+def ring_total_kernel(count, up_ref, down_ref, last_up_ref, last_down_ref, parts, me_ref, out_ref, mine, sems):
     middle = parts.shape[2] // 2
     left, right = slice(0, middle), slice(middle, 2 * middle)
-    copies = [
-        pltpu.make_async_copy(parts.at[me_ref[1]], mine, sems.at[0]),
-        pltpu.make_async_copy(down_ref.at[:, left], first.at[:, left], sems.at[1]),
-        pltpu.make_async_copy(up_ref.at[:, right], first.at[:, right], sems.at[2]),
-        pltpu.make_async_copy(last_up_ref, last.at[:, left], sems.at[3]),
-        pltpu.make_async_copy(last_down_ref, last.at[:, right], sems.at[4]),
-    ]
-    finish(start_all(copies))
-    total = mine[...].astype(F32) + first[...].astype(F32) + last[...].astype(F32)
-    out_ref[...] = total.astype(BF16)
+    finish(start_all([pltpu.make_async_copy(parts.at[me_ref[1]], mine, sems.at[0])]))
+    for lanes, first, last in ((left, down_ref, last_up_ref), (right, up_ref, last_down_ref)):
+        total = mine[:, lanes].astype(F32) + first[:, lanes].astype(F32) + last[...].astype(F32)
+        out_ref[:, lanes] = total.astype(BF16)
 
 
 class ScatterRing:
@@ -201,10 +191,10 @@
             self.added = call(
                 functools.partial(ring_add_kernel, self.count, self.at),
                 [shaped((rows, width), BF16)] * 2,
-                [],
-                [self.parts, hold(self.up, *others), self.down],
+                [hold(self.up, *others), self.down],
+                [self.parts],
                 [self.me],
-                [pltpu.VMEM((2, rows, columns), BF16)] + [pltpu.VMEM((rows, columns), BF16)] * 2 + [dma(6)],
+                [pltpu.VMEM((2, rows, columns), BF16), dma(4)],
             )
         up, down = self.added
         self.up = lax.ppermute(up, "dp", forward)
@@ -223,10 +213,10 @@
         return call(
             functools.partial(ring_total_kernel, self.count),
             [shaped((rows, columns), BF16)],
-            [],
-            [self.parts, *self.before, hold(self.up, *others), self.down],
+            [*self.before, hold(self.up, *others), self.down],
+            [self.parts],
             [self.me],
-            [pltpu.VMEM((rows, columns), BF16)] * 3 + [dma(5)],
+            [pltpu.VMEM((rows, columns), BF16), dma(1)],
         )[0]
 
 
@@ -916,7 +906,7 @@
     grad_resid, sums_two, *sends = call(
         branch_back_kernel,
         [shaped((tok, width), F32), shaped((8, width), F32)] + [shaped((tok, 2 * part), BF16)] * 4,
-        [hold(own_two, *feed_grads.sums()), resid, cotangent[0], norm_gain],
+        [own_two, resid, cotangent[0], norm_gain],
         [near_two, last_two, out_columns, out_near, out_far, out_last],
         [me],
         [

time: 193 us -> 193 us (level)
  no operation moved by 1% of the time
where the time goes in v7:
time: 193 us; the launch traced here: 192 us
  waiting for transfers between devices  89.5 us (46%)
  Pallas kernels  51.2 us (27%)
  starting transfers between devices  47.5 us (25%)
    pallas_call x26, Pallas kernels, call(): pl.pallas_call(kernel, out_shape=(*outs, *hbm_outs), in_specs=specs, out_...  51.2 us
    ppermute x16, waiting for transfers between devices, step(): self.up = lax.ppermute(up, 'dp', forward)  41.4 us
    ppermute x25, waiting for transfers between devices, swap(): return lax.ppermute(values, 'sp', [(i, i ^ bit) for i in range(count)])  33.3 us
    ppermute x16, starting transfers between devices, step(): self.up = lax.ppermute(up, 'dp', forward)  20.4 us
    ppermute x16, waiting for transfers between devices, step(): self.down = lax.ppermute(down, 'dp', backward)  14.8 us
    ppermute x16, starting transfers between devices, step(): self.down = lax.ppermute(down, 'dp', backward)  13.5 us
    ppermute x25, starting transfers between devices, swap(): return lax.ppermute(values, 'sp', [(i, i ^ bit) for i in range(count)])  13.5 us
  transfers between devices with their start and end apart: 57, of which 39 were waited for; matrix products, arithmetic and copies ran while one was open for 1% of the time, Pallas kernels for 20%

profile of v7, /device:TPU:0, one launch (start us, length us, event | category | flops | bytes accessed | tf_op | source)
XLA Modules:
  0.0 192.3 jit_solution(5643193018681241235)
XLA Ops:
  0.7 1.5 shard_map.178.refs_0_.refs_3_.refs_17_
  2.3 3.1 %collective-permute-start = (bf16[128,1024]{1,0:T(8,128)(2,1)S(1)}, bf16[128,1024]{1,0:T(8,128)(2,1)S(1)}, u32[]{:S(2)}, u32[]{:S(2)}) collective-permute-start(bf16[128,1024]{1,0:T(8,128)(2,1)S(1)} %shard_map.178.refs_0_.refs_3_.refs_17_), channel_id=1, source_target_pairs={{0,8},{8,16},{16,24},{24,28},{28,20},{20,12},{12,4},{4,0},{1,9},{9... | collective-permute-start | bytes 786440 | tf_op jit(solution)/shard_map/ppermute | solution.py:128
  5.4 1.1 pad_maximum_fusion.refs_2_
  6.4 2.0 %collective-permute-start.5 = (bf16[256,1024]{1,0:T(8,128)(2,1)S(1)}, bf16[256,1024]{1,0:T(8,128)(2,1)S(1)}, u32[]{:S(2)}, u32[]{:S(2)}) collective-permute-start(bf16[256,1024]{1,0:T(8,128)(2,1)S(1)} %pad_maximum_fusion.refs_2_), channel_id=1, source_target_pairs={{0,2},{1,3},{2,0},{3,1},{4,6},{5,7},{6,4},{7,5},{8,10},{9,11},{10,... | collective-permute-start | bytes 1572872 | tf_op jit(solution)/shard_map/ppermute | solution.py:225
  8.4 1.7 shard_map.180.refs_5_.refs_26_
  10.2 1.2 shard_map.179
  11.6 1.5 collective-permute-done.1.refs_2_.refs_5_.refs_19_
  13.1 1.6 collective-permute-start.2
  15.2 4.7 %collective-permute-done.5.refs_4_ = bf16[256,1024]{1,0:T(8,128)(2,1)S(1)} collective-permute-done((bf16[256,1024]{1,0:T(8,128)(2,1)S(1)}, bf16[256,1024]{1,0:T(8,128)(2,1)S(1)}, u32[]{:S(2)}, u32[]{:S(2)}) %collective-permute-start.5) | collective-permute-done | bytes 524320 | tf_op jit(solution)/shard_map/ppermute | solution.py:225
  20.0 1.3 collective-permute-done.3.refs_4_.refs_7_.refs_21_
  21.3 1.6 collective-permute-start.7
  23.3 4.3 %collective-permute-done.7.up_ref.refs_5_.refs_8_.refs_22_ = bf16[128,1024]{1,0:T(8,128)(2,1)S(1)} collective-permute-done((bf16[128,1024]{1,0:T(8,128)(2,1)S(1)}, bf16[128,1024]{1,0:T(8,128)(2,1)S(1)}, u32[]{:S(2)}, u32[]{:S(2)}) %collective-permute-start.7) | collective-permute-done | bytes 262176 | tf_op jit(solution)/shard_map/ppermute | solution.py:128
  27.7 1.6 collective-permute-done.8.down_ref.refs_6_.refs_9_.refs_23_
  29.6 1.6 collective-permute-start.9
  31.6 2.9 %collective-permute-done.9.refs_7_.refs_10_.refs_24_ = bf16[64,1024]{1,0:T(8,128)(2,1)S(1)} collective-permute-done((bf16[64,1024]{1,0:T(8,128)(2,1)S(1)}, bf16[64,1024]{1,0:T(8,128)(2,1)S(1)}, u32[]{:S(2)}, u32[]{:S(2)}) %collective-permute-start.9) | collective-permute-done | bytes 131104 | tf_op jit(solution)/shard_map/ppermute | solution.py:128
  34.6 1.6 collective-permute-done.10.refs_8_.refs_11_.refs_25_
  36.8 1.4 collective-permute-start.12
  39.0 1.6 collective-permute-start.17
  40.6 1.5 shard_map.181
  43.1 4.8 %shard_map.184 = (bf16[512,768]{1,0:T(8,128)(2,1)S(1)}, bf16[512,256]{1,0:T(8,128)(2,1)S(1)}, f32[8,256]{1,0:T(8,128)S(1)}) custom-call(bf16[512,1024]{1,0:T(8,128)(2,1)S(1)} %get-tuple-element.113.refs_0_.refs_4_, f32[4,4,128,128]{3,2,1,0:T(8,128)S(1)} %get-tuple-element.102.refs_1_.refs_2_, f32[4,512,128]{2,1,0:T(8,128)S(1)} %get-tuple-element.114.refs_2_.refs_3_, ...), custom_call_target="tpu_custom_call" | custom-call | bytes 16500000 | tf_op jit(solution)/shard_map/pallas_call | solution.py:60
  49.8 1.1 collective-permute-start.23
  50.9 5.8 %collective-permute-done.14.refs_5_.refs_11_ = bf16[512,256]{1,0:T(8,128)(2,1)S(1)} collective-permute-done((bf16[512,256]{1,0:T(8,128)(2,1)S(1)}, bf16[512,256]{1,0:T(8,128)(2,1)S(1)}, u32[]{:S(2)}, u32[]{:S(2)}) %collective-permute-start.14) | collective-permute-done | bytes 262176 | tf_op jit(solution)/shard_map/ppermute | solution.py:225
  56.7 1.5 collective-permute-done.15.refs_6_.refs_12_
  58.2 1.6 shard_map.185
  59.9 3.3 %collective-permute-done.22.refs_8_.refs_29_ = bf16[128,2048]{1,0:T(8,128)(2,1)S(1)} collective-permute-done((bf16[128,2048]{1,0:T(8,128)(2,1)S(1)}, bf16[128,2048]{1,0:T(8,128)(2,1)S(1)}, u32[]{:S(2)}, u32[]{:S(2)}) %collective-permute-start.22) | collective-permute-done | bytes 524320 | tf_op jit(solution)/shard_map/ppermute | solution.py:128
  64.8 1.1 collective-permute-start.25
  65.9 1.5 collective-permute-start.20
  67.4 5.6 %collective-permute-done.20.refs_3_.refs_5_ = bf16[128,1024]{1,0:T(8,128)(2,1)S(1)} collective-permute-done((bf16[128,1024]{1,0:T(8,128)(2,1)S(1)}, bf16[128,1024]{1,0:T(8,128)(2,1)S(1)}, u32[]{:S(2)}, u32[]{:S(2)}) %collective-permute-start.20) | collective-permute-done | bytes 262176 | tf_op jit(solution)/shard_map/ppermute | solution.py:225
  73.5 3.6 %collective-permute-done.24.up_ref.refs_10_.refs_31_ = bf16[128,2048]{1,0:T(8,128)(2,1)S(1)} collective-permute-done((bf16[128,2048]{1,0:T(8,128)(2,1)S(1)}, bf16[128,2048]{1,0:T(8,128)(2,1)S(1)}, u32[]{:S(2)}, u32[]{:S(2)}) %collective-permute-start.24) | collective-permute-done | bytes 524320 | tf_op jit(solution)/shard_map/ppermute | solution.py:128
  77.9 1.0 collective-permute-start.26
  78.9 1.1 collective-permute-start.27
  80.0 4.4 %collective-permute-done.26.refs_12_.refs_33_ = bf16[64,2048]{1,0:T(8,128)(2,1)S(1)} collective-permute-done((bf16[64,2048]{1,0:T(8,128)(2,1)S(1)}, bf16[64,2048]{1,0:T(8,128)(2,1)S(1)}, u32[]{:S(2)}, u32[]{:S(2)}) %collective-permute-start.26) | collective-permute-done | bytes 262176 | tf_op jit(solution)/shard_map/ppermute | solution.py:128
  86.0 7.8 %shard_map.187 = (bf16[128,2048]{1,0:T(8,128)(2,1)S(1)}, bf16[128,2048]{1,0:T(8,128)(2,1)S(1)}, f32[128,1024]{1,0:T(8,128)S(1)}, f32[128,1024]{1,0:T(8,128)S(1)}...) custom-call(bf16[512,1024]{1,0:T(8,128)(2,1)} %copy-done.3, ...), custom_call_target="tpu_custom_call" | custom-call | bytes 23100000 | tf_op jit(solution)/shard_map/pallas_call | solution.py:60
  94.6 1.4 collective-permute-start.31
  96.1 1.6 collective-permute-start.30
  97.6 4.0 %shard_map.189.parts = bf16[8,128,2048]{2,1,0:T(8,128)(2,1)S(1)} custom-call(bf16[512,1024]{1,0:T(8,128)(2,1)S(1)} %get-tuple-element.135.refs_0_, bf16[512,1024]{1,0:T(8,128)(2,1)S(1)} %get-tuple-element.136.refs_1_.refs_8_, bf16[512,1024]{1,0:T(8,128)(2,1)} %copy-done.3, bf16[128,1024]{1,0:T(8,128)(2,1)} %copy-done.5, bf16[128,1024]{1,0:T(8,128)(2,1)} %copy-done.18, ...), custom_call_target="tpu_custom_call" | custom-call | bytes 9900000 | tf_op jit(solution)/shard_map/pallas_call | solution.py:60
  101.6 6.6 %collective-permute-done.28.up_ref = bf16[128,2048]{1,0:T(8,128)(2,1)S(1)} collective-permute-done((bf16[128,2048]{1,0:T(8,128)(2,1)S(1)}, bf16[128,2048]{1,0:T(8,128)(2,1)S(1)}, u32[]{:S(2)}, u32[]{:S(2)}) %collective-permute-start.28) | collective-permute-done | bytes 524320 | tf_op jit(solution)/shard_map/ppermute | solution.py:200
  110.2 1.5 collective-permute-start.36
  111.6 2.4 %shard_map.191 = (f32[128,1024]{1,0:T(8,128)S(1)}, f32[8,1024]{1,0:T(8,128)S(1)}, bf16[128,512]{1,0:T(8,128)(2,1)S(1)}, bf16[128,512]{1,0:T(8,128)(2,1)S(1)}, bf...) custom-call(f32[128,1024]{1,0:T(8,128)S(1)} %get-tuple-element.138.refs_0_, ...), custom_call_target="tpu_custom_call" | custom-call | bytes 8250000 | tf_op jit(solution)/shard_map/pallas_call | solution.py:60
  114.1 1.6 collective-permute-start.34
  116.0 4.5 %collective-permute-done.34.refs_15_ = bf16[128,512]{1,0:T(8,128)(2,1)S(1)} collective-permute-done((bf16[128,512]{1,0:T(8,128)(2,1)S(1)}, bf16[128,512]{1,0:T(8,128)(2,1)S(1)}, u32[]{:S(2)}, u32[]{:S(2)}) %collective-permute-start.34) | collective-permute-done | bytes 131104 | tf_op jit(solution)/shard_map/ppermute | solution.py:225
  120.5 1.9 collective-permute-done.35.refs_16_
  124.9 1.2 collective-permute-start.38
  126.1 9.7 %shard_map.193 = (bf16[8,144,1024]{2,1,0:T(8,128)(2,1)S(1)}, bf16[144,1024]{1,0:T(8,128)(2,1)S(1)}, bf16[144,1024]{1,0:T(8,128)(2,1)S(1)}, f32[8,1024]{1,0:T(8,1...) custom-call(bf16[512,768]{1,0:T(8,128)(2,1)S(1)} %get-tuple-element., ...), custom_call_target="tpu_custom_call" | custom-call | bytes 31020000 | tf_op jit(solution)/shard_map/pallas_call | solution.py:60
  135.9 1.9 %collective-permute-done.37.up_ref = bf16[128,2048]{1,0:T(8,128)(2,1)S(1)} collective-permute-done((bf16[128,2048]{1,0:T(8,128)(2,1)S(1)}, bf16[128,2048]{1,0:T(8,128)(2,1)S(1)}, u32[]{:S(2)}, u32[]{:S(2)}) %collective-permute-start.37) | collective-permute-done | bytes 524320 | tf_op jit(solution)/shard_map/ppermute | solution.py:200
  139.0 1.1 collective-permute-start.41
  141.8 1.1 collective-permute-start.44
  143.0 4.9 %collective-permute-done.39.up_ref = bf16[144,1024]{1,0:T(8,128)(2,1)S(1)} collective-permute-done((bf16[144,1024]{1,0:T(8,128)(2,1)S(1)}, bf16[144,1024]{1,0:T(8,128)(2,1)S(1)}, u32[]{:S(2)}, u32[]{:S(2)}) %collective-permute-start.39) | collective-permute-done | bytes 294944 | tf_op jit(solution)/shard_map/ppermute | solution.py:200
  149.7 1.6 collective-permute-start.42
  151.9 1.2 collective-permute-start.48
  155.2 1.2 collective-permute-start.54
  156.4 3.0 %collective-permute-done.42.up_ref = bf16[144,1024]{1,0:T(8,128)(2,1)S(1)} collective-permute-done((bf16[144,1024]{1,0:T(8,128)(2,1)S(1)}, bf16[144,1024]{1,0:T(8,128)(2,1)S(1)}, u32[]{:S(2)}, u32[]{:S(2)}) %collective-permute-start.42) | collective-permute-done | bytes 294944 | tf_op jit(solution)/shard_map/ppermute | solution.py:200
  160.9 1.6 collective-permute-start.46
  163.0 3.9 %collective-permute-done.48.refs_1_ = bf16[256,1024]{1,0:T(8,128)(2,1)S(1)} collective-permute-done((bf16[256,1024]{1,0:T(8,128)(2,1)S(1)}, bf16[256,1024]{1,0:T(8,128)(2,1)S(1)}, u32[]{:S(2)}, u32[]{:S(2)}) %collective-permute-start.48) | collective-permute-done | bytes 524320 | tf_op jit(solution)/shard_map/ppermute | solution.py:225
  166.8 2.1 %collective-permute-done.46.up_ref = bf16[144,1024]{1,0:T(8,128)(2,1)S(1)} collective-permute-done((bf16[144,1024]{1,0:T(8,128)(2,1)S(1)}, bf16[144,1024]{1,0:T(8,128)(2,1)S(1)}, u32[]{:S(2)}, u32[]{:S(2)}) %collective-permute-start.46) | collective-permute-done | bytes 294944 | tf_op jit(solution)/shard_map/ppermute | solution.py:200
  169.0 1.4 collective-permute-done.47.down_ref
  171.1 1.8 collective-permute-start.49
  173.1 3.1 %collective-permute-done.49.last_up_ref = bf16[144,512]{1,0:T(8,128)(2,1)S(1)} collective-permute-done((bf16[144,512]{1,0:T(8,128)(2,1)S(1)}, bf16[144,512]{1,0:T(8,128)(2,1)S(1)}, u32[]{:S(2)}, u32[]{:S(2)}) %collective-permute-start.49) | collective-permute-done | bytes 147488 | tf_op jit(solution)/shard_map/ppermute | solution.py:200
  176.3 1.7 collective-permute-done.50.last_down_ref
  179.8 1.5 shard_map.201
  181.3 3.1 %shard_map.202 = (f32[128,4096]{1,0:T(8,128)}, f32[512,1024]{1,0:T(8,128)}) custom-call(bf16[128,2048]{1,0:T(8,128)(2,1)S(1)} %shard_map.197.refs_0_, bf16[128,2048]{1,0:T(8,128)(2,1)S(1)} %collective-permute-done.53.refs_1_, bf16[128,2048]{1,0:T(8,128)(2,1)S(1)} %collective-permute-done.54.refs_2_, bf16[128,2048]{1,0:T(8,128)(2,1)S(1)} %collective-permute-done.55.refs_3_, ...), custom_call_target="tpu_custom_call" | custom-call | bytes 9900000 | tf_op jit(solution)/shard_map/pallas_call | solution.py:60
  184.5 3.8 %collective-permute-done.52.refs_2_ = bf16[144,1024]{1,0:T(8,128)(2,1)S(1)} collective-permute-done((bf16[144,1024]{1,0:T(8,128)(2,1)S(1)}, bf16[144,1024]{1,0:T(8,128)(2,1)S(1)}, u32[]{:S(2)}, u32[]{:S(2)}) %collective-permute-start.52) | collective-permute-done | bytes 294944 | tf_op jit(solution)/shard_map/ppermute | solution.py:225
  188.3 1.6 collective-permute-done.56.refs_3_
  189.8 2.3 %shard_map.203 = (f32[128,3072]{1,0:T(8,128)}, f32[128,1024]{1,0:T(8,128)}, f32[2,128]{1,0:T(2,128)}, f32[2,128]{1,0:T(2,128)}, f32[1,64]{1,0:T(1,128)}) custom-call(bf16[144,1024]{1,0:T(8,128)(2,1)S(1)} %shard_map.200.refs_0_, bf16[144,1024]{1,0:T(8,128)(2,1)S(1)} %collective-permute-done.51.refs_1_, bf16[144,1024]{1,0:T(8,128)(2,1)S(1)} %collective-permute-done.52.refs_2_, ...), custom_call_target="tpu_custom_call" | custom-call | bytes 7589999 | tf_op jit(solution)/shard_map/pallas_call | solution.py:60
  (120 shorter events, 28.6 us)
Async XLA Ops:
  2.3 9.3 %collective-permute-start = (bf16[128,1024]{1,0:T(8,128)(2,1)S(1)}, bf16[128,1024]{1,0:T(8,128)(2,1)S(1)}, u32[]{:S(2)}, u32[]{:S(2)}) collective-permute-start(bf16[128,1024]{1,0:T(8,128)(2,1)S(1)} %shard_map.178.refs_0_.refs_3_.refs_17_), channel_id=1, source_target_pairs={{0,8},{8,16},{16,24},{24,28},{28,20},{20,12},{12,4},{4,0},{1,9},{9... | collective-permute-start | bytes 786440 | tf_op jit(solution)/shard_map/ppermute | solution.py:128
  5.4 7.8 %collective-permute-start.1 = (bf16[128,1024]{1,0:T(8,128)(2,1)S(1)}, bf16[128,1024]{1,0:T(8,128)(2,1)S(1)}, u32[]{:S(2)}, u32[]{:S(2)}) collective-permute-start(bf16[128,1024]{1,0:T(8,128)(2,1)S(1)} %shard_map.178.refs_0_.refs_3_.refs_17_), channel_id=1, source_target_pairs={{8,0},{16,8},{24,16},{28,24},{20,28},{12,20},{4,12},{0,4},{9,1},{1... | collective-permute-start | bytes 786440 | tf_op jit(solution)/shard_map/ppermute | solution.py:129
  6.4 13.4 %collective-permute-start.5 = (bf16[256,1024]{1,0:T(8,128)(2,1)S(1)}, bf16[256,1024]{1,0:T(8,128)(2,1)S(1)}, u32[]{:S(2)}, u32[]{:S(2)}) collective-permute-start(bf16[256,1024]{1,0:T(8,128)(2,1)S(1)} %pad_maximum_fusion.refs_2_), channel_id=1, source_target_pairs={{0,2},{1,3},{2,0},{3,1},{4,6},{5,7},{6,4},{7,5},{8,10},{9,11},{10,... | collective-permute-start | bytes 1572872 | tf_op jit(solution)/shard_map/ppermute | solution.py:225
  10.2 31.9 %copy-start.2 = (bf16[128,2048]{1,0:T(8,128)(2,1)}, bf16[128,2048]{1,0:T(8,128)(2,1)S(1)}, u32[]{:S(2)}) copy-start(bf16[128,2048]{1,0:T(8,128)(2,1)S(1)} %shard_map.180.refs_5_.refs_26_) | copy-start | bytes 1572868
  10.2 30.3 %copy-start.7 = (f32[2,1024]{1,0:T(2,128)S(1)}, f32[2,1024]{1,0:T(2,128)}, u32[]{:S(2)}) copy-start(f32[2,1024]{1,0:T(2,128)} %gain_ref.1) | copy-start | bytes 24580
  10.2 30.3 %copy-start.8 = (f32[2,1024]{1,0:T(2,128)S(1)}, f32[2,1024]{1,0:T(2,128)}, u32[]{:S(2)}) copy-start(f32[2,1024]{1,0:T(2,128)} %refs_2_.1) | copy-start | bytes 24580
  13.1 6.9 %collective-permute-start.2 = (bf16[128,1024]{1,0:T(8,128)(2,1)S(1)}, bf16[128,1024]{1,0:T(8,128)(2,1)S(1)}, u32[]{:S(2)}, u32[]{:S(2)}) collective-permute-start(bf16[128,1024]{1,0:T(8,128)(2,1)S(1)} %collective-permute-done.refs_1_.refs_4_.refs_18_), channel_id=1, source_target_pairs={{0,8},{8,16},{16,24},{24,28},{28,20},{20,12},{12,4},{4,0},{1,9},{9... | collective-permute-start | bytes 786440 | tf_op jit(solution)/shard_map/ppermute | solution.py:128
  14.7 6.6 %collective-permute-start.3 = (bf16[128,1024]{1,0:T(8,128)(2,1)S(1)}, bf16[128,1024]{1,0:T(8,128)(2,1)S(1)}, u32[]{:S(2)}, u32[]{:S(2)}) collective-permute-start(bf16[128,1024]{1,0:T(8,128)(2,1)S(1)} %collective-permute-done.1.refs_2_.refs_5_.refs_19_), channel_id=1, source_target_pairs={{8,0},{16,8},{24,16},{28,24},{20,28},{12,20},{4,12},{0,4},{9,1},{1... | collective-permute-start | bytes 786440 | tf_op jit(solution)/shard_map/ppermute | solution.py:129
  21.3 6.4 %collective-permute-start.7 = (bf16[128,1024]{1,0:T(8,128)(2,1)S(1)}, bf16[128,1024]{1,0:T(8,128)(2,1)S(1)}, u32[]{:S(2)}, u32[]{:S(2)}) collective-permute-start(bf16[128,1024]{1,0:T(8,128)(2,1)S(1)} %collective-permute-done.2.refs_3_.refs_6_.refs_20_), channel_id=1, source_target_pairs={{0,8},{8,16},{16,24},{24,28},{28,20},{20,12},{12,4},{4,0},{1,9},{9... | collective-permute-start | bytes 786440 | tf_op jit(solution)/shard_map/ppermute | solution.py:128
  22.9 6.4 %collective-permute-start.8 = (bf16[128,1024]{1,0:T(8,128)(2,1)S(1)}, bf16[128,1024]{1,0:T(8,128)(2,1)S(1)}, u32[]{:S(2)}, u32[]{:S(2)}) collective-permute-start(bf16[128,1024]{1,0:T(8,128)(2,1)S(1)} %collective-permute-done.3.refs_4_.refs_7_.refs_21_), channel_id=1, source_target_pairs={{8,0},{16,8},{24,16},{28,24},{20,28},{12,20},{4,12},{0,4},{9,1},{1... | collective-permute-start | bytes 786440 | tf_op jit(solution)/shard_map/ppermute | solution.py:129
  23.3 17.2 %collective-permute-start.4 = (bf16[256,1024]{1,0:T(8,128)(2,1)S(1)}, bf16[256,1024]{1,0:T(8,128)(2,1)S(1)}, u32[]{:S(2)}, u32[]{:S(2)}) collective-permute-start(bf16[256,1024]{1,0:T(8,128)(2,1)S(1)} %pad_maximum_fusion.refs_2_), channel_id=1, source_target_pairs={{0,1},{1,0},{2,3},{3,2},{4,5},{5,4},{6,7},{7,6},{8,9},{9,8},{10,11... | collective-permute-start | bytes 1572872 | tf_op jit(solution)/shard_map/ppermute | solution.py:225
  29.6 5.0 %collective-permute-start.9 = (bf16[64,1024]{1,0:T(8,128)(2,1)S(1)}, bf16[64,1024]{1,0:T(8,128)(2,1)S(1)}, u32[]{:S(2)}, u32[]{:S(2)}) collective-permute-start(bf16[64,1024]{1,0:T(8,128)(2,1)S(1)} %get-tuple-element.111), channel_id=1, source_target_pairs={{0,8},{8,16},{16,24},{24,28},{28,20},{20,12},{12,4},{4,0},{1,9},{9... | collective-permute-start | bytes 393224 | tf_op jit(solution)/shard_map/ppermute | solution.py:128
  31.1 5.0 %collective-permute-start.10 = (bf16[64,1024]{1,0:T(8,128)(2,1)S(1)}, bf16[64,1024]{1,0:T(8,128)(2,1)S(1)}, u32[]{:S(2)}, u32[]{:S(2)}) collective-permute-start(bf16[64,1024]{1,0:T(8,128)(2,1)S(1)} %get-tuple-element.112), channel_id=1, source_target_pairs={{8,0},{16,8},{24,16},{28,24},{20,28},{12,20},{4,12},{0,4},{9,1},{1... | collective-permute-start | bytes 393224 | tf_op jit(solution)/shard_map/ppermute | solution.py:129
  31.6 8.9 %collective-permute-start.6 = (bf16[256,1024]{1,0:T(8,128)(2,1)S(1)}, bf16[256,1024]{1,0:T(8,128)(2,1)S(1)}, u32[]{:S(2)}, u32[]{:S(2)}) collective-permute-start(bf16[256,1024]{1,0:T(8,128)(2,1)S(1)} %collective-permute-done.5.refs_4_), channel_id=1, source_target_pairs={{0,1},{1,0},{2,3},{3,2},{4,5},{5,4},{6,7},{7,6},{8,9},{9,8},{10,11... | collective-permute-start | bytes 1572872 | tf_op jit(solution)/shard_map/ppermute | solution.py:225
  36.2 11.7 %collective-permute-start.11 = (bf16[128,2048]{1,0:T(8,128)(2,1)S(1)}, bf16[128,2048]{1,0:T(8,128)(2,1)S(1)}, u32[]{:S(2)}, u32[]{:S(2)}) collective-permute-start(bf16[128,2048]{1,0:T(8,128)(2,1)S(1)} %shard_map.180.refs_5_.refs_26_), channel_id=1, source_target_pairs={{0,8},{8,16},{16,24},{24,28},{28,20},{20,12},{12,4},{4,0},{1,9},{9... | collective-permute-start | bytes 1572872 | tf_op jit(solution)/shard_map/ppermute | solution.py:128
  36.8 11.1 %collective-permute-start.12 = (bf16[128,2048]{1,0:T(8,128)(2,1)S(1)}, bf16[128,2048]{1,0:T(8,128)(2,1)S(1)}, u32[]{:S(2)}, u32[]{:S(2)}) collective-permute-start(bf16[128,2048]{1,0:T(8,128)(2,1)S(1)} %shard_map.180.refs_5_.refs_26_), channel_id=1, source_target_pairs={{8,0},{16,8},{24,16},{28,24},{20,28},{12,20},{4,12},{0,4},{9,1},{1... | collective-permute-start | bytes 1572872 | tf_op jit(solution)/shard_map/ppermute | solution.py:129
  39.0 9.9 %collective-permute-start.17 = (bf16[1024,256]{1,0:T(8,128)(2,1)S(1)}, bf16[1024,256]{1,0:T(8,128)(2,1)S(1)}, u32[]{:S(2)}, u32[]{:S(2)}) collective-permute-start(bf16[1024,256]{1,0:T(8,128)(2,1)S(1)} %shard_map.183.refs_7_.refs_6_), channel_id=1, source_target_pairs={{0,2},{1,3},{2,0},{3,1},{4,6},{5,7},{6,4},{7,5},{8,10},{9,11},{10,... | collective-permute-start | bytes 1572872 | tf_op jit(solution)/shard_map/ppermute | solution.py:225
  40.5 10.3 %collective-permute-start.16 = (bf16[1024,256]{1,0:T(8,128)(2,1)S(1)}, bf16[1024,256]{1,0:T(8,128)(2,1)S(1)}, u32[]{:S(2)}, u32[]{:S(2)}) collective-permute-start(bf16[1024,256]{1,0:T(8,128)(2,1)S(1)} %shard_map.183.refs_7_.refs_6_), channel_id=1, source_target_pairs={{0,1},{1,0},{2,3},{3,2},{4,5},{5,4},{6,7},{7,6},{8,9},{9,8},{10,11... | collective-permute-start | bytes 1572872 | tf_op jit(solution)/shard_map/ppermute | solution.py:225
  47.9 30.0 %copy-start.12 = (bf16[128,2048]{1,0:T(8,128)(2,1)}, bf16[128,2048]{1,0:T(8,128)(2,1)S(1)}, u32[]{:S(2)}) copy-start(bf16[128,2048]{1,0:T(8,128)(2,1)S(1)} %collective-permute-done.11.refs_6_.refs_27_) | copy-start | bytes 1572868
  47.9 30.0 %copy-start.13 = (bf16[128,2048]{1,0:T(8,128)(2,1)}, bf16[128,2048]{1,0:T(8,128)(2,1)S(1)}, u32[]{:S(2)}) copy-start(bf16[128,2048]{1,0:T(8,128)(2,1)S(1)} %collective-permute-done.12.refs_7_.refs_28_) | copy-start | bytes 1572868
  47.9 8.8 %collective-permute-start.14 = (bf16[512,256]{1,0:T(8,128)(2,1)S(1)}, bf16[512,256]{1,0:T(8,128)(2,1)S(1)}, u32[]{:S(2)}, u32[]{:S(2)}) collective-permute-start(bf16[512,256]{1,0:T(8,128)(2,1)S(1)} %get-tuple-element.120.refs_3_.refs_9_), channel_id=1, source_target_pairs={{0,2},{1,3},{2,0},{3,1},{4,6},{5,7},{6,4},{7,5},{8,10},{9,11},{10,... | collective-permute-start | bytes 786440 | tf_op jit(solution)/shard_map/ppermute | solution.py:225
  48.8 9.4 %collective-permute-start.18 = (bf16[1024,256]{1,0:T(8,128)(2,1)S(1)}, bf16[1024,256]{1,0:T(8,128)(2,1)S(1)}, u32[]{:S(2)}, u32[]{:S(2)}) collective-permute-start(bf16[1024,256]{1,0:T(8,128)(2,1)S(1)} %collective-permute-done.17.refs_9_.refs_8_), channel_id=1, source_target_pairs={{0,1},{1,0},{2,3},{3,2},{4,5},{5,4},{6,7},{7,6},{8,9},{9,8},{10,11... | collective-permute-start | bytes 1572872 | tf_op jit(solution)/shard_map/ppermute | solution.py:225
  48.8 14.3 %collective-permute-start.22 = (bf16[128,2048]{1,0:T(8,128)(2,1)S(1)}, bf16[128,2048]{1,0:T(8,128)(2,1)S(1)}, u32[]{:S(2)}, u32[]{:S(2)}) collective-permute-start(bf16[128,2048]{1,0:T(8,128)(2,1)S(1)} %collective-permute-done.11.refs_6_.refs_27_), channel_id=1, source_target_pairs={{0,8},{8,16},{16,24},{24,28},{28,20},{20,12},{12,4},{4,0},{1,9},{9... | collective-permute-start | bytes 1572872 | tf_op jit(solution)/shard_map/ppermute | solution.py:128
  49.8 14.1 %collective-permute-start.23 = (bf16[128,2048]{1,0:T(8,128)(2,1)S(1)}, bf16[128,2048]{1,0:T(8,128)(2,1)S(1)}, u32[]{:S(2)}, u32[]{:S(2)}) collective-permute-start(bf16[128,2048]{1,0:T(8,128)(2,1)S(1)} %collective-permute-done.12.refs_7_.refs_28_), channel_id=1, source_target_pairs={{8,0},{16,8},{24,16},{28,24},{20,28},{12,20},{4,12},{0,4},{9,1},{1... | collective-permute-start | bytes 1572872 | tf_op jit(solution)/shard_map/ppermute | solution.py:129
  50.9 5.8 %collective-permute-start.13 = (bf16[512,256]{1,0:T(8,128)(2,1)S(1)}, bf16[512,256]{1,0:T(8,128)(2,1)S(1)}, u32[]{:S(2)}, u32[]{:S(2)}) collective-permute-start(bf16[512,256]{1,0:T(8,128)(2,1)S(1)} %get-tuple-element.120.refs_3_.refs_9_), channel_id=1, source_target_pairs={{0,1},{1,0},{2,3},{3,2},{4,5},{5,4},{6,7},{7,6},{8,9},{9,8},{10,11... | collective-permute-start | bytes 786440 | tf_op jit(solution)/shard_map/ppermute | solution.py:225
  56.7 1.5 collective-permute-start.15
  59.9 25.4 %copy-start.5 = (bf16[128,1024]{1,0:T(8,128)(2,1)}, bf16[128,1024]{1,0:T(8,128)(2,1)S(1)}, u32[]{:S(2)}) copy-start(bf16[128,1024]{1,0:T(8,128)(2,1)S(1)} %get-tuple-element.121.refs_1_.refs_3_) | copy-start | bytes 786436
  63.2 22.1 %copy-start.14 = (bf16[128,2048]{1,0:T(8,128)(2,1)}, bf16[128,2048]{1,0:T(8,128)(2,1)S(1)}, u32[]{:S(2)}) copy-start(bf16[128,2048]{1,0:T(8,128)(2,1)S(1)} %collective-permute-done.22.refs_8_.refs_29_) | copy-start | bytes 1572868
  63.9 13.2 %collective-permute-start.24 = (bf16[128,2048]{1,0:T(8,128)(2,1)S(1)}, bf16[128,2048]{1,0:T(8,128)(2,1)S(1)}, u32[]{:S(2)}, u32[]{:S(2)}) collective-permute-start(bf16[128,2048]{1,0:T(8,128)(2,1)S(1)} %collective-permute-done.22.refs_8_.refs_29_), channel_id=1, source_target_pairs={{0,8},{8,16},{16,24},{24,28},{28,20},{20,12},{12,4},{4,0},{1,9},{9... | collective-permute-start | bytes 1572872 | tf_op jit(solution)/shard_map/ppermute | solution.py:128
  64.8 13.0 %collective-permute-start.25 = (bf16[128,2048]{1,0:T(8,128)(2,1)S(1)}, bf16[128,2048]{1,0:T(8,128)(2,1)S(1)}, u32[]{:S(2)}, u32[]{:S(2)}) collective-permute-start(bf16[128,2048]{1,0:T(8,128)(2,1)S(1)} %collective-permute-done.23.refs_9_.refs_30_), channel_id=1, source_target_pairs={{8,0},{16,8},{24,16},{28,24},{20,28},{12,20},{4,12},{0,4},{9,1},{1... | collective-permute-start | bytes 1572872 | tf_op jit(solution)/shard_map/ppermute | solution.py:129
  65.9 7.1 %collective-permute-start.20 = (bf16[128,1024]{1,0:T(8,128)(2,1)S(1)}, bf16[128,1024]{1,0:T(8,128)(2,1)S(1)}, u32[]{:S(2)}, u32[]{:S(2)}) collective-permute-start(bf16[128,1024]{1,0:T(8,128)(2,1)S(1)} %get-tuple-element.121.refs_1_.refs_3_), channel_id=1, source_target_pairs={{0,2},{1,3},{2,0},{3,1},{4,6},{5,7},{6,4},{7,5},{8,10},{9,11},{10,... | collective-permute-start | bytes 786440 | tf_op jit(solution)/shard_map/ppermute | solution.py:225
  73.0 4.9 %collective-permute-start.21 = (bf16[128,1024]{1,0:T(8,128)(2,1)S(1)}, bf16[128,1024]{1,0:T(8,128)(2,1)S(1)}, u32[]{:S(2)}, u32[]{:S(2)}) collective-permute-start(bf16[128,1024]{1,0:T(8,128)(2,1)S(1)} %collective-permute-done.20.refs_3_.refs_5_), channel_id=1, source_target_pairs={{0,1},{1,0},{2,3},{3,2},{4,5},{5,4},{6,7},{7,6},{8,9},{9,8},{10,11... | collective-permute-start | bytes 786440 | tf_op jit(solution)/shard_map/ppermute | solution.py:225
  73.0 7.0 %collective-permute-start.19 = (bf16[128,1024]{1,0:T(8,128)(2,1)S(1)}, bf16[128,1024]{1,0:T(8,128)(2,1)S(1)}, u32[]{:S(2)}, u32[]{:S(2)}) collective-permute-start(bf16[128,1024]{1,0:T(8,128)(2,1)S(1)} %get-tuple-element.121.refs_1_.refs_3_), channel_id=1, source_target_pairs={{0,1},{1,0},{2,3},{3,2},{4,5},{5,4},{6,7},{7,6},{8,9},{9,8},{10,11... | collective-permute-start | bytes 786440 | tf_op jit(solution)/shard_map/ppermute | solution.py:225
  77.9 6.5 %collective-permute-start.26 = (bf16[64,2048]{1,0:T(8,128)(2,1)S(1)}, bf16[64,2048]{1,0:T(8,128)(2,1)S(1)}, u32[]{:S(2)}, u32[]{:S(2)}) collective-permute-start(bf16[64,2048]{1,0:T(8,128)(2,1)S(1)} %get-tuple-element.128), channel_id=1, source_target_pairs={{0,8},{8,16},{16,24},{24,28},{28,20},{20,12},{12,4},{4,0},{1,9},{9... | collective-permute-start | bytes 786440 | tf_op jit(solution)/shard_map/ppermute | solution.py:128
  78.9 6.4 %collective-permute-start.27 = (bf16[64,2048]{1,0:T(8,128)(2,1)S(1)}, bf16[64,2048]{1,0:T(8,128)(2,1)S(1)}, u32[]{:S(2)}, u32[]{:S(2)}) collective-permute-start(bf16[64,2048]{1,0:T(8,128)(2,1)S(1)} %get-tuple-element.129), channel_id=1, source_target_pairs={{8,0},{16,8},{24,16},{28,24},{20,28},{12,20},{4,12},{0,4},{9,1},{1... | collective-permute-start | bytes 786440 | tf_op jit(solution)/shard_map/ppermute | solution.py:129
  93.8 2.2 %collective-permute-start.29 = (bf16[256,1024]{1,0:T(8,128)(2,1)S(1)}, bf16[256,1024]{1,0:T(8,128)(2,1)S(1)}, u32[]{:S(2)}, u32[]{:S(2)}) collective-permute-start(bf16[256,1024]{1,0:T(8,128)(2,1)S(1)} %get-tuple-element.132), channel_id=1, source_target_pairs={{0,1},{1,0},{2,3},{3,2},{4,5},{5,4},{6,7},{7,6},{8,9},{9,8},{10,11... | collective-permute-start | bytes 1572872 | tf_op jit(solution)/shard_map/ppermute | solution.py:225
  93.9 14.3 %collective-permute-start.28 = (bf16[128,2048]{1,0:T(8,128)(2,1)S(1)}, bf16[128,2048]{1,0:T(8,128)(2,1)S(1)}, u32[]{:S(2)}, u32[]{:S(2)}) collective-permute-start(bf16[128,2048]{1,0:T(8,128)(2,1)S(1)} %get-tuple-element.130), channel_id=1, source_target_pairs={{0,8},{8,16},{16,24},{24,28},{28,20},{20,12},{12,4},{4,0},{1,9},{9... | collective-permute-start | bytes 1572872 | tf_op jit(solution)/shard_map/ppermute | solution.py:200
  94.6 14.0 %collective-permute-start.31 = (bf16[128,2048]{1,0:T(8,128)(2,1)S(1)}, bf16[128,2048]{1,0:T(8,128)(2,1)S(1)}, u32[]{:S(2)}, u32[]{:S(2)}) collective-permute-start(bf16[128,2048]{1,0:T(8,128)(2,1)S(1)} %get-tuple-element.134), channel_id=1, source_target_pairs={{8,0},{16,8},{24,16},{28,24},{20,28},{12,20},{4,12},{0,4},{9,1},{1... | collective-permute-start | bytes 1572872 | tf_op jit(solution)/shard_map/ppermute | solution.py:201
  96.1 12.2 %collective-permute-start.30 = (bf16[128,1024]{1,0:T(8,128)(2,1)S(1)}, bf16[128,1024]{1,0:T(8,128)(2,1)S(1)}, u32[]{:S(2)}, u32[]{:S(2)}) collective-permute-start(bf16[128,1024]{1,0:T(8,128)(2,1)S(1)} %shard_map.188), channel_id=1, source_target_pairs={{0,2},{1,3},{2,0},{3,1},{4,6},{5,7},{6,4},{7,5},{8,10},{9,11},{10,... | collective-permute-start | bytes 786440 | tf_op jit(solution)/shard_map/ppermute | solution.py:225
  109.6 13.2 %collective-permute-start.32 = (bf16[128,2048]{1,0:T(8,128)(2,1)S(1)}, bf16[128,2048]{1,0:T(8,128)(2,1)S(1)}, u32[]{:S(2)}, u32[]{:S(2)}) collective-permute-start(bf16[128,2048]{1,0:T(8,128)(2,1)S(1)} %get-tuple-element.137), channel_id=1, source_target_pairs={{0,8},{8,16},{16,24},{24,28},{28,20},{20,12},{12,4},{4,0},{1,9},{9... | collective-permute-start | bytes 1572872 | tf_op jit(solution)/shard_map/ppermute | solution.py:200
  110.2 13.0 %collective-permute-start.36 = (bf16[128,2048]{1,0:T(8,128)(2,1)S(1)}, bf16[128,2048]{1,0:T(8,128)(2,1)S(1)}, u32[]{:S(2)}, u32[]{:S(2)}) collective-permute-start(bf16[128,2048]{1,0:T(8,128)(2,1)S(1)} %get-tuple-element.144), channel_id=1, source_target_pairs={{8,0},{16,8},{24,16},{28,24},{20,28},{12,20},{4,12},{0,4},{9,1},{1... | collective-permute-start | bytes 1572872 | tf_op jit(solution)/shard_map/ppermute | solution.py:201
  114.1 1.9 %collective-permute-start.33 = (bf16[128,512]{1,0:T(8,128)(2,1)S(1)}, bf16[128,512]{1,0:T(8,128)(2,1)S(1)}, u32[]{:S(2)}, u32[]{:S(2)}) collective-permute-start(bf16[128,512]{1,0:T(8,128)(2,1)S(1)} %get-tuple-element.140), channel_id=1, source_target_pairs={{0,1},{1,0},{2,3},{3,2},{4,5},{5,4},{6,7},{7,6},{8,9},{9,8},{10,11... | collective-permute-start | bytes 393224 | tf_op jit(solution)/shard_map/ppermute | solution.py:225
  114.1 6.4 %collective-permute-start.34 = (bf16[128,512]{1,0:T(8,128)(2,1)S(1)}, bf16[128,512]{1,0:T(8,128)(2,1)S(1)}, u32[]{:S(2)}, u32[]{:S(2)}) collective-permute-start(bf16[128,512]{1,0:T(8,128)(2,1)S(1)} %get-tuple-element.141), channel_id=1, source_target_pairs={{0,2},{1,3},{2,0},{3,1},{4,6},{5,7},{6,4},{7,5},{8,10},{9,11},{10,... | collective-permute-start | bytes 393224 | tf_op jit(solution)/shard_map/ppermute | solution.py:225
  115.7 6.7 %collective-permute-start.35 = (bf16[128,512]{1,0:T(8,128)(2,1)S(1)}, bf16[128,512]{1,0:T(8,128)(2,1)S(1)}, u32[]{:S(2)}, u32[]{:S(2)}) collective-permute-start(bf16[128,512]{1,0:T(8,128)(2,1)S(1)} %get-tuple-element.142), channel_id=1, source_target_pairs={{0,3},{1,2},{2,1},{3,0},{4,7},{5,6},{6,5},{7,4},{8,11},{9,10},{10,... | collective-permute-start | bytes 393224 | tf_op jit(solution)/shard_map/ppermute | solution.py:225
  124.0 13.8 %collective-permute-start.37 = (bf16[128,2048]{1,0:T(8,128)(2,1)S(1)}, bf16[128,2048]{1,0:T(8,128)(2,1)S(1)}, u32[]{:S(2)}, u32[]{:S(2)}) collective-permute-start(bf16[128,2048]{1,0:T(8,128)(2,1)S(1)} %get-tuple-element.145), channel_id=1, source_target_pairs={{0,8},{8,16},{16,24},{24,28},{28,20},{20,12},{12,4},{4,0},{1,9},{9... | collective-permute-start | bytes 1572872 | tf_op jit(solution)/shard_map/ppermute | solution.py:200
  124.9 13.1 %collective-permute-start.38 = (bf16[128,2048]{1,0:T(8,128)(2,1)S(1)}, bf16[128,2048]{1,0:T(8,128)(2,1)S(1)}, u32[]{:S(2)}, u32[]{:S(2)}) collective-permute-start(bf16[128,2048]{1,0:T(8,128)(2,1)S(1)} %get-tuple-element.146), channel_id=1, source_target_pairs={{8,0},{16,8},{24,16},{28,24},{20,28},{12,20},{4,12},{0,4},{9,1},{1... | collective-permute-start | bytes 1572872 | tf_op jit(solution)/shard_map/ppermute | solution.py:201
  138.1 9.8 %collective-permute-start.40 = (bf16[512,1024]{1,0:T(8,128)(2,1)S(1)}, bf16[512,1024]{1,0:T(8,128)(2,1)S(1)}, u32[]{:S(2)}, u32[]{:S(2)}) collective-permute-start(bf16[512,1024]{1,0:T(8,128)(2,1)S(1)} %get-tuple-element.159), channel_id=1, source_target_pairs={{0,1},{1,0},{2,3},{3,2},{4,5},{5,4},{6,7},{7,6},{8,9},{9,8},{10,11... | collective-permute-start | bytes 3145736 | tf_op jit(solution)/shard_map/ppermute | solution.py:225
  138.1 9.8 %collective-permute-start.39 = (bf16[144,1024]{1,0:T(8,128)(2,1)S(1)}, bf16[144,1024]{1,0:T(8,128)(2,1)S(1)}, u32[]{:S(2)}, u32[]{:S(2)}) collective-permute-start(bf16[144,1024]{1,0:T(8,128)(2,1)S(1)} %get-tuple-element.155), channel_id=1, source_target_pairs={{0,8},{8,16},{16,24},{24,28},{28,20},{20,12},{12,4},{4,0},{1,9},{9... | collective-permute-start | bytes 884744 | tf_op jit(solution)/shard_map/ppermute | solution.py:200
  139.0 9.8 %collective-permute-start.41 = (bf16[144,1024]{1,0:T(8,128)(2,1)S(1)}, bf16[144,1024]{1,0:T(8,128)(2,1)S(1)}, u32[]{:S(2)}, u32[]{:S(2)}) collective-permute-start(bf16[144,1024]{1,0:T(8,128)(2,1)S(1)} %get-tuple-element.161), channel_id=1, source_target_pairs={{8,0},{16,8},{24,16},{28,24},{20,28},{12,20},{4,12},{0,4},{9,1},{1... | collective-permute-start | bytes 884744 | tf_op jit(solution)/shard_map/ppermute | solution.py:201
  140.9 12.6 %collective-permute-start.43 = (bf16[128,1024]{1,0:T(8,128)(2,1)S(1)}, bf16[128,1024]{1,0:T(8,128)(2,1)S(1)}, u32[]{:S(2)}, u32[]{:S(2)}) collective-permute-start(bf16[128,1024]{1,0:T(8,128)(2,1)S(1)} %get-tuple-element.156), channel_id=1, source_target_pairs={{0,8},{8,16},{16,24},{24,28},{28,20},{20,12},{12,4},{4,0},{1,9},{9... | collective-permute-start | bytes 786440 | tf_op jit(solution)/shard_map/ppermute | solution.py:200
  141.8 12.6 %collective-permute-start.44 = (bf16[128,1024]{1,0:T(8,128)(2,1)S(1)}, bf16[128,1024]{1,0:T(8,128)(2,1)S(1)}, u32[]{:S(2)}, u32[]{:S(2)}) collective-permute-start(bf16[128,1024]{1,0:T(8,128)(2,1)S(1)} %get-tuple-element.157), channel_id=1, source_target_pairs={{8,0},{16,8},{24,16},{28,24},{20,28},{12,20},{4,12},{0,4},{9,1},{1... | collective-permute-start | bytes 786440 | tf_op jit(solution)/shard_map/ppermute | solution.py:201
  149.7 9.8 %collective-permute-start.42 = (bf16[144,1024]{1,0:T(8,128)(2,1)S(1)}, bf16[144,1024]{1,0:T(8,128)(2,1)S(1)}, u32[]{:S(2)}, u32[]{:S(2)}) collective-permute-start(bf16[144,1024]{1,0:T(8,128)(2,1)S(1)} %get-tuple-element.163), channel_id=1, source_target_pairs={{0,8},{8,16},{16,24},{24,28},{28,20},{20,12},{12,4},{4,0},{1,9},{9... | collective-permute-start | bytes 884744 | tf_op jit(solution)/shard_map/ppermute | solution.py:200
  151.3 8.8 %collective-permute-start.45 = (bf16[144,1024]{1,0:T(8,128)(2,1)S(1)}, bf16[144,1024]{1,0:T(8,128)(2,1)S(1)}, u32[]{:S(2)}, u32[]{:S(2)}) collective-permute-start(bf16[144,1024]{1,0:T(8,128)(2,1)S(1)} %get-tuple-element.165), channel_id=1, source_target_pairs={{8,0},{16,8},{24,16},{28,24},{20,28},{12,20},{4,12},{0,4},{9,1},{1... | collective-permute-start | bytes 884744 | tf_op jit(solution)/shard_map/ppermute | solution.py:201
  151.9 14.9 %collective-permute-start.48 = (bf16[256,1024]{1,0:T(8,128)(2,1)S(1)}, bf16[256,1024]{1,0:T(8,128)(2,1)S(1)}, u32[]{:S(2)}, u32[]{:S(2)}) collective-permute-start(bf16[256,1024]{1,0:T(8,128)(2,1)S(1)} %shard_map.196), channel_id=1, source_target_pairs={{0,2},{1,3},{2,0},{3,1},{4,6},{5,7},{6,4},{7,5},{8,10},{9,11},{10,... | collective-permute-start | bytes 1572872 | tf_op jit(solution)/shard_map/ppermute | solution.py:225
  155.2 23.5 %collective-permute-start.54 = (bf16[128,2048]{1,0:T(8,128)(2,1)S(1)}, bf16[128,2048]{1,0:T(8,128)(2,1)S(1)}, u32[]{:S(2)}, u32[]{:S(2)}) collective-permute-start(bf16[128,2048]{1,0:T(8,128)(2,1)S(1)} %shard_map.197.refs_0_), channel_id=1, source_target_pairs={{0,2},{1,3},{2,0},{3,1},{4,6},{5,7},{6,4},{7,5},{8,10},{9,11},{10,... | collective-permute-start | bytes 1572872 | tf_op jit(solution)/shard_map/ppermute | solution.py:225
  160.9 8.1 %collective-permute-start.46 = (bf16[144,1024]{1,0:T(8,128)(2,1)S(1)}, bf16[144,1024]{1,0:T(8,128)(2,1)S(1)}, u32[]{:S(2)}, u32[]{:S(2)}) collective-permute-start(bf16[144,1024]{1,0:T(8,128)(2,1)S(1)} %get-tuple-element.169), channel_id=1, source_target_pairs={{0,8},{8,16},{16,24},{24,28},{28,20},{20,12},{12,4},{4,0},{1,9},{9... | collective-permute-start | bytes 884744 | tf_op jit(solution)/shard_map/ppermute | solution.py:200
  162.5 7.8 %collective-permute-start.47 = (bf16[144,1024]{1,0:T(8,128)(2,1)S(1)}, bf16[144,1024]{1,0:T(8,128)(2,1)S(1)}, u32[]{:S(2)}, u32[]{:S(2)}) collective-permute-start(bf16[144,1024]{1,0:T(8,128)(2,1)S(1)} %get-tuple-element.170), channel_id=1, source_target_pairs={{8,0},{16,8},{24,16},{28,24},{20,28},{12,20},{4,12},{0,4},{9,1},{1... | collective-permute-start | bytes 884744 | tf_op jit(solution)/shard_map/ppermute | solution.py:201
  171.1 5.2 %collective-permute-start.49 = (bf16[144,512]{1,0:T(8,128)(2,1)S(1)}, bf16[144,512]{1,0:T(8,128)(2,1)S(1)}, u32[]{:S(2)}, u32[]{:S(2)}) collective-permute-start(bf16[144,512]{1,0:T(8,128)(2,1)S(1)} %get-tuple-element.172), channel_id=1, source_target_pairs={{0,8},{8,16},{16,24},{24,28},{28,20},{20,12},{12,4},{4,0},{1,9},{9... | collective-permute-start | bytes 442376 | tf_op jit(solution)/shard_map/ppermute | solution.py:200
  172.9 5.1 %collective-permute-start.50 = (bf16[144,512]{1,0:T(8,128)(2,1)S(1)}, bf16[144,512]{1,0:T(8,128)(2,1)S(1)}, u32[]{:S(2)}, u32[]{:S(2)}) collective-permute-start(bf16[144,512]{1,0:T(8,128)(2,1)S(1)} %get-tuple-element.173), channel_id=1, source_target_pairs={{8,0},{16,8},{24,16},{28,24},{20,28},{12,20},{4,12},{0,4},{9,1},{1... | collective-permute-start | bytes 442376 | tf_op jit(solution)/shard_map/ppermute | solution.py:201
  173.1 8.2 %collective-permute-start.53 = (bf16[128,2048]{1,0:T(8,128)(2,1)S(1)}, bf16[128,2048]{1,0:T(8,128)(2,1)S(1)}, u32[]{:S(2)}, u32[]{:S(2)}) collective-permute-start(bf16[128,2048]{1,0:T(8,128)(2,1)S(1)} %shard_map.197.refs_0_), channel_id=1, source_target_pairs={{0,1},{1,0},{2,3},{3,2},{4,5},{5,4},{6,7},{7,6},{8,9},{9,8},{10,11... | collective-permute-start | bytes 1572872 | tf_op jit(solution)/shard_map/ppermute | solution.py:225
  178.8 2.6 %collective-permute-start.55 = (bf16[128,2048]{1,0:T(8,128)(2,1)S(1)}, bf16[128,2048]{1,0:T(8,128)(2,1)S(1)}, u32[]{:S(2)}, u32[]{:S(2)}) collective-permute-start(bf16[128,2048]{1,0:T(8,128)(2,1)S(1)} %collective-permute-done.54.refs_2_), channel_id=1, source_target_pairs={{0,1},{1,0},{2,3},{3,2},{4,5},{5,4},{6,7},{7,6},{8,9},{9,8},{10,11... | collective-permute-start | bytes 1572872 | tf_op jit(solution)/shard_map/ppermute | solution.py:225
  178.8 9.4 %collective-permute-start.52 = (bf16[144,1024]{1,0:T(8,128)(2,1)S(1)}, bf16[144,1024]{1,0:T(8,128)(2,1)S(1)}, u32[]{:S(2)}, u32[]{:S(2)}) collective-permute-start(bf16[144,1024]{1,0:T(8,128)(2,1)S(1)} %shard_map.200.refs_0_), channel_id=1, source_target_pairs={{0,2},{1,3},{2,0},{3,1},{4,6},{5,7},{6,4},{7,5},{8,10},{9,11},{10,... | collective-permute-start | bytes 884744 | tf_op jit(solution)/shard_map/ppermute | solution.py:225
  179.6 8.6 %collective-permute-start.51 = (bf16[144,1024]{1,0:T(8,128)(2,1)S(1)}, bf16[144,1024]{1,0:T(8,128)(2,1)S(1)}, u32[]{:S(2)}, u32[]{:S(2)}) collective-permute-start(bf16[144,1024]{1,0:T(8,128)(2,1)S(1)} %shard_map.200.refs_0_), channel_id=1, source_target_pairs={{0,1},{1,0},{2,3},{3,2},{4,5},{5,4},{6,7},{7,6},{8,9},{9,8},{10,11... | collective-permute-start | bytes 884744 | tf_op jit(solution)/shard_map/ppermute | solution.py:225
  188.3 1.6 collective-permute-start.56
  (14 other events, 114.0 us)
